TPU v7x, 32 devices: a whole 2x2x4 slice. The times are simulated.
32 devices in a mesh: seq: 4 (over y, x), dp: 2 (over core), mp: 4 (over z).
Axes of the slice: x: 2, y: 2, z: 4, core: 2. Of those that a mesh axis runs over, the one named last changes fastest.
Arguments:
- inputs: bfloat16 [8, 512, 768], P('dp', 'seq'), may hold values from -6 to 6
- lengths: int32 [8], P('dp'), may hold values from 40 to 512, as said below
- query_weight: bfloat16 [768, 768], P(None, 'mp'), may hold values from -0.21875 to 0.21875
- query_bias: float32 [768], P('mp'), may hold values from -3 to 3
- key_weight: bfloat16 [768, 768], P(None, 'mp'), may hold values from -0.21875 to 0.21875
- value_weight: bfloat16 [768, 768], P(None, 'mp'), may hold values from -0.21875 to 0.21875
- value_bias: float32 [768], P('mp'), may hold values from -3 to 3
- rel_weight: float32 [12, 8], P('mp'), may hold values from -6 to 6
- out_weight: bfloat16 [768, 768], P('mp'), may hold values from -0.875 to 0.875
- out_bias: float32 [768], replicated, may hold values from -1.75 to 1.75
- attn_gain: float32 [768], replicated, may hold values from 0.5 to 1.5
- attn_shift: float32 [768], replicated, may hold values from -1.75 to 1.75
- up_weight: bfloat16 [768, 3072], P(None, 'mp'), may hold values from -0.21875 to 0.21875
- up_bias: float32 [3072], P('mp'), may hold values from -3 to 3
- down_weight: bfloat16 [3072, 768], P('mp'), may hold values from -0.109375 to 0.109375
- down_bias: float32 [768], replicated, may hold values from -1.75 to 1.75
- ffn_gain: float32 [768], replicated, may hold values from 0.5 to 1.5
- ffn_shift: float32 [768], replicated, may hold values from -1.75 to 1.75
- cotangent: bfloat16 [8, 256, 768], P('dp', 'seq'), may hold values from -6 to 6
Outputs:
- output: bfloat16 [8, 256, 768], P('dp', 'seq')
- input_grad: float32 [8, 512, 768], P('dp', 'seq')
- query_weight_grad: float32 [768, 768], P(None, 'mp')
- query_bias_grad: float32 [768], P('mp')
- key_weight_grad: float32 [768, 768], P(None, 'mp')
- value_weight_grad: float32 [768, 768], P(None, 'mp')
- value_bias_grad: float32 [768], P('mp')
- rel_weight_grad: float32 [12, 8], P('mp')
- out_weight_grad: float32 [768, 768], P('mp')
- out_bias_grad: float32 [768], replicated
- attn_gain_grad: float32 [768], replicated
- attn_shift_grad: float32 [768], replicated
- up_weight_grad: float32 [768, 3072], P(None, 'mp')
- up_bias_grad: float32 [3072], P('mp')
- down_weight_grad: float32 [3072, 768], P('mp')
- down_bias_grad: float32 [768], replicated
- ffn_gain_grad: float32 [768], replicated
- ffn_shift_grad: float32 [768], replicated
Inputs may be any that keep to these rules, and one draw needn't show every extreme that they name: `lengths`: the number of valid tokens of each sentence, which are its first ones; in each aligned block of 4 sentences one, drawn from the seed, has all 512.
All inputs are finite; a program needn't handle non-finite values.
Results may differ from a plain program's by a relative error of at most 0.019.
Values may be sent and summed in bfloat16 or wider, within the bound.
No kernel may reach another device: no remote copies, remote signals or barrier semaphores. Data moves between devices by JAX's collectives and lax.ppermute only.
A program may use at most 64 MiB of HBM per device.

v0:
```python
import functools

import jax
import jax.numpy as jnp
from jax import lax
from jax.experimental import pallas as pl
from jax.experimental.pallas import tpu as pltpu
from jax.sharding import PartitionSpec as P

BASES = 8
EPSILON = 1e-05
MASKED_SCORE = -1e30
F32 = jnp.float32
LOW = jnp.bfloat16
SMALL_ROWS = 16
MIB = 1024 * 1024


def f32(*shape):
    return jax.ShapeDtypeStruct(shape, F32)


def low(*shape):
    return jax.ShapeDtypeStruct(shape, LOW)


def kernel(body, outs, args, smem=0, scratch=(), micros=1.0, limit=16, hbm=()):
    in_specs = [pl.BlockSpec(memory_space=pltpu.SMEM)] * smem
    in_specs += [pl.BlockSpec(memory_space=pltpu.VMEM)] * (len(args) - smem)
    whole = pl.BlockSpec(memory_space=pltpu.VMEM)
    if isinstance(outs, list):
        out_specs = [pl.BlockSpec(memory_space=pltpu.HBM) if n in hbm else whole for n in range(len(outs))]
    else:
        out_specs = whole
    return pl.pallas_call(
        body,
        out_shape=outs,
        in_specs=in_specs,
        out_specs=out_specs,
        scratch_shapes=list(scratch),
        compiler_params=pltpu.CompilerParams(vmem_limit_bytes=limit * MIB),
        cost_estimate=pl.CostEstimate(
            flops=int(micros * 4e8), bytes_accessed=int(micros * 3e6), transcendentals=0
        ),
    )(*args)


def after(value, *events):
    return lax.optimization_barrier((value, events))[0]


def dot_of(dims, a, b):
    return lax.dot_general(a, b, (dims, ((), ())), preferred_element_type=F32)


mm = functools.partial(dot_of, ((1,), (0,)))
mm_nt = functools.partial(dot_of, ((1,), (1,)))
mm_tn = functools.partial(dot_of, ((0,), (0,)))


def swap(block, axis, size, k):
    return lax.ppermute(block, axis, [(s, s ^ k) for s in range(size)])


def gather_low(block, axis, size):
    return [swap(block, axis, size, k) for k in range(1, size)]


def scatter_low(blocks, axis, size):
    return [swap(blocks[k - 1], axis, size, k) for k in range(1, size)]


def pick(stacked, index):
    return lax.dynamic_index_in_dim(stacked, index, 0, keepdims=False)


def norm_stats(rows):
    center = rows - jnp.mean(rows, axis=-1, keepdims=True)
    scale_inv = lax.rsqrt(jnp.mean(center * center, axis=-1, keepdims=True) + EPSILON)
    return center * scale_inv, scale_inv


def norm_back(grad_out, normed, scale_inv, gain):
    grad_normed = grad_out * gain
    centered = grad_normed - jnp.mean(grad_normed, axis=-1, keepdims=True)
    return scale_inv * (centered - normed * jnp.mean(grad_normed * normed, axis=-1, keepdims=True))


def total_of(own_ref, arrived_refs):
    total = own_ref[...]
    for ref in arrived_refs:
        total = total + ref[...].astype(F32)
    return total


def pair_matrix(rows, cols, tall):
    r = lax.broadcasted_iota(jnp.int32, (rows, cols), 0)
    c = lax.broadcasted_iota(jnp.int32, (rows, cols), 1)
    hit = (r >> 1) == c if tall else r == (c >> 1)
    return jnp.where(hit, 0.5, 0.0).astype(LOW)


def distances(ids, chunk, rows, block_len, slots):
    j = ids[0]
    start = chunk * rows
    token = (j ^ (start // block_len)) * block_len + start % block_len
    token = token + lax.broadcasted_iota(jnp.int32, (rows, slots), 0)
    s = lax.broadcasted_iota(jnp.int32, (rows, slots), 1)
    half = block_len // 2
    slot = (j ^ (s // half)) * half + s % half
    return token, (token - 2 * slot).astype(F32)


def basis_of(distance, index, span):
    degree = index % (BASES // 2)
    inverse = 64.0 / (span * 4.0**degree)
    if index < BASES // 2:
        return jnp.exp(jnp.abs(distance) * (-inverse))
    return jnp.tanh(distance * inverse)


def bias_body(heads, block_len, rows, ids, rel, out):
    full, slots = out.shape[1:]

    def step(chunk, carry):
        token, distance = distances(ids, chunk, rows, block_len, slots)
        sums = [jnp.zeros((rows, slots), F32)] * heads
        for index in range(BASES):
            base = basis_of(distance, index, full)
            sums = [sums[h] + rel[h, index] * base for h in range(heads)]
        valid = token < ids[3]
        for h in range(heads):
            out[h, pl.ds(pl.multiple_of(chunk * rows, rows), rows), :] = jnp.where(valid, sums[h], MASKED_SCORE)
        return carry

    lax.fori_loop(0, full // rows, step, 0)


def rel_body(heads, block_len, rows, ids, scores_ref, out, acc):
    full, slots = scores_ref.shape[1:]
    acc[...] = jnp.zeros_like(acc)

    def step(chunk, carry):
        _, distance = distances(ids, chunk, rows, block_len, slots)
        at = pl.ds(pl.multiple_of(chunk * rows, rows), rows)
        grads = [scores_ref[h, at, :] for h in range(heads)]
        for index in range(BASES):
            base = basis_of(distance, index, full)
            for h in range(heads):
                acc[h * BASES + index] += jnp.sum((grads[h] * base).reshape(rows // 8, 8, slots), axis=0)
        return carry

    lax.fori_loop(0, full // rows, step, 0)
    for row in range(heads * BASES):
        col = jnp.sum(jnp.sum(acc[row], axis=0, keepdims=True), axis=1, keepdims=True)
        out[row : row + 1, :] = jnp.broadcast_to(col, (1, out.shape[1]))


def attend_body(heads, query_scale, ids, *refs):
    x = refs[:4]
    wq, wk, wv, wo, qb, vb, ob, bias, own_out, p1, p2, p3 = refs[4:16]
    hbm = refs[16:23]
    scr, probs_ref, qt, kt, vt, ct, pooled_low, sem = refs[23:]
    probs_hbm, qt_hbm, kt_hbm, vt_hbm, ct_hbm, pooled_hbm, x_hbm = hbm
    block_len = x[0].shape[0]
    half = block_len // 2
    head = wq.shape[0] // heads
    copies = []

    def send(source, target):
        copy = pltpu.make_async_copy(source, target, sem.at[len(copies)])
        copy.start()
        copies.append(copy)

    for b in range(4):
        send(x[b], x_hbm.at[pl.ds(b * block_len, block_len), :])
    pairs = pair_matrix(half, block_len, False)
    for b in range(4):
        span = slice(b * block_len, (b + 1) * block_len)
        kt[:, span] = mm_nt(wk[...], x[b][...]).astype(LOW)
        vt[:, span] = (mm_nt(wv[...], x[b][...]) + vb[...]).astype(LOW)
        pooled = mm(pairs, x[b][...])
        scr[b] = pooled
        pooled_low[b * half : (b + 1) * half, :] = pooled.astype(LOW)
    turn = ids[0] ^ ids[1]
    own_out[...] = scr[turn] + ob[...]
    qt[...] = ((mm_nt(wq[...], pooled_low[...]) + qb[...]) * query_scale).astype(LOW)
    send(kt, kt_hbm)
    send(vt, vt_hbm)
    send(qt, qt_hbm)
    send(pooled_low, pooled_hbm)
    for h in range(heads):
        at = slice(h * head, (h + 1) * head)
        scores = mm_tn(kt[at, :], qt[at, :]) + bias[h]
        grown = jnp.exp(scores - jnp.max(scores, axis=0, keepdims=True))
        probs = grown * (1.0 / jnp.sum(grown, axis=0, keepdims=True))
        probs_ref[h] = probs
        send(probs_ref.at[h], probs_hbm.at[h])
        ct[at, :] = mm(vt[at, :], probs.astype(LOW)).astype(LOW)
    send(ct, ct_hbm)
    result = mm_tn(ct[...], wo[...])
    for b in range(4):
        scr[b] = result[b * half : (b + 1) * half, :]
    own_out[...] += scr[turn]
    for k, out in ((1, p1), (2, p2), (3, p3)):
        out[...] = scr[turn ^ k].astype(LOW)
    for copy in copies:
        copy.wait()


def feed_body(ids, a0, a1, a2, a3, gain, shift, wu, ub, wd, db, own, p1, p2, p3, *refs):
    hidden_out, slope_out, normed_out, unit_out, inv_out, scr = refs
    rows, width = a0.shape
    turn = ids[0] ^ ids[1]
    for k, a in enumerate((a0, a1, a2, a3)):
        scr[turn ^ k] = a[...].astype(F32)
    unit, inv = norm_stats(scr[...].reshape(4 * rows, width))
    normed = unit * gain[...] + shift[...]
    unit_out[...] = unit
    inv_out[...] = jnp.broadcast_to(inv, inv_out.shape)
    normed_low = normed.astype(LOW)
    normed_out[...] = normed_low
    scr[...] = normed.reshape(scr.shape)
    own[...] = scr[turn] + db[...]
    up = mm(normed_low, wu[...]) + ub[...]
    phi = 0.5 * (1.0 + lax.erf(up * (0.5**0.5)))
    density = jnp.exp(up * up * -0.5) * 0.3989422804014327
    hidden = (up * phi).astype(LOW)
    hidden_out[...] = hidden
    slope_out[...] = phi + up * density
    scr[...] = mm(hidden, wd[...]).reshape(scr.shape)
    own[...] += scr[turn]
    for k, out in ((1, p1), (2, p2), (3, p3)):
        out[...] = scr[turn ^ k].astype(LOW)


def small_rows(*sums):
    return jnp.concatenate(list(sums) + [jnp.zeros((SMALL_ROWS - len(sums), sums[0].shape[1]), F32)])


def feed_back_body(ids, *refs):
    pieces, cots = refs[:4], refs[4:8]
    gain, shift, slope, wd, wu, own, p1, p2, p3 = refs[8:17]
    outs = refs[17:21]
    grad_out, upward_out, small_out, scr, low_scr = refs[21:]
    rows, width = own.shape
    slots = 4 * rows
    turn = ids[0] ^ ids[1]
    for k, piece in enumerate(pieces):
        scr[turn ^ k] = piece[...].astype(F32)
    unit, inv = norm_stats(scr[...].reshape(slots, width))
    s = lax.broadcasted_iota(jnp.int32, (slots, 1), 0)
    slot = (ids[0] ^ (s // rows)) * rows + s % rows
    valid = jnp.where(2 * slot < ids[3], 1.0, 0.0)
    output = ((unit * gain[...] + shift[...]) * valid).astype(LOW)
    for b in range(4):
        outs[b][...] = output[b * rows : (b + 1) * rows, :]
        low_scr[b * rows : (b + 1) * rows, :] = cots[b][...]
    top = low_scr[...].astype(F32) * valid
    grad = norm_back(top, unit, inv, gain[...])
    grad_low = grad.astype(LOW)
    grad_out[...] = grad_low
    scr[...] = grad.reshape(scr.shape)
    own[...] = scr[turn]
    hidden = mm_nt(grad_low, wd[...]).astype(LOW).astype(F32)
    upward = hidden * slope[...]
    upward_low = upward.astype(LOW)
    upward_out[...] = upward_low
    total = lambda a: jnp.sum(a, axis=0, keepdims=True)
    small_out[...] = small_rows(total(top * unit), total(top), total(grad), total(upward))
    scr[...] = mm_nt(upward_low, wu[...]).reshape(scr.shape)
    own[...] += scr[turn]
    for k, out in ((1, p1), (2, p2), (3, p3)):
        out[...] = scr[turn ^ k].astype(LOW)


def feed_weights_body(flip, ids, hidden, grad, normed, upward, out, left, right):
    which = ids[2] ^ flip

    @pl.when(which == 0)
    def _():
        left[...] = hidden[...]
        right[...] = grad[...]

    @pl.when(which != 0)
    def _():
        left[...] = normed[...]
        right[...] = upward[...]

    step = 256
    for at in range(0, left.shape[1], step):
        out[at : at + step, :] = mm_tn(left[:, at : at + step], right[...]).astype(out.dtype)


def row_sums(rows):
    high = rows.astype(LOW)
    rest = (rows - high.astype(F32)).astype(LOW)
    ones = jnp.ones((8, rows.shape[1]), LOW)
    return mm_nt(ones, high) + mm_nt(ones, rest)


def attend_back_body(heads, query_scale, ids, *refs):
    s = refs[:4]
    unit, inv, gain, wq, wk, wv, wo, probs_ref, qt, kt, vt = refs[4:15]
    o = refs[15:19]
    scores_out, stack, grad_out, small_out, sums_out, scr, weights, dct, repeated, result = refs[19:]
    part = wq.shape[0]
    head = part // heads
    slots, full = qt.shape[1], kt.shape[1]
    half, block_len = slots // 4, full // 4
    quarter = block_len // 4
    turn = ids[0] ^ ids[1]
    for k in range(4):
        scr[turn ^ k] = s[k][...].astype(F32)
    grad_normed = scr[...].reshape(unit.shape)
    grad = norm_back(grad_normed, unit[...], inv[:, :1], gain[...])
    grad_low = grad.astype(LOW)
    grad_out[...] = grad_low
    total = lambda a: jnp.sum(a, axis=0, keepdims=True)
    small_out[...] = small_rows(total(grad_normed * unit[...]), total(grad_normed), total(grad))
    weights[:part, :] = wk[...]
    weights[part : 2 * part, :] = wv[...]
    weights[2 * part :, :] = wq[...]
    dct[...] = mm_nt(wo[...], grad_low).astype(LOW)
    for h in range(heads):
        at = slice(h * head, (h + 1) * head)
        probs = probs_ref[h]
        grad_probs = mm_tn(vt[at, :], dct[at, :])
        grad_values = mm_nt(dct[at, :], probs.astype(LOW))
        scores = probs * (grad_probs - jnp.sum(probs * grad_probs, axis=0, keepdims=True))
        scores_out[h] = scores
        scores_low = scores.astype(LOW)
        grad_queries = mm(kt[at, :], scores_low) * query_scale
        stack[at, :] = mm_nt(qt[at, :], scores_low).astype(LOW)
        stack[part + h * head : part + (h + 1) * head, :] = grad_values.astype(LOW)
        stack[2 * part + h * head : 2 * part + (h + 1) * head, :slots] = grad_queries.astype(LOW)
        sums_out[h, :8, :] = row_sums(grad_queries)
        sums_out[h, 8:, :] = row_sums(grad_values)
    pairs = pair_matrix(half, block_len, False)
    for b in range(4):
        repeated[:, b * block_len : (b + 1) * block_len] = mm(
            stack[2 * part :, b * half : (b + 1) * half], pairs
        ).astype(LOW)
    result[...] = mm_tn(stack[: 2 * part, :], weights[: 2 * part, :]) + mm_tn(repeated[...], weights[2 * part :, :])
    spread = pair_matrix(quarter, quarter // 2, True)
    scr[...] = grad.reshape(scr.shape)
    for b in range(4):
        to = slice(b * quarter, (b + 1) * quarter)
        rows = lambda k: pl.ds(pl.multiple_of(b * block_len + (ids[1] ^ k) * quarter, quarter), quarter)
        residual = scr[b, pl.ds(pl.multiple_of(ids[1] * (quarter // 2), quarter // 2), quarter // 2), :]
        high = residual.astype(LOW)
        rest = (residual - high.astype(F32)).astype(LOW)
        o[0][to, :] = result[rows(0), :] + (mm(spread, high) + mm(spread, rest))
        for k in range(1, 4):
            o[k][to, :] = result[rows(k), :].astype(LOW)


def attend_weights_body(ids, x, grad, pooled_low, stack, ct, small_feed, small_attend, sums, rel, keep, send, scr):
    part, slots = ct.shape
    heads = sums.shape[0]
    scr[0, :part, :] = mm(stack[2 * part :, :slots], pooled_low[...])
    scr[0, part : 2 * part, :] = mm(stack[:part, :], x[...])
    scr[1, :part, :] = mm(stack[part : 2 * part, :], x[...])
    scr[1, part : 2 * part, :] = mm(ct[...], grad[...])
    scr[:, 2 * part :, :] = jnp.zeros((2, scr.shape[1] - 2 * part, scr.shape[2]), F32)
    scr[0, 2 * part : 2 * part + SMALL_ROWS, :] = small_feed[...]
    scr[0, 2 * part + SMALL_ROWS : 2 * part + 2 * SMALL_ROWS, :] = small_attend[...]
    for h in range(heads):
        scr[1, 2 * part + h * SMALL_ROWS : 2 * part + (h + 1) * SMALL_ROWS, : sums.shape[2]] = sums[h]
    scr[0, 2 * part + 2 * SMALL_ROWS :, : rel.shape[1]] = rel[...]
    keep[...] = scr[ids[2]]
    send[...] = scr[1 - ids[2]].astype(LOW)


def halves_body(ids, keep, arrived, own, p1, p2, p3):
    rows = own.shape[0]
    for k, out in enumerate((own, p1, p2, p3)):
        at = pl.ds(pl.multiple_of((ids[0] ^ k) * rows, rows), rows)
        out[...] = (keep[at, :] + arrived[at, :].astype(F32)).astype(out.dtype)


def total_body(own, r1, r2, r3, out):
    out[...] = total_of(own, (r1, r2, r3)).astype(LOW)


def stack_body(ids, t0, t1, t2, t3, out):
    rows = t0.shape[0]
    for k, t in enumerate((t0, t1, t2, t3)):
        out[pl.ds(pl.multiple_of((ids[0] ^ k) * rows, rows), rows), :] = t[...]


def unpack_feed_body(ids, mine, other, first, second):
    for c, (a, b) in ((0, (mine, other)), (1, (other, mine))):

        @pl.when(ids[2] == c)
        def _(a=a, b=b):
            first[...] = a[...].astype(F32)
            second[...] = b[...].astype(F32)


def unpack_attend_body(ids, mine, other, dq, dk, dv, do, tail_a, tail_b):
    part = dq.shape[0]
    for c, (a, b) in ((0, (mine, other)), (1, (other, mine))):

        @pl.when(ids[2] == c)
        def _(a=a, b=b):
            dq[...] = a[:part, :].astype(F32)
            dk[...] = a[part : 2 * part, :].astype(F32)
            tail_a[...] = a[2 * part :, :].astype(F32)
            dv[...] = b[:part, :].astype(F32)
            do[...] = b[part : 2 * part, :].astype(F32)
            tail_b[...] = b[2 * part :, :].astype(F32)


def quarters_body(own, r1, r2, r3, q0, q1, q2, q3):
    total = total_of(own, (r1, r2, r3)).astype(LOW)
    rows = q0.shape[0]
    for b, q in enumerate((q0, q1, q2, q3)):
        q[...] = total[b * rows : (b + 1) * rows, :]


def join_body(q0, q1, q2, q3, out):
    rows = q0.shape[0]
    for b, q in enumerate((q0, q1, q2, q3)):
        out[b * rows : (b + 1) * rows, :] = q[...]


def place_body(ids, t0, t1, t2, t3, out):
    rows = out.shape[1] // 4
    for k, t in enumerate((t0, t1, t2, t3)):
        at = pl.ds(pl.multiple_of((ids[1] ^ k) * rows, rows), rows)
        for b in range(4):
            out[ids[0] ^ b, at, :] = t[b * rows : (b + 1) * rows, :].astype(out.dtype)


def place_output_body(ids, t0, t1, t2, t3, out):
    for b, t in enumerate((t0, t1, t2, t3)):
        out[ids[0] ^ b] = t[...]


def plane_halves(ids, keep, arrived):
    rows, width = keep.shape[0] // 4, keep.shape[1]
    return kernel(
        halves_body, [f32(rows, width)] + [low(rows, width)] * 3, (ids, keep, arrived), smem=1, micros=1.5
    )


def plane_total(own, arrived, dp_size):
    total = kernel(total_body, low(*own.shape), (own, *arrived), micros=0.5)
    step = 2
    while step < dp_size:
        total = (total.astype(F32) + swap(total, "dp", dp_size, step).astype(F32)).astype(LOW)
        step *= 2
    return total


def plane_join(ids, pieces):
    rows, width = pieces[0].shape
    return kernel(stack_body, low(4 * rows, width), (ids, *pieces), smem=1, micros=0.8)


def shards(
    inputs,
    lengths,
    query_weight,
    query_bias,
    key_weight,
    value_weight,
    value_bias,
    rel_weight,
    out_weight,
    out_bias,
    attn_gain,
    attn_shift,
    up_weight,
    up_bias,
    down_weight,
    down_bias,
    ffn_gain,
    ffn_shift,
    cotangent,
):
    seq_size, dp_size, mp_size = (lax.axis_size(a) for a in ("seq", "dp", "mp"))
    j, m, c = lax.axis_index("seq"), lax.axis_index("mp"), lax.axis_index("dp") % 2
    sentences, block_len, width = inputs.shape
    assert sentences == seq_size == mp_size == 4 and dp_size % 2 == 0
    half = block_len // 2
    full, slots = 4 * block_len, 4 * half
    heads = rel_weight.shape[0]
    part = query_weight.shape[1]
    head = part // heads
    hidden_here = up_weight.shape[1]
    assert hidden_here == width
    query_scale = head ** (-0.5)
    row = lambda v: v.reshape(1, -1)
    column = lambda v: v.reshape(-1, 1)
    ids = jnp.stack([j, m, c, pick(lengths, j)]).astype(jnp.int32)
    wq, wk, wv = query_weight.T, key_weight.T, value_weight.T

    x = [pick(inputs, j)] + [swap(pick(inputs, j ^ k), "seq", seq_size, k) for k in range(1, 4)]
    bias = kernel(
        functools.partial(bias_body, heads, block_len, 32), f32(heads, full, slots), (ids, rel_weight), smem=2, micros=3.0
    )
    own, p1, p2, p3, probs, qt, kt, vt, ct, pooled_low, tokens = kernel(
        functools.partial(attend_body, heads, query_scale),
        [f32(half, width)]
        + [low(half, width)] * 3
        + [f32(heads, full, slots), low(part, slots), low(part, full), low(part, full), low(part, slots)]
        + [low(slots, width), low(full, width)],
        (ids, *x, wq, wk, wv, out_weight, column(query_bias), column(value_bias), row(out_bias), bias),
        smem=1,
        scratch=[
            pltpu.VMEM((4, half, width), F32),
            pltpu.VMEM((heads, full, slots), F32),
            pltpu.VMEM((part, slots), LOW),
            pltpu.VMEM((part, full), LOW),
            pltpu.VMEM((part, full), LOW),
            pltpu.VMEM((part, slots), LOW),
            pltpu.VMEM((slots, width), LOW),
            pltpu.SemaphoreType.DMA((9 + heads,)),
        ],
        micros=5.0,
        hbm=range(4, 11),
    )
    arrived = scatter_low((p1, p2, p3), "mp", mp_size)
    later = after(cotangent, arrived[0])
    cots = [pick(later, j)] + [swap(pick(later, j ^ k), "seq", seq_size, k) for k in range(1, 4)]
    attended = kernel(total_body, low(half, width), (own, *arrived), micros=0.5)
    own, p1, p2, p3, hidden, slope, normed, unit, inv = kernel(
        feed_body,
        [f32(half, width)]
        + [low(half, width)] * 3
        + [low(slots, hidden_here), f32(slots, hidden_here), low(slots, width), f32(slots, width), f32(slots, 128)],
        (ids, attended, *gather_low(attended, "mp", mp_size), row(attn_gain), row(attn_shift), up_weight)
        + (row(up_bias), down_weight, row(down_bias)),
        smem=1,
        scratch=[pltpu.VMEM((4, half, width), F32)],
        micros=3.0,
    )
    mixed = kernel(total_body, low(half, width), (own, *scatter_low((p1, p2, p3), "mp", mp_size)), micros=0.5)
    own, p1, p2, p3, *rest = kernel(
        feed_back_body,
        [f32(half, width)]
        + [low(half, width)] * 7
        + [low(slots, width), low(slots, hidden_here), f32(SMALL_ROWS, width)],
        (ids, mixed, *gather_low(mixed, "mp", mp_size), *cots, row(ffn_gain), row(ffn_shift), slope)
        + (down_weight, up_weight),
        smem=1,
        scratch=[pltpu.VMEM((4, half, width), F32), pltpu.VMEM((slots, width), LOW)],
        micros=3.0,
    )
    outputs, (grad_mixed, upward, small_feed) = rest[:4], rest[4:]
    arrived = scatter_low((p1, p2, p3), "mp", mp_size)
    feed_weights = lambda flip, out, event: kernel(
        functools.partial(feed_weights_body, flip),
        out,
        (ids, after(hidden, event), grad_mixed, normed, upward),
        smem=1,
        scratch=[pltpu.VMEM((slots, hidden_here), LOW)] * 2,
        micros=1.5,
    )
    feed_send = feed_weights(1, low(width, width), arrived[0])
    feed_arrived = swap(feed_send, "dp", dp_size, 1)
    feed_keep = feed_weights(0, f32(width, width), feed_send)
    grad_normed = kernel(total_body, low(half, width), (own, *arrived), micros=0.5)
    s = gather_low(grad_normed, "mp", mp_size)
    feed_own, *feed_blocks = plane_halves(ids, after(feed_keep, s[0]), feed_arrived)
    feed_landed = scatter_low(feed_blocks, "seq", seq_size)
    o0, o1, o2, o3, scores, stack, grad_attended, small_attend, sums = kernel(
        functools.partial(attend_back_body, heads, query_scale),
        [f32(block_len, width)]
        + [low(block_len, width)] * 3
        + [f32(heads, full, slots), low(3 * part, full), low(slots, width)]
        + [f32(SMALL_ROWS, width), f32(heads, 16, head)],
        (ids, grad_normed, *s, unit, inv, row(attn_gain), wq, wk, wv, out_weight, probs, qt, kt, vt),
        smem=1,
        scratch=[
            pltpu.VMEM((4, half, width), F32),
            pltpu.VMEM((3 * part, width), LOW),
            pltpu.VMEM((part, slots), LOW),
            pltpu.VMEM((part, full), LOW),
            pltpu.VMEM((full, width), F32),
        ],
        micros=6.0,
    )
    landed = scatter_low((o1, o2, o3), "mp", mp_size)
    rel = kernel(
        functools.partial(rel_body, heads, block_len, 32),
        f32(32, 128),
        (ids, after(scores, landed[0])),
        smem=1,
        scratch=[pltpu.VMEM((heads * BASES, 8, slots), F32)],
        micros=3.0,
    )
    half_rows = 2 * part + 2 * SMALL_ROWS + 32
    attend_keep, attend_send = kernel(
        attend_weights_body,
        [f32(half_rows, width), low(half_rows, width)],
        (ids, tokens, grad_attended, pooled_low, stack, ct, small_feed, small_attend, sums, rel),
        smem=1,
        scratch=[pltpu.VMEM((2, half_rows, width), F32)],
        micros=3.0,
    )
    attend_arrived = swap(attend_send, "dp", dp_size, 1)
    feed_total = plane_total(after(feed_own, attend_send), feed_landed, dp_size)
    feed_pieces = [feed_total] + gather_low(feed_total, "seq", seq_size)
    attend_own, *attend_blocks = plane_halves(ids, attend_keep, attend_arrived)
    attend_landed = scatter_low(attend_blocks, "seq", seq_size)

    quarter = block_len // 4
    q = kernel(quarters_body, [low(quarter, width)] * 4, (o0, *landed), micros=0.5)
    q = [q[0]] + scatter_low(q[1:], "seq", seq_size)
    joined = kernel(join_body, low(block_len, width), tuple(q), micros=0.5)
    spread = gather_low(joined, "mp", mp_size)
    attend_total = plane_total(after(attend_own, spread[0]), attend_landed, dp_size)
    attend_pieces = [attend_total] + gather_low(attend_total, "seq", seq_size)
    feed_mine = plane_join(ids, after(feed_pieces, attend_total))
    feed_other = swap(feed_mine, "dp", dp_size, 1)
    outputs = after(outputs, s[0])
    output_all = kernel(
        place_output_body,
        low(4, half, width),
        (ids, outputs[0], *scatter_low(outputs[1:], "seq", seq_size)),
        smem=1,
    )
    attend_mine = plane_join(ids, attend_pieces)
    attend_other = swap(attend_mine, "dp", dp_size, 1)
    input_all = kernel(place_body, f32(4, block_len, width), (ids, joined, *spread), smem=1)
    down_grad, up_grad = kernel(
        unpack_feed_body, [f32(width, width)] * 2, (ids, feed_mine, feed_other), smem=1, micros=2.0
    )
    tail_rows = half_rows - 2 * part
    dq, dk, dv, do, tail_a, tail_b = kernel(
        unpack_attend_body,
        [f32(part, width)] * 4 + [f32(tail_rows, width)] * 2,
        (ids, attend_mine, attend_other),
        smem=1,
        micros=1.5,
    )
    bias_sums = tail_b[: heads * SMALL_ROWS, :head].reshape(heads, SMALL_ROWS, head)
    rel_sums = tail_a[2 * SMALL_ROWS : 2 * SMALL_ROWS + heads * BASES, 0].reshape(heads, BASES)
    first = SMALL_ROWS
    return (
        output_all,
        input_all,
        dq.T,
        bias_sums[:, 0].reshape(-1),
        dk.T,
        dv.T,
        bias_sums[:, 8].reshape(-1),
        rel_sums,
        do,
        tail_a[first + 2],
        tail_a[first],
        tail_a[first + 1],
        up_grad,
        tail_a[3],
        down_grad,
        tail_a[2],
        tail_a[0],
        tail_a[1],
    )


def solution(mesh):
    return jax.shard_map(
        shards,
        mesh=mesh,
        in_specs=(
            P("dp", "seq", None),
            P("dp"),
            P(None, "mp"),
            P("mp"),
            P(None, "mp"),
            P(None, "mp"),
            P("mp"),
            P("mp", None),
            P("mp", None),
            P(),
            P(),
            P(),
            P(None, "mp"),
            P("mp"),
            P("mp", None),
            P(),
            P(),
            P(),
            P("dp", "seq", None),
        ),
        out_specs=(
            P("dp", "seq", None),
            P("dp", "seq", None),
            P(None, "mp"),
            P("mp"),
            P(None, "mp"),
            P(None, "mp"),
            P("mp"),
            P("mp", None),
            P("mp", None),
            P(),
            P(),
            P(),
            P(None, "mp"),
            P("mp"),
            P("mp", None),
            P(),
            P(),
            P(),
        ),
        check_vma=False,
    )
```

profile of v0, /device:TPU:0, one launch (start us, length us, event | category | flops | bytes accessed | tf_op | source)
XLA Modules:
  0.0 201.8 jit_solution(16826636933432519745)
XLA Ops:
  2.0 3.0 %collective-permute-start = (bf16[128,768]{1,0:T(8,128)(2,1)S(1)}, bf16[128,768]{1,0:T(8,128)(2,1)S(1)}, u32[]{:S(2)}, u32[]{:S(2)}) collective-permute-start(bf16[128,768]{1,0:T(8,128)(2,1)S(1)} %get-tuple-element.182), channel_id=1, source_target_pairs={{0,8},{8,0},{16,24},{24,16},{1,9},{9,1},{17,25},{25,17},{2,10},{10... | collective-permute-start | bytes 589832 | tf_op jit(solution)/shard_map/ppermute | solution.py:62
  5.0 1.5 collective-permute-start.1
  8.2 2.1 %shard_map.322.refs_11_ = f32[3,512,256]{2,1,0:T(8,128)S(1)} custom-call(s32[4]{0:T(128)S(1)} %pad_add_fusion.ids, f32[3,8]{1,0:T(4,128)S(1)} %copy-done.6), custom_call_target="tpu_custom_call" | custom-call | flops 1200000000 | bytes 9000000 | tf_op jit(solution)/shard_map/pallas_call | solution.py:35
  10.7 4.8 %collective-permute-done.1.refs_2_ = bf16[128,768]{1,0:T(8,128)(2,1)S(1)} collective-permute-done((bf16[128,768]{1,0:T(8,128)(2,1)S(1)}, bf16[128,768]{1,0:T(8,128)(2,1)S(1)}, u32[]{:S(2)}, u32[]{:S(2)}) %collective-permute-start.1) | collective-permute-done | bytes 196640 | tf_op jit(solution)/shard_map/ppermute | solution.py:62
  15.7 6.3 %shard_map.323 = (f32[64,768]{1,0:T(8,128)S(1)}, bf16[64,768]{1,0:T(8,128)(2,1)S(1)}, bf16[64,768]{1,0:T(8,128)(2,1)S(1)}, bf16[64,768]{1,0:T(8,128)(2,1)S(1)}, ...) custom-call(s32[4]{0:T(128)S(1)} %pad_add_fusion.ids, ...), custom_call_target="tpu_custom_call" | custom-call | flops 2000000000 | bytes 15000000 | tf_op jit(solution)/shard_map/pallas_call | solution.py:35
  22.0 1.6 collective-permute-start.3
  23.7 2.6 %collective-permute-start.4 = (bf16[64,768]{1,0:T(8,128)(2,1)S(1)}, bf16[64,768]{1,0:T(8,128)(2,1)S(1)}, u32[]{:S(2)}, u32[]{:S(2)}) collective-permute-start(bf16[64,768]{1,0:T(8,128)(2,1)S(1)} %get-tuple-element.97), channel_id=1, source_target_pairs={{0,2},{1,3},{2,0},{3,1},{4,6},{5,7},{6,4},{7,5},{8,10},{9,11},{10,... | collective-permute-start | bytes 294920 | tf_op jit(solution)/shard_map/ppermute | solution.py:62
  27.7 5.3 %collective-permute-done.4.r2 = bf16[64,768]{1,0:T(8,128)(2,1)S(1)} collective-permute-done((bf16[64,768]{1,0:T(8,128)(2,1)S(1)}, bf16[64,768]{1,0:T(8,128)(2,1)S(1)}, u32[]{:S(2)}, u32[]{:S(2)}) %collective-permute-start.4) | collective-permute-done | bytes 98336 | tf_op jit(solution)/shard_map/ppermute | solution.py:62
  33.1 1.7 collective-permute-start.6
  34.7 1.4 collective-permute-start.7
  36.2 1.3 collective-permute-start.8
  37.8 5.4 %collective-permute-done.7.a2 = bf16[64,768]{1,0:T(8,128)(2,1)S(1)} collective-permute-done((bf16[64,768]{1,0:T(8,128)(2,1)S(1)}, bf16[64,768]{1,0:T(8,128)(2,1)S(1)}, u32[]{:S(2)}, u32[]{:S(2)}) %collective-permute-start.7) | collective-permute-done | bytes 98336 | tf_op jit(solution)/shard_map/ppermute | solution.py:62
  43.2 1.9 shard_map.325
  45.1 2.7 %collective-permute-start.10 = (bf16[64,768]{1,0:T(8,128)(2,1)S(1)}, bf16[64,768]{1,0:T(8,128)(2,1)S(1)}, u32[]{:S(2)}, u32[]{:S(2)}) collective-permute-start(bf16[64,768]{1,0:T(8,128)(2,1)S(1)} %get-tuple-element.101), channel_id=1, source_target_pairs={{0,2},{1,3},{2,0},{3,1},{4,6},{5,7},{6,4},{7,5},{8,10},{9,11},{10,... | collective-permute-start | bytes 294920 | tf_op jit(solution)/shard_map/ppermute | solution.py:62
  47.8 1.3 collective-permute-start.11
  49.2 2.2 %collective-permute-start.15 = (bf16[64,768]{1,0:T(8,128)(2,1)S(1)}, bf16[64,768]{1,0:T(8,128)(2,1)S(1)}, u32[]{:S(2)}, u32[]{:S(2)}) collective-permute-start(bf16[64,768]{1,0:T(8,128)(2,1)S(1)} %get-tuple-element.187), channel_id=1, source_target_pairs={{0,8},{8,0},{16,24},{24,16},{1,9},{9,1},{17,25},{25,17},{2,10},{10... | collective-permute-start | bytes 294920 | tf_op jit(solution)/shard_map/ppermute | solution.py:62
  51.4 2.4 %collective-permute-done.10.r2 = bf16[64,768]{1,0:T(8,128)(2,1)S(1)} collective-permute-done((bf16[64,768]{1,0:T(8,128)(2,1)S(1)}, bf16[64,768]{1,0:T(8,128)(2,1)S(1)}, u32[]{:S(2)}, u32[]{:S(2)}) %collective-permute-start.10) | collective-permute-done | bytes 98336 | tf_op jit(solution)/shard_map/ppermute | solution.py:62
  56.3 2.0 %collective-permute-start.13 = (bf16[64,768]{1,0:T(8,128)(2,1)S(1)}, bf16[64,768]{1,0:T(8,128)(2,1)S(1)}, u32[]{:S(2)}, u32[]{:S(2)}) collective-permute-start(bf16[64,768]{1,0:T(8,128)(2,1)S(1)} %shard_map.326.refs_0_), channel_id=1, source_target_pairs={{0,2},{1,3},{2,0},{3,1},{4,6},{5,7},{6,4},{7,5},{8,10},{9,11},{10,... | collective-permute-start | bytes 294920 | tf_op jit(solution)/shard_map/ppermute | solution.py:62
  58.3 2.0 %collective-permute-start.14 = (bf16[64,768]{1,0:T(8,128)(2,1)S(1)}, bf16[64,768]{1,0:T(8,128)(2,1)S(1)}, u32[]{:S(2)}, u32[]{:S(2)}) collective-permute-start(bf16[64,768]{1,0:T(8,128)(2,1)S(1)} %shard_map.326.refs_0_), channel_id=1, source_target_pairs={{0,3},{1,2},{2,1},{3,0},{4,7},{5,6},{6,5},{7,4},{8,11},{9,10},{10,... | collective-permute-start | bytes 294920 | tf_op jit(solution)/shard_map/ppermute | solution.py:62
  60.4 2.0 collective-permute-done.12.refs_1_
  63.3 1.6 collective-permute-done.14.refs_3_
  64.8 2.2 %shard_map.327 = (f32[64,768]{1,0:T(8,128)S(1)}, bf16[64,768]{1,0:T(8,128)(2,1)S(1)}, bf16[64,768]{1,0:T(8,128)(2,1)S(1)}, bf16[64,768]{1,0:T(8,128)(2,1)S(1)}, ...) custom-call(s32[4]{0:T(128)S(1)} %pad_add_fusion.ids, ...), custom_call_target="tpu_custom_call" | custom-call | flops 1200000000 | bytes 9000000 | tf_op jit(solution)/shard_map/pallas_call | solution.py:35
  68.2 1.5 collective-permute-start.19
  69.7 1.8 collective-permute-start.20
  71.5 1.3 collective-permute-done.18.r1
  72.9 2.1 %collective-permute-done.19.r2 = bf16[64,768]{1,0:T(8,128)(2,1)S(1)} collective-permute-done((bf16[64,768]{1,0:T(8,128)(2,1)S(1)}, bf16[64,768]{1,0:T(8,128)(2,1)S(1)}, u32[]{:S(2)}, u32[]{:S(2)}) %collective-permute-start.19) | collective-permute-done | bytes 98336 | tf_op jit(solution)/shard_map/ppermute | solution.py:62
  75.0 1.3 collective-permute-done.20.r3
  76.4 1.4 collective-permute-start.21
  77.8 1.4 collective-permute-start.25
  79.2 1.6 collective-permute-start.26
  82.2 2.1 %collective-permute-done.25.refs_2_ = bf16[64,768]{1,0:T(8,128)(2,1)S(1)} collective-permute-done((bf16[64,768]{1,0:T(8,128)(2,1)S(1)}, bf16[64,768]{1,0:T(8,128)(2,1)S(1)}, u32[]{:S(2)}, u32[]{:S(2)}) %collective-permute-start.25) | collective-permute-done | bytes 98336 | tf_op jit(solution)/shard_map/ppermute | solution.py:62
  84.3 1.4 collective-permute-done.26.refs_3_
  85.7 4.0 %shard_map.330 = (f32[128,768]{1,0:T(8,128)S(1)}, bf16[128,768]{1,0:T(8,128)(2,1)S(1)}, bf16[128,768]{1,0:T(8,128)(2,1)S(1)}, bf16[128,768]{1,0:T(8,128)(2,1)S(1...) custom-call(s32[4]{0:T(128)S(1)} %pad_add_fusion.ids, ...), custom_call_target="tpu_custom_call" | custom-call | flops 2400000000 | bytes 18000000 | tf_op jit(solution)/shard_map/pallas_call | solution.py:35
  89.7 1.3 collective-permute-start.27
  91.1 4.4 %collective-permute-done.27.r1 = bf16[128,768]{1,0:T(8,128)(2,1)S(1)} collective-permute-done((bf16[128,768]{1,0:T(8,128)(2,1)S(1)}, bf16[128,768]{1,0:T(8,128)(2,1)S(1)}, u32[]{:S(2)}, u32[]{:S(2)}) %collective-permute-start.27) | collective-permute-done | bytes 196640 | tf_op jit(solution)/shard_map/ppermute | solution.py:62
  95.4 2.1 %shard_map.334.rel = f32[32,128]{1,0:T(8,128)S(1)} custom-call(s32[4]{0:T(128)S(1)} %pad_add_fusion.ids, f32[3,512,256]{2,1,0:T(8,128)S(1)} %get-tuple-element.140.scores_ref), custom_call_target="tpu_custom_call" | custom-call | flops 1200000000 | bytes 9000000 | tf_op jit(solution)/shard_map/pallas_call | solution.py:35
  97.6 1.3 shard_map.335
  99.0 2.2 %collective-permute-start.28 = (bf16[128,768]{1,0:T(8,128)(2,1)S(1)}, bf16[128,768]{1,0:T(8,128)(2,1)S(1)}, u32[]{:S(2)}, u32[]{:S(2)}) collective-permute-start(bf16[128,768]{1,0:T(8,128)(2,1)S(1)} %get-tuple-element.125), channel_id=1, source_target_pairs={{0,2},{1,3},{2,0},{3,1},{4,6},{5,7},{6,4},{7,5},{8,10},{9,11},{10,... | collective-permute-start | bytes 589832 | tf_op jit(solution)/shard_map/ppermute | solution.py:62
  101.2 1.5 collective-permute-start.29
  104.7 7.7 %collective-permute-start.45 = (bf16[192,768]{1,0:T(8,128)(2,1)S(1)}, bf16[192,768]{1,0:T(8,128)(2,1)S(1)}, u32[]{:S(2)}, u32[]{:S(2)}) collective-permute-start(bf16[192,768]{1,0:T(8,128)(2,1)S(1)} %get-tuple-element.163), channel_id=1, source_target_pairs={{0,8},{8,0},{16,24},{24,16},{1,9},{9,1},{17,25},{25,17},{2,10},{10... | collective-permute-start | bytes 884744 | tf_op jit(solution)/shard_map/ppermute | solution.py:62
  112.3 3.8 %collective-permute-done.28.r2 = bf16[128,768]{1,0:T(8,128)(2,1)S(1)} collective-permute-done((bf16[128,768]{1,0:T(8,128)(2,1)S(1)}, bf16[128,768]{1,0:T(8,128)(2,1)S(1)}, u32[]{:S(2)}, u32[]{:S(2)}) %collective-permute-start.28) | collective-permute-done | bytes 196640 | tf_op jit(solution)/shard_map/ppermute | solution.py:62
  116.1 1.6 collective-permute-start.47
  117.8 5.6 %collective-permute-start.30 = (bf16[32,768]{1,0:T(8,128)(2,1)S(1)}, bf16[32,768]{1,0:T(8,128)(2,1)S(1)}, u32[]{:S(2)}, u32[]{:S(2)}) collective-permute-start(bf16[32,768]{1,0:T(8,128)(2,1)S(1)} %get-tuple-element.128), channel_id=1, source_target_pairs={{0,8},{8,0},{16,24},{24,16},{1,9},{9,1},{17,25},{25,17},{2,10},{10... | collective-permute-start | bytes 147464 | tf_op jit(solution)/shard_map/ppermute | solution.py:62
  123.4 7.2 %collective-permute-done.30.q1 = bf16[32,768]{1,0:T(8,128)(2,1)S(1)} collective-permute-done((bf16[32,768]{1,0:T(8,128)(2,1)S(1)}, bf16[32,768]{1,0:T(8,128)(2,1)S(1)}, u32[]{:S(2)}, u32[]{:S(2)}) %collective-permute-start.30) | collective-permute-done | bytes 49184 | tf_op jit(solution)/shard_map/ppermute | solution.py:62
  131.4 3.4 %collective-permute-done.31.q2 = bf16[32,768]{1,0:T(8,128)(2,1)S(1)} collective-permute-done((bf16[32,768]{1,0:T(8,128)(2,1)S(1)}, bf16[32,768]{1,0:T(8,128)(2,1)S(1)}, u32[]{:S(2)}, u32[]{:S(2)}) %collective-permute-start.31) | collective-permute-done | bytes 49184 | tf_op jit(solution)/shard_map/ppermute | solution.py:62
  134.8 2.6 %collective-permute-start.32 = (bf16[32,768]{1,0:T(8,128)(2,1)S(1)}, bf16[32,768]{1,0:T(8,128)(2,1)S(1)}, u32[]{:S(2)}, u32[]{:S(2)}) collective-permute-start(bf16[32,768]{1,0:T(8,128)(2,1)S(1)} %get-tuple-element.130), channel_id=1, source_target_pairs={{0,24},{8,16},{16,8},{24,0},{1,25},{9,17},{17,9},{25,1},{2,26},{10... | collective-permute-start | bytes 147464 | tf_op jit(solution)/shard_map/ppermute | solution.py:62
  137.4 2.3 %collective-permute-done.32.q3 = bf16[32,768]{1,0:T(8,128)(2,1)S(1)} collective-permute-done((bf16[32,768]{1,0:T(8,128)(2,1)S(1)}, bf16[32,768]{1,0:T(8,128)(2,1)S(1)}, u32[]{:S(2)}, u32[]{:S(2)}) %collective-permute-start.32) | collective-permute-done | bytes 49184 | tf_op jit(solution)/shard_map/ppermute | solution.py:62
  142.9 1.7 collective-permute-start.49
  144.5 1.4 collective-permute-start.50
  145.9 2.0 %collective-permute-start.38 = (bf16[112,768]{1,0:T(8,128)(2,1)S(1)}, bf16[112,768]{1,0:T(8,128)(2,1)S(1)}, u32[]{:S(2)}, u32[]{:S(2)}) collective-permute-start(bf16[112,768]{1,0:T(8,128)(2,1)S(1)} %get-tuple-element.146), channel_id=1, source_target_pairs={{0,16},{8,24},{16,0},{24,8},{1,17},{9,25},{17,1},{25,9},{2,18},{10... | collective-permute-start | bytes 516104 | tf_op jit(solution)/shard_map/ppermute | solution.py:62
  148.0 3.0 %collective-permute-start.39 = (bf16[112,768]{1,0:T(8,128)(2,1)S(1)}, bf16[112,768]{1,0:T(8,128)(2,1)S(1)}, u32[]{:S(2)}, u32[]{:S(2)}) collective-permute-start(bf16[112,768]{1,0:T(8,128)(2,1)S(1)} %get-tuple-element.147), channel_id=1, source_target_pairs={{0,24},{8,16},{16,8},{24,0},{1,25},{9,17},{17,9},{25,1},{2,26},{10... | collective-permute-start | bytes 516104 | tf_op jit(solution)/shard_map/ppermute | solution.py:62
  151.0 10.7 %collective-permute-done.38.r2 = bf16[112,768]{1,0:T(8,128)(2,1)S(1)} collective-permute-done((bf16[112,768]{1,0:T(8,128)(2,1)S(1)}, bf16[112,768]{1,0:T(8,128)(2,1)S(1)}, u32[]{:S(2)}, u32[]{:S(2)}) %collective-permute-start.38) | collective-permute-done | bytes 172064 | tf_op jit(solution)/shard_map/ppermute | solution.py:62
  161.8 2.5 %collective-permute-start.40 = (bf16[112,768]{1,0:T(8,128)(2,1)S(1)}, bf16[112,768]{1,0:T(8,128)(2,1)S(1)}, u32[]{:S(2)}, u32[]{:S(2)}) collective-permute-start(bf16[112,768]{1,0:T(8,128)(2,1)S(1)} %shard_map.337.t0), channel_id=1, source_target_pairs={{0,8},{8,0},{16,24},{24,16},{1,9},{9,1},{17,25},{25,17},{2,10},{10... | collective-permute-start | bytes 516104 | tf_op jit(solution)/shard_map/ppermute | solution.py:62
  164.3 2.6 %collective-permute-start.41 = (bf16[112,768]{1,0:T(8,128)(2,1)S(1)}, bf16[112,768]{1,0:T(8,128)(2,1)S(1)}, u32[]{:S(2)}, u32[]{:S(2)}) collective-permute-start(bf16[112,768]{1,0:T(8,128)(2,1)S(1)} %shard_map.337.t0), channel_id=1, source_target_pairs={{0,16},{8,24},{16,0},{24,8},{1,17},{9,25},{17,1},{25,9},{2,18},{10... | collective-permute-start | bytes 516104 | tf_op jit(solution)/shard_map/ppermute | solution.py:62
  167.7 4.0 %collective-permute-done.41.t2 = bf16[112,768]{1,0:T(8,128)(2,1)S(1)} collective-permute-done((bf16[112,768]{1,0:T(8,128)(2,1)S(1)}, bf16[112,768]{1,0:T(8,128)(2,1)S(1)}, u32[]{:S(2)}, u32[]{:S(2)}) %collective-permute-start.41) | collective-permute-done | bytes 172064 | tf_op jit(solution)/shard_map/ppermute | solution.py:62
  171.7 1.5 collective-permute-done.42.t3
  175.0 2.7 %collective-permute-start.34 = (bf16[128,768]{1,0:T(8,128)(2,1)S(1)}, bf16[128,768]{1,0:T(8,128)(2,1)S(1)}, u32[]{:S(2)}, u32[]{:S(2)}) collective-permute-start(bf16[128,768]{1,0:T(8,128)(2,1)S(1)} %shard_map.332.t0), channel_id=1, source_target_pairs={{0,2},{1,3},{2,0},{3,1},{4,6},{5,7},{6,4},{7,5},{8,10},{9,11},{10,... | collective-permute-start | bytes 589832 | tf_op jit(solution)/shard_map/ppermute | solution.py:62
  177.8 1.4 collective-permute-done.22.t1
  179.2 2.1 %collective-permute-start.35 = (bf16[128,768]{1,0:T(8,128)(2,1)S(1)}, bf16[128,768]{1,0:T(8,128)(2,1)S(1)}, u32[]{:S(2)}, u32[]{:S(2)}) collective-permute-start(bf16[128,768]{1,0:T(8,128)(2,1)S(1)} %shard_map.332.t0), channel_id=1, source_target_pairs={{0,3},{1,2},{2,1},{3,0},{4,7},{5,6},{6,5},{7,4},{8,11},{9,10},{10,... | collective-permute-start | bytes 589832 | tf_op jit(solution)/shard_map/ppermute | solution.py:62
  182.2 4.5 %collective-permute-done.24.t3 = bf16[64,768]{1,0:T(8,128)(2,1)S(1)} collective-permute-done((bf16[64,768]{1,0:T(8,128)(2,1)S(1)}, bf16[64,768]{1,0:T(8,128)(2,1)S(1)}, u32[]{:S(2)}, u32[]{:S(2)}) %collective-permute-start.24) | collective-permute-done | bytes 98336 | tf_op jit(solution)/shard_map/ppermute | solution.py:62
  188.1 4.0 %collective-permute-done.34.t2 = bf16[128,768]{1,0:T(8,128)(2,1)S(1)} collective-permute-done((bf16[128,768]{1,0:T(8,128)(2,1)S(1)}, bf16[128,768]{1,0:T(8,128)(2,1)S(1)}, u32[]{:S(2)}, u32[]{:S(2)}) %collective-permute-start.34) | collective-permute-done | bytes 196640 | tf_op jit(solution)/shard_map/ppermute | solution.py:62
  192.1 1.8 shard_map.333
  193.9 2.1 %shard_map.339 = (f32[192,768]{1,0:T(8,128)}, f32[192,768]{1,0:T(8,128)}, f32[192,768]{1,0:T(8,128)}, f32[192,768]{1,0:T(8,128)}, f32[64,768]{1,0:T(8,128)S(1)}, /*index=5*/f32[64,768]{1,0:T(8,128)S(1)}) custom-call(s32[4]{0:T(128)S(1)} %pad_add_fusion.ids, bf16[448,768]{1,0:T(8,128)(2,1)S(1)} %shard_map.338.mine, ...), custom_call_target="tpu_custom_call" | custom-call | flops 600000000 | bytes 4500000 | tf_op jit(solution)/shard_map/pallas_call | solution.py:35
  198.8 3.0 %shard_map.345 = (f32[768,768]{1,0:T(8,128)}, f32[768,768]{1,0:T(8,128)}) custom-call(s32[4]{0:T(128)S(1)} %pad_add_fusion.ids, bf16[768,768]{1,0:T(8,128)(2,1)S(1)} %shard_map.344.mine, bf16[768,768]{1,0:T(8,128)(2,1)S(1)} %collective-permute-done.51.other), custom_call_target="tpu_custom_call" | custom-call | flops 800000000 | bytes 6000000 | tf_op jit(solution)/shard_map/pallas_call | solution.py:35
  (120 shorter events, 24.6 us)
Async XLA Ops:
  0.7 7.5 %copy-start.6 = (f32[3,8]{1,0:T(4,128)S(1)}, f32[3,8]{1,0:T(4,128)}, u32[]{:S(2)}) copy-start(f32[3,8]{1,0:T(4,128)} %rel.1) | copy-start | bytes 292
  2.0 8.7 %collective-permute-start = (bf16[128,768]{1,0:T(8,128)(2,1)S(1)}, bf16[128,768]{1,0:T(8,128)(2,1)S(1)}, u32[]{:S(2)}, u32[]{:S(2)}) collective-permute-start(bf16[128,768]{1,0:T(8,128)(2,1)S(1)} %get-tuple-element.182), channel_id=1, source_target_pairs={{0,8},{8,0},{16,24},{24,16},{1,9},{9,1},{17,25},{25,17},{2,10},{10... | collective-permute-start | bytes 589832 | tf_op jit(solution)/shard_map/ppermute | solution.py:62
  5.0 10.6 %collective-permute-start.1 = (bf16[128,768]{1,0:T(8,128)(2,1)S(1)}, bf16[128,768]{1,0:T(8,128)(2,1)S(1)}, u32[]{:S(2)}, u32[]{:S(2)}) collective-permute-start(bf16[128,768]{1,0:T(8,128)(2,1)S(1)} %get-tuple-element.184), channel_id=1, source_target_pairs={{0,16},{8,24},{16,0},{24,8},{1,17},{9,25},{17,1},{25,9},{2,18},{10... | collective-permute-start | bytes 589832 | tf_op jit(solution)/shard_map/ppermute | solution.py:62
  6.5 9.1 %collective-permute-start.2 = (bf16[128,768]{1,0:T(8,128)(2,1)S(1)}, bf16[128,768]{1,0:T(8,128)(2,1)S(1)}, u32[]{:S(2)}, u32[]{:S(2)}) collective-permute-start(bf16[128,768]{1,0:T(8,128)(2,1)S(1)} %get-tuple-element.181), channel_id=1, source_target_pairs={{0,24},{8,16},{16,8},{24,0},{1,25},{9,17},{17,9},{25,1},{2,26},{10... | collective-permute-start | bytes 589832 | tf_op jit(solution)/shard_map/ppermute | solution.py:62
  8.2 7.4 %copy-start.3 = (bf16[768,192]{0,1:T(8,128)(2,1)S(1)}, bf16[768,192]{0,1:T(8,128)(2,1)}, u32[]{:S(2)}) copy-start(bf16[768,192]{0,1:T(8,128)(2,1)} %param.23) | copy-start | bytes 884740
  8.2 7.4 %copy-start.4 = (bf16[768,192]{0,1:T(8,128)(2,1)S(1)}, bf16[768,192]{0,1:T(8,128)(2,1)}, u32[]{:S(2)}) copy-start(bf16[768,192]{0,1:T(8,128)(2,1)} %param.24) | copy-start | bytes 884740
  15.6 21.9 %copy-start.9 = (f32[768]{0:T(1024)S(1)}, f32[768]{0:T(1024)}, u32[]{:S(2)}) copy-start(f32[768]{0:T(1024)} %param.29) | copy-start | bytes 9220
  15.6 21.9 %copy-start.10 = (f32[768]{0:T(1024)S(1)}, f32[768]{0:T(1024)}, u32[]{:S(2)}) copy-start(f32[768]{0:T(1024)} %param.30) | copy-start | bytes 9220
  15.6 21.9 %copy-start.11 = (f32[768]{0:T(1024)S(1)}, f32[768]{0:T(1024)}, u32[]{:S(2)}) copy-start(f32[768]{0:T(1024)} %param.32) | copy-start | bytes 9220
  15.7 21.9 %copy-start.12 = (f32[768]{0:T(1024)S(1)}, f32[768]{0:T(1024)}, u32[]{:S(2)}) copy-start(f32[768]{0:T(1024)} %param.34) | copy-start | bytes 9220
  15.7 27.5 %copy-start = (bf16[768,768]{1,0:T(8,128)(2,1)S(1)}, bf16[768,768]{1,0:T(8,128)(2,1)}, u32[]{:S(2)}) copy-start(bf16[768,768]{1,0:T(8,128)(2,1)} %refs_12_.1) | copy-start | bytes 3538948
  15.7 27.5 %copy-start.1 = (bf16[768,768]{1,0:T(8,128)(2,1)S(1)}, bf16[768,768]{1,0:T(8,128)(2,1)}, u32[]{:S(2)}) copy-start(bf16[768,768]{1,0:T(8,128)(2,1)} %refs_11_.1) | copy-start | bytes 3538948
  22.0 5.6 %collective-permute-start.3 = (bf16[64,768]{1,0:T(8,128)(2,1)S(1)}, bf16[64,768]{1,0:T(8,128)(2,1)S(1)}, u32[]{:S(2)}, u32[]{:S(2)}) collective-permute-start(bf16[64,768]{1,0:T(8,128)(2,1)S(1)} %get-tuple-element.96), channel_id=1, source_target_pairs={{0,1},{1,0},{2,3},{3,2},{4,5},{5,4},{6,7},{7,6},{8,9},{9,8},{10,11... | collective-permute-start | bytes 294920 | tf_op jit(solution)/shard_map/ppermute | solution.py:62
  23.7 9.3 %collective-permute-start.4 = (bf16[64,768]{1,0:T(8,128)(2,1)S(1)}, bf16[64,768]{1,0:T(8,128)(2,1)S(1)}, u32[]{:S(2)}, u32[]{:S(2)}) collective-permute-start(bf16[64,768]{1,0:T(8,128)(2,1)S(1)} %get-tuple-element.97), channel_id=1, source_target_pairs={{0,2},{1,3},{2,0},{3,1},{4,6},{5,7},{6,4},{7,5},{8,10},{9,11},{10,... | collective-permute-start | bytes 294920 | tf_op jit(solution)/shard_map/ppermute | solution.py:62
  26.3 6.7 %collective-permute-start.5 = (bf16[64,768]{1,0:T(8,128)(2,1)S(1)}, bf16[64,768]{1,0:T(8,128)(2,1)S(1)}, u32[]{:S(2)}, u32[]{:S(2)}) collective-permute-start(bf16[64,768]{1,0:T(8,128)(2,1)S(1)} %get-tuple-element.98), channel_id=1, source_target_pairs={{0,3},{1,2},{2,1},{3,0},{4,7},{5,6},{6,5},{7,4},{8,11},{9,10},{10,... | collective-permute-start | bytes 294920 | tf_op jit(solution)/shard_map/ppermute | solution.py:62
  33.1 4.7 %collective-permute-start.6 = (bf16[64,768]{1,0:T(8,128)(2,1)S(1)}, bf16[64,768]{1,0:T(8,128)(2,1)S(1)}, u32[]{:S(2)}, u32[]{:S(2)}) collective-permute-start(bf16[64,768]{1,0:T(8,128)(2,1)S(1)} %shard_map.324.a0), channel_id=1, source_target_pairs={{0,1},{1,0},{2,3},{3,2},{4,5},{5,4},{6,7},{7,6},{8,9},{9,8},{10,11... | collective-permute-start | bytes 294920 | tf_op jit(solution)/shard_map/ppermute | solution.py:62
  34.7 8.4 %collective-permute-start.7 = (bf16[64,768]{1,0:T(8,128)(2,1)S(1)}, bf16[64,768]{1,0:T(8,128)(2,1)S(1)}, u32[]{:S(2)}, u32[]{:S(2)}) collective-permute-start(bf16[64,768]{1,0:T(8,128)(2,1)S(1)} %shard_map.324.a0), channel_id=1, source_target_pairs={{0,2},{1,3},{2,0},{3,1},{4,6},{5,7},{6,4},{7,5},{8,10},{9,11},{10,... | collective-permute-start | bytes 294920 | tf_op jit(solution)/shard_map/ppermute | solution.py:62
  36.2 7.0 %collective-permute-start.8 = (bf16[64,768]{1,0:T(8,128)(2,1)S(1)}, bf16[64,768]{1,0:T(8,128)(2,1)S(1)}, u32[]{:S(2)}, u32[]{:S(2)}) collective-permute-start(bf16[64,768]{1,0:T(8,128)(2,1)S(1)} %shard_map.324.a0), channel_id=1, source_target_pairs={{0,3},{1,2},{2,1},{3,0},{4,7},{5,6},{6,5},{7,4},{8,11},{9,10},{10,... | collective-permute-start | bytes 294920 | tf_op jit(solution)/shard_map/ppermute | solution.py:62
  37.6 11.6 %copy-start.7 = (bf16[4,64,768]{2,1,0:T(8,128)(2,1)S(1)}, bf16[4,64,768]{2,1,0:T(8,128)(2,1)}, u32[]{:S(2)}) copy-start(bf16[4,64,768]{2,1,0:T(8,128)(2,1)} %param.37) | copy-start | bytes 1179652
  37.6 22.7 %copy-start.13 = (f32[768]{0:T(1024)S(1)}, f32[768]{0:T(1024)}, u32[]{:S(2)}) copy-start(f32[768]{0:T(1024)} %param.35) | copy-start | bytes 9220
  37.6 22.7 %copy-start.14 = (f32[768]{0:T(1024)S(1)}, f32[768]{0:T(1024)}, u32[]{:S(2)}) copy-start(f32[768]{0:T(1024)} %param.36) | copy-start | bytes 9220
  45.1 8.7 %collective-permute-start.10 = (bf16[64,768]{1,0:T(8,128)(2,1)S(1)}, bf16[64,768]{1,0:T(8,128)(2,1)S(1)}, u32[]{:S(2)}, u32[]{:S(2)}) collective-permute-start(bf16[64,768]{1,0:T(8,128)(2,1)S(1)} %get-tuple-element.101), channel_id=1, source_target_pairs={{0,2},{1,3},{2,0},{3,1},{4,6},{5,7},{6,4},{7,5},{8,10},{9,11},{10,... | collective-permute-start | bytes 294920 | tf_op jit(solution)/shard_map/ppermute | solution.py:62
  47.8 7.3 %collective-permute-start.11 = (bf16[64,768]{1,0:T(8,128)(2,1)S(1)}, bf16[64,768]{1,0:T(8,128)(2,1)S(1)}, u32[]{:S(2)}, u32[]{:S(2)}) collective-permute-start(bf16[64,768]{1,0:T(8,128)(2,1)S(1)} %get-tuple-element.102), channel_id=1, source_target_pairs={{0,3},{1,2},{2,1},{3,0},{4,7},{5,6},{6,5},{7,4},{8,11},{9,10},{10,... | collective-permute-start | bytes 294920 | tf_op jit(solution)/shard_map/ppermute | solution.py:62
  49.2 6.7 %collective-permute-start.9 = (bf16[64,768]{1,0:T(8,128)(2,1)S(1)}, bf16[64,768]{1,0:T(8,128)(2,1)S(1)}, u32[]{:S(2)}, u32[]{:S(2)}) collective-permute-start(bf16[64,768]{1,0:T(8,128)(2,1)S(1)} %get-tuple-element.100), channel_id=1, source_target_pairs={{0,1},{1,0},{2,3},{3,2},{4,5},{5,4},{6,7},{7,6},{8,9},{9,8},{10,11... | collective-permute-start | bytes 294920 | tf_op jit(solution)/shard_map/ppermute | solution.py:62
  49.2 9.1 %collective-permute-start.15 = (bf16[64,768]{1,0:T(8,128)(2,1)S(1)}, bf16[64,768]{1,0:T(8,128)(2,1)S(1)}, u32[]{:S(2)}, u32[]{:S(2)}) collective-permute-start(bf16[64,768]{1,0:T(8,128)(2,1)S(1)} %get-tuple-element.187), channel_id=1, source_target_pairs={{0,8},{8,0},{16,24},{24,16},{1,9},{9,1},{17,25},{25,17},{2,10},{10... | collective-permute-start | bytes 294920 | tf_op jit(solution)/shard_map/ppermute | solution.py:62
  51.4 9.0 %collective-permute-start.16 = (bf16[64,768]{1,0:T(8,128)(2,1)S(1)}, bf16[64,768]{1,0:T(8,128)(2,1)S(1)}, u32[]{:S(2)}, u32[]{:S(2)}) collective-permute-start(bf16[64,768]{1,0:T(8,128)(2,1)S(1)} %get-tuple-element.186), channel_id=1, source_target_pairs={{0,16},{8,24},{16,0},{24,8},{1,17},{9,25},{17,1},{25,9},{2,18},{10... | collective-permute-start | bytes 294920 | tf_op jit(solution)/shard_map/ppermute | solution.py:62
  53.8 6.6 %collective-permute-start.17 = (bf16[64,768]{1,0:T(8,128)(2,1)S(1)}, bf16[64,768]{1,0:T(8,128)(2,1)S(1)}, u32[]{:S(2)}, u32[]{:S(2)}) collective-permute-start(bf16[64,768]{1,0:T(8,128)(2,1)S(1)} %get-tuple-element.185), channel_id=1, source_target_pairs={{0,24},{8,16},{16,8},{24,0},{1,25},{9,17},{17,9},{25,1},{2,26},{10... | collective-permute-start | bytes 294920 | tf_op jit(solution)/shard_map/ppermute | solution.py:62
  55.9 6.5 %collective-permute-start.12 = (bf16[64,768]{1,0:T(8,128)(2,1)S(1)}, bf16[64,768]{1,0:T(8,128)(2,1)S(1)}, u32[]{:S(2)}, u32[]{:S(2)}) collective-permute-start(bf16[64,768]{1,0:T(8,128)(2,1)S(1)} %shard_map.326.refs_0_), channel_id=1, source_target_pairs={{0,1},{1,0},{2,3},{3,2},{4,5},{5,4},{6,7},{7,6},{8,9},{9,8},{10,11... | collective-permute-start | bytes 294920 | tf_op jit(solution)/shard_map/ppermute | solution.py:62
  56.3 7.0 %collective-permute-start.13 = (bf16[64,768]{1,0:T(8,128)(2,1)S(1)}, bf16[64,768]{1,0:T(8,128)(2,1)S(1)}, u32[]{:S(2)}, u32[]{:S(2)}) collective-permute-start(bf16[64,768]{1,0:T(8,128)(2,1)S(1)} %shard_map.326.refs_0_), channel_id=1, source_target_pairs={{0,2},{1,3},{2,0},{3,1},{4,6},{5,7},{6,4},{7,5},{8,10},{9,11},{10,... | collective-permute-start | bytes 294920 | tf_op jit(solution)/shard_map/ppermute | solution.py:62
  58.3 6.5 %collective-permute-start.14 = (bf16[64,768]{1,0:T(8,128)(2,1)S(1)}, bf16[64,768]{1,0:T(8,128)(2,1)S(1)}, u32[]{:S(2)}, u32[]{:S(2)}) collective-permute-start(bf16[64,768]{1,0:T(8,128)(2,1)S(1)} %shard_map.326.refs_0_), channel_id=1, source_target_pairs={{0,3},{1,2},{2,1},{3,0},{4,7},{5,6},{6,5},{7,4},{8,11},{9,10},{10,... | collective-permute-start | bytes 294920 | tf_op jit(solution)/shard_map/ppermute | solution.py:62
  67.1 5.8 %collective-permute-start.18 = (bf16[64,768]{1,0:T(8,128)(2,1)S(1)}, bf16[64,768]{1,0:T(8,128)(2,1)S(1)}, u32[]{:S(2)}, u32[]{:S(2)}) collective-permute-start(bf16[64,768]{1,0:T(8,128)(2,1)S(1)} %get-tuple-element.110), channel_id=1, source_target_pairs={{0,1},{1,0},{2,3},{3,2},{4,5},{5,4},{6,7},{7,6},{8,9},{9,8},{10,11... | collective-permute-start | bytes 294920 | tf_op jit(solution)/shard_map/ppermute | solution.py:62
  68.2 6.7 %collective-permute-start.19 = (bf16[64,768]{1,0:T(8,128)(2,1)S(1)}, bf16[64,768]{1,0:T(8,128)(2,1)S(1)}, u32[]{:S(2)}, u32[]{:S(2)}) collective-permute-start(bf16[64,768]{1,0:T(8,128)(2,1)S(1)} %get-tuple-element.111), channel_id=1, source_target_pairs={{0,2},{1,3},{2,0},{3,1},{4,6},{5,7},{6,4},{7,5},{8,10},{9,11},{10,... | collective-permute-start | bytes 294920 | tf_op jit(solution)/shard_map/ppermute | solution.py:62
  69.7 6.6 %collective-permute-start.20 = (bf16[64,768]{1,0:T(8,128)(2,1)S(1)}, bf16[64,768]{1,0:T(8,128)(2,1)S(1)}, u32[]{:S(2)}, u32[]{:S(2)}) collective-permute-start(bf16[64,768]{1,0:T(8,128)(2,1)S(1)} %get-tuple-element.112), channel_id=1, source_target_pairs={{0,3},{1,2},{2,1},{3,0},{4,7},{5,6},{6,5},{7,4},{8,11},{9,10},{10,... | collective-permute-start | bytes 294920 | tf_op jit(solution)/shard_map/ppermute | solution.py:62
  76.4 5.8 %collective-permute-start.21 = (bf16[64,768]{1,0:T(8,128)(2,1)S(1)}, bf16[64,768]{1,0:T(8,128)(2,1)S(1)}, u32[]{:S(2)}, u32[]{:S(2)}) collective-permute-start(bf16[64,768]{1,0:T(8,128)(2,1)S(1)} %shard_map.328.refs_0_), channel_id=1, source_target_pairs={{0,1},{1,0},{2,3},{3,2},{4,5},{5,4},{6,7},{7,6},{8,9},{9,8},{10,11... | collective-permute-start | bytes 294920 | tf_op jit(solution)/shard_map/ppermute | solution.py:62
  77.8 6.6 %collective-permute-start.25 = (bf16[64,768]{1,0:T(8,128)(2,1)S(1)}, bf16[64,768]{1,0:T(8,128)(2,1)S(1)}, u32[]{:S(2)}, u32[]{:S(2)}) collective-permute-start(bf16[64,768]{1,0:T(8,128)(2,1)S(1)} %shard_map.328.refs_0_), channel_id=1, source_target_pairs={{0,2},{1,3},{2,0},{3,1},{4,6},{5,7},{6,4},{7,5},{8,10},{9,11},{10,... | collective-permute-start | bytes 294920 | tf_op jit(solution)/shard_map/ppermute | solution.py:62
  79.2 6.5 %collective-permute-start.26 = (bf16[64,768]{1,0:T(8,128)(2,1)S(1)}, bf16[64,768]{1,0:T(8,128)(2,1)S(1)}, u32[]{:S(2)}, u32[]{:S(2)}) collective-permute-start(bf16[64,768]{1,0:T(8,128)(2,1)S(1)} %shard_map.328.refs_0_), channel_id=1, source_target_pairs={{0,3},{1,2},{2,1},{3,0},{4,7},{5,6},{6,5},{7,4},{8,11},{9,10},{10,... | collective-permute-start | bytes 294920 | tf_op jit(solution)/shard_map/ppermute | solution.py:62
  82.1 21.7 %collective-permute-start.44 = (bf16[768,768]{1,0:T(8,128)(2,1)S(1)}, bf16[768,768]{1,0:T(8,128)(2,1)S(1)}, u32[]{:S(2)}, u32[]{:S(2)}) collective-permute-start(bf16[768,768]{1,0:T(8,128)(2,1)S(1)} %shard_map.340), channel_id=1, source_target_pairs={{0,4},{4,0},{1,5},{5,1},{2,6},{6,2},{3,7},{7,3},{8,12},{12,8},{9,1... | collective-permute-start | bytes 3538952 | tf_op jit(solution)/shard_map/ppermute | solution.py:62
  89.7 5.7 %collective-permute-start.27 = (bf16[128,768]{1,0:T(8,128)(2,1)S(1)}, bf16[128,768]{1,0:T(8,128)(2,1)S(1)}, u32[]{:S(2)}, u32[]{:S(2)}) collective-permute-start(bf16[128,768]{1,0:T(8,128)(2,1)S(1)} %get-tuple-element.124), channel_id=1, source_target_pairs={{0,1},{1,0},{2,3},{3,2},{4,5},{5,4},{6,7},{7,6},{8,9},{9,8},{10,11... | collective-permute-start | bytes 589832 | tf_op jit(solution)/shard_map/ppermute | solution.py:62
  98.9 40.9 %collective-permute-start.36 = (bf16[448,768]{1,0:T(8,128)(2,1)S(1)}, bf16[448,768]{1,0:T(8,128)(2,1)S(1)}, u32[]{:S(2)}, u32[]{:S(2)}) collective-permute-start(bf16[448,768]{1,0:T(8,128)(2,1)S(1)} %get-tuple-element.142), channel_id=1, source_target_pairs={{0,4},{4,0},{1,5},{5,1},{2,6},{6,2},{3,7},{7,3},{8,12},{12,8},{9,1... | collective-permute-start | bytes 2064392 | tf_op jit(solution)/shard_map/ppermute | solution.py:62
  99.0 17.1 %collective-permute-start.28 = (bf16[128,768]{1,0:T(8,128)(2,1)S(1)}, bf16[128,768]{1,0:T(8,128)(2,1)S(1)}, u32[]{:S(2)}, u32[]{:S(2)}) collective-permute-start(bf16[128,768]{1,0:T(8,128)(2,1)S(1)} %get-tuple-element.125), channel_id=1, source_target_pairs={{0,2},{1,3},{2,0},{3,1},{4,6},{5,7},{6,4},{7,5},{8,10},{9,11},{10,... | collective-permute-start | bytes 589832 | tf_op jit(solution)/shard_map/ppermute | solution.py:62
  101.2 16.4 %collective-permute-start.29 = (bf16[128,768]{1,0:T(8,128)(2,1)S(1)}, bf16[128,768]{1,0:T(8,128)(2,1)S(1)}, u32[]{:S(2)}, u32[]{:S(2)}) collective-permute-start(bf16[128,768]{1,0:T(8,128)(2,1)S(1)} %get-tuple-element.126), channel_id=1, source_target_pairs={{0,3},{1,2},{2,1},{3,0},{4,7},{5,6},{6,5},{7,4},{8,11},{9,10},{10,... | collective-permute-start | bytes 589832 | tf_op jit(solution)/shard_map/ppermute | solution.py:62
  104.7 37.1 %collective-permute-start.45 = (bf16[192,768]{1,0:T(8,128)(2,1)S(1)}, bf16[192,768]{1,0:T(8,128)(2,1)S(1)}, u32[]{:S(2)}, u32[]{:S(2)}) collective-permute-start(bf16[192,768]{1,0:T(8,128)(2,1)S(1)} %get-tuple-element.163), channel_id=1, source_target_pairs={{0,8},{8,0},{16,24},{24,16},{1,9},{9,1},{17,25},{25,17},{2,10},{10... | collective-permute-start | bytes 884744 | tf_op jit(solution)/shard_map/ppermute | solution.py:62
  112.3 29.5 %collective-permute-start.46 = (bf16[192,768]{1,0:T(8,128)(2,1)S(1)}, bf16[192,768]{1,0:T(8,128)(2,1)S(1)}, u32[]{:S(2)}, u32[]{:S(2)}) collective-permute-start(bf16[192,768]{1,0:T(8,128)(2,1)S(1)} %get-tuple-element.164), channel_id=1, source_target_pairs={{0,16},{8,24},{16,0},{24,8},{1,17},{9,25},{17,1},{25,9},{2,18},{10... | collective-permute-start | bytes 884744 | tf_op jit(solution)/shard_map/ppermute | solution.py:62
  116.1 25.7 %collective-permute-start.47 = (bf16[192,768]{1,0:T(8,128)(2,1)S(1)}, bf16[192,768]{1,0:T(8,128)(2,1)S(1)}, u32[]{:S(2)}, u32[]{:S(2)}) collective-permute-start(bf16[192,768]{1,0:T(8,128)(2,1)S(1)} %get-tuple-element.165), channel_id=1, source_target_pairs={{0,24},{8,16},{16,8},{24,0},{1,25},{9,17},{17,9},{25,1},{2,26},{10... | collective-permute-start | bytes 884744 | tf_op jit(solution)/shard_map/ppermute | solution.py:62
  117.8 12.9 %collective-permute-start.30 = (bf16[32,768]{1,0:T(8,128)(2,1)S(1)}, bf16[32,768]{1,0:T(8,128)(2,1)S(1)}, u32[]{:S(2)}, u32[]{:S(2)}) collective-permute-start(bf16[32,768]{1,0:T(8,128)(2,1)S(1)} %get-tuple-element.128), channel_id=1, source_target_pairs={{0,8},{8,0},{16,24},{24,16},{1,9},{9,1},{17,25},{25,17},{2,10},{10... | collective-permute-start | bytes 147464 | tf_op jit(solution)/shard_map/ppermute | solution.py:62
  130.7 4.1 %collective-permute-start.31 = (bf16[32,768]{1,0:T(8,128)(2,1)S(1)}, bf16[32,768]{1,0:T(8,128)(2,1)S(1)}, u32[]{:S(2)}, u32[]{:S(2)}) collective-permute-start(bf16[32,768]{1,0:T(8,128)(2,1)S(1)} %get-tuple-element.129), channel_id=1, source_target_pairs={{0,16},{8,24},{16,0},{24,8},{1,17},{9,25},{17,1},{25,9},{2,18},{10... | collective-permute-start | bytes 147464 | tf_op jit(solution)/shard_map/ppermute | solution.py:62
  134.8 5.0 %collective-permute-start.32 = (bf16[32,768]{1,0:T(8,128)(2,1)S(1)}, bf16[32,768]{1,0:T(8,128)(2,1)S(1)}, u32[]{:S(2)}, u32[]{:S(2)}) collective-permute-start(bf16[32,768]{1,0:T(8,128)(2,1)S(1)} %get-tuple-element.130), channel_id=1, source_target_pairs={{0,24},{8,16},{16,8},{24,0},{1,25},{9,17},{17,9},{25,1},{2,26},{10... | collective-permute-start | bytes 147464 | tf_op jit(solution)/shard_map/ppermute | solution.py:62
  139.8 6.2 %collective-permute-start.33 = (bf16[128,768]{1,0:T(8,128)(2,1)S(1)}, bf16[128,768]{1,0:T(8,128)(2,1)S(1)}, u32[]{:S(2)}, u32[]{:S(2)}) collective-permute-start(bf16[128,768]{1,0:T(8,128)(2,1)S(1)} %shard_map.332.t0), channel_id=1, source_target_pairs={{0,1},{1,0},{2,3},{3,2},{4,5},{5,4},{6,7},{7,6},{8,9},{9,8},{10,11... | collective-permute-start | bytes 589832 | tf_op jit(solution)/shard_map/ppermute | solution.py:62
  140.5 7.4 %collective-permute-start.37 = (bf16[112,768]{1,0:T(8,128)(2,1)S(1)}, bf16[112,768]{1,0:T(8,128)(2,1)S(1)}, u32[]{:S(2)}, u32[]{:S(2)}) collective-permute-start(bf16[112,768]{1,0:T(8,128)(2,1)S(1)} %get-tuple-element.145), channel_id=1, source_target_pairs={{0,8},{8,0},{16,24},{24,16},{1,9},{9,1},{17,25},{25,17},{2,10},{10... | collective-permute-start | bytes 516104 | tf_op jit(solution)/shard_map/ppermute | solution.py:62
  141.9 25.0 %collective-permute-start.48 = (bf16[192,768]{1,0:T(8,128)(2,1)S(1)}, bf16[192,768]{1,0:T(8,128)(2,1)S(1)}, u32[]{:S(2)}, u32[]{:S(2)}) collective-permute-start(bf16[192,768]{1,0:T(8,128)(2,1)S(1)} %shard_map.343.t0), channel_id=1, source_target_pairs={{0,8},{8,0},{16,24},{24,16},{1,9},{9,1},{17,25},{25,17},{2,10},{10... | collective-permute-start | bytes 884744 | tf_op jit(solution)/shard_map/ppermute | solution.py:62
  142.9 24.1 %collective-permute-start.49 = (bf16[192,768]{1,0:T(8,128)(2,1)S(1)}, bf16[192,768]{1,0:T(8,128)(2,1)S(1)}, u32[]{:S(2)}, u32[]{:S(2)}) collective-permute-start(bf16[192,768]{1,0:T(8,128)(2,1)S(1)} %shard_map.343.t0), channel_id=1, source_target_pairs={{0,16},{8,24},{16,0},{24,8},{1,17},{9,25},{17,1},{25,9},{2,18},{10... | collective-permute-start | bytes 884744 | tf_op jit(solution)/shard_map/ppermute | solution.py:62
  144.5 22.4 %collective-permute-start.50 = (bf16[192,768]{1,0:T(8,128)(2,1)S(1)}, bf16[192,768]{1,0:T(8,128)(2,1)S(1)}, u32[]{:S(2)}, u32[]{:S(2)}) collective-permute-start(bf16[192,768]{1,0:T(8,128)(2,1)S(1)} %shard_map.343.t0), channel_id=1, source_target_pairs={{0,24},{8,16},{16,8},{24,0},{1,25},{9,17},{17,9},{25,1},{2,26},{10... | collective-permute-start | bytes 884744 | tf_op jit(solution)/shard_map/ppermute | solution.py:62
  145.9 15.8 %collective-permute-start.38 = (bf16[112,768]{1,0:T(8,128)(2,1)S(1)}, bf16[112,768]{1,0:T(8,128)(2,1)S(1)}, u32[]{:S(2)}, u32[]{:S(2)}) collective-permute-start(bf16[112,768]{1,0:T(8,128)(2,1)S(1)} %get-tuple-element.146), channel_id=1, source_target_pairs={{0,16},{8,24},{16,0},{24,8},{1,17},{9,25},{17,1},{25,9},{2,18},{10... | collective-permute-start | bytes 516104 | tf_op jit(solution)/shard_map/ppermute | solution.py:62
  148.0 13.7 %collective-permute-start.39 = (bf16[112,768]{1,0:T(8,128)(2,1)S(1)}, bf16[112,768]{1,0:T(8,128)(2,1)S(1)}, u32[]{:S(2)}, u32[]{:S(2)}) collective-permute-start(bf16[112,768]{1,0:T(8,128)(2,1)S(1)} %get-tuple-element.147), channel_id=1, source_target_pairs={{0,24},{8,16},{16,8},{24,0},{1,25},{9,17},{17,9},{25,1},{2,26},{10... | collective-permute-start | bytes 516104 | tf_op jit(solution)/shard_map/ppermute | solution.py:62
  161.8 5.9 %collective-permute-start.40 = (bf16[112,768]{1,0:T(8,128)(2,1)S(1)}, bf16[112,768]{1,0:T(8,128)(2,1)S(1)}, u32[]{:S(2)}, u32[]{:S(2)}) collective-permute-start(bf16[112,768]{1,0:T(8,128)(2,1)S(1)} %shard_map.337.t0), channel_id=1, source_target_pairs={{0,8},{8,0},{16,24},{24,16},{1,9},{9,1},{17,25},{25,17},{2,10},{10... | collective-permute-start | bytes 516104 | tf_op jit(solution)/shard_map/ppermute | solution.py:62
  164.3 7.4 %collective-permute-start.41 = (bf16[112,768]{1,0:T(8,128)(2,1)S(1)}, bf16[112,768]{1,0:T(8,128)(2,1)S(1)}, u32[]{:S(2)}, u32[]{:S(2)}) collective-permute-start(bf16[112,768]{1,0:T(8,128)(2,1)S(1)} %shard_map.337.t0), channel_id=1, source_target_pairs={{0,16},{8,24},{16,0},{24,8},{1,17},{9,25},{17,1},{25,9},{2,18},{10... | collective-permute-start | bytes 516104 | tf_op jit(solution)/shard_map/ppermute | solution.py:62
  167.0 6.3 %collective-permute-start.42 = (bf16[112,768]{1,0:T(8,128)(2,1)S(1)}, bf16[112,768]{1,0:T(8,128)(2,1)S(1)}, u32[]{:S(2)}, u32[]{:S(2)}) collective-permute-start(bf16[112,768]{1,0:T(8,128)(2,1)S(1)} %shard_map.337.t0), channel_id=1, source_target_pairs={{0,24},{8,16},{16,8},{24,0},{1,25},{9,17},{17,9},{25,1},{2,26},{10... | collective-permute-start | bytes 516104 | tf_op jit(solution)/shard_map/ppermute | solution.py:62
  167.6 31.2 %collective-permute-start.51 = (bf16[768,768]{1,0:T(8,128)(2,1)S(1)}, bf16[768,768]{1,0:T(8,128)(2,1)S(1)}, u32[]{:S(2)}, u32[]{:S(2)}) collective-permute-start(bf16[768,768]{1,0:T(8,128)(2,1)S(1)} %shard_map.344.mine), channel_id=1, source_target_pairs={{0,4},{4,0},{1,5},{5,1},{2,6},{6,2},{3,7},{7,3},{8,12},{12,8},{9,1... | collective-permute-start | bytes 3538952 | tf_op jit(solution)/shard_map/ppermute | solution.py:62
  173.9 20.0 %collective-permute-start.43 = (bf16[448,768]{1,0:T(8,128)(2,1)S(1)}, bf16[448,768]{1,0:T(8,128)(2,1)S(1)}, u32[]{:S(2)}, u32[]{:S(2)}) collective-permute-start(bf16[448,768]{1,0:T(8,128)(2,1)S(1)} %shard_map.338.mine), channel_id=1, source_target_pairs={{0,4},{4,0},{1,5},{5,1},{2,6},{6,2},{3,7},{7,3},{8,12},{12,8},{9,1... | collective-permute-start | bytes 2064392 | tf_op jit(solution)/shard_map/ppermute | solution.py:62
  174.0 5.2 %collective-permute-start.22 = (bf16[64,768]{1,0:T(8,128)(2,1)S(1)}, bf16[64,768]{1,0:T(8,128)(2,1)S(1)}, u32[]{:S(2)}, u32[]{:S(2)}) collective-permute-start(bf16[64,768]{1,0:T(8,128)(2,1)S(1)} %get-tuple-element.114), channel_id=1, source_target_pairs={{0,8},{8,0},{16,24},{24,16},{1,9},{9,1},{17,25},{25,17},{2,10},{10... | collective-permute-start | bytes 294920 | tf_op jit(solution)/shard_map/ppermute | solution.py:62
  174.4 6.9 %collective-permute-start.23 = (bf16[64,768]{1,0:T(8,128)(2,1)S(1)}, bf16[64,768]{1,0:T(8,128)(2,1)S(1)}, u32[]{:S(2)}, u32[]{:S(2)}) collective-permute-start(bf16[64,768]{1,0:T(8,128)(2,1)S(1)} %get-tuple-element.115), channel_id=1, source_target_pairs={{0,16},{8,24},{16,0},{24,8},{1,17},{9,25},{17,1},{25,9},{2,18},{10... | collective-permute-start | bytes 294920 | tf_op jit(solution)/shard_map/ppermute | solution.py:62
  175.0 17.1 %collective-permute-start.34 = (bf16[128,768]{1,0:T(8,128)(2,1)S(1)}, bf16[128,768]{1,0:T(8,128)(2,1)S(1)}, u32[]{:S(2)}, u32[]{:S(2)}) collective-permute-start(bf16[128,768]{1,0:T(8,128)(2,1)S(1)} %shard_map.332.t0), channel_id=1, source_target_pairs={{0,2},{1,3},{2,0},{3,1},{4,6},{5,7},{6,4},{7,5},{8,10},{9,11},{10,... | collective-permute-start | bytes 589832 | tf_op jit(solution)/shard_map/ppermute | solution.py:62
  179.2 12.9 %collective-permute-start.35 = (bf16[128,768]{1,0:T(8,128)(2,1)S(1)}, bf16[128,768]{1,0:T(8,128)(2,1)S(1)}, u32[]{:S(2)}, u32[]{:S(2)}) collective-permute-start(bf16[128,768]{1,0:T(8,128)(2,1)S(1)} %shard_map.332.t0), channel_id=1, source_target_pairs={{0,3},{1,2},{2,1},{3,0},{4,7},{5,6},{6,5},{7,4},{8,11},{9,10},{10,... | collective-permute-start | bytes 589832 | tf_op jit(solution)/shard_map/ppermute | solution.py:62
  181.2 5.5 %collective-permute-start.24 = (bf16[64,768]{1,0:T(8,128)(2,1)S(1)}, bf16[64,768]{1,0:T(8,128)(2,1)S(1)}, u32[]{:S(2)}, u32[]{:S(2)}) collective-permute-start(bf16[64,768]{1,0:T(8,128)(2,1)S(1)} %get-tuple-element.116), channel_id=1, source_target_pairs={{0,24},{8,16},{16,8},{24,0},{1,25},{9,17},{17,9},{25,1},{2,26},{10... | collective-permute-start | bytes 294920 | tf_op jit(solution)/shard_map/ppermute | solution.py:62
  (6 other events, 40.6 us)
where the time goes:
time: 203 us; the launch traced here: 202 us
  waiting for transfers between devices  80.7 us (40%)
  starting transfers between devices  80.3 us (40%)
  Pallas kernels  34 us (17%)
  local copies, waits for them, and re-layouts  4.99 us (2%)
    ppermute x52, waiting for transfers between devices, swap(): return lax.ppermute(block, axis, [(s, s ^ k) for s in range(size)])  80.7 us
    ppermute x52, starting transfers between devices, swap(): return lax.ppermute(block, axis, [(s, s ^ k) for s in range(size)])  80.3 us
    pallas_call x24, Pallas kernels, kernel(): pl.pallas_call(body, out_shape=outs, in_specs=in_specs, out_specs=out_spe...  34 us
  transfers between devices with their start and end apart: 52, of which 27 were waited for; matrix products, arithmetic and copies ran while one was open for 2% of the time, Pallas kernels for 10%

commit v1 on v0

--- a/solution.py
+++ b/solution.py
@@ -14,6 +14,7 @@
 LOW = jnp.bfloat16
 SMALL_ROWS = 16
 MIB = 1024 * 1024
+DEPTH = 2
 
 
 def f32(*shape):
@@ -62,12 +63,20 @@
     return lax.ppermute(block, axis, [(s, s ^ k) for s in range(size)])
 
 
+def deep(values):
+    for _ in range(DEPTH):
+        values = lax.optimization_barrier(values)
+    return values
+
+
 def gather_low(block, axis, size):
-    return [swap(block, axis, size, k) for k in range(1, size)]
+    landed = [swap(block, axis, size, k) for k in range(1, size)]
+    return deep(landed) if axis == "mp" else landed
 
 
 def scatter_low(blocks, axis, size):
-    return [swap(blocks[k - 1], axis, size, k) for k in range(1, size)]
+    landed = [swap(blocks[k - 1], axis, size, k) for k in range(1, size)]
+    return deep(landed) if axis == "mp" else landed
 
 
 def pick(stacked, index):
@@ -274,9 +283,7 @@
         out[...] = scr[turn ^ k].astype(LOW)
 
 
-def feed_weights_body(flip, ids, hidden, grad, normed, upward, out, left, right):
-    which = ids[2] ^ flip
-
+def feed_product(which, hidden, grad, normed, upward, left, right, put):
     @pl.when(which == 0)
     def _():
         left[...] = hidden[...]
@@ -289,7 +296,121 @@
 
     step = 256
     for at in range(0, left.shape[1], step):
-        out[at : at + step, :] = mm_tn(left[:, at : at + step], right[...]).astype(out.dtype)
+        put(slice(at, at + step), mm_tn(left[:, at : at + step], right[...]))
+
+
+def first_step(base, total, kept, along1, along2):
+    rows = along1[0] // 2
+    block = lambda half, k: total(pl.ds(pl.multiple_of((4 * half + (base ^ k)) * rows, rows), rows))
+    for n, (half, k) in enumerate(((0, 0), (0, 2), (1, 0), (1, 1))):
+        kept[n * rows : (n + 1) * rows, :] = block(half, k)
+    for (_, out), picks in ((along1, ((0, 1), (0, 3))), (along2, ((1, 2), (1, 3)))):
+        for n, (half, k) in enumerate(picks):
+            out[n * rows : (n + 1) * rows, :] = block(half, k).astype(LOW)
+
+
+def second_step(kept, came1, came2, own, along1, along2):
+    rows = along1.shape[0]
+    part = lambda n: kept[n * rows : (n + 1) * rows, :]
+    came = lambda ref, n: ref[n * rows : (n + 1) * rows, :].astype(F32)
+    own[:rows, :] = part(0) + came(came1, 0)
+    own[rows:, :] = part(2) + came(came2, 0)
+    along2[...] = (part(1) + came(came1, 1)).astype(LOW)
+    along1[...] = (part(3) + came(came2, 1)).astype(LOW)
+
+
+def last_sums(own, came1, came2):
+    rows = came1.shape[0]
+    upper = own[:rows, :] + came2[...].astype(F32)
+    lower = own[rows:, :] + came1[...].astype(F32)
+    return upper.astype(LOW), lower.astype(LOW)
+
+
+def join_half(base, mine1, mine2, came1, came2, out):
+    rows = out.shape[0] // 8
+    order = ((mine1, 0, (0, 2)), (came1, 0, (1, 3)), (mine2, 1, (0, 1)), (came2, 1, (2, 3)))
+    for ref, half, ks in order:
+        for n, k in enumerate(ks):
+            at = pl.ds(pl.multiple_of((4 * half + (base ^ k)) * rows, rows), rows)
+            out[at, :] = ref[n * rows : (n + 1) * rows, :]
+
+
+def feed_send_body(ids, hidden, grad, normed, upward, out, left, right):
+    def put(at, value):
+        out[at, :] = value.astype(LOW)
+
+    feed_product(1 - ids[2], hidden, grad, normed, upward, left, right, put)
+
+
+def feed_keep_body(ids, hidden, grad, normed, upward, arrived, kept, along1, along2, left, right, scr):
+    def put(at, value):
+        scr[at, :] = value + arrived[at, :].astype(F32)
+
+    feed_product(ids[2], hidden, grad, normed, upward, left, right, put)
+    rows = along1.shape[0]
+    first_step(ids[0], lambda at: scr[at, :], kept, (rows, along1), (rows, along2))
+
+
+def feed_second_body(kept, came1, came2, own, along1, along2):
+    second_step(kept, came1, came2, own, along1, along2)
+
+
+def attend_first_body(ids, keep, arrived, rel, feed_own, came1, came2, kept, along1, along2, scr):
+    rows = keep.shape[0] // 4
+    scr[...] = keep[...] + arrived[...].astype(F32)
+    scr[-rel.shape[0] :, : rel.shape[1]] = rel[...]
+    first_step(ids[0], lambda at: scr[at, :], kept, (rows, along1), (rows, along2))
+    upper, lower = last_sums(feed_own, came1, came2)
+    for out, parts in ((along1, (lower, upper)), (along2, (upper, lower))):
+        for n, part in enumerate(parts):
+            out[rows + n * part.shape[0] : rows + (n + 1) * part.shape[0], :] = part
+
+
+def attend_second_body(kept, came1, came2, own, along1, along2):
+    rows = own.shape[0] // 2
+    done = along1.shape[0] - rows
+    at = slice(2 * rows, 2 * rows + done)
+    along1[:done, :] = came2[at, :]
+    along2[:done, :] = came1[at, :]
+    second_step(kept, came1, came2, own, along1.at[done:, :], along2.at[done:, :])
+
+
+def third_body(ids, own, sent1, sent2, near1, near2, came1, came2, feed, along1, along2):
+    rows = along1.shape[0]
+    done = came1.shape[0] - rows
+    first, second = slice(2 * rows, 2 * rows + done), slice(2 * rows + done, 2 * (rows + done))
+    upper = ((sent2, first), (near1, second), (near2, first), (came1, slice(0, done)))
+    lower = ((sent1, first), (near1, first), (near2, second), (came2, slice(0, done)))
+    for half, blocks in enumerate((upper, lower)):
+        for k, (ref, at) in enumerate(blocks):
+            to = pl.multiple_of((4 * half + (ids[0] ^ k)) * done, done)
+            feed[pl.ds(to, done), :] = ref[at, :]
+    along2[...], along1[...] = last_sums(own, came1.at[done:, :], came2.at[done:, :])
+
+
+def fourth_body(sent1, sent2, came1, came2, along1, along2):
+    rows = sent1.shape[0]
+    along1[:rows, :] = sent2[...]
+    along1[rows:, :] = came2[...]
+    along2[:rows, :] = sent1[...]
+    along2[rows:, :] = came1[...]
+
+
+def attend_join_body(ids, sent1, sent2, came1, came2, out):
+    join_half(ids[0], sent1, sent2, came1, came2, out)
+
+
+def norm_back_body(ids, *refs):
+    pieces, (unit, inv, gain, grad_out, low_out, small_out) = refs[:4], refs[4:]
+    turn = ids[0] ^ ids[1]
+    for k, piece in enumerate(pieces):
+        grad_out[turn ^ k] = piece[...].astype(F32)
+    grad_normed = grad_out[...].reshape(unit.shape)
+    grad = norm_back(grad_normed, unit[...], inv[:, :1], gain[...])
+    grad_out[...] = grad.reshape(grad_out.shape)
+    low_out[...] = grad.astype(LOW)
+    total = lambda a: jnp.sum(a, axis=0, keepdims=True)
+    small_out[...] = small_rows(total(grad_normed * unit[...]), total(grad_normed), total(grad))
 
 
 def row_sums(rows):
@@ -300,28 +421,18 @@
 
 
 def attend_back_body(heads, query_scale, ids, *refs):
-    s = refs[:4]
-    unit, inv, gain, wq, wk, wv, wo, probs_ref, qt, kt, vt = refs[4:15]
-    o = refs[15:19]
-    scores_out, stack, grad_out, small_out, sums_out, scr, weights, dct, repeated, result = refs[19:]
+    grad, grad_low, wq, wk, wv, wo, probs_ref, qt, kt, vt = refs[:10]
+    o = refs[10:14]
+    scores_out, stack, sums_out, weights, dct, repeated, result = refs[14:]
     part = wq.shape[0]
     head = part // heads
     slots, full = qt.shape[1], kt.shape[1]
     half, block_len = slots // 4, full // 4
     quarter = block_len // 4
-    turn = ids[0] ^ ids[1]
-    for k in range(4):
-        scr[turn ^ k] = s[k][...].astype(F32)
-    grad_normed = scr[...].reshape(unit.shape)
-    grad = norm_back(grad_normed, unit[...], inv[:, :1], gain[...])
-    grad_low = grad.astype(LOW)
-    grad_out[...] = grad_low
-    total = lambda a: jnp.sum(a, axis=0, keepdims=True)
-    small_out[...] = small_rows(total(grad_normed * unit[...]), total(grad_normed), total(grad))
     weights[:part, :] = wk[...]
     weights[part : 2 * part, :] = wv[...]
     weights[2 * part :, :] = wq[...]
-    dct[...] = mm_nt(wo[...], grad_low).astype(LOW)
+    dct[...] = mm_nt(wo[...], grad_low[...]).astype(LOW)
     for h in range(heads):
         at = slice(h * head, (h + 1) * head)
         probs = probs_ref[h]
@@ -343,11 +454,10 @@
         ).astype(LOW)
     result[...] = mm_tn(stack[: 2 * part, :], weights[: 2 * part, :]) + mm_tn(repeated[...], weights[2 * part :, :])
     spread = pair_matrix(quarter, quarter // 2, True)
-    scr[...] = grad.reshape(scr.shape)
     for b in range(4):
         to = slice(b * quarter, (b + 1) * quarter)
         rows = lambda k: pl.ds(pl.multiple_of(b * block_len + (ids[1] ^ k) * quarter, quarter), quarter)
-        residual = scr[b, pl.ds(pl.multiple_of(ids[1] * (quarter // 2), quarter // 2), quarter // 2), :]
+        residual = grad[b, pl.ds(pl.multiple_of(ids[1] * (quarter // 2), quarter // 2), quarter // 2), :]
         high = residual.astype(LOW)
         rest = (residual - high.astype(F32)).astype(LOW)
         o[0][to, :] = result[rows(0), :] + (mm(spread, high) + mm(spread, rest))
@@ -355,7 +465,7 @@
             o[k][to, :] = result[rows(k), :].astype(LOW)
 
 
-def attend_weights_body(ids, x, grad, pooled_low, stack, ct, small_feed, small_attend, sums, rel, keep, send, scr):
+def attend_weights_body(ids, x, grad, pooled_low, stack, ct, small_feed, small_attend, sums, keep, send, scr):
     part, slots = ct.shape
     heads = sums.shape[0]
     scr[0, :part, :] = mm(stack[2 * part :, :slots], pooled_low[...])
@@ -367,26 +477,12 @@
     scr[0, 2 * part + SMALL_ROWS : 2 * part + 2 * SMALL_ROWS, :] = small_attend[...]
     for h in range(heads):
         scr[1, 2 * part + h * SMALL_ROWS : 2 * part + (h + 1) * SMALL_ROWS, : sums.shape[2]] = sums[h]
-    scr[0, 2 * part + 2 * SMALL_ROWS :, : rel.shape[1]] = rel[...]
     keep[...] = scr[ids[2]]
     send[...] = scr[1 - ids[2]].astype(LOW)
 
 
-def halves_body(ids, keep, arrived, own, p1, p2, p3):
-    rows = own.shape[0]
-    for k, out in enumerate((own, p1, p2, p3)):
-        at = pl.ds(pl.multiple_of((ids[0] ^ k) * rows, rows), rows)
-        out[...] = (keep[at, :] + arrived[at, :].astype(F32)).astype(out.dtype)
-
-
-def total_body(own, r1, r2, r3, out):
+def total_body(r1, r2, r3, own, out):
     out[...] = total_of(own, (r1, r2, r3)).astype(LOW)
-
-
-def stack_body(ids, t0, t1, t2, t3, out):
-    rows = t0.shape[0]
-    for k, t in enumerate((t0, t1, t2, t3)):
-        out[pl.ds(pl.multiple_of((ids[0] ^ k) * rows, rows), rows), :] = t[...]
 
 
 def unpack_feed_body(ids, mine, other, first, second):
@@ -412,17 +508,22 @@
             tail_b[...] = b[2 * part :, :].astype(F32)
 
 
-def quarters_body(own, r1, r2, r3, q0, q1, q2, q3):
+def quarters_body(r1, r2, r3, own, n1, n2, n3, q0, q1, q2, q3):
     total = total_of(own, (r1, r2, r3)).astype(LOW)
     rows = q0.shape[0]
-    for b, q in enumerate((q0, q1, q2, q3)):
-        q[...] = total[b * rows : (b + 1) * rows, :]
-
-
-def join_body(q0, q1, q2, q3, out):
+    q0[...] = total[:rows]
+    for b, (q, n) in enumerate(((q1, n1), (q2, n2), (q3, n3)), 1):
+        q[:rows, :] = total[b * rows : (b + 1) * rows]
+        q[rows:, :] = n[...]
+
+
+def join_body(ids, q0, q1, q2, q3, n0, joined, output):
     rows = q0.shape[0]
     for b, q in enumerate((q0, q1, q2, q3)):
-        out[b * rows : (b + 1) * rows, :] = q[...]
+        joined[b * rows : (b + 1) * rows, :] = q[:rows, :]
+    output[ids[0]] = n0[...]
+    for b, q in ((1, q1), (2, q2), (3, q3)):
+        output[ids[0] ^ b] = q[rows:, :]
 
 
 def place_body(ids, t0, t1, t2, t3, out):
@@ -433,30 +534,18 @@
             out[ids[0] ^ b, at, :] = t[b * rows : (b + 1) * rows, :].astype(out.dtype)
 
 
-def place_output_body(ids, t0, t1, t2, t3, out):
-    for b, t in enumerate((t0, t1, t2, t3)):
-        out[ids[0] ^ b] = t[...]
-
-
-def plane_halves(ids, keep, arrived):
-    rows, width = keep.shape[0] // 4, keep.shape[1]
-    return kernel(
-        halves_body, [f32(rows, width)] + [low(rows, width)] * 3, (ids, keep, arrived), smem=1, micros=1.5
-    )
-
-
-def plane_total(own, arrived, dp_size):
-    total = kernel(total_body, low(*own.shape), (own, *arrived), micros=0.5)
+def dp_sum(values, dp_size):
     step = 2
     while step < dp_size:
-        total = (total.astype(F32) + swap(total, "dp", dp_size, step).astype(F32)).astype(LOW)
+        values = [
+            (v.astype(F32) + swap(v, "dp", dp_size, step).astype(F32)).astype(v.dtype) for v in values
+        ]
         step *= 2
-    return total
-
-
-def plane_join(ids, pieces):
-    rows, width = pieces[0].shape
-    return kernel(stack_body, low(4 * rows, width), (ids, *pieces), smem=1, micros=0.8)
+    return values
+
+
+def both_ways(along1, along2, size):
+    return swap(along1, "seq", size, 1), swap(along2, "seq", size, 2)
 
 
 def shards(
@@ -523,9 +612,9 @@
         hbm=range(4, 11),
     )
     arrived = scatter_low((p1, p2, p3), "mp", mp_size)
-    later = after(cotangent, arrived[0])
+    attended = kernel(total_body, low(half, width), (*arrived, own), micros=0.5)
+    later = after(cotangent, attended)
     cots = [pick(later, j)] + [swap(pick(later, j ^ k), "seq", seq_size, k) for k in range(1, 4)]
-    attended = kernel(total_body, low(half, width), (own, *arrived), micros=0.5)
     own, p1, p2, p3, hidden, slope, normed, unit, inv = kernel(
         feed_body,
         [f32(half, width)]
@@ -537,7 +626,8 @@
         scratch=[pltpu.VMEM((4, half, width), F32)],
         micros=3.0,
     )
-    mixed = kernel(total_body, low(half, width), (own, *scatter_low((p1, p2, p3), "mp", mp_size)), micros=0.5)
+    p1, p2, p3 = after((p1, p2, p3), cots)
+    mixed = kernel(total_body, low(half, width), (*scatter_low((p1, p2, p3), "mp", mp_size), own), micros=0.5)
     own, p1, p2, p3, *rest = kernel(
         feed_back_body,
         [f32(half, width)]
@@ -550,32 +640,44 @@
         micros=3.0,
     )
     outputs, (grad_mixed, upward, small_feed) = rest[:4], rest[4:]
+    operands = (hidden, grad_mixed, normed, upward)
+    sides = [pltpu.VMEM((slots, width), LOW)] * 2
+    feed_send = kernel(
+        feed_send_body, low(width, width), (ids, *operands), smem=1, scratch=sides, micros=1.2
+    )
+    feed_arrived = swap(feed_send, "dp", dp_size, 1)
     arrived = scatter_low((p1, p2, p3), "mp", mp_size)
-    feed_weights = lambda flip, out, event: kernel(
-        functools.partial(feed_weights_body, flip),
-        out,
-        (ids, after(hidden, event), grad_mixed, normed, upward),
-        smem=1,
-        scratch=[pltpu.VMEM((slots, hidden_here), LOW)] * 2,
+    grad_normed = kernel(total_body, low(half, width), (*arrived, after(own, feed_arrived)), micros=0.5)
+    rows = width // 8
+    feed_kept, along1, along2 = kernel(
+        feed_keep_body,
+        [f32(4 * rows, width)] + [low(2 * rows, width)] * 2,
+        (ids, *operands, after(feed_arrived, grad_normed)),
+        smem=1,
+        scratch=sides + [pltpu.VMEM((width, width), F32)],
         micros=1.5,
     )
-    feed_send = feed_weights(1, low(width, width), arrived[0])
-    feed_arrived = swap(feed_send, "dp", dp_size, 1)
-    feed_keep = feed_weights(0, f32(width, width), feed_send)
-    grad_normed = kernel(total_body, low(half, width), (own, *arrived), micros=0.5)
-    s = gather_low(grad_normed, "mp", mp_size)
-    feed_own, *feed_blocks = plane_halves(ids, after(feed_keep, s[0]), feed_arrived)
-    feed_landed = scatter_low(feed_blocks, "seq", seq_size)
-    o0, o1, o2, o3, scores, stack, grad_attended, small_attend, sums = kernel(
+    s = gather_low(after(grad_normed, along1), "mp", mp_size)
+    came = both_ways(along1, along2, seq_size)
+    grad, grad_attended, small_attend = kernel(
+        norm_back_body,
+        [f32(4, half, width), low(slots, width), f32(SMALL_ROWS, width)],
+        (ids, grad_normed, *s, unit, inv, row(attn_gain)),
+        smem=1,
+        micros=6.5,
+    )
+    feed_own, along1, along2 = kernel(
+        feed_second_body, [f32(2 * rows, width)] + [low(rows, width)] * 2, (feed_kept, came[0], after(came[1], grad_attended)), micros=0.2
+    )
+    came = both_ways(along1, along2, seq_size)
+    own_input, o1, o2, o3, scores, stack, sums = kernel(
         functools.partial(attend_back_body, heads, query_scale),
         [f32(block_len, width)]
         + [low(block_len, width)] * 3
-        + [f32(heads, full, slots), low(3 * part, full), low(slots, width)]
-        + [f32(SMALL_ROWS, width), f32(heads, 16, head)],
-        (ids, grad_normed, *s, unit, inv, row(attn_gain), wq, wk, wv, out_weight, probs, qt, kt, vt),
+        + [f32(heads, full, slots), low(3 * part, full), f32(heads, 16, head)],
+        (ids, grad, grad_attended, wq, wk, wv, out_weight, probs, qt, kt, after(vt, along1)),
         smem=1,
         scratch=[
-            pltpu.VMEM((4, half, width), F32),
             pltpu.VMEM((3 * part, width), LOW),
             pltpu.VMEM((part, slots), LOW),
             pltpu.VMEM((part, full), LOW),
@@ -583,52 +685,88 @@
         ],
         micros=6.0,
     )
-    landed = scatter_low((o1, o2, o3), "mp", mp_size)
     rel = kernel(
         functools.partial(rel_body, heads, block_len, 32),
         f32(32, 128),
-        (ids, after(scores, landed[0])),
+        (ids, scores),
         smem=1,
         scratch=[pltpu.VMEM((heads * BASES, 8, slots), F32)],
-        micros=3.0,
-    )
-    half_rows = 2 * part + 2 * SMALL_ROWS + 32
+        micros=0.1,
+    )
+    half_rows = 2 * part + 128
     attend_keep, attend_send = kernel(
         attend_weights_body,
         [f32(half_rows, width), low(half_rows, width)],
-        (ids, tokens, grad_attended, pooled_low, stack, ct, small_feed, small_attend, sums, rel),
+        (ids, after(tokens, came), grad_attended, pooled_low, stack, ct, small_feed, small_attend, sums),
         smem=1,
         scratch=[pltpu.VMEM((2, half_rows, width), F32)],
-        micros=3.0,
-    )
+        micros=1.5,
+    )
+    landed = scatter_low((o1, o2, o3), "mp", mp_size)
     attend_arrived = swap(attend_send, "dp", dp_size, 1)
-    feed_total = plane_total(after(feed_own, attend_send), feed_landed, dp_size)
-    feed_pieces = [feed_total] + gather_low(feed_total, "seq", seq_size)
-    attend_own, *attend_blocks = plane_halves(ids, attend_keep, attend_arrived)
-    attend_landed = scatter_low(attend_blocks, "seq", seq_size)
-
+    few = half_rows // 8
+    attend_kept, sent1, sent2 = kernel(
+        attend_first_body,
+        [f32(4 * few, width)] + [low(2 * few + 2 * rows, width)] * 2,
+        (ids, attend_keep, attend_arrived, rel, feed_own, *came),
+        smem=1,
+        scratch=[pltpu.VMEM((half_rows, width), F32)],
+        micros=0.1,
+    )
+    early = both_ways(sent1, sent2, seq_size)
     quarter = block_len // 4
-    q = kernel(quarters_body, [low(quarter, width)] * 4, (o0, *landed), micros=0.5)
-    q = [q[0]] + scatter_low(q[1:], "seq", seq_size)
-    joined = kernel(join_body, low(block_len, width), tuple(q), micros=0.5)
+    q0, *q = kernel(
+        quarters_body,
+        [low(quarter, width)] + [low(quarter + half, width)] * 3,
+        (*landed, own_input, *outputs[1:]),
+        micros=8.0,
+    )
+    attend_own, along1, along2 = kernel(
+        attend_second_body,
+        [f32(2 * few, width)] + [low(rows + few, width)] * 2,
+        (attend_kept, early[0], after(early[1], q0)),
+        micros=0.2,
+    )
+    q = deep(scatter_low(q, "seq", seq_size))
+    came = both_ways(along1, along2, seq_size)
+    joined, output_all = kernel(
+        join_body,
+        [low(block_len, width), low(4, half, width)],
+        (ids, q0, *q, outputs[0]),
+        smem=1,
+        micros=2.8,
+    )
     spread = gather_low(joined, "mp", mp_size)
-    attend_total = plane_total(after(attend_own, spread[0]), attend_landed, dp_size)
-    attend_pieces = [attend_total] + gather_low(attend_total, "seq", seq_size)
-    feed_mine = plane_join(ids, after(feed_pieces, attend_total))
+    feed_mine, along1, along2 = dp_sum(
+        kernel(
+            third_body,
+            [low(width, width)] + [low(few, width)] * 2,
+            (ids, after(attend_own, joined), sent1, sent2, *early, *came),
+            smem=1,
+            micros=0.2,
+        ),
+        dp_size,
+    )
     feed_other = swap(feed_mine, "dp", dp_size, 1)
-    outputs = after(outputs, s[0])
-    output_all = kernel(
-        place_output_body,
-        low(4, half, width),
-        (ids, outputs[0], *scatter_low(outputs[1:], "seq", seq_size)),
-        smem=1,
-    )
-    attend_mine = plane_join(ids, attend_pieces)
+    sent = (after(along1, feed_other), along2)
+    down_grad, up_grad = kernel(
+        unpack_feed_body, [f32(width, width)] * 2, (ids, feed_mine, feed_other), smem=1, micros=0.1
+    )
+    along1, along2 = kernel(
+        fourth_body, [low(2 * few, width)] * 2, (*sent, *after(both_ways(*sent, seq_size), down_grad)), micros=0.1
+    )
+    came = both_ways(along1, along2, seq_size)
+    input_all = kernel(
+        place_body, f32(4, block_len, width), (ids, joined, *spread), smem=1, micros=3.0
+    )
+    attend_mine = kernel(
+        attend_join_body,
+        low(half_rows, width),
+        (ids, along1, along2, came[0], after(came[1], input_all)),
+        smem=1,
+        micros=0.2,
+    )
     attend_other = swap(attend_mine, "dp", dp_size, 1)
-    input_all = kernel(place_body, f32(4, block_len, width), (ids, joined, *spread), smem=1)
-    down_grad, up_grad = kernel(
-        unpack_feed_body, [f32(width, width)] * 2, (ids, feed_mine, feed_other), smem=1, micros=2.0
-    )
     tail_rows = half_rows - 2 * part
     dq, dk, dv, do, tail_a, tail_b = kernel(
         unpack_attend_body,
@@ -638,7 +776,7 @@
         micros=1.5,
     )
     bias_sums = tail_b[: heads * SMALL_ROWS, :head].reshape(heads, SMALL_ROWS, head)
-    rel_sums = tail_a[2 * SMALL_ROWS : 2 * SMALL_ROWS + heads * BASES, 0].reshape(heads, BASES)
+    rel_sums = (tail_a + tail_b)[tail_rows - 32 : tail_rows - 32 + heads * BASES, 0].reshape(heads, BASES)
     first = SMALL_ROWS
     return (
         output_all,

time: 203 us -> 170 us (0.84)
  starting transfers between devices: 80.3 us -> 62.8 us
  waiting for transfers between devices: 80.7 us -> 65.6 us
    ppermute x52 -> x49, starting transfers between devices: 80.3 us -> 62.8 us  [swap(): return lax.ppermute(block, axis, [(s, s ^ k) for s in range(size)])]
    ppermute x52 -> x49, waiting for transfers between devices: 80.7 us -> 65.6 us  [swap(): return lax.ppermute(block, axis, [(s, s ^ k) for s in range(size)])]
  transfers between devices with their start and end apart: 52 -> 49, of which waited for: 27 -> 26; matrix products, arithmetic and copies ran while one was open for 2% -> 1% of each run, Pallas kernels for 10% -> 11%
where the time goes in v1:
time: 170 us
  waiting for transfers between devices  65.6 us (39%)
  starting transfers between devices  62.8 us (37%)
  Pallas kernels  34.3 us (20%)
  local copies, waits for them, and re-layouts  4.87 us (3%)
    ppermute x49, waiting for transfers between devices, swap(): return lax.ppermute(block, axis, [(s, s ^ k) for s in range(size)])  65.6 us
    ppermute x49, starting transfers between devices, swap(): return lax.ppermute(block, axis, [(s, s ^ k) for s in range(size)])  62.8 us
    pallas_call x24, Pallas kernels, kernel(): pl.pallas_call(body, out_shape=outs, in_specs=in_specs, out_specs=out_spe...  34.3 us
  transfers between devices with their start and end apart: 49, of which 26 were waited for; matrix products, arithmetic and copies ran while one was open for 1% of the time, Pallas kernels for 11%

profile of v1, /device:TPU:0, one launch (start us, length us, event | category | flops | bytes accessed | tf_op | source)
XLA Modules:
  0.0 169.5 jit_solution(17174992839679500057)
XLA Ops:
  0.7 1.3 dynamic-slice_bitcast_fusion
  2.0 4.0 %collective-permute-start.2 = (bf16[128,768]{1,0:T(8,128)(2,1)S(1)}, bf16[128,768]{1,0:T(8,128)(2,1)S(1)}, u32[]{:S(2)}, u32[]{:S(2)}) collective-permute-start(bf16[128,768]{1,0:T(8,128)(2,1)S(1)} %get-tuple-element.261), channel_id=1, source_target_pairs={{0,24},{8,16},{16,8},{24,0},{1,25},{9,17},{17,9},{25,1},{2,26},{10... | collective-permute-start | bytes 589832 | tf_op jit(solution)/shard_map/ppermute | solution.py:63
  8.2 2.1 %shard_map.322.refs_11_ = f32[3,512,256]{2,1,0:T(8,128)S(1)} custom-call(s32[4]{0:T(128)S(1)} %pad_add_fusion.ids, f32[3,8]{1,0:T(4,128)S(1)} %copy-done.6), custom_call_target="tpu_custom_call" | custom-call | flops 1200000000 | bytes 9000000 | tf_op jit(solution)/shard_map/pallas_call | solution.py:36
  10.3 1.4 collective-permute-done.2.refs_3_
  11.7 3.7 %collective-permute-done.refs_1_ = bf16[128,768]{1,0:T(8,128)(2,1)S(1)} collective-permute-done((bf16[128,768]{1,0:T(8,128)(2,1)S(1)}, bf16[128,768]{1,0:T(8,128)(2,1)S(1)}, u32[]{:S(2)}, u32[]{:S(2)}) %collective-permute-start) | collective-permute-done | bytes 196640 | tf_op jit(solution)/shard_map/ppermute | solution.py:63
  15.5 6.3 %shard_map.323 = (f32[64,768]{1,0:T(8,128)S(1)}, bf16[64,768]{1,0:T(8,128)(2,1)S(1)}, bf16[64,768]{1,0:T(8,128)(2,1)S(1)}, bf16[64,768]{1,0:T(8,128)(2,1)S(1)}, ...) custom-call(s32[4]{0:T(128)S(1)} %pad_add_fusion.ids, ...), custom_call_target="tpu_custom_call" | custom-call | flops 2000000000 | bytes 15000000 | tf_op jit(solution)/shard_map/pallas_call | solution.py:36
  21.8 1.6 collective-permute-start.3
  23.5 2.6 %collective-permute-start.4 = (bf16[64,768]{1,0:T(8,128)(2,1)S(1)}, bf16[64,768]{1,0:T(8,128)(2,1)S(1)}, u32[]{:S(2)}, u32[]{:S(2)}) collective-permute-start(bf16[64,768]{1,0:T(8,128)(2,1)S(1)} %get-tuple-element.136), channel_id=1, source_target_pairs={{0,2},{1,3},{2,0},{3,1},{4,6},{5,7},{6,4},{7,5},{8,10},{9,11},{10,... | collective-permute-start | bytes 294920 | tf_op jit(solution)/shard_map/ppermute | solution.py:63
  26.5 7.5 %collective-permute-done.4.r2 = bf16[64,768]{1,0:T(8,128)(2,1)S(1)} collective-permute-done((bf16[64,768]{1,0:T(8,128)(2,1)S(1)}, bf16[64,768]{1,0:T(8,128)(2,1)S(1)}, u32[]{:S(2)}, u32[]{:S(2)}) %collective-permute-start.4) | collective-permute-done | bytes 98336 | tf_op jit(solution)/shard_map/ppermute | solution.py:63
  34.0 2.6 %collective-permute-start.8 = (bf16[64,768]{1,0:T(8,128)(2,1)S(1)}, bf16[64,768]{1,0:T(8,128)(2,1)S(1)}, u32[]{:S(2)}, u32[]{:S(2)}) collective-permute-start(bf16[64,768]{1,0:T(8,128)(2,1)S(1)} %shard_map.324.a0), channel_id=1, source_target_pairs={{0,3},{1,2},{2,1},{3,0},{4,7},{5,6},{6,5},{7,4},{8,11},{9,10},{10,... | collective-permute-start | bytes 294920 | tf_op jit(solution)/shard_map/ppermute | solution.py:63
  36.6 1.3 collective-permute-start.7
  38.5 2.5 %collective-permute-start.11 = (bf16[64,768]{1,0:T(8,128)(2,1)S(1)}, bf16[64,768]{1,0:T(8,128)(2,1)S(1)}, u32[]{:S(2)}, u32[]{:S(2)}) collective-permute-start(bf16[64,768]{1,0:T(8,128)(2,1)S(1)} %get-tuple-element.265), channel_id=1, source_target_pairs={{0,24},{8,16},{16,8},{24,0},{1,25},{9,17},{17,9},{25,1},{2,26},{10... | collective-permute-start | bytes 294920 | tf_op jit(solution)/shard_map/ppermute | solution.py:63
  41.7 1.5 collective-permute-start.9
  43.2 1.7 %collective-permute-done.7.a2 = bf16[64,768]{1,0:T(8,128)(2,1)S(1)} collective-permute-done((bf16[64,768]{1,0:T(8,128)(2,1)S(1)}, bf16[64,768]{1,0:T(8,128)(2,1)S(1)}, u32[]{:S(2)}, u32[]{:S(2)}) %collective-permute-start.7) | collective-permute-done | bytes 98336 | tf_op jit(solution)/shard_map/ppermute | solution.py:63
  44.9 2.0 %shard_map.325 = (f32[64,768]{1,0:T(8,128)S(1)}, bf16[64,768]{1,0:T(8,128)(2,1)S(1)}, bf16[64,768]{1,0:T(8,128)(2,1)S(1)}, bf16[64,768]{1,0:T(8,128)(2,1)S(1)}, ...) custom-call(s32[4]{0:T(128)S(1)} %pad_add_fusion.ids, ...), custom_call_target="tpu_custom_call" | custom-call | flops 1200000000 | bytes 9000000 | tf_op jit(solution)/shard_map/pallas_call | solution.py:36
  46.9 2.1 %collective-permute-start.12 = (bf16[64,768]{1,0:T(8,128)(2,1)S(1)}, bf16[64,768]{1,0:T(8,128)(2,1)S(1)}, u32[]{:S(2)}, u32[]{:S(2)}) collective-permute-start(bf16[64,768]{1,0:T(8,128)(2,1)S(1)} %get-tuple-element.149), channel_id=1, source_target_pairs={{0,1},{1,0},{2,3},{3,2},{4,5},{5,4},{6,7},{7,6},{8,9},{9,8},{10,11... | collective-permute-start | bytes 294920 | tf_op jit(solution)/shard_map/ppermute | solution.py:63
  49.2 2.2 %collective-permute-start.14 = (bf16[64,768]{1,0:T(8,128)(2,1)S(1)}, bf16[64,768]{1,0:T(8,128)(2,1)S(1)}, u32[]{:S(2)}, u32[]{:S(2)}) collective-permute-start(bf16[64,768]{1,0:T(8,128)(2,1)S(1)} %get-tuple-element.151), channel_id=1, source_target_pairs={{0,3},{1,2},{2,1},{3,0},{4,7},{5,6},{6,5},{7,4},{8,11},{9,10},{10,... | collective-permute-start | bytes 294920 | tf_op jit(solution)/shard_map/ppermute | solution.py:63
  51.8 5.1 %collective-permute-done.13.r2 = bf16[64,768]{1,0:T(8,128)(2,1)S(1)} collective-permute-done((bf16[64,768]{1,0:T(8,128)(2,1)S(1)}, bf16[64,768]{1,0:T(8,128)(2,1)S(1)}, u32[]{:S(2)}, u32[]{:S(2)}) %collective-permute-start.13) | collective-permute-done | bytes 98336 | tf_op jit(solution)/shard_map/ppermute | solution.py:63
  57.0 1.8 %collective-permute-start.17 = (bf16[64,768]{1,0:T(8,128)(2,1)S(1)}, bf16[64,768]{1,0:T(8,128)(2,1)S(1)}, u32[]{:S(2)}, u32[]{:S(2)}) collective-permute-start(bf16[64,768]{1,0:T(8,128)(2,1)S(1)} %shard_map.326.refs_0_), channel_id=1, source_target_pairs={{0,3},{1,2},{2,1},{3,0},{4,7},{5,6},{6,5},{7,4},{8,11},{9,10},{10,... | collective-permute-start | bytes 294920 | tf_op jit(solution)/shard_map/ppermute | solution.py:63
  58.8 4.5 %collective-permute-start.16 = (bf16[64,768]{1,0:T(8,128)(2,1)S(1)}, bf16[64,768]{1,0:T(8,128)(2,1)S(1)}, u32[]{:S(2)}, u32[]{:S(2)}) collective-permute-start(bf16[64,768]{1,0:T(8,128)(2,1)S(1)} %shard_map.326.refs_0_), channel_id=1, source_target_pairs={{0,2},{1,3},{2,0},{3,1},{4,6},{5,7},{6,4},{7,5},{8,10},{9,11},{10,... | collective-permute-start | bytes 294920 | tf_op jit(solution)/shard_map/ppermute | solution.py:63
  63.5 4.6 %collective-permute-done.16.refs_2_ = bf16[64,768]{1,0:T(8,128)(2,1)S(1)} collective-permute-done((bf16[64,768]{1,0:T(8,128)(2,1)S(1)}, bf16[64,768]{1,0:T(8,128)(2,1)S(1)}, u32[]{:S(2)}, u32[]{:S(2)}) %collective-permute-start.16) | collective-permute-done | bytes 98336 | tf_op jit(solution)/shard_map/ppermute | solution.py:63
  68.2 2.3 %shard_map.327 = (f32[64,768]{1,0:T(8,128)S(1)}, bf16[64,768]{1,0:T(8,128)(2,1)S(1)}, bf16[64,768]{1,0:T(8,128)(2,1)S(1)}, bf16[64,768]{1,0:T(8,128)(2,1)S(1)}, ...) custom-call(s32[4]{0:T(128)S(1)} %pad_add_fusion.ids, ...), custom_call_target="tpu_custom_call" | custom-call | flops 1200000000 | bytes 9000000 | tf_op jit(solution)/shard_map/pallas_call | solution.py:36
  70.5 1.1 shard_map.328
  71.7 0.8 collective-permute-start.18
  72.6 1.3 collective-permute-start.19
  73.9 2.3 %collective-permute-start.20 = (bf16[64,768]{1,0:T(8,128)(2,1)S(1)}, bf16[64,768]{1,0:T(8,128)(2,1)S(1)}, u32[]{:S(2)}, u32[]{:S(2)}) collective-permute-start(bf16[64,768]{1,0:T(8,128)(2,1)S(1)} %get-tuple-element.162), channel_id=1, source_target_pairs={{0,3},{1,2},{2,1},{3,0},{4,7},{5,6},{6,5},{7,4},{8,11},{9,10},{10,... | collective-permute-start | bytes 294920 | tf_op jit(solution)/shard_map/ppermute | solution.py:63
  76.2 2.1 %collective-permute-done.18.r1 = bf16[64,768]{1,0:T(8,128)(2,1)S(1)} collective-permute-done((bf16[64,768]{1,0:T(8,128)(2,1)S(1)}, bf16[64,768]{1,0:T(8,128)(2,1)S(1)}, u32[]{:S(2)}, u32[]{:S(2)}) %collective-permute-start.18) | collective-permute-done | bytes 98336 | tf_op jit(solution)/shard_map/ppermute | solution.py:63
  78.3 5.0 %collective-permute-done.19.r2 = bf16[64,768]{1,0:T(8,128)(2,1)S(1)} collective-permute-done((bf16[64,768]{1,0:T(8,128)(2,1)S(1)}, bf16[64,768]{1,0:T(8,128)(2,1)S(1)}, u32[]{:S(2)}, u32[]{:S(2)}) %collective-permute-start.19) | collective-permute-done | bytes 98336 | tf_op jit(solution)/shard_map/ppermute | solution.py:63
  83.4 1.4 shard_map.330
  84.8 1.9 %collective-permute-start.24 = (bf16[64,768]{1,0:T(8,128)(2,1)S(1)}, bf16[64,768]{1,0:T(8,128)(2,1)S(1)}, u32[]{:S(2)}, u32[]{:S(2)}) collective-permute-start(bf16[64,768]{1,0:T(8,128)(2,1)S(1)} %shard_map.329.refs_0_), channel_id=1, source_target_pairs={{0,3},{1,2},{2,1},{3,0},{4,7},{5,6},{6,5},{7,4},{8,11},{9,10},{10,... | collective-permute-start | bytes 294920 | tf_op jit(solution)/shard_map/ppermute | solution.py:63
  86.7 1.5 collective-permute-start.23
  88.2 1.0 collective-permute-start.22
  89.3 0.8 collective-permute-start.25
  90.0 2.3 %collective-permute-done.24.refs_3_ = bf16[64,768]{1,0:T(8,128)(2,1)S(1)} collective-permute-done((bf16[64,768]{1,0:T(8,128)(2,1)S(1)}, bf16[64,768]{1,0:T(8,128)(2,1)S(1)}, u32[]{:S(2)}, u32[]{:S(2)}) %collective-permute-start.24) | collective-permute-done | bytes 98336 | tf_op jit(solution)/shard_map/ppermute | solution.py:63
  92.3 3.4 %collective-permute-done.23.refs_2_ = bf16[64,768]{1,0:T(8,128)(2,1)S(1)} collective-permute-done((bf16[64,768]{1,0:T(8,128)(2,1)S(1)}, bf16[64,768]{1,0:T(8,128)(2,1)S(1)}, u32[]{:S(2)}, u32[]{:S(2)}) %collective-permute-start.23) | collective-permute-done | bytes 98336 | tf_op jit(solution)/shard_map/ppermute | solution.py:63
  95.8 1.1 shard_map.331
  97.3 1.4 collective-permute-start.37
  98.7 3.5 %shard_map.333 = (f32[128,768]{1,0:T(8,128)S(1)}, bf16[128,768]{1,0:T(8,128)(2,1)S(1)}, bf16[128,768]{1,0:T(8,128)(2,1)S(1)}, bf16[128,768]{1,0:T(8,128)(2,1)S(1...) custom-call(s32[4]{0:T(128)S(1)} %pad_add_fusion.ids, ...), custom_call_target="tpu_custom_call" | custom-call | flops 2400000000 | bytes 18000000 | tf_op jit(solution)/shard_map/pallas_call | solution.py:36
  102.5 1.4 shard_map.337
  103.9 1.5 collective-permute-start.27
  105.4 1.0 collective-permute-start.28
  106.4 2.0 %collective-permute-start.29 = (bf16[128,768]{1,0:T(8,128)(2,1)S(1)}, bf16[128,768]{1,0:T(8,128)(2,1)S(1)}, u32[]{:S(2)}, u32[]{:S(2)}) collective-permute-start(bf16[128,768]{1,0:T(8,128)(2,1)S(1)} %get-tuple-element.193), channel_id=1, source_target_pairs={{0,3},{1,2},{2,1},{3,0},{4,7},{5,6},{6,5},{7,4},{8,11},{9,10},{10,... | collective-permute-start | bytes 589832 | tf_op jit(solution)/shard_map/ppermute | solution.py:63
  108.4 2.2 %shard_map.338.rel = f32[32,128]{1,0:T(8,128)S(1)} custom-call(s32[4]{0:T(128)S(1)} %pad_add_fusion.ids, f32[3,512,256]{2,1,0:T(8,128)S(1)} %get-tuple-element.225.scores_ref), custom_call_target="tpu_custom_call" | custom-call | flops 40000000 | bytes 300000 | tf_op jit(solution)/shard_map/pallas_call | solution.py:36
  110.5 0.9 shard_map.339
  111.5 1.4 collective-permute-start.40
  112.9 1.5 collective-permute-start.39
  114.5 8.0 %collective-permute-done.28.r2 = bf16[128,768]{1,0:T(8,128)(2,1)S(1)} collective-permute-done((bf16[128,768]{1,0:T(8,128)(2,1)S(1)}, bf16[128,768]{1,0:T(8,128)(2,1)S(1)}, u32[]{:S(2)}, u32[]{:S(2)}) %collective-permute-start.28) | collective-permute-done | bytes 196640 | tf_op jit(solution)/shard_map/ppermute | solution.py:63
  122.6 1.4 collective-permute-start.30
  124.0 1.6 collective-permute-start.31
  126.9 1.7 %collective-permute-start.41 = (bf16[160,768]{1,0:T(8,128)(2,1)S(1)}, bf16[160,768]{1,0:T(8,128)(2,1)S(1)}, u32[]{:S(2)}, u32[]{:S(2)}) collective-permute-start(bf16[160,768]{1,0:T(8,128)(2,1)S(1)} %get-tuple-element.233), channel_id=1, source_target_pairs={{0,8},{8,0},{16,24},{24,16},{1,9},{9,1},{17,25},{25,17},{2,10},{10... | collective-permute-start | bytes 737288 | tf_op jit(solution)/shard_map/ppermute | solution.py:63
  129.2 0.7 collective-permute-done.30.q1
  130.0 3.6 %collective-permute-done.31.q2 = bf16[96,768]{1,0:T(8,128)(2,1)S(1)} collective-permute-done((bf16[96,768]{1,0:T(8,128)(2,1)S(1)}, bf16[96,768]{1,0:T(8,128)(2,1)S(1)}, u32[]{:S(2)}, u32[]{:S(2)}) %collective-permute-start.31) | collective-permute-done | bytes 147488 | tf_op jit(solution)/shard_map/ppermute | solution.py:63
  133.6 1.3 shard_map.335
  134.9 2.0 %collective-permute-done.41.came1 = bf16[160,768]{1,0:T(8,128)(2,1)S(1)} collective-permute-done((bf16[160,768]{1,0:T(8,128)(2,1)S(1)}, bf16[160,768]{1,0:T(8,128)(2,1)S(1)}, u32[]{:S(2)}, u32[]{:S(2)}) %collective-permute-start.41) | collective-permute-done | bytes 245792 | tf_op jit(solution)/shard_map/ppermute | solution.py:63
  138.1 2.0 %collective-permute-start.35 = (bf16[128,768]{1,0:T(8,128)(2,1)S(1)}, bf16[128,768]{1,0:T(8,128)(2,1)S(1)}, u32[]{:S(2)}, u32[]{:S(2)}) collective-permute-start(bf16[128,768]{1,0:T(8,128)(2,1)S(1)} %get-tuple-element.210.t0), channel_id=1, source_target_pairs={{0,3},{1,2},{2,1},{3,0},{4,7},{5,6},{6,5},{7,4},{8,11},{9,10},{10,... | collective-permute-start | bytes 589832 | tf_op jit(solution)/shard_map/ppermute | solution.py:63
  140.1 3.8 %collective-permute-start.34 = (bf16[128,768]{1,0:T(8,128)(2,1)S(1)}, bf16[128,768]{1,0:T(8,128)(2,1)S(1)}, u32[]{:S(2)}, u32[]{:S(2)}) collective-permute-start(bf16[128,768]{1,0:T(8,128)(2,1)S(1)} %get-tuple-element.210.t0), channel_id=1, source_target_pairs={{0,2},{1,3},{2,0},{3,1},{4,6},{5,7},{6,4},{7,5},{8,10},{9,11},{10,... | collective-permute-start | bytes 589832 | tf_op jit(solution)/shard_map/ppermute | solution.py:63
  143.9 1.2 collective-permute-start.45
  145.5 3.0 %shard_map.342 = (f32[768,768]{1,0:T(8,128)}, f32[768,768]{1,0:T(8,128)}) custom-call(s32[4]{0:T(128)S(1)} %pad_add_fusion.ids, bf16[768,768]{1,0:T(8,128)(2,1)S(1)} %get-tuple-element.236.mine, bf16[768,768]{1,0:T(8,128)(2,1)S(1)} %collective-permute-done.43.other), custom_call_target="tpu_custom_call" | custom-call | flops 40000000 | bytes 300000 | tf_op jit(solution)/shard_map/pallas_call | solution.py:36
  148.5 1.2 collective-permute-done.44.came1
  149.7 0.9 collective-permute-start.47
  151.3 8.5 %collective-permute-done.34.t2 = bf16[128,768]{1,0:T(8,128)(2,1)S(1)} collective-permute-done((bf16[128,768]{1,0:T(8,128)(2,1)S(1)}, bf16[128,768]{1,0:T(8,128)(2,1)S(1)}, u32[]{:S(2)}, u32[]{:S(2)}) %collective-permute-start.34) | collective-permute-done | bytes 196640 | tf_op jit(solution)/shard_map/ppermute | solution.py:63
  159.9 1.8 %shard_map.336 = f32[4,128,768]{2,1,0:T(8,128)} custom-call(s32[4]{0:T(128)S(1)} %pad_add_fusion.ids, bf16[128,768]{1,0:T(8,128)(2,1)S(1)} %get-tuple-element.210.t0, bf16[128,768]{1,0:T(8,128)(2,1)S(1)} %collective-permute-done.33.t1, bf16[128,768]{1,0:T(8,128)(2,1)S(1)} %collective-permute-done.34.t2, bf16[128,768]{1,0:T(8,128)(2,1)S(1)} %collective-permute-done.35.t3), custom_call_target="tpu_custom_call" | custom-call | flops 1200000000 | bytes 9000000 | tf_op jit(solution)/shard_map/pallas_call | solution.py:36
  162.4 2.2 %collective-permute-done.48.other = bf16[512,768]{1,0:T(8,128)(2,1)S(1)} collective-permute-done((bf16[512,768]{1,0:T(8,128)(2,1)S(1)}, bf16[512,768]{1,0:T(8,128)(2,1)S(1)}, u32[]{:S(2)}, u32[]{:S(2)}) %collective-permute-start.48) | collective-permute-done | bytes 786464 | tf_op jit(solution)/shard_map/ppermute | solution.py:63
  164.6 2.2 %shard_map.345 = (f32[192,768]{1,0:T(8,128)}, f32[192,768]{1,0:T(8,128)}, f32[192,768]{1,0:T(8,128)}, f32[192,768]{1,0:T(8,128)}, f32[128,768]{1,0:T(8,128)S(1)}, /*index=5*/f32[128,768]{1,0:T(8,128)S(1)}) custom-call(s32[4]{0:T(128)S(1)} %pad_add_fusion.ids, bf16[512,768]{1,0:T(8,128)(2,1)S(1)} %shard_map.344.mine, ...), custom_call_target="tpu_custom_call" | custom-call | flops 600000000 | bytes 4500000 | tf_op jit(solution)/shard_map/pallas_call | solution.py:36
  (114 shorter events, 13.7 us)
Async XLA Ops:
  0.7 6.7 %copy-start.16 = (f32[192]{0:T(256)S(1)}, f32[192]{0:T(256)}, u32[]{:S(2)}) copy-start(f32[192]{0:T(256)} %param.25) | copy-start | bytes 2308
  0.7 7.5 %copy-start.6 = (f32[3,8]{1,0:T(4,128)S(1)}, f32[3,8]{1,0:T(4,128)}, u32[]{:S(2)}) copy-start(f32[3,8]{1,0:T(4,128)} %rel.1) | copy-start | bytes 292
  2.0 9.7 %collective-permute-start.2 = (bf16[128,768]{1,0:T(8,128)(2,1)S(1)}, bf16[128,768]{1,0:T(8,128)(2,1)S(1)}, u32[]{:S(2)}, u32[]{:S(2)}) collective-permute-start(bf16[128,768]{1,0:T(8,128)(2,1)S(1)} %get-tuple-element.261), channel_id=1, source_target_pairs={{0,24},{8,16},{16,8},{24,0},{1,25},{9,17},{17,9},{25,1},{2,26},{10... | collective-permute-start | bytes 589832 | tf_op jit(solution)/shard_map/ppermute | solution.py:63
  6.0 9.4 %collective-permute-start = (bf16[128,768]{1,0:T(8,128)(2,1)S(1)}, bf16[128,768]{1,0:T(8,128)(2,1)S(1)}, u32[]{:S(2)}, u32[]{:S(2)}) collective-permute-start(bf16[128,768]{1,0:T(8,128)(2,1)S(1)} %get-tuple-element.262), channel_id=1, source_target_pairs={{0,8},{8,0},{16,24},{24,16},{1,9},{9,1},{17,25},{25,17},{2,10},{10... | collective-permute-start | bytes 589832 | tf_op jit(solution)/shard_map/ppermute | solution.py:63
  6.5 8.9 %collective-permute-start.1 = (bf16[128,768]{1,0:T(8,128)(2,1)S(1)}, bf16[128,768]{1,0:T(8,128)(2,1)S(1)}, u32[]{:S(2)}, u32[]{:S(2)}) collective-permute-start(bf16[128,768]{1,0:T(8,128)(2,1)S(1)} %get-tuple-element.264), channel_id=1, source_target_pairs={{0,16},{8,24},{16,0},{24,8},{1,17},{9,25},{17,1},{25,9},{2,18},{10... | collective-permute-start | bytes 589832 | tf_op jit(solution)/shard_map/ppermute | solution.py:63
  8.2 7.2 %copy-start.2 = (bf16[768,192]{0,1:T(8,128)(2,1)S(1)}, bf16[768,192]{0,1:T(8,128)(2,1)}, u32[]{:S(2)}) copy-start(bf16[768,192]{0,1:T(8,128)(2,1)} %param.21) | copy-start | bytes 884740
  8.2 7.2 %copy-start.3 = (bf16[768,192]{0,1:T(8,128)(2,1)S(1)}, bf16[768,192]{0,1:T(8,128)(2,1)}, u32[]{:S(2)}) copy-start(bf16[768,192]{0,1:T(8,128)(2,1)} %param.23) | copy-start | bytes 884740
  8.2 7.2 %copy-start.4 = (bf16[768,192]{0,1:T(8,128)(2,1)S(1)}, bf16[768,192]{0,1:T(8,128)(2,1)}, u32[]{:S(2)}) copy-start(bf16[768,192]{0,1:T(8,128)(2,1)} %param.24) | copy-start | bytes 884740
  8.2 7.2 %copy-start.5 = (bf16[192,768]{1,0:T(8,128)(2,1)S(1)}, bf16[192,768]{1,0:T(8,128)(2,1)}, u32[]{:S(2)}) copy-start(bf16[192,768]{1,0:T(8,128)(2,1)} %refs_5_.1) | copy-start | bytes 884740
  15.4 10.9 %copy-start.9 = (f32[768]{0:T(1024)S(1)}, f32[768]{0:T(1024)}, u32[]{:S(2)}) copy-start(f32[768]{0:T(1024)} %param.29) | copy-start | bytes 9220
  15.4 10.9 %copy-start.10 = (f32[768]{0:T(1024)S(1)}, f32[768]{0:T(1024)}, u32[]{:S(2)}) copy-start(f32[768]{0:T(1024)} %param.30) | copy-start | bytes 9220
  15.4 10.9 %copy-start.11 = (f32[768]{0:T(1024)S(1)}, f32[768]{0:T(1024)}, u32[]{:S(2)}) copy-start(f32[768]{0:T(1024)} %param.32) | copy-start | bytes 9220
  15.4 10.9 %copy-start.12 = (f32[768]{0:T(1024)S(1)}, f32[768]{0:T(1024)}, u32[]{:S(2)}) copy-start(f32[768]{0:T(1024)} %param.34) | copy-start | bytes 9220
  15.5 23.0 %copy-start.7 = (bf16[4,64,768]{2,1,0:T(8,128)(2,1)S(1)}, bf16[4,64,768]{2,1,0:T(8,128)(2,1)}, u32[]{:S(2)}) copy-start(bf16[4,64,768]{2,1,0:T(8,128)(2,1)} %param.37) | copy-start | bytes 1179652
  15.5 29.4 %copy-start = (bf16[768,768]{1,0:T(8,128)(2,1)S(1)}, bf16[768,768]{1,0:T(8,128)(2,1)}, u32[]{:S(2)}) copy-start(bf16[768,768]{1,0:T(8,128)(2,1)} %refs_12_.1) | copy-start | bytes 3538948
  15.5 29.4 %copy-start.1 = (bf16[768,768]{1,0:T(8,128)(2,1)S(1)}, bf16[768,768]{1,0:T(8,128)(2,1)}, u32[]{:S(2)}) copy-start(bf16[768,768]{1,0:T(8,128)(2,1)} %refs_11_.1) | copy-start | bytes 3538948
  21.8 4.7 %collective-permute-start.3 = (bf16[64,768]{1,0:T(8,128)(2,1)S(1)}, bf16[64,768]{1,0:T(8,128)(2,1)S(1)}, u32[]{:S(2)}, u32[]{:S(2)}) collective-permute-start(bf16[64,768]{1,0:T(8,128)(2,1)S(1)} %get-tuple-element.135), channel_id=1, source_target_pairs={{0,1},{1,0},{2,3},{3,2},{4,5},{5,4},{6,7},{7,6},{8,9},{9,8},{10,11... | collective-permute-start | bytes 294920 | tf_op jit(solution)/shard_map/ppermute | solution.py:63
  23.5 10.5 %collective-permute-start.4 = (bf16[64,768]{1,0:T(8,128)(2,1)S(1)}, bf16[64,768]{1,0:T(8,128)(2,1)S(1)}, u32[]{:S(2)}, u32[]{:S(2)}) collective-permute-start(bf16[64,768]{1,0:T(8,128)(2,1)S(1)} %get-tuple-element.136), channel_id=1, source_target_pairs={{0,2},{1,3},{2,0},{3,1},{4,6},{5,7},{6,4},{7,5},{8,10},{9,11},{10,... | collective-permute-start | bytes 294920 | tf_op jit(solution)/shard_map/ppermute | solution.py:63
  26.1 7.9 %collective-permute-start.5 = (bf16[64,768]{1,0:T(8,128)(2,1)S(1)}, bf16[64,768]{1,0:T(8,128)(2,1)S(1)}, u32[]{:S(2)}, u32[]{:S(2)}) collective-permute-start(bf16[64,768]{1,0:T(8,128)(2,1)S(1)} %get-tuple-element.137), channel_id=1, source_target_pairs={{0,3},{1,2},{2,1},{3,0},{4,7},{5,6},{6,5},{7,4},{8,11},{9,10},{10,... | collective-permute-start | bytes 294920 | tf_op jit(solution)/shard_map/ppermute | solution.py:63
  34.0 7.6 %collective-permute-start.8 = (bf16[64,768]{1,0:T(8,128)(2,1)S(1)}, bf16[64,768]{1,0:T(8,128)(2,1)S(1)}, u32[]{:S(2)}, u32[]{:S(2)}) collective-permute-start(bf16[64,768]{1,0:T(8,128)(2,1)S(1)} %shard_map.324.a0), channel_id=1, source_target_pairs={{0,3},{1,2},{2,1},{3,0},{4,7},{5,6},{6,5},{7,4},{8,11},{9,10},{10,... | collective-permute-start | bytes 294920 | tf_op jit(solution)/shard_map/ppermute | solution.py:63
  36.6 8.3 %collective-permute-start.7 = (bf16[64,768]{1,0:T(8,128)(2,1)S(1)}, bf16[64,768]{1,0:T(8,128)(2,1)S(1)}, u32[]{:S(2)}, u32[]{:S(2)}) collective-permute-start(bf16[64,768]{1,0:T(8,128)(2,1)S(1)} %shard_map.324.a0), channel_id=1, source_target_pairs={{0,2},{1,3},{2,0},{3,1},{4,6},{5,7},{6,4},{7,5},{8,10},{9,11},{10,... | collective-permute-start | bytes 294920 | tf_op jit(solution)/shard_map/ppermute | solution.py:63
  37.9 7.0 %collective-permute-start.6 = (bf16[64,768]{1,0:T(8,128)(2,1)S(1)}, bf16[64,768]{1,0:T(8,128)(2,1)S(1)}, u32[]{:S(2)}, u32[]{:S(2)}) collective-permute-start(bf16[64,768]{1,0:T(8,128)(2,1)S(1)} %shard_map.324.a0), channel_id=1, source_target_pairs={{0,1},{1,0},{2,3},{3,2},{4,5},{5,4},{6,7},{7,6},{8,9},{9,8},{10,11... | collective-permute-start | bytes 294920 | tf_op jit(solution)/shard_map/ppermute | solution.py:63
  38.5 8.4 %collective-permute-start.11 = (bf16[64,768]{1,0:T(8,128)(2,1)S(1)}, bf16[64,768]{1,0:T(8,128)(2,1)S(1)}, u32[]{:S(2)}, u32[]{:S(2)}) collective-permute-start(bf16[64,768]{1,0:T(8,128)(2,1)S(1)} %get-tuple-element.265), channel_id=1, source_target_pairs={{0,24},{8,16},{16,8},{24,0},{1,25},{9,17},{17,9},{25,1},{2,26},{10... | collective-permute-start | bytes 294920 | tf_op jit(solution)/shard_map/ppermute | solution.py:63
  41.0 5.9 %collective-permute-start.10 = (bf16[64,768]{1,0:T(8,128)(2,1)S(1)}, bf16[64,768]{1,0:T(8,128)(2,1)S(1)}, u32[]{:S(2)}, u32[]{:S(2)}) collective-permute-start(bf16[64,768]{1,0:T(8,128)(2,1)S(1)} %get-tuple-element.266), channel_id=1, source_target_pairs={{0,16},{8,24},{16,0},{24,8},{1,17},{9,25},{17,1},{25,9},{2,18},{10... | collective-permute-start | bytes 294920 | tf_op jit(solution)/shard_map/ppermute | solution.py:63
  41.7 21.7 %copy-start.13 = (f32[768]{0:T(1024)S(1)}, f32[768]{0:T(1024)}, u32[]{:S(2)}) copy-start(f32[768]{0:T(1024)} %param.35) | copy-start | bytes 9220
  41.7 21.7 %copy-start.14 = (f32[768]{0:T(1024)S(1)}, f32[768]{0:T(1024)}, u32[]{:S(2)}) copy-start(f32[768]{0:T(1024)} %param.36) | copy-start | bytes 9220
  41.7 5.3 %collective-permute-start.9 = (bf16[64,768]{1,0:T(8,128)(2,1)S(1)}, bf16[64,768]{1,0:T(8,128)(2,1)S(1)}, u32[]{:S(2)}, u32[]{:S(2)}) collective-permute-start(bf16[64,768]{1,0:T(8,128)(2,1)S(1)} %get-tuple-element.267), channel_id=1, source_target_pairs={{0,8},{8,0},{16,24},{24,16},{1,9},{9,1},{17,25},{25,17},{2,10},{10... | collective-permute-start | bytes 294920 | tf_op jit(solution)/shard_map/ppermute | solution.py:63
  46.9 4.9 %collective-permute-start.12 = (bf16[64,768]{1,0:T(8,128)(2,1)S(1)}, bf16[64,768]{1,0:T(8,128)(2,1)S(1)}, u32[]{:S(2)}, u32[]{:S(2)}) collective-permute-start(bf16[64,768]{1,0:T(8,128)(2,1)S(1)} %get-tuple-element.149), channel_id=1, source_target_pairs={{0,1},{1,0},{2,3},{3,2},{4,5},{5,4},{6,7},{7,6},{8,9},{9,8},{10,11... | collective-permute-start | bytes 294920 | tf_op jit(solution)/shard_map/ppermute | solution.py:63
  49.0 8.0 %collective-permute-start.13 = (bf16[64,768]{1,0:T(8,128)(2,1)S(1)}, bf16[64,768]{1,0:T(8,128)(2,1)S(1)}, u32[]{:S(2)}, u32[]{:S(2)}) collective-permute-start(bf16[64,768]{1,0:T(8,128)(2,1)S(1)} %get-tuple-element.150), channel_id=1, source_target_pairs={{0,2},{1,3},{2,0},{3,1},{4,6},{5,7},{6,4},{7,5},{8,10},{9,11},{10,... | collective-permute-start | bytes 294920 | tf_op jit(solution)/shard_map/ppermute | solution.py:63
  49.2 7.8 %collective-permute-start.14 = (bf16[64,768]{1,0:T(8,128)(2,1)S(1)}, bf16[64,768]{1,0:T(8,128)(2,1)S(1)}, u32[]{:S(2)}, u32[]{:S(2)}) collective-permute-start(bf16[64,768]{1,0:T(8,128)(2,1)S(1)} %get-tuple-element.151), channel_id=1, source_target_pairs={{0,3},{1,2},{2,1},{3,0},{4,7},{5,6},{6,5},{7,4},{8,11},{9,10},{10,... | collective-permute-start | bytes 294920 | tf_op jit(solution)/shard_map/ppermute | solution.py:63
  57.0 6.5 %collective-permute-start.17 = (bf16[64,768]{1,0:T(8,128)(2,1)S(1)}, bf16[64,768]{1,0:T(8,128)(2,1)S(1)}, u32[]{:S(2)}, u32[]{:S(2)}) collective-permute-start(bf16[64,768]{1,0:T(8,128)(2,1)S(1)} %shard_map.326.refs_0_), channel_id=1, source_target_pairs={{0,3},{1,2},{2,1},{3,0},{4,7},{5,6},{6,5},{7,4},{8,11},{9,10},{10,... | collective-permute-start | bytes 294920 | tf_op jit(solution)/shard_map/ppermute | solution.py:63
  58.8 9.3 %collective-permute-start.16 = (bf16[64,768]{1,0:T(8,128)(2,1)S(1)}, bf16[64,768]{1,0:T(8,128)(2,1)S(1)}, u32[]{:S(2)}, u32[]{:S(2)}) collective-permute-start(bf16[64,768]{1,0:T(8,128)(2,1)S(1)} %shard_map.326.refs_0_), channel_id=1, source_target_pairs={{0,2},{1,3},{2,0},{3,1},{4,6},{5,7},{6,4},{7,5},{8,10},{9,11},{10,... | collective-permute-start | bytes 294920 | tf_op jit(solution)/shard_map/ppermute | solution.py:63
  63.3 4.9 %collective-permute-start.15 = (bf16[64,768]{1,0:T(8,128)(2,1)S(1)}, bf16[64,768]{1,0:T(8,128)(2,1)S(1)}, u32[]{:S(2)}, u32[]{:S(2)}) collective-permute-start(bf16[64,768]{1,0:T(8,128)(2,1)S(1)} %shard_map.326.refs_0_), channel_id=1, source_target_pairs={{0,1},{1,0},{2,3},{3,2},{4,5},{5,4},{6,7},{7,6},{8,9},{9,8},{10,11... | collective-permute-start | bytes 294920 | tf_op jit(solution)/shard_map/ppermute | solution.py:63
  71.6 11.7 %collective-permute-start.21 = (bf16[768,768]{1,0:T(8,128)(2,1)S(1)}, bf16[768,768]{1,0:T(8,128)(2,1)S(1)}, u32[]{:S(2)}, u32[]{:S(2)}) collective-permute-start(bf16[768,768]{1,0:T(8,128)(2,1)S(1)} %shard_map.328), channel_id=1, source_target_pairs={{0,4},{4,0},{1,5},{5,1},{2,6},{6,2},{3,7},{7,3},{8,12},{12,8},{9,1... | collective-permute-start | bytes 3538952 | tf_op jit(solution)/shard_map/ppermute | solution.py:63
  71.7 6.5 %collective-permute-start.18 = (bf16[64,768]{1,0:T(8,128)(2,1)S(1)}, bf16[64,768]{1,0:T(8,128)(2,1)S(1)}, u32[]{:S(2)}, u32[]{:S(2)}) collective-permute-start(bf16[64,768]{1,0:T(8,128)(2,1)S(1)} %get-tuple-element.160), channel_id=1, source_target_pairs={{0,1},{1,0},{2,3},{3,2},{4,5},{5,4},{6,7},{7,6},{8,9},{9,8},{10,11... | collective-permute-start | bytes 294920 | tf_op jit(solution)/shard_map/ppermute | solution.py:63
  72.6 10.7 %collective-permute-start.19 = (bf16[64,768]{1,0:T(8,128)(2,1)S(1)}, bf16[64,768]{1,0:T(8,128)(2,1)S(1)}, u32[]{:S(2)}, u32[]{:S(2)}) collective-permute-start(bf16[64,768]{1,0:T(8,128)(2,1)S(1)} %get-tuple-element.161), channel_id=1, source_target_pairs={{0,2},{1,3},{2,0},{3,1},{4,6},{5,7},{6,4},{7,5},{8,10},{9,11},{10,... | collective-permute-start | bytes 294920 | tf_op jit(solution)/shard_map/ppermute | solution.py:63
  73.9 9.4 %collective-permute-start.20 = (bf16[64,768]{1,0:T(8,128)(2,1)S(1)}, bf16[64,768]{1,0:T(8,128)(2,1)S(1)}, u32[]{:S(2)}, u32[]{:S(2)}) collective-permute-start(bf16[64,768]{1,0:T(8,128)(2,1)S(1)} %get-tuple-element.162), channel_id=1, source_target_pairs={{0,3},{1,2},{2,1},{3,0},{4,7},{5,6},{6,5},{7,4},{8,11},{9,10},{10,... | collective-permute-start | bytes 294920 | tf_op jit(solution)/shard_map/ppermute | solution.py:63
  84.8 7.5 %collective-permute-start.24 = (bf16[64,768]{1,0:T(8,128)(2,1)S(1)}, bf16[64,768]{1,0:T(8,128)(2,1)S(1)}, u32[]{:S(2)}, u32[]{:S(2)}) collective-permute-start(bf16[64,768]{1,0:T(8,128)(2,1)S(1)} %shard_map.329.refs_0_), channel_id=1, source_target_pairs={{0,3},{1,2},{2,1},{3,0},{4,7},{5,6},{6,5},{7,4},{8,11},{9,10},{10,... | collective-permute-start | bytes 294920 | tf_op jit(solution)/shard_map/ppermute | solution.py:63
  86.7 9.1 %collective-permute-start.23 = (bf16[64,768]{1,0:T(8,128)(2,1)S(1)}, bf16[64,768]{1,0:T(8,128)(2,1)S(1)}, u32[]{:S(2)}, u32[]{:S(2)}) collective-permute-start(bf16[64,768]{1,0:T(8,128)(2,1)S(1)} %shard_map.329.refs_0_), channel_id=1, source_target_pairs={{0,2},{1,3},{2,0},{3,1},{4,6},{5,7},{6,4},{7,5},{8,10},{9,11},{10,... | collective-permute-start | bytes 294920 | tf_op jit(solution)/shard_map/ppermute | solution.py:63
  88.2 7.5 %collective-permute-start.22 = (bf16[64,768]{1,0:T(8,128)(2,1)S(1)}, bf16[64,768]{1,0:T(8,128)(2,1)S(1)}, u32[]{:S(2)}, u32[]{:S(2)}) collective-permute-start(bf16[64,768]{1,0:T(8,128)(2,1)S(1)} %shard_map.329.refs_0_), channel_id=1, source_target_pairs={{0,1},{1,0},{2,3},{3,2},{4,5},{5,4},{6,7},{7,6},{8,9},{9,8},{10,11... | collective-permute-start | bytes 294920 | tf_op jit(solution)/shard_map/ppermute | solution.py:63
  89.3 7.6 %collective-permute-start.26 = (bf16[192,768]{1,0:T(8,128)(2,1)S(1)}, bf16[192,768]{1,0:T(8,128)(2,1)S(1)}, u32[]{:S(2)}, u32[]{:S(2)}) collective-permute-start(bf16[192,768]{1,0:T(8,128)(2,1)S(1)} %get-tuple-element.187), channel_id=1, source_target_pairs={{0,16},{8,24},{16,0},{24,8},{1,17},{9,25},{17,1},{25,9},{2,18},{10... | collective-permute-start | bytes 884744 | tf_op jit(solution)/shard_map/ppermute | solution.py:63
  89.3 7.6 %collective-permute-start.25 = (bf16[192,768]{1,0:T(8,128)(2,1)S(1)}, bf16[192,768]{1,0:T(8,128)(2,1)S(1)}, u32[]{:S(2)}, u32[]{:S(2)}) collective-permute-start(bf16[192,768]{1,0:T(8,128)(2,1)S(1)} %get-tuple-element.173), channel_id=1, source_target_pairs={{0,8},{8,0},{16,24},{24,16},{1,9},{9,1},{17,25},{25,17},{2,10},{10... | collective-permute-start | bytes 884744 | tf_op jit(solution)/shard_map/ppermute | solution.py:63
  97.0 5.5 %collective-permute-start.36 = (bf16[96,768]{1,0:T(8,128)(2,1)S(1)}, bf16[96,768]{1,0:T(8,128)(2,1)S(1)}, u32[]{:S(2)}, u32[]{:S(2)}) collective-permute-start(bf16[96,768]{1,0:T(8,128)(2,1)S(1)} %get-tuple-element.189), channel_id=1, source_target_pairs={{0,8},{8,0},{16,24},{24,16},{1,9},{9,1},{17,25},{25,17},{2,10},{10... | collective-permute-start | bytes 442376 | tf_op jit(solution)/shard_map/ppermute | solution.py:63
  97.3 5.1 %collective-permute-start.37 = (bf16[96,768]{1,0:T(8,128)(2,1)S(1)}, bf16[96,768]{1,0:T(8,128)(2,1)S(1)}, u32[]{:S(2)}, u32[]{:S(2)}) collective-permute-start(bf16[96,768]{1,0:T(8,128)(2,1)S(1)} %get-tuple-element.215), channel_id=1, source_target_pairs={{0,16},{8,24},{16,0},{24,8},{1,17},{9,25},{17,1},{25,9},{2,18},{10... | collective-permute-start | bytes 442376 | tf_op jit(solution)/shard_map/ppermute | solution.py:63
  103.8 6.7 %collective-permute-start.38 = (bf16[512,768]{1,0:T(8,128)(2,1)S(1)}, bf16[512,768]{1,0:T(8,128)(2,1)S(1)}, u32[]{:S(2)}, u32[]{:S(2)}) collective-permute-start(bf16[512,768]{1,0:T(8,128)(2,1)S(1)} %get-tuple-element.224), channel_id=1, source_target_pairs={{0,4},{4,0},{1,5},{5,1},{2,6},{6,2},{3,7},{7,3},{8,12},{12,8},{9,1... | collective-permute-start | bytes 2359304 | tf_op jit(solution)/shard_map/ppermute | solution.py:63
  103.9 10.6 %collective-permute-start.27 = (bf16[128,768]{1,0:T(8,128)(2,1)S(1)}, bf16[128,768]{1,0:T(8,128)(2,1)S(1)}, u32[]{:S(2)}, u32[]{:S(2)}) collective-permute-start(bf16[128,768]{1,0:T(8,128)(2,1)S(1)} %get-tuple-element.191), channel_id=1, source_target_pairs={{0,1},{1,0},{2,3},{3,2},{4,5},{5,4},{6,7},{7,6},{8,9},{9,8},{10,11... | collective-permute-start | bytes 589832 | tf_op jit(solution)/shard_map/ppermute | solution.py:63
  105.4 17.1 %collective-permute-start.28 = (bf16[128,768]{1,0:T(8,128)(2,1)S(1)}, bf16[128,768]{1,0:T(8,128)(2,1)S(1)}, u32[]{:S(2)}, u32[]{:S(2)}) collective-permute-start(bf16[128,768]{1,0:T(8,128)(2,1)S(1)} %get-tuple-element.192), channel_id=1, source_target_pairs={{0,2},{1,3},{2,0},{3,1},{4,6},{5,7},{6,4},{7,5},{8,10},{9,11},{10,... | collective-permute-start | bytes 589832 | tf_op jit(solution)/shard_map/ppermute | solution.py:63
  106.4 16.2 %collective-permute-start.29 = (bf16[128,768]{1,0:T(8,128)(2,1)S(1)}, bf16[128,768]{1,0:T(8,128)(2,1)S(1)}, u32[]{:S(2)}, u32[]{:S(2)}) collective-permute-start(bf16[128,768]{1,0:T(8,128)(2,1)S(1)} %get-tuple-element.193), channel_id=1, source_target_pairs={{0,3},{1,2},{2,1},{3,0},{4,7},{5,6},{6,5},{7,4},{8,11},{9,10},{10,... | collective-permute-start | bytes 589832 | tf_op jit(solution)/shard_map/ppermute | solution.py:63
  111.5 14.7 %collective-permute-start.40 = (bf16[320,768]{1,0:T(8,128)(2,1)S(1)}, bf16[320,768]{1,0:T(8,128)(2,1)S(1)}, u32[]{:S(2)}, u32[]{:S(2)}) collective-permute-start(bf16[320,768]{1,0:T(8,128)(2,1)S(1)} %get-tuple-element.229.sent2), channel_id=1, source_target_pairs={{0,16},{8,24},{16,0},{24,8},{1,17},{9,25},{17,1},{25,9},{2,18},{10... | collective-permute-start | bytes 1474568 | tf_op jit(solution)/shard_map/ppermute | solution.py:63
  112.9 13.9 %collective-permute-start.39 = (bf16[320,768]{1,0:T(8,128)(2,1)S(1)}, bf16[320,768]{1,0:T(8,128)(2,1)S(1)}, u32[]{:S(2)}, u32[]{:S(2)}) collective-permute-start(bf16[320,768]{1,0:T(8,128)(2,1)S(1)} %get-tuple-element.228.sent1), channel_id=1, source_target_pairs={{0,8},{8,0},{16,24},{24,16},{1,9},{9,1},{17,25},{25,17},{2,10},{10... | collective-permute-start | bytes 1474568 | tf_op jit(solution)/shard_map/ppermute | solution.py:63
  122.6 7.3 %collective-permute-start.30 = (bf16[96,768]{1,0:T(8,128)(2,1)S(1)}, bf16[96,768]{1,0:T(8,128)(2,1)S(1)}, u32[]{:S(2)}, u32[]{:S(2)}) collective-permute-start(bf16[96,768]{1,0:T(8,128)(2,1)S(1)} %get-tuple-element.202), channel_id=1, source_target_pairs={{0,8},{8,0},{16,24},{24,16},{1,9},{9,1},{17,25},{25,17},{2,10},{10... | collective-permute-start | bytes 442376 | tf_op jit(solution)/shard_map/ppermute | solution.py:63
  124.0 9.6 %collective-permute-start.31 = (bf16[96,768]{1,0:T(8,128)(2,1)S(1)}, bf16[96,768]{1,0:T(8,128)(2,1)S(1)}, u32[]{:S(2)}, u32[]{:S(2)}) collective-permute-start(bf16[96,768]{1,0:T(8,128)(2,1)S(1)} %get-tuple-element.203), channel_id=1, source_target_pairs={{0,16},{8,24},{16,0},{24,8},{1,17},{9,25},{17,1},{25,9},{2,18},{10... | collective-permute-start | bytes 442376 | tf_op jit(solution)/shard_map/ppermute | solution.py:63
  125.6 8.0 %collective-permute-start.32 = (bf16[96,768]{1,0:T(8,128)(2,1)S(1)}, bf16[96,768]{1,0:T(8,128)(2,1)S(1)}, u32[]{:S(2)}, u32[]{:S(2)}) collective-permute-start(bf16[96,768]{1,0:T(8,128)(2,1)S(1)} %get-tuple-element.204), channel_id=1, source_target_pairs={{0,24},{8,16},{16,8},{24,0},{1,25},{9,17},{17,9},{25,1},{2,26},{10... | collective-permute-start | bytes 442376 | tf_op jit(solution)/shard_map/ppermute | solution.py:63
  126.9 10.1 %collective-permute-start.41 = (bf16[160,768]{1,0:T(8,128)(2,1)S(1)}, bf16[160,768]{1,0:T(8,128)(2,1)S(1)}, u32[]{:S(2)}, u32[]{:S(2)}) collective-permute-start(bf16[160,768]{1,0:T(8,128)(2,1)S(1)} %get-tuple-element.233), channel_id=1, source_target_pairs={{0,8},{8,0},{16,24},{24,16},{1,9},{9,1},{17,25},{25,17},{2,10},{10... | collective-permute-start | bytes 737288 | tf_op jit(solution)/shard_map/ppermute | solution.py:63
  128.6 8.7 %collective-permute-start.42 = (bf16[160,768]{1,0:T(8,128)(2,1)S(1)}, bf16[160,768]{1,0:T(8,128)(2,1)S(1)}, u32[]{:S(2)}, u32[]{:S(2)}) collective-permute-start(bf16[160,768]{1,0:T(8,128)(2,1)S(1)} %get-tuple-element.234), channel_id=1, source_target_pairs={{0,16},{8,24},{16,0},{24,8},{1,17},{9,25},{17,1},{25,9},{2,18},{10... | collective-permute-start | bytes 737288 | tf_op jit(solution)/shard_map/ppermute | solution.py:63
  138.0 7.1 %collective-permute-start.43 = (bf16[768,768]{1,0:T(8,128)(2,1)S(1)}, bf16[768,768]{1,0:T(8,128)(2,1)S(1)}, u32[]{:S(2)}, u32[]{:S(2)}) collective-permute-start(bf16[768,768]{1,0:T(8,128)(2,1)S(1)} %get-tuple-element.236.mine), channel_id=1, source_target_pairs={{0,4},{4,0},{1,5},{5,1},{2,6},{6,2},{3,7},{7,3},{8,12},{12,8},{9,1... | collective-permute-start | bytes 3538952 | tf_op jit(solution)/shard_map/ppermute | solution.py:63
  138.1 13.2 %collective-permute-start.35 = (bf16[128,768]{1,0:T(8,128)(2,1)S(1)}, bf16[128,768]{1,0:T(8,128)(2,1)S(1)}, u32[]{:S(2)}, u32[]{:S(2)}) collective-permute-start(bf16[128,768]{1,0:T(8,128)(2,1)S(1)} %get-tuple-element.210.t0), channel_id=1, source_target_pairs={{0,3},{1,2},{2,1},{3,0},{4,7},{5,6},{6,5},{7,4},{8,11},{9,10},{10,... | collective-permute-start | bytes 589832 | tf_op jit(solution)/shard_map/ppermute | solution.py:63
  140.1 19.8 %collective-permute-start.34 = (bf16[128,768]{1,0:T(8,128)(2,1)S(1)}, bf16[128,768]{1,0:T(8,128)(2,1)S(1)}, u32[]{:S(2)}, u32[]{:S(2)}) collective-permute-start(bf16[128,768]{1,0:T(8,128)(2,1)S(1)} %get-tuple-element.210.t0), channel_id=1, source_target_pairs={{0,2},{1,3},{2,0},{3,1},{4,6},{5,7},{6,4},{7,5},{8,10},{9,11},{10,... | collective-permute-start | bytes 589832 | tf_op jit(solution)/shard_map/ppermute | solution.py:63
  143.9 16.0 %collective-permute-start.33 = (bf16[128,768]{1,0:T(8,128)(2,1)S(1)}, bf16[128,768]{1,0:T(8,128)(2,1)S(1)}, u32[]{:S(2)}, u32[]{:S(2)}) collective-permute-start(bf16[128,768]{1,0:T(8,128)(2,1)S(1)} %get-tuple-element.210.t0), channel_id=1, source_target_pairs={{0,1},{1,0},{2,3},{3,2},{4,5},{5,4},{6,7},{7,6},{8,9},{9,8},{10,11... | collective-permute-start | bytes 589832 | tf_op jit(solution)/shard_map/ppermute | solution.py:63
  143.9 4.7 %collective-permute-start.45 = (bf16[64,768]{1,0:T(8,128)(2,1)S(1)}, bf16[64,768]{1,0:T(8,128)(2,1)S(1)}, u32[]{:S(2)}, u32[]{:S(2)}) collective-permute-start(bf16[64,768]{1,0:T(8,128)(2,1)S(1)} %get-tuple-element.238.sent2), channel_id=1, source_target_pairs={{0,16},{8,24},{16,0},{24,8},{1,17},{9,25},{17,1},{25,9},{2,18},{10... | collective-permute-start | bytes 294920 | tf_op jit(solution)/shard_map/ppermute | solution.py:63
  145.1 4.6 %collective-permute-start.44 = (bf16[64,768]{1,0:T(8,128)(2,1)S(1)}, bf16[64,768]{1,0:T(8,128)(2,1)S(1)}, u32[]{:S(2)}, u32[]{:S(2)}) collective-permute-start(bf16[64,768]{1,0:T(8,128)(2,1)S(1)} %get-tuple-element.237.sent1), channel_id=1, source_target_pairs={{0,8},{8,0},{16,24},{24,16},{1,9},{9,1},{17,25},{25,17},{2,10},{10... | collective-permute-start | bytes 294920 | tf_op jit(solution)/shard_map/ppermute | solution.py:63
  149.7 11.9 %collective-permute-start.47 = (bf16[128,768]{1,0:T(8,128)(2,1)S(1)}, bf16[128,768]{1,0:T(8,128)(2,1)S(1)}, u32[]{:S(2)}, u32[]{:S(2)}) collective-permute-start(bf16[128,768]{1,0:T(8,128)(2,1)S(1)} %get-tuple-element.243.sent2), channel_id=1, source_target_pairs={{0,16},{8,24},{16,0},{24,8},{1,17},{9,25},{17,1},{25,9},{2,18},{10... | collective-permute-start | bytes 589832 | tf_op jit(solution)/shard_map/ppermute | solution.py:63
  150.6 11.1 %collective-permute-start.46 = (bf16[128,768]{1,0:T(8,128)(2,1)S(1)}, bf16[128,768]{1,0:T(8,128)(2,1)S(1)}, u32[]{:S(2)}, u32[]{:S(2)}) collective-permute-start(bf16[128,768]{1,0:T(8,128)(2,1)S(1)} %get-tuple-element.242.sent1), channel_id=1, source_target_pairs={{0,8},{8,0},{16,24},{24,16},{1,9},{9,1},{17,25},{25,17},{2,10},{10... | collective-permute-start | bytes 589832 | tf_op jit(solution)/shard_map/ppermute | solution.py:63
  162.3 2.4 %collective-permute-start.48 = (bf16[512,768]{1,0:T(8,128)(2,1)S(1)}, bf16[512,768]{1,0:T(8,128)(2,1)S(1)}, u32[]{:S(2)}, u32[]{:S(2)}) collective-permute-start(bf16[512,768]{1,0:T(8,128)(2,1)S(1)} %shard_map.344.mine), channel_id=1, source_target_pairs={{0,4},{4,0},{1,5},{5,1},{2,6},{6,2},{3,7},{7,3},{8,12},{12,8},{9,1... | collective-permute-start | bytes 2359304 | tf_op jit(solution)/shard_map/ppermute | solution.py:63
  (3 other events, 19.0 us)

commit v2 on v1

--- a/solution.py
+++ b/solution.py
@@ -25,9 +25,10 @@
     return jax.ShapeDtypeStruct(shape, LOW)
 
 
-def kernel(body, outs, args, smem=0, scratch=(), micros=1.0, limit=16, hbm=()):
+def kernel(body, outs, args, smem=0, scratch=(), micros=1.0, limit=16, hbm=(), reused=0):
     in_specs = [pl.BlockSpec(memory_space=pltpu.SMEM)] * smem
-    in_specs += [pl.BlockSpec(memory_space=pltpu.VMEM)] * (len(args) - smem)
+    in_specs += [pl.BlockSpec(memory_space=pltpu.VMEM)] * (len(args) - smem - reused)
+    in_specs += [pl.BlockSpec(memory_space=pltpu.HBM)] * reused
     whole = pl.BlockSpec(memory_space=pltpu.VMEM)
     if isinstance(outs, list):
         out_specs = [pl.BlockSpec(memory_space=pltpu.HBM) if n in hbm else whole for n in range(len(outs))]
@@ -39,6 +40,7 @@
         in_specs=in_specs,
         out_specs=out_specs,
         scratch_shapes=list(scratch),
+        input_output_aliases={len(args) - reused + n: n for n in range(reused)},
         compiler_params=pltpu.CompilerParams(vmem_limit_bytes=limit * MIB),
         cost_estimate=pl.CostEstimate(
             flops=int(micros * 4e8), bytes_accessed=int(micros * 3e6), transcendentals=0
@@ -351,52 +353,55 @@
     first_step(ids[0], lambda at: scr[at, :], kept, (rows, along1), (rows, along2))
 
 
-def feed_second_body(kept, came1, came2, own, along1, along2):
-    second_step(kept, came1, came2, own, along1, along2)
-
-
-def attend_first_body(ids, keep, arrived, rel, feed_own, came1, came2, kept, along1, along2, scr):
+def step_a_body(ids, keep, arrived, rel, feed_kept, came1, came2, kept, feed_own, along1, along2, scr):
     rows = keep.shape[0] // 4
     scr[...] = keep[...] + arrived[...].astype(F32)
     scr[-rel.shape[0] :, : rel.shape[1]] = rel[...]
     first_step(ids[0], lambda at: scr[at, :], kept, (rows, along1), (rows, along2))
-    upper, lower = last_sums(feed_own, came1, came2)
+    second_step(feed_kept, came1, came2, feed_own, along1.at[rows:, :], along2.at[rows:, :])
+
+
+def step_b_body(kept, feed_own, came1, came2, own, along1, along2):
+    few = own.shape[0] // 2
+    skip = 2 * few
+    first = slice(0, skip)
+    second_step(
+        kept, came1.at[first, :], came2.at[first, :], own, along1.at[slice(0, few), :], along2.at[slice(0, few), :]
+    )
+    upper, lower = last_sums(feed_own, came1.at[skip:, :], came2.at[skip:, :])
     for out, parts in ((along1, (lower, upper)), (along2, (upper, lower))):
         for n, part in enumerate(parts):
-            out[rows + n * part.shape[0] : rows + (n + 1) * part.shape[0], :] = part
-
-
-def attend_second_body(kept, came1, came2, own, along1, along2):
-    rows = own.shape[0] // 2
-    done = along1.shape[0] - rows
-    at = slice(2 * rows, 2 * rows + done)
-    along1[:done, :] = came2[at, :]
-    along2[:done, :] = came1[at, :]
-    second_step(kept, came1, came2, own, along1.at[done:, :], along2.at[done:, :])
-
-
-def third_body(ids, own, sent1, sent2, near1, near2, came1, came2, feed, along1, along2):
-    rows = along1.shape[0]
-    done = came1.shape[0] - rows
-    first, second = slice(2 * rows, 2 * rows + done), slice(2 * rows + done, 2 * (rows + done))
-    upper = ((sent2, first), (near1, second), (near2, first), (came1, slice(0, done)))
-    lower = ((sent1, first), (near1, first), (near2, second), (came2, slice(0, done)))
+            out[few + n * part.shape[0] : few + (n + 1) * part.shape[0], :] = part
+
+
+def step_c_body(own, came1, came2, along1, along2):
+    first = slice(0, along1.shape[0])
+    along2[...], along1[...] = last_sums(own, came1.at[first, :], came2.at[first, :])
+
+
+def step_d_body(mid1, mid2, came1, came2, near1, near2, along1, along2):
+    few = mid1.shape[0]
+    done = along1.shape[0] - 2 * few
+    for out, own, came, near in ((along1, mid2, came2, near2), (along2, mid1, came1, near1)):
+        out[:few, :] = own[...]
+        out[few : 2 * few, :] = came[...]
+        out[2 * few :, :] = near[few : few + done, :]
+
+
+def feed_join_body(ids, sent1, sent2, near1, near2, came1, came2, out):
+    rows = out.shape[0] // 8
+    few = sent1.shape[0] - 2 * rows
+    skip = came1.shape[0] - rows
+    first, second, last = slice(few, few + rows), slice(few + rows, few + 2 * rows), slice(skip, skip + rows)
+    upper = ((sent2, first), (near1, second), (near2, first), (came1, last))
+    lower = ((sent1, first), (near1, first), (near2, second), (came2, last))
     for half, blocks in enumerate((upper, lower)):
         for k, (ref, at) in enumerate(blocks):
-            to = pl.multiple_of((4 * half + (ids[0] ^ k)) * done, done)
-            feed[pl.ds(to, done), :] = ref[at, :]
-    along2[...], along1[...] = last_sums(own, came1.at[done:, :], came2.at[done:, :])
-
-
-def fourth_body(sent1, sent2, came1, came2, along1, along2):
-    rows = sent1.shape[0]
-    along1[:rows, :] = sent2[...]
-    along1[rows:, :] = came2[...]
-    along2[:rows, :] = sent1[...]
-    along2[rows:, :] = came1[...]
-
-
-def attend_join_body(ids, sent1, sent2, came1, came2, out):
+            to = pl.multiple_of((4 * half + (ids[0] ^ k)) * rows, rows)
+            out[pl.ds(to, rows), :] = ref[at, :]
+
+
+def attend_join_body(ids, sent1, sent2, came1, came2, seen, out):
     join_half(ids[0], sent1, sent2, came1, came2, out)
 
 
@@ -485,30 +490,61 @@
     out[...] = total_of(own, (r1, r2, r3)).astype(LOW)
 
 
-def unpack_feed_body(ids, mine, other, first, second):
-    for c, (a, b) in ((0, (mine, other)), (1, (other, mine))):
-
-        @pl.when(ids[2] == c)
-        def _(a=a, b=b):
-            first[...] = a[...].astype(F32)
-            second[...] = b[...].astype(F32)
-
-
-def unpack_attend_body(ids, mine, other, dq, dk, dv, do, tail_a, tail_b):
+def widen_body(flip, ids, rows, *refs):
+    first, second, scr, sem = refs[-4:]
+    step = rows.shape[0] // 4
+    for c, out in ((0, first), (1, second)):
+
+        @pl.when((ids[2] ^ flip) == c)
+        def _(out=out):
+            copies = []
+            for n in range(4):
+                span = pl.ds(n * step, step)
+                scr[span, :] = rows[span, :].astype(F32)
+                copies.append(pltpu.make_async_copy(scr.at[span, :], out.at[span, :], sem.at[n]))
+                copies[-1].start()
+            for copy in copies:
+                copy.wait()
+
+
+def output_body(ids, n0, q1, q2, q3, output):
+    rows = n0.shape[0]
+    output[ids[0]] = n0[...]
+    for b, q in ((1, q1), (2, q2), (3, q3)):
+        output[ids[0] ^ b] = q[q.shape[0] - rows :, :]
+
+
+def unpack_attend_body(ids, mine, other, dq, dk, dv, do, *rest):
+    *rows_out, query_out, value_out, rel_out = rest
     part = dq.shape[0]
+    heads = rel_out.shape[0]
+    head = part // heads
     for c, (a, b) in ((0, (mine, other)), (1, (other, mine))):
 
         @pl.when(ids[2] == c)
         def _(a=a, b=b):
             dq[...] = a[:part, :].astype(F32)
             dk[...] = a[part : 2 * part, :].astype(F32)
-            tail_a[...] = a[2 * part :, :].astype(F32)
             dv[...] = b[:part, :].astype(F32)
             do[...] = b[part : 2 * part, :].astype(F32)
-            tail_b[...] = b[2 * part :, :].astype(F32)
-
-
-def quarters_body(r1, r2, r3, own, n1, n2, n3, q0, q1, q2, q3):
+            small_a = a[2 * part :, :].astype(F32)
+            small_b = b[2 * part :, :].astype(F32)
+            for n, out in enumerate(rows_out):
+                row = n if n < 4 else SMALL_ROWS + n - 4
+                out[...] = small_a[row, :]
+            for out, row in ((query_out, 0), (value_out, 8)):
+                out[...] = jnp.concatenate(
+                    [small_b[h * SMALL_ROWS + row : h * SMALL_ROWS + row + 1, :head] for h in range(heads)], axis=1
+                )[0]
+            last = small_a.shape[0] - 32
+            table = small_a[last:, :128] + small_b[last:, :128]
+            for h in range(heads):
+                for index in range(BASES):
+                    at = h * BASES + index
+                    rel_out[h : h + 1, index : index + 1] = table[at : at + 1, :1]
+
+
+def quarters_body(met, r1, r2, r3, own, n1, n2, n3, q0, q1, q2, q3):
     total = total_of(own, (r1, r2, r3)).astype(LOW)
     rows = q0.shape[0]
     q0[...] = total[:rows]
@@ -517,13 +553,15 @@
         q[rows:, :] = n[...]
 
 
-def join_body(ids, q0, q1, q2, q3, n0, joined, output):
+def join_body(q0, q1, q2, q3, joined):
     rows = q0.shape[0]
     for b, q in enumerate((q0, q1, q2, q3)):
         joined[b * rows : (b + 1) * rows, :] = q[:rows, :]
-    output[ids[0]] = n0[...]
-    for b, q in ((1, q1), (2, q2), (3, q3)):
-        output[ids[0] ^ b] = q[rows:, :]
+
+
+def touch_body(t1, t2, t3, out):
+    rows = out.shape[0]
+    out[...] = t1[:rows, :] + t2[:rows, :] + t3[:rows, :]
 
 
 def place_body(ids, t0, t1, t2, t3, out):
@@ -643,11 +681,11 @@
     operands = (hidden, grad_mixed, normed, upward)
     sides = [pltpu.VMEM((slots, width), LOW)] * 2
     feed_send = kernel(
-        feed_send_body, low(width, width), (ids, *operands), smem=1, scratch=sides, micros=1.2
+        feed_send_body, low(width, width), (ids, *operands), smem=1, scratch=sides, micros=0.1
     )
     feed_arrived = swap(feed_send, "dp", dp_size, 1)
     arrived = scatter_low((p1, p2, p3), "mp", mp_size)
-    grad_normed = kernel(total_body, low(half, width), (*arrived, after(own, feed_arrived)), micros=0.5)
+    grad_normed = kernel(total_body, low(half, width), (*arrived, own), micros=40.0)
     rows = width // 8
     feed_kept, along1, along2 = kernel(
         feed_keep_body,
@@ -655,9 +693,9 @@
         (ids, *operands, after(feed_arrived, grad_normed)),
         smem=1,
         scratch=sides + [pltpu.VMEM((width, width), F32)],
-        micros=1.5,
-    )
-    s = gather_low(after(grad_normed, along1), "mp", mp_size)
+        micros=0.1,
+    )
+    s = gather_low(grad_normed, "mp", mp_size)
     came = both_ways(along1, along2, seq_size)
     grad, grad_attended, small_attend = kernel(
         norm_back_body,
@@ -666,16 +704,12 @@
         smem=1,
         micros=6.5,
     )
-    feed_own, along1, along2 = kernel(
-        feed_second_body, [f32(2 * rows, width)] + [low(rows, width)] * 2, (feed_kept, came[0], after(came[1], grad_attended)), micros=0.2
-    )
-    came = both_ways(along1, along2, seq_size)
     own_input, o1, o2, o3, scores, stack, sums = kernel(
         functools.partial(attend_back_body, heads, query_scale),
         [f32(block_len, width)]
         + [low(block_len, width)] * 3
         + [f32(heads, full, slots), low(3 * part, full), f32(heads, 16, head)],
-        (ids, grad, grad_attended, wq, wk, wv, out_weight, probs, qt, kt, after(vt, along1)),
+        (ids, grad, grad_attended, wq, wk, wv, out_weight, probs, qt, kt, vt),
         smem=1,
         scratch=[
             pltpu.VMEM((3 * part, width), LOW),
@@ -683,7 +717,7 @@
             pltpu.VMEM((part, full), LOW),
             pltpu.VMEM((full, width), F32),
         ],
-        micros=6.0,
+        micros=0.1,
     )
     rel = kernel(
         functools.partial(rel_body, heads, block_len, 32),
@@ -700,103 +734,108 @@
         (ids, after(tokens, came), grad_attended, pooled_low, stack, ct, small_feed, small_attend, sums),
         smem=1,
         scratch=[pltpu.VMEM((2, half_rows, width), F32)],
-        micros=1.5,
+        micros=0.1,
     )
     landed = scatter_low((o1, o2, o3), "mp", mp_size)
     attend_arrived = swap(attend_send, "dp", dp_size, 1)
     few = half_rows // 8
-    attend_kept, sent1, sent2 = kernel(
-        attend_first_body,
-        [f32(4 * few, width)] + [low(2 * few + 2 * rows, width)] * 2,
-        (ids, attend_keep, attend_arrived, rel, feed_own, *came),
+    attend_kept, feed_own, along1, along2 = kernel(
+        step_a_body,
+        [f32(4 * few, width), f32(2 * rows, width)] + [low(2 * few + rows, width)] * 2,
+        (ids, attend_keep, attend_arrived, rel, feed_kept, *came),
         smem=1,
         scratch=[pltpu.VMEM((half_rows, width), F32)],
         micros=0.1,
     )
-    early = both_ways(sent1, sent2, seq_size)
+    met = kernel(touch_body, low(SMALL_ROWS, width), tuple(landed), micros=6.0)
     quarter = block_len // 4
     q0, *q = kernel(
         quarters_body,
         [low(quarter, width)] + [low(quarter + half, width)] * 3,
-        (*landed, own_input, *outputs[1:]),
-        micros=8.0,
-    )
-    attend_own, along1, along2 = kernel(
-        attend_second_body,
-        [f32(2 * few, width)] + [low(rows + few, width)] * 2,
-        (attend_kept, early[0], after(early[1], q0)),
-        micros=0.2,
-    )
+        (met, *landed, own_input, *outputs[1:]),
+        micros=0.5,
+    )
+    attend_own, sent1, sent2 = kernel(
+        step_b_body,
+        [f32(2 * few, width)] + [low(few + 2 * rows, width)] * 2,
+        (attend_kept, after(feed_own, q0), *both_ways(along1, along2, seq_size)),
+        micros=0.1,
+    )
+    near = both_ways(sent1, sent2, seq_size)
     q = deep(scatter_low(q, "seq", seq_size))
+    joined = kernel(join_body, low(block_len, width), (q0, *q), micros=8.0)
+    spread = gather_low(joined, "mp", mp_size)
+    mid = kernel(
+        step_c_body, [low(few, width)] * 2, (after(attend_own, joined), *near), micros=0.1
+    )
+    output_all = kernel(output_body, low(4, half, width), (ids, outputs[0], *q), smem=1, micros=0.1)
+    along1, along2 = kernel(
+        step_d_body,
+        [low(2 * few + rows, width)] * 2,
+        (after(mid[0], output_all), mid[1], *both_ways(*mid, seq_size), *near),
+        micros=0.1,
+    )
     came = both_ways(along1, along2, seq_size)
-    joined, output_all = kernel(
-        join_body,
-        [low(block_len, width), low(4, half, width)],
-        (ids, q0, *q, outputs[0]),
-        smem=1,
-        micros=2.8,
-    )
-    spread = gather_low(joined, "mp", mp_size)
-    feed_mine, along1, along2 = dp_sum(
-        kernel(
-            third_body,
-            [low(width, width)] + [low(few, width)] * 2,
-            (ids, after(attend_own, joined), sent1, sent2, *early, *came),
-            smem=1,
-            micros=0.2,
-        ),
-        dp_size,
-    )
-    feed_other = swap(feed_mine, "dp", dp_size, 1)
-    sent = (after(along1, feed_other), along2)
-    down_grad, up_grad = kernel(
-        unpack_feed_body, [f32(width, width)] * 2, (ids, feed_mine, feed_other), smem=1, micros=0.1
-    )
-    along1, along2 = kernel(
-        fourth_body, [low(2 * few, width)] * 2, (*sent, *after(both_ways(*sent, seq_size), down_grad)), micros=0.1
-    )
-    came = both_ways(along1, along2, seq_size)
-    input_all = kernel(
-        place_body, f32(4, block_len, width), (ids, joined, *spread), smem=1, micros=3.0
-    )
+    seen = kernel(touch_body, low(SMALL_ROWS, width), tuple(spread), micros=8.0)
     attend_mine = kernel(
         attend_join_body,
         low(half_rows, width),
-        (ids, along1, along2, came[0], after(came[1], input_all)),
+        (ids, along1, along2, *came, seen),
         smem=1,
         micros=0.2,
     )
+    feed_mine = kernel(
+        feed_join_body,
+        low(width, width),
+        (ids, sent1, sent2, *near, came[0], after(came[1], attend_mine)),
+        smem=1,
+        micros=0.1,
+    )
+    attend_mine, feed_mine = dp_sum((attend_mine, feed_mine), dp_size)
     attend_other = swap(attend_mine, "dp", dp_size, 1)
-    tail_rows = half_rows - 2 * part
-    dq, dk, dv, do, tail_a, tail_b = kernel(
+    feed_other = swap(feed_mine, "dp", dp_size, 1)
+    widen = lambda flip, *args: kernel(
+        functools.partial(widen_body, flip),
+        [f32(width, width)] * 2,
+        (ids, *args),
+        smem=1,
+        scratch=[pltpu.VMEM((width, width), F32), pltpu.SemaphoreType.DMA((4,))],
+        micros=0.1,
+        hbm=(0, 1),
+        reused=len(args) - 1,
+    )
+    halves = widen(0, feed_mine)
+    down_grad, up_grad = widen(1, feed_other, *halves)
+    input_all = kernel(
+        place_body, f32(4, block_len, width), (ids, joined, *spread), smem=1, micros=0.1
+    )
+    dq, dk, dv, do, *small, query_sum, value_sum, rel_sum = kernel(
         unpack_attend_body,
-        [f32(part, width)] * 4 + [f32(tail_rows, width)] * 2,
-        (ids, attend_mine, attend_other),
+        [f32(part, width)] * 4 + [f32(width)] * 7 + [f32(part)] * 2 + [f32(heads, BASES)],
+        (ids, after(attend_mine, halves), attend_other),
         smem=1,
         micros=1.5,
     )
-    bias_sums = tail_b[: heads * SMALL_ROWS, :head].reshape(heads, SMALL_ROWS, head)
-    rel_sums = (tail_a + tail_b)[tail_rows - 32 : tail_rows - 32 + heads * BASES, 0].reshape(heads, BASES)
-    first = SMALL_ROWS
+    ffn_gain_sum, ffn_shift_sum, down_bias_sum, up_bias_sum, attn_gain_sum, attn_shift_sum, out_bias_sum = small
     return (
         output_all,
         input_all,
         dq.T,
-        bias_sums[:, 0].reshape(-1),
+        query_sum,
         dk.T,
         dv.T,
-        bias_sums[:, 8].reshape(-1),
-        rel_sums,
+        value_sum,
+        rel_sum,
         do,
-        tail_a[first + 2],
-        tail_a[first],
-        tail_a[first + 1],
+        out_bias_sum,
+        attn_gain_sum,
+        attn_shift_sum,
         up_grad,
-        tail_a[3],
+        up_bias_sum,
         down_grad,
-        tail_a[2],
-        tail_a[0],
-        tail_a[1],
+        down_bias_sum,
+        ffn_gain_sum,
+        ffn_shift_sum,
     )
 
 

time: 170 us -> 163 us (0.959)
  waiting for transfers between devices: 65.6 us -> 55.6 us
  starting transfers between devices: 62.8 us -> 65.6 us
  local copies, waits for them, and re-layouts: 4.87 us -> 2.24 us
    ppermute x49 -> x47, waiting for transfers between devices: 65.6 us -> 55.6 us  [swap(): return lax.ppermute(block, axis, [(s, s ^ k) for s in range(size)])]
    ppermute x49 -> x47, starting transfers between devices: 62.8 us -> 65.6 us  [swap(): return lax.ppermute(block, axis, [(s, s ^ k) for s in range(size)])]
    another operation x3 -> x0, local copies, waits for them, and re-layouts: 1.94 us -> none  [the longest x1 0.66 us: shards(): (tail_a + tail_b)[tail_rows - 32:tail_rows - 32 + heads * BASES, 0]]
    pallas_call x24 -> x28, Pallas kernels: 34.3 us -> 35.5 us  [kernel(): pl.pallas_call(body, out_shape=outs, in_specs=in_specs, out_specs=out_spe...]
  transfers between devices with their start and end apart: 49 -> 47, of which waited for: 26 -> 22; matrix products, arithmetic and copies ran while one was open for 1% -> 1% of each run, Pallas kernels for 11% -> 14%
where the time goes in v2:
time: 163 us; the launch traced here: 161 us
  starting transfers between devices  65.6 us (40%)
  waiting for transfers between devices  55.6 us (34%)
  Pallas kernels  35.5 us (22%)
  local copies, waits for them, and re-layouts  2.24 us (1%)
    ppermute x47, starting transfers between devices, swap(): return lax.ppermute(block, axis, [(s, s ^ k) for s in range(size)])  65.6 us
    ppermute x47, waiting for transfers between devices, swap(): return lax.ppermute(block, axis, [(s, s ^ k) for s in range(size)])  55.6 us
    pallas_call x28, Pallas kernels, kernel(): pl.pallas_call(body, out_shape=outs, in_specs=in_specs, out_specs=out_spe...  35.5 us
  transfers between devices with their start and end apart: 47, of which 22 were waited for; matrix products, arithmetic and copies ran while one was open for 1% of the time, Pallas kernels for 14%

profile of v2, /device:TPU:0, one launch (start us, length us, event | category | flops | bytes accessed | tf_op | source)
XLA Modules:
  0.0 161.0 jit_solution(8495191381932716195)
XLA Ops:
  0.7 1.3 dynamic-slice_bitcast_fusion
  2.0 3.0 %collective-permute-start = (bf16[128,768]{1,0:T(8,128)(2,1)S(1)}, bf16[128,768]{1,0:T(8,128)(2,1)S(1)}, u32[]{:S(2)}, u32[]{:S(2)}) collective-permute-start(bf16[128,768]{1,0:T(8,128)(2,1)S(1)} %get-tuple-element.253), channel_id=1, source_target_pairs={{0,8},{8,0},{16,24},{24,16},{1,9},{9,1},{17,25},{25,17},{2,10},{10... | collective-permute-start | bytes 589832 | tf_op jit(solution)/shard_map/ppermute | solution.py:65
  5.0 1.5 collective-permute-start.1
  8.2 2.1 %shard_map.322.refs_11_ = f32[3,512,256]{2,1,0:T(8,128)S(1)} custom-call(s32[4]{0:T(128)S(1)} %pad_add_fusion.ids, f32[3,8]{1,0:T(4,128)S(1)} %copy-done.6), custom_call_target="tpu_custom_call" | custom-call | flops 1200000000 | bytes 9000000 | tf_op jit(solution)/shard_map/pallas_call | solution.py:37
  10.7 4.8 %collective-permute-done.1.refs_2_ = bf16[128,768]{1,0:T(8,128)(2,1)S(1)} collective-permute-done((bf16[128,768]{1,0:T(8,128)(2,1)S(1)}, bf16[128,768]{1,0:T(8,128)(2,1)S(1)}, u32[]{:S(2)}, u32[]{:S(2)}) %collective-permute-start.1) | collective-permute-done | bytes 196640 | tf_op jit(solution)/shard_map/ppermute | solution.py:65
  15.7 6.3 %shard_map.323 = (f32[64,768]{1,0:T(8,128)S(1)}, bf16[64,768]{1,0:T(8,128)(2,1)S(1)}, bf16[64,768]{1,0:T(8,128)(2,1)S(1)}, bf16[64,768]{1,0:T(8,128)(2,1)S(1)}, ...) custom-call(s32[4]{0:T(128)S(1)} %pad_add_fusion.ids, ...), custom_call_target="tpu_custom_call" | custom-call | flops 2000000000 | bytes 15000000 | tf_op jit(solution)/shard_map/pallas_call | solution.py:37
  22.1 1.6 %collective-permute-start.3 = (bf16[64,768]{1,0:T(8,128)(2,1)S(1)}, bf16[64,768]{1,0:T(8,128)(2,1)S(1)}, u32[]{:S(2)}, u32[]{:S(2)}) collective-permute-start(bf16[64,768]{1,0:T(8,128)(2,1)S(1)} %get-tuple-element.135), channel_id=1, source_target_pairs={{0,1},{1,0},{2,3},{3,2},{4,5},{5,4},{6,7},{7,6},{8,9},{9,8},{10,11... | collective-permute-start | bytes 294920 | tf_op jit(solution)/shard_map/ppermute | solution.py:65
  23.7 2.6 %collective-permute-start.4 = (bf16[64,768]{1,0:T(8,128)(2,1)S(1)}, bf16[64,768]{1,0:T(8,128)(2,1)S(1)}, u32[]{:S(2)}, u32[]{:S(2)}) collective-permute-start(bf16[64,768]{1,0:T(8,128)(2,1)S(1)} %get-tuple-element.136), channel_id=1, source_target_pairs={{0,2},{1,3},{2,0},{3,1},{4,6},{5,7},{6,4},{7,5},{8,10},{9,11},{10,... | collective-permute-start | bytes 294920 | tf_op jit(solution)/shard_map/ppermute | solution.py:65
  26.6 1.1 collective-permute-done.3.r1
  27.7 5.3 %collective-permute-done.4.r2 = bf16[64,768]{1,0:T(8,128)(2,1)S(1)} collective-permute-done((bf16[64,768]{1,0:T(8,128)(2,1)S(1)}, bf16[64,768]{1,0:T(8,128)(2,1)S(1)}, u32[]{:S(2)}, u32[]{:S(2)}) %collective-permute-start.4) | collective-permute-done | bytes 98336 | tf_op jit(solution)/shard_map/ppermute | solution.py:65
  33.1 1.7 %collective-permute-start.6 = (bf16[64,768]{1,0:T(8,128)(2,1)S(1)}, bf16[64,768]{1,0:T(8,128)(2,1)S(1)}, u32[]{:S(2)}, u32[]{:S(2)}) collective-permute-start(bf16[64,768]{1,0:T(8,128)(2,1)S(1)} %shard_map.324.a0), channel_id=1, source_target_pairs={{0,1},{1,0},{2,3},{3,2},{4,5},{5,4},{6,7},{7,6},{8,9},{9,8},{10,11... | collective-permute-start | bytes 294920 | tf_op jit(solution)/shard_map/ppermute | solution.py:65
  34.8 1.4 collective-permute-start.7
  36.2 1.3 collective-permute-start.8
  37.6 1.4 collective-permute-start.10
  39.0 1.6 collective-permute-start.11
  41.1 2.0 %collective-permute-done.7.a2 = bf16[64,768]{1,0:T(8,128)(2,1)S(1)} collective-permute-done((bf16[64,768]{1,0:T(8,128)(2,1)S(1)}, bf16[64,768]{1,0:T(8,128)(2,1)S(1)}, u32[]{:S(2)}, u32[]{:S(2)}) %collective-permute-start.7) | collective-permute-done | bytes 98336 | tf_op jit(solution)/shard_map/ppermute | solution.py:65
  43.2 2.0 %shard_map.325 = (f32[64,768]{1,0:T(8,128)S(1)}, bf16[64,768]{1,0:T(8,128)(2,1)S(1)}, bf16[64,768]{1,0:T(8,128)(2,1)S(1)}, bf16[64,768]{1,0:T(8,128)(2,1)S(1)}, ...) custom-call(s32[4]{0:T(128)S(1)} %pad_add_fusion.ids, ...), custom_call_target="tpu_custom_call" | custom-call | flops 1200000000 | bytes 9000000 | tf_op jit(solution)/shard_map/pallas_call | solution.py:37
  45.2 1.7 %collective-permute-start.12 = (bf16[64,768]{1,0:T(8,128)(2,1)S(1)}, bf16[64,768]{1,0:T(8,128)(2,1)S(1)}, u32[]{:S(2)}, u32[]{:S(2)}) collective-permute-start(bf16[64,768]{1,0:T(8,128)(2,1)S(1)} %get-tuple-element.149), channel_id=1, source_target_pairs={{0,1},{1,0},{2,3},{3,2},{4,5},{5,4},{6,7},{7,6},{8,9},{9,8},{10,11... | collective-permute-start | bytes 294920 | tf_op jit(solution)/shard_map/ppermute | solution.py:65
  46.9 1.4 collective-permute-start.13
  48.3 1.3 collective-permute-start.14
  50.6 5.3 %collective-permute-done.13.r2 = bf16[64,768]{1,0:T(8,128)(2,1)S(1)} collective-permute-done((bf16[64,768]{1,0:T(8,128)(2,1)S(1)}, bf16[64,768]{1,0:T(8,128)(2,1)S(1)}, u32[]{:S(2)}, u32[]{:S(2)}) %collective-permute-start.13) | collective-permute-done | bytes 98336 | tf_op jit(solution)/shard_map/ppermute | solution.py:65
  56.0 1.7 %collective-permute-start.15 = (bf16[64,768]{1,0:T(8,128)(2,1)S(1)}, bf16[64,768]{1,0:T(8,128)(2,1)S(1)}, u32[]{:S(2)}, u32[]{:S(2)}) collective-permute-start(bf16[64,768]{1,0:T(8,128)(2,1)S(1)} %shard_map.326.refs_0_), channel_id=1, source_target_pairs={{0,1},{1,0},{2,3},{3,2},{4,5},{5,4},{6,7},{7,6},{8,9},{9,8},{10,11... | collective-permute-start | bytes 294920 | tf_op jit(solution)/shard_map/ppermute | solution.py:65
  57.7 1.1 collective-permute-start.16
  58.8 1.7 %collective-permute-start.17 = (bf16[64,768]{1,0:T(8,128)(2,1)S(1)}, bf16[64,768]{1,0:T(8,128)(2,1)S(1)}, u32[]{:S(2)}, u32[]{:S(2)}) collective-permute-start(bf16[64,768]{1,0:T(8,128)(2,1)S(1)} %shard_map.326.refs_0_), channel_id=1, source_target_pairs={{0,3},{1,2},{2,1},{3,0},{4,7},{5,6},{6,5},{7,4},{8,11},{9,10},{10,... | collective-permute-start | bytes 294920 | tf_op jit(solution)/shard_map/ppermute | solution.py:65
  60.5 1.1 collective-permute-done.15.refs_1_
  61.6 5.6 %collective-permute-done.16.refs_2_ = bf16[64,768]{1,0:T(8,128)(2,1)S(1)} collective-permute-done((bf16[64,768]{1,0:T(8,128)(2,1)S(1)}, bf16[64,768]{1,0:T(8,128)(2,1)S(1)}, u32[]{:S(2)}, u32[]{:S(2)}) %collective-permute-start.16) | collective-permute-done | bytes 98336 | tf_op jit(solution)/shard_map/ppermute | solution.py:65
  67.2 2.3 %shard_map.327 = (f32[64,768]{1,0:T(8,128)S(1)}, bf16[64,768]{1,0:T(8,128)(2,1)S(1)}, bf16[64,768]{1,0:T(8,128)(2,1)S(1)}, bf16[64,768]{1,0:T(8,128)(2,1)S(1)}, ...) custom-call(s32[4]{0:T(128)S(1)} %pad_add_fusion.ids, ...), custom_call_target="tpu_custom_call" | custom-call | flops 1200000000 | bytes 9000000 | tf_op jit(solution)/shard_map/pallas_call | solution.py:37
  69.4 1.7 %collective-permute-start.18 = (bf16[64,768]{1,0:T(8,128)(2,1)S(1)}, bf16[64,768]{1,0:T(8,128)(2,1)S(1)}, u32[]{:S(2)}, u32[]{:S(2)}) collective-permute-start(bf16[64,768]{1,0:T(8,128)(2,1)S(1)} %get-tuple-element.161), channel_id=1, source_target_pairs={{0,1},{1,0},{2,3},{3,2},{4,5},{5,4},{6,7},{7,6},{8,9},{9,8},{10,11... | collective-permute-start | bytes 294920 | tf_op jit(solution)/shard_map/ppermute | solution.py:65
  71.1 1.1 collective-permute-start.19
  72.2 1.6 %collective-permute-start.20 = (bf16[64,768]{1,0:T(8,128)(2,1)S(1)}, bf16[64,768]{1,0:T(8,128)(2,1)S(1)}, u32[]{:S(2)}, u32[]{:S(2)}) collective-permute-start(bf16[64,768]{1,0:T(8,128)(2,1)S(1)} %get-tuple-element.163), channel_id=1, source_target_pairs={{0,3},{1,2},{2,1},{3,0},{4,7},{5,6},{6,5},{7,4},{8,11},{9,10},{10,... | collective-permute-start | bytes 294920 | tf_op jit(solution)/shard_map/ppermute | solution.py:65
  73.9 1.1 shard_map.336
  75.1 5.7 %collective-permute-done.19.r2 = bf16[64,768]{1,0:T(8,128)(2,1)S(1)} collective-permute-done((bf16[64,768]{1,0:T(8,128)(2,1)S(1)}, bf16[64,768]{1,0:T(8,128)(2,1)S(1)}, u32[]{:S(2)}, u32[]{:S(2)}) %collective-permute-start.19) | collective-permute-done | bytes 98336 | tf_op jit(solution)/shard_map/ppermute | solution.py:65
  80.9 1.7 %collective-permute-start.21 = (bf16[64,768]{1,0:T(8,128)(2,1)S(1)}, bf16[64,768]{1,0:T(8,128)(2,1)S(1)}, u32[]{:S(2)}, u32[]{:S(2)}) collective-permute-start(bf16[64,768]{1,0:T(8,128)(2,1)S(1)} %shard_map.328.refs_0_), channel_id=1, source_target_pairs={{0,1},{1,0},{2,3},{3,2},{4,5},{5,4},{6,7},{7,6},{8,9},{9,8},{10,11... | collective-permute-start | bytes 294920 | tf_op jit(solution)/shard_map/ppermute | solution.py:65
  82.5 1.2 collective-permute-start.22
  83.7 1.6 collective-permute-start.23
  85.3 1.4 shard_map.337
  86.8 3.2 %collective-permute-start.34 = (bf16[192,768]{1,0:T(8,128)(2,1)S(1)}, bf16[192,768]{1,0:T(8,128)(2,1)S(1)}, u32[]{:S(2)}, u32[]{:S(2)}) collective-permute-start(bf16[192,768]{1,0:T(8,128)(2,1)S(1)} %get-tuple-element.205), channel_id=1, source_target_pairs={{0,8},{8,0},{16,24},{24,16},{1,9},{9,1},{17,25},{25,17},{2,10},{10... | collective-permute-start | bytes 884744 | tf_op jit(solution)/shard_map/ppermute | solution.py:65
  90.0 2.2 %collective-permute-done.22.refs_2_ = bf16[64,768]{1,0:T(8,128)(2,1)S(1)} collective-permute-done((bf16[64,768]{1,0:T(8,128)(2,1)S(1)}, bf16[64,768]{1,0:T(8,128)(2,1)S(1)}, u32[]{:S(2)}, u32[]{:S(2)}) %collective-permute-start.22) | collective-permute-done | bytes 98336 | tf_op jit(solution)/shard_map/ppermute | solution.py:65
  92.2 1.1 shard_map.329
  93.3 3.6 %shard_map.330 = (f32[128,768]{1,0:T(8,128)S(1)}, bf16[128,768]{1,0:T(8,128)(2,1)S(1)}, bf16[128,768]{1,0:T(8,128)(2,1)S(1)}, bf16[128,768]{1,0:T(8,128)(2,1)S(1...) custom-call(s32[4]{0:T(128)S(1)} %pad_add_fusion.ids, ...), custom_call_target="tpu_custom_call" | custom-call | flops 40000000 | bytes 300000 | tf_op jit(solution)/shard_map/pallas_call | solution.py:37
  97.5 1.4 shard_map.338
  98.9 1.1 collective-permute-start.24
  100.0 1.2 collective-permute-start.25
  101.2 2.2 %collective-permute-start.26 = (bf16[128,768]{1,0:T(8,128)(2,1)S(1)}, bf16[128,768]{1,0:T(8,128)(2,1)S(1)}, u32[]{:S(2)}, u32[]{:S(2)}) collective-permute-start(bf16[128,768]{1,0:T(8,128)(2,1)S(1)} %get-tuple-element.181), channel_id=1, source_target_pairs={{0,3},{1,2},{2,1},{3,0},{4,7},{5,6},{6,5},{7,4},{8,11},{9,10},{10,... | collective-permute-start | bytes 589832 | tf_op jit(solution)/shard_map/ppermute | solution.py:65
  103.4 2.2 %shard_map.339.rel = f32[32,128]{1,0:T(8,128)S(1)} custom-call(s32[4]{0:T(128)S(1)} %pad_add_fusion.ids, f32[3,512,256]{2,1,0:T(8,128)S(1)} %get-tuple-element.216.scores_ref), custom_call_target="tpu_custom_call" | custom-call | flops 40000000 | bytes 300000 | tf_op jit(solution)/shard_map/pallas_call | solution.py:37
  106.5 2.9 %collective-permute-start.37 = (bf16[224,768]{1,0:T(8,128)(2,1)S(1)}, bf16[224,768]{1,0:T(8,128)(2,1)S(1)}, u32[]{:S(2)}, u32[]{:S(2)}) collective-permute-start(bf16[224,768]{1,0:T(8,128)(2,1)S(1)} %get-tuple-element.221), channel_id=1, source_target_pairs={{0,8},{8,0},{16,24},{24,16},{1,9},{9,1},{17,25},{25,17},{2,10},{10... | collective-permute-start | bytes 1032200 | tf_op jit(solution)/shard_map/ppermute | solution.py:65
  110.0 7.1 %collective-permute-done.25.t2.r2 = bf16[128,768]{1,0:T(8,128)(2,1)S(1)} collective-permute-done((bf16[128,768]{1,0:T(8,128)(2,1)S(1)}, bf16[128,768]{1,0:T(8,128)(2,1)S(1)}, u32[]{:S(2)}, u32[]{:S(2)}) %collective-permute-start.25) | collective-permute-done | bytes 196640 | tf_op jit(solution)/shard_map/ppermute | solution.py:65
  117.3 3.8 %collective-permute-start.27 = (bf16[96,768]{1,0:T(8,128)(2,1)S(1)}, bf16[96,768]{1,0:T(8,128)(2,1)S(1)}, u32[]{:S(2)}, u32[]{:S(2)}) collective-permute-start(bf16[96,768]{1,0:T(8,128)(2,1)S(1)} %get-tuple-element.189), channel_id=1, source_target_pairs={{0,8},{8,0},{16,24},{24,16},{1,9},{9,1},{17,25},{25,17},{2,10},{10... | collective-permute-start | bytes 442376 | tf_op jit(solution)/shard_map/ppermute | solution.py:65
  121.0 1.5 collective-permute-start.29
  122.7 2.0 %collective-permute-start.39 = (bf16[256,768]{1,0:T(8,128)(2,1)S(1)}, bf16[256,768]{1,0:T(8,128)(2,1)S(1)}, u32[]{:S(2)}, u32[]{:S(2)}) collective-permute-start(bf16[256,768]{1,0:T(8,128)(2,1)S(1)} %get-tuple-element.225.sent1), channel_id=1, source_target_pairs={{0,8},{8,0},{16,24},{24,16},{1,9},{9,1},{17,25},{25,17},{2,10},{10... | collective-permute-start | bytes 1179656 | tf_op jit(solution)/shard_map/ppermute | solution.py:65
  125.3 4.1 %collective-permute-done.28.q2 = bf16[96,768]{1,0:T(8,128)(2,1)S(1)} collective-permute-done((bf16[96,768]{1,0:T(8,128)(2,1)S(1)}, bf16[96,768]{1,0:T(8,128)(2,1)S(1)}, u32[]{:S(2)}, u32[]{:S(2)}) %collective-permute-start.28) | collective-permute-done | bytes 147488 | tf_op jit(solution)/shard_map/ppermute | solution.py:65
  129.4 4.7 %collective-permute-start.30 = (bf16[128,768]{1,0:T(8,128)(2,1)S(1)}, bf16[128,768]{1,0:T(8,128)(2,1)S(1)}, u32[]{:S(2)}, u32[]{:S(2)}) collective-permute-start(bf16[128,768]{1,0:T(8,128)(2,1)S(1)} %shard_map.334.t0), channel_id=1, source_target_pairs={{0,1},{1,0},{2,3},{3,2},{4,5},{5,4},{6,7},{7,6},{8,9},{9,8},{10,11... | collective-permute-start | bytes 589832 | tf_op jit(solution)/shard_map/ppermute | solution.py:65
  134.2 2.4 %collective-permute-start.32 = (bf16[128,768]{1,0:T(8,128)(2,1)S(1)}, bf16[128,768]{1,0:T(8,128)(2,1)S(1)}, u32[]{:S(2)}, u32[]{:S(2)}) collective-permute-start(bf16[128,768]{1,0:T(8,128)(2,1)S(1)} %shard_map.334.t0), channel_id=1, source_target_pairs={{0,3},{1,2},{2,1},{3,0},{4,7},{5,6},{6,5},{7,4},{8,11},{9,10},{10,... | collective-permute-start | bytes 589832 | tf_op jit(solution)/shard_map/ppermute | solution.py:65
  137.3 1.8 %collective-permute-start.42 = (bf16[64,768]{1,0:T(8,128)(2,1)S(1)}, bf16[64,768]{1,0:T(8,128)(2,1)S(1)}, u32[]{:S(2)}, u32[]{:S(2)}) collective-permute-start(bf16[64,768]{1,0:T(8,128)(2,1)S(1)} %get-tuple-element.229.mid2), channel_id=1, source_target_pairs={{0,16},{8,24},{16,0},{24,8},{1,17},{9,25},{17,1},{25,9},{2,18},{10... | collective-permute-start | bytes 294920 | tf_op jit(solution)/shard_map/ppermute | solution.py:65
  139.1 1.3 shard_map.333
  140.4 1.0 collective-permute-done.41.came1
  141.9 1.6 collective-permute-start.43
  143.5 1.1 collective-permute-start.44
  144.6 4.3 %collective-permute-done.31.t2 = bf16[128,768]{1,0:T(8,128)(2,1)S(1)} collective-permute-done((bf16[128,768]{1,0:T(8,128)(2,1)S(1)}, bf16[128,768]{1,0:T(8,128)(2,1)S(1)}, u32[]{:S(2)}, u32[]{:S(2)}) %collective-permute-start.31) | collective-permute-done | bytes 196640 | tf_op jit(solution)/shard_map/ppermute | solution.py:65
  149.6 1.4 collective-permute-done.44.came2
  152.8 1.8 %shard_map.335 = f32[4,128,768]{2,1,0:T(8,128)} custom-call(s32[4]{0:T(128)S(1)} %pad_add_fusion.ids, bf16[128,768]{1,0:T(8,128)(2,1)S(1)} %shard_map.334.t0, bf16[128,768]{1,0:T(8,128)(2,1)S(1)} %collective-permute-done.30.t1, bf16[128,768]{1,0:T(8,128)(2,1)S(1)} %collective-permute-done.31.t2, bf16[128,768]{1,0:T(8,128)(2,1)S(1)} %collective-permute-done.32.t3), custom_call_target="tpu_custom_call" | custom-call | flops 40000000 | bytes 300000 | tf_op jit(solution)/shard_map/pallas_call | solution.py:37
  154.6 2.0 %shard_map.347 = (f32[768,768]{1,0:T(8,128)}, f32[768,768]{1,0:T(8,128)}) custom-call(s32[4]{0:T(128)S(1)} %pad_add_fusion.ids, bf16[768,768]{1,0:T(8,128)(2,1)S(1)} %shard_map.346.rows), custom_call_target="tpu_custom_call" | custom-call | flops 40000000 | bytes 300000 | tf_op jit(solution)/shard_map/pallas_call | solution.py:37
  156.7 2.2 %shard_map.348 = (f32[192,768]{1,0:T(8,128)}, f32[192,768]{1,0:T(8,128)}, f32[192,768]{1,0:T(8,128)}, f32[192,768]{1,0:T(8,128)}, f32[768]{0:T(1024)}, /*index=5...) custom-call(s32[4]{0:T(128)S(1)} %pad_add_fusion.ids, ...), custom_call_target="tpu_custom_call" | custom-call | flops 600000000 | bytes 4500000 | tf_op jit(solution)/shard_map/pallas_call | solution.py:37
  158.8 2.0 %shard_map.349 = (f32[768,768]{1,0:T(8,128)}, f32[768,768]{1,0:T(8,128)}) custom-call(s32[4]{0:T(128)S(1)} %pad_add_fusion.ids, bf16[768,768]{1,0:T(8,128)(2,1)S(1)} %collective-permute-done.46.rows, f32[768,768]{1,0:T(8,128)} %get-tuple-element.233.refs_0_, f32[768,768]{1,0:T(8,128)} %get-tuple-element.234.refs_1_), custom_call_target="tpu_custom_call", output_to_operand_aliasing={{0}: (2, {}), {1}: (3, {})} | custom-call | flops 40000000 | bytes 300000 | tf_op jit(solution)/shard_map/pallas_call | solution.py:37
  (107 shorter events, 11.1 us)
Async XLA Ops:
  0.7 6.5 %copy-start.15 = (f32[192]{0:T(256)S(1)}, f32[192]{0:T(256)}, u32[]{:S(2)}) copy-start(f32[192]{0:T(256)} %param.22) | copy-start | bytes 2308
  0.7 6.6 %copy-start.16 = (f32[192]{0:T(256)S(1)}, f32[192]{0:T(256)}, u32[]{:S(2)}) copy-start(f32[192]{0:T(256)} %param.25) | copy-start | bytes 2308
  0.7 6.7 %copy-start.8 = (f32[768]{0:T(1024)S(1)}, f32[768]{0:T(1024)}, u32[]{:S(2)}) copy-start(f32[768]{0:T(1024)} %param.28) | copy-start | bytes 9220
  0.7 7.5 %copy-start.6 = (f32[3,8]{1,0:T(4,128)S(1)}, f32[3,8]{1,0:T(4,128)}, u32[]{:S(2)}) copy-start(f32[3,8]{1,0:T(4,128)} %rel.1) | copy-start | bytes 292
  2.0 8.7 %collective-permute-start = (bf16[128,768]{1,0:T(8,128)(2,1)S(1)}, bf16[128,768]{1,0:T(8,128)(2,1)S(1)}, u32[]{:S(2)}, u32[]{:S(2)}) collective-permute-start(bf16[128,768]{1,0:T(8,128)(2,1)S(1)} %get-tuple-element.253), channel_id=1, source_target_pairs={{0,8},{8,0},{16,24},{24,16},{1,9},{9,1},{17,25},{25,17},{2,10},{10... | collective-permute-start | bytes 589832 | tf_op jit(solution)/shard_map/ppermute | solution.py:65
  5.0 10.6 %collective-permute-start.1 = (bf16[128,768]{1,0:T(8,128)(2,1)S(1)}, bf16[128,768]{1,0:T(8,128)(2,1)S(1)}, u32[]{:S(2)}, u32[]{:S(2)}) collective-permute-start(bf16[128,768]{1,0:T(8,128)(2,1)S(1)} %get-tuple-element.255), channel_id=1, source_target_pairs={{0,16},{8,24},{16,0},{24,8},{1,17},{9,25},{17,1},{25,9},{2,18},{10... | collective-permute-start | bytes 589832 | tf_op jit(solution)/shard_map/ppermute | solution.py:65
  6.5 9.1 %collective-permute-start.2 = (bf16[128,768]{1,0:T(8,128)(2,1)S(1)}, bf16[128,768]{1,0:T(8,128)(2,1)S(1)}, u32[]{:S(2)}, u32[]{:S(2)}) collective-permute-start(bf16[128,768]{1,0:T(8,128)(2,1)S(1)} %get-tuple-element.252), channel_id=1, source_target_pairs={{0,24},{8,16},{16,8},{24,0},{1,25},{9,17},{17,9},{25,1},{2,26},{10... | collective-permute-start | bytes 589832 | tf_op jit(solution)/shard_map/ppermute | solution.py:65
  8.2 7.4 %copy-start = (bf16[768,192]{0,1:T(8,128)(2,1)S(1)}, bf16[768,192]{0,1:T(8,128)(2,1)}, u32[]{:S(2)}) copy-start(bf16[768,192]{0,1:T(8,128)(2,1)} %param.21) | copy-start | bytes 884740
  8.2 7.4 %copy-start.1 = (bf16[768,192]{0,1:T(8,128)(2,1)S(1)}, bf16[768,192]{0,1:T(8,128)(2,1)}, u32[]{:S(2)}) copy-start(bf16[768,192]{0,1:T(8,128)(2,1)} %param.23) | copy-start | bytes 884740
  8.2 7.4 %copy-start.2 = (bf16[768,192]{0,1:T(8,128)(2,1)S(1)}, bf16[768,192]{0,1:T(8,128)(2,1)}, u32[]{:S(2)}) copy-start(bf16[768,192]{0,1:T(8,128)(2,1)} %param.24) | copy-start | bytes 884740
  8.2 7.4 %copy-start.3 = (bf16[192,768]{1,0:T(8,128)(2,1)S(1)}, bf16[192,768]{1,0:T(8,128)(2,1)}, u32[]{:S(2)}) copy-start(bf16[192,768]{1,0:T(8,128)(2,1)} %refs_5_.1) | copy-start | bytes 884740
  15.6 10.9 %copy-start.9 = (f32[768]{0:T(1024)S(1)}, f32[768]{0:T(1024)}, u32[]{:S(2)}) copy-start(f32[768]{0:T(1024)} %param.29) | copy-start | bytes 9220
  15.6 10.9 %copy-start.10 = (f32[768]{0:T(1024)S(1)}, f32[768]{0:T(1024)}, u32[]{:S(2)}) copy-start(f32[768]{0:T(1024)} %param.30) | copy-start | bytes 9220
  15.6 10.9 %copy-start.11 = (f32[768]{0:T(1024)S(1)}, f32[768]{0:T(1024)}, u32[]{:S(2)}) copy-start(f32[768]{0:T(1024)} %param.32) | copy-start | bytes 9220
  15.7 10.9 %copy-start.12 = (f32[768]{0:T(1024)S(1)}, f32[768]{0:T(1024)}, u32[]{:S(2)}) copy-start(f32[768]{0:T(1024)} %param.34) | copy-start | bytes 9220
  15.7 21.9 %copy-start.7 = (bf16[4,64,768]{2,1,0:T(8,128)(2,1)S(1)}, bf16[4,64,768]{2,1,0:T(8,128)(2,1)}, u32[]{:S(2)}) copy-start(bf16[4,64,768]{2,1,0:T(8,128)(2,1)} %param.37) | copy-start | bytes 1179652
  15.7 27.5 %copy-start.4 = (bf16[768,768]{1,0:T(8,128)(2,1)S(1)}, bf16[768,768]{1,0:T(8,128)(2,1)}, u32[]{:S(2)}) copy-start(bf16[768,768]{1,0:T(8,128)(2,1)} %refs_12_.1) | copy-start | bytes 3538948
  15.7 27.5 %copy-start.5 = (bf16[768,768]{1,0:T(8,128)(2,1)S(1)}, bf16[768,768]{1,0:T(8,128)(2,1)}, u32[]{:S(2)}) copy-start(bf16[768,768]{1,0:T(8,128)(2,1)} %refs_11_.1) | copy-start | bytes 3538948
  22.1 5.6 %collective-permute-start.3 = (bf16[64,768]{1,0:T(8,128)(2,1)S(1)}, bf16[64,768]{1,0:T(8,128)(2,1)S(1)}, u32[]{:S(2)}, u32[]{:S(2)}) collective-permute-start(bf16[64,768]{1,0:T(8,128)(2,1)S(1)} %get-tuple-element.135), channel_id=1, source_target_pairs={{0,1},{1,0},{2,3},{3,2},{4,5},{5,4},{6,7},{7,6},{8,9},{9,8},{10,11... | collective-permute-start | bytes 294920 | tf_op jit(solution)/shard_map/ppermute | solution.py:65
  23.7 9.3 %collective-permute-start.4 = (bf16[64,768]{1,0:T(8,128)(2,1)S(1)}, bf16[64,768]{1,0:T(8,128)(2,1)S(1)}, u32[]{:S(2)}, u32[]{:S(2)}) collective-permute-start(bf16[64,768]{1,0:T(8,128)(2,1)S(1)} %get-tuple-element.136), channel_id=1, source_target_pairs={{0,2},{1,3},{2,0},{3,1},{4,6},{5,7},{6,4},{7,5},{8,10},{9,11},{10,... | collective-permute-start | bytes 294920 | tf_op jit(solution)/shard_map/ppermute | solution.py:65
  26.3 6.7 %collective-permute-start.5 = (bf16[64,768]{1,0:T(8,128)(2,1)S(1)}, bf16[64,768]{1,0:T(8,128)(2,1)S(1)}, u32[]{:S(2)}, u32[]{:S(2)}) collective-permute-start(bf16[64,768]{1,0:T(8,128)(2,1)S(1)} %get-tuple-element.137), channel_id=1, source_target_pairs={{0,3},{1,2},{2,1},{3,0},{4,7},{5,6},{6,5},{7,4},{8,11},{9,10},{10,... | collective-permute-start | bytes 294920 | tf_op jit(solution)/shard_map/ppermute | solution.py:65
  33.1 7.5 %collective-permute-start.6 = (bf16[64,768]{1,0:T(8,128)(2,1)S(1)}, bf16[64,768]{1,0:T(8,128)(2,1)S(1)}, u32[]{:S(2)}, u32[]{:S(2)}) collective-permute-start(bf16[64,768]{1,0:T(8,128)(2,1)S(1)} %shard_map.324.a0), channel_id=1, source_target_pairs={{0,1},{1,0},{2,3},{3,2},{4,5},{5,4},{6,7},{7,6},{8,9},{9,8},{10,11... | collective-permute-start | bytes 294920 | tf_op jit(solution)/shard_map/ppermute | solution.py:65
  34.8 8.4 %collective-permute-start.7 = (bf16[64,768]{1,0:T(8,128)(2,1)S(1)}, bf16[64,768]{1,0:T(8,128)(2,1)S(1)}, u32[]{:S(2)}, u32[]{:S(2)}) collective-permute-start(bf16[64,768]{1,0:T(8,128)(2,1)S(1)} %shard_map.324.a0), channel_id=1, source_target_pairs={{0,2},{1,3},{2,0},{3,1},{4,6},{5,7},{6,4},{7,5},{8,10},{9,11},{10,... | collective-permute-start | bytes 294920 | tf_op jit(solution)/shard_map/ppermute | solution.py:65
  36.2 7.0 %collective-permute-start.8 = (bf16[64,768]{1,0:T(8,128)(2,1)S(1)}, bf16[64,768]{1,0:T(8,128)(2,1)S(1)}, u32[]{:S(2)}, u32[]{:S(2)}) collective-permute-start(bf16[64,768]{1,0:T(8,128)(2,1)S(1)} %shard_map.324.a0), channel_id=1, source_target_pairs={{0,3},{1,2},{2,1},{3,0},{4,7},{5,6},{6,5},{7,4},{8,11},{9,10},{10,... | collective-permute-start | bytes 294920 | tf_op jit(solution)/shard_map/ppermute | solution.py:65
  37.6 7.6 %collective-permute-start.10 = (bf16[64,768]{1,0:T(8,128)(2,1)S(1)}, bf16[64,768]{1,0:T(8,128)(2,1)S(1)}, u32[]{:S(2)}, u32[]{:S(2)}) collective-permute-start(bf16[64,768]{1,0:T(8,128)(2,1)S(1)} %get-tuple-element.257), channel_id=1, source_target_pairs={{0,16},{8,24},{16,0},{24,8},{1,17},{9,25},{17,1},{25,9},{2,18},{10... | collective-permute-start | bytes 294920 | tf_op jit(solution)/shard_map/ppermute | solution.py:65
  39.0 6.2 %collective-permute-start.11 = (bf16[64,768]{1,0:T(8,128)(2,1)S(1)}, bf16[64,768]{1,0:T(8,128)(2,1)S(1)}, u32[]{:S(2)}, u32[]{:S(2)}) collective-permute-start(bf16[64,768]{1,0:T(8,128)(2,1)S(1)} %get-tuple-element.256), channel_id=1, source_target_pairs={{0,24},{8,16},{16,8},{24,0},{1,25},{9,17},{17,9},{25,1},{2,26},{10... | collective-permute-start | bytes 294920 | tf_op jit(solution)/shard_map/ppermute | solution.py:65
  40.6 19.9 %copy-start.13 = (f32[768]{0:T(1024)S(1)}, f32[768]{0:T(1024)}, u32[]{:S(2)}) copy-start(f32[768]{0:T(1024)} %param.35) | copy-start | bytes 9220
  40.6 19.9 %copy-start.14 = (f32[768]{0:T(1024)S(1)}, f32[768]{0:T(1024)}, u32[]{:S(2)}) copy-start(f32[768]{0:T(1024)} %param.36) | copy-start | bytes 9220
  40.6 4.6 %collective-permute-start.9 = (bf16[64,768]{1,0:T(8,128)(2,1)S(1)}, bf16[64,768]{1,0:T(8,128)(2,1)S(1)}, u32[]{:S(2)}, u32[]{:S(2)}) collective-permute-start(bf16[64,768]{1,0:T(8,128)(2,1)S(1)} %get-tuple-element.258), channel_id=1, source_target_pairs={{0,8},{8,0},{16,24},{24,16},{1,9},{9,1},{17,25},{25,17},{2,10},{10... | collective-permute-start | bytes 294920 | tf_op jit(solution)/shard_map/ppermute | solution.py:65
  45.2 5.4 %collective-permute-start.12 = (bf16[64,768]{1,0:T(8,128)(2,1)S(1)}, bf16[64,768]{1,0:T(8,128)(2,1)S(1)}, u32[]{:S(2)}, u32[]{:S(2)}) collective-permute-start(bf16[64,768]{1,0:T(8,128)(2,1)S(1)} %get-tuple-element.149), channel_id=1, source_target_pairs={{0,1},{1,0},{2,3},{3,2},{4,5},{5,4},{6,7},{7,6},{8,9},{9,8},{10,11... | collective-permute-start | bytes 294920 | tf_op jit(solution)/shard_map/ppermute | solution.py:65
  46.9 9.1 %collective-permute-start.13 = (bf16[64,768]{1,0:T(8,128)(2,1)S(1)}, bf16[64,768]{1,0:T(8,128)(2,1)S(1)}, u32[]{:S(2)}, u32[]{:S(2)}) collective-permute-start(bf16[64,768]{1,0:T(8,128)(2,1)S(1)} %get-tuple-element.150), channel_id=1, source_target_pairs={{0,2},{1,3},{2,0},{3,1},{4,6},{5,7},{6,4},{7,5},{8,10},{9,11},{10,... | collective-permute-start | bytes 294920 | tf_op jit(solution)/shard_map/ppermute | solution.py:65
  48.3 7.6 %collective-permute-start.14 = (bf16[64,768]{1,0:T(8,128)(2,1)S(1)}, bf16[64,768]{1,0:T(8,128)(2,1)S(1)}, u32[]{:S(2)}, u32[]{:S(2)}) collective-permute-start(bf16[64,768]{1,0:T(8,128)(2,1)S(1)} %get-tuple-element.151), channel_id=1, source_target_pairs={{0,3},{1,2},{2,1},{3,0},{4,7},{5,6},{6,5},{7,4},{8,11},{9,10},{10,... | collective-permute-start | bytes 294920 | tf_op jit(solution)/shard_map/ppermute | solution.py:65
  56.0 5.6 %collective-permute-start.15 = (bf16[64,768]{1,0:T(8,128)(2,1)S(1)}, bf16[64,768]{1,0:T(8,128)(2,1)S(1)}, u32[]{:S(2)}, u32[]{:S(2)}) collective-permute-start(bf16[64,768]{1,0:T(8,128)(2,1)S(1)} %shard_map.326.refs_0_), channel_id=1, source_target_pairs={{0,1},{1,0},{2,3},{3,2},{4,5},{5,4},{6,7},{7,6},{8,9},{9,8},{10,11... | collective-permute-start | bytes 294920 | tf_op jit(solution)/shard_map/ppermute | solution.py:65
  57.7 9.5 %collective-permute-start.16 = (bf16[64,768]{1,0:T(8,128)(2,1)S(1)}, bf16[64,768]{1,0:T(8,128)(2,1)S(1)}, u32[]{:S(2)}, u32[]{:S(2)}) collective-permute-start(bf16[64,768]{1,0:T(8,128)(2,1)S(1)} %shard_map.326.refs_0_), channel_id=1, source_target_pairs={{0,2},{1,3},{2,0},{3,1},{4,6},{5,7},{6,4},{7,5},{8,10},{9,11},{10,... | collective-permute-start | bytes 294920 | tf_op jit(solution)/shard_map/ppermute | solution.py:65
  58.8 8.4 %collective-permute-start.17 = (bf16[64,768]{1,0:T(8,128)(2,1)S(1)}, bf16[64,768]{1,0:T(8,128)(2,1)S(1)}, u32[]{:S(2)}, u32[]{:S(2)}) collective-permute-start(bf16[64,768]{1,0:T(8,128)(2,1)S(1)} %shard_map.326.refs_0_), channel_id=1, source_target_pairs={{0,3},{1,2},{2,1},{3,0},{4,7},{5,6},{6,5},{7,4},{8,11},{9,10},{10,... | collective-permute-start | bytes 294920 | tf_op jit(solution)/shard_map/ppermute | solution.py:65
  69.4 5.7 %collective-permute-start.18 = (bf16[64,768]{1,0:T(8,128)(2,1)S(1)}, bf16[64,768]{1,0:T(8,128)(2,1)S(1)}, u32[]{:S(2)}, u32[]{:S(2)}) collective-permute-start(bf16[64,768]{1,0:T(8,128)(2,1)S(1)} %get-tuple-element.161), channel_id=1, source_target_pairs={{0,1},{1,0},{2,3},{3,2},{4,5},{5,4},{6,7},{7,6},{8,9},{9,8},{10,11... | collective-permute-start | bytes 294920 | tf_op jit(solution)/shard_map/ppermute | solution.py:65
  71.1 9.7 %collective-permute-start.19 = (bf16[64,768]{1,0:T(8,128)(2,1)S(1)}, bf16[64,768]{1,0:T(8,128)(2,1)S(1)}, u32[]{:S(2)}, u32[]{:S(2)}) collective-permute-start(bf16[64,768]{1,0:T(8,128)(2,1)S(1)} %get-tuple-element.162), channel_id=1, source_target_pairs={{0,2},{1,3},{2,0},{3,1},{4,6},{5,7},{6,4},{7,5},{8,10},{9,11},{10,... | collective-permute-start | bytes 294920 | tf_op jit(solution)/shard_map/ppermute | solution.py:65
  72.2 8.6 %collective-permute-start.20 = (bf16[64,768]{1,0:T(8,128)(2,1)S(1)}, bf16[64,768]{1,0:T(8,128)(2,1)S(1)}, u32[]{:S(2)}, u32[]{:S(2)}) collective-permute-start(bf16[64,768]{1,0:T(8,128)(2,1)S(1)} %get-tuple-element.163), channel_id=1, source_target_pairs={{0,3},{1,2},{2,1},{3,0},{4,7},{5,6},{6,5},{7,4},{8,11},{9,10},{10,... | collective-permute-start | bytes 294920 | tf_op jit(solution)/shard_map/ppermute | solution.py:65
  75.0 10.3 %collective-permute-start.33 = (bf16[768,768]{1,0:T(8,128)(2,1)S(1)}, bf16[768,768]{1,0:T(8,128)(2,1)S(1)}, u32[]{:S(2)}, u32[]{:S(2)}) collective-permute-start(bf16[768,768]{1,0:T(8,128)(2,1)S(1)} %shard_map.336), channel_id=1, source_target_pairs={{0,4},{4,0},{1,5},{5,1},{2,6},{6,2},{3,7},{7,3},{8,12},{12,8},{9,1... | collective-permute-start | bytes 3538952 | tf_op jit(solution)/shard_map/ppermute | solution.py:65
  80.9 9.1 %collective-permute-start.21 = (bf16[64,768]{1,0:T(8,128)(2,1)S(1)}, bf16[64,768]{1,0:T(8,128)(2,1)S(1)}, u32[]{:S(2)}, u32[]{:S(2)}) collective-permute-start(bf16[64,768]{1,0:T(8,128)(2,1)S(1)} %shard_map.328.refs_0_), channel_id=1, source_target_pairs={{0,1},{1,0},{2,3},{3,2},{4,5},{5,4},{6,7},{7,6},{8,9},{9,8},{10,11... | collective-permute-start | bytes 294920 | tf_op jit(solution)/shard_map/ppermute | solution.py:65
  82.5 9.6 %collective-permute-start.22 = (bf16[64,768]{1,0:T(8,128)(2,1)S(1)}, bf16[64,768]{1,0:T(8,128)(2,1)S(1)}, u32[]{:S(2)}, u32[]{:S(2)}) collective-permute-start(bf16[64,768]{1,0:T(8,128)(2,1)S(1)} %shard_map.328.refs_0_), channel_id=1, source_target_pairs={{0,2},{1,3},{2,0},{3,1},{4,6},{5,7},{6,4},{7,5},{8,10},{9,11},{10,... | collective-permute-start | bytes 294920 | tf_op jit(solution)/shard_map/ppermute | solution.py:65
  83.7 8.4 %collective-permute-start.23 = (bf16[64,768]{1,0:T(8,128)(2,1)S(1)}, bf16[64,768]{1,0:T(8,128)(2,1)S(1)}, u32[]{:S(2)}, u32[]{:S(2)}) collective-permute-start(bf16[64,768]{1,0:T(8,128)(2,1)S(1)} %shard_map.328.refs_0_), channel_id=1, source_target_pairs={{0,3},{1,2},{2,1},{3,0},{4,7},{5,6},{6,5},{7,4},{8,11},{9,10},{10,... | collective-permute-start | bytes 294920 | tf_op jit(solution)/shard_map/ppermute | solution.py:65
  86.8 10.1 %collective-permute-start.34 = (bf16[192,768]{1,0:T(8,128)(2,1)S(1)}, bf16[192,768]{1,0:T(8,128)(2,1)S(1)}, u32[]{:S(2)}, u32[]{:S(2)}) collective-permute-start(bf16[192,768]{1,0:T(8,128)(2,1)S(1)} %get-tuple-element.205), channel_id=1, source_target_pairs={{0,8},{8,0},{16,24},{24,16},{1,9},{9,1},{17,25},{25,17},{2,10},{10... | collective-permute-start | bytes 884744 | tf_op jit(solution)/shard_map/ppermute | solution.py:65
  90.0 7.5 %collective-permute-start.35 = (bf16[192,768]{1,0:T(8,128)(2,1)S(1)}, bf16[192,768]{1,0:T(8,128)(2,1)S(1)}, u32[]{:S(2)}, u32[]{:S(2)}) collective-permute-start(bf16[192,768]{1,0:T(8,128)(2,1)S(1)} %get-tuple-element.206), channel_id=1, source_target_pairs={{0,16},{8,24},{16,0},{24,8},{1,17},{9,25},{17,1},{25,9},{2,18},{10... | collective-permute-start | bytes 884744 | tf_op jit(solution)/shard_map/ppermute | solution.py:65
  98.9 6.7 %collective-permute-start.36 = (bf16[512,768]{1,0:T(8,128)(2,1)S(1)}, bf16[512,768]{1,0:T(8,128)(2,1)S(1)}, u32[]{:S(2)}, u32[]{:S(2)}) collective-permute-start(bf16[512,768]{1,0:T(8,128)(2,1)S(1)} %get-tuple-element.215), channel_id=1, source_target_pairs={{0,4},{4,0},{1,5},{5,1},{2,6},{6,2},{3,7},{7,3},{8,12},{12,8},{9,1... | collective-permute-start | bytes 2359304 | tf_op jit(solution)/shard_map/ppermute | solution.py:65
  98.9 11.1 %collective-permute-start.24 = (bf16[128,768]{1,0:T(8,128)(2,1)S(1)}, bf16[128,768]{1,0:T(8,128)(2,1)S(1)}, u32[]{:S(2)}, u32[]{:S(2)}) collective-permute-start(bf16[128,768]{1,0:T(8,128)(2,1)S(1)} %get-tuple-element.179), channel_id=1, source_target_pairs={{0,1},{1,0},{2,3},{3,2},{4,5},{5,4},{6,7},{7,6},{8,9},{9,8},{10,11... | collective-permute-start | bytes 589832 | tf_op jit(solution)/shard_map/ppermute | solution.py:65
  100.0 17.1 %collective-permute-start.25 = (bf16[128,768]{1,0:T(8,128)(2,1)S(1)}, bf16[128,768]{1,0:T(8,128)(2,1)S(1)}, u32[]{:S(2)}, u32[]{:S(2)}) collective-permute-start(bf16[128,768]{1,0:T(8,128)(2,1)S(1)} %get-tuple-element.180), channel_id=1, source_target_pairs={{0,2},{1,3},{2,0},{3,1},{4,6},{5,7},{6,4},{7,5},{8,10},{9,11},{10,... | collective-permute-start | bytes 589832 | tf_op jit(solution)/shard_map/ppermute | solution.py:65
  101.2 15.9 %collective-permute-start.26 = (bf16[128,768]{1,0:T(8,128)(2,1)S(1)}, bf16[128,768]{1,0:T(8,128)(2,1)S(1)}, u32[]{:S(2)}, u32[]{:S(2)}) collective-permute-start(bf16[128,768]{1,0:T(8,128)(2,1)S(1)} %get-tuple-element.181), channel_id=1, source_target_pairs={{0,3},{1,2},{2,1},{3,0},{4,7},{5,6},{6,5},{7,4},{8,11},{9,10},{10,... | collective-permute-start | bytes 589832 | tf_op jit(solution)/shard_map/ppermute | solution.py:65
  106.5 16.1 %collective-permute-start.37 = (bf16[224,768]{1,0:T(8,128)(2,1)S(1)}, bf16[224,768]{1,0:T(8,128)(2,1)S(1)}, u32[]{:S(2)}, u32[]{:S(2)}) collective-permute-start(bf16[224,768]{1,0:T(8,128)(2,1)S(1)} %get-tuple-element.221), channel_id=1, source_target_pairs={{0,8},{8,0},{16,24},{24,16},{1,9},{9,1},{17,25},{25,17},{2,10},{10... | collective-permute-start | bytes 1032200 | tf_op jit(solution)/shard_map/ppermute | solution.py:65
  109.4 13.2 %collective-permute-start.38 = (bf16[224,768]{1,0:T(8,128)(2,1)S(1)}, bf16[224,768]{1,0:T(8,128)(2,1)S(1)}, u32[]{:S(2)}, u32[]{:S(2)}) collective-permute-start(bf16[224,768]{1,0:T(8,128)(2,1)S(1)} %get-tuple-element.222), channel_id=1, source_target_pairs={{0,16},{8,24},{16,0},{24,8},{1,17},{9,25},{17,1},{25,9},{2,18},{10... | collective-permute-start | bytes 1032200 | tf_op jit(solution)/shard_map/ppermute | solution.py:65
  117.3 8.1 %collective-permute-start.27 = (bf16[96,768]{1,0:T(8,128)(2,1)S(1)}, bf16[96,768]{1,0:T(8,128)(2,1)S(1)}, u32[]{:S(2)}, u32[]{:S(2)}) collective-permute-start(bf16[96,768]{1,0:T(8,128)(2,1)S(1)} %get-tuple-element.189), channel_id=1, source_target_pairs={{0,8},{8,0},{16,24},{24,16},{1,9},{9,1},{17,25},{25,17},{2,10},{10... | collective-permute-start | bytes 442376 | tf_op jit(solution)/shard_map/ppermute | solution.py:65
  121.0 8.4 %collective-permute-start.28 = (bf16[96,768]{1,0:T(8,128)(2,1)S(1)}, bf16[96,768]{1,0:T(8,128)(2,1)S(1)}, u32[]{:S(2)}, u32[]{:S(2)}) collective-permute-start(bf16[96,768]{1,0:T(8,128)(2,1)S(1)} %get-tuple-element.190), channel_id=1, source_target_pairs={{0,16},{8,24},{16,0},{24,8},{1,17},{9,25},{17,1},{25,9},{2,18},{10... | collective-permute-start | bytes 442376 | tf_op jit(solution)/shard_map/ppermute | solution.py:65
  121.0 8.4 %collective-permute-start.29 = (bf16[96,768]{1,0:T(8,128)(2,1)S(1)}, bf16[96,768]{1,0:T(8,128)(2,1)S(1)}, u32[]{:S(2)}, u32[]{:S(2)}) collective-permute-start(bf16[96,768]{1,0:T(8,128)(2,1)S(1)} %get-tuple-element.191), channel_id=1, source_target_pairs={{0,24},{8,16},{16,8},{24,0},{1,25},{9,17},{17,9},{25,1},{2,26},{10... | collective-permute-start | bytes 442376 | tf_op jit(solution)/shard_map/ppermute | solution.py:65
  122.7 13.9 %collective-permute-start.39 = (bf16[256,768]{1,0:T(8,128)(2,1)S(1)}, bf16[256,768]{1,0:T(8,128)(2,1)S(1)}, u32[]{:S(2)}, u32[]{:S(2)}) collective-permute-start(bf16[256,768]{1,0:T(8,128)(2,1)S(1)} %get-tuple-element.225.sent1), channel_id=1, source_target_pairs={{0,8},{8,0},{16,24},{24,16},{1,9},{9,1},{17,25},{25,17},{2,10},{10... | collective-permute-start | bytes 1179656 | tf_op jit(solution)/shard_map/ppermute | solution.py:65
  124.8 11.9 %collective-permute-start.40 = (bf16[256,768]{1,0:T(8,128)(2,1)S(1)}, bf16[256,768]{1,0:T(8,128)(2,1)S(1)}, u32[]{:S(2)}, u32[]{:S(2)}) collective-permute-start(bf16[256,768]{1,0:T(8,128)(2,1)S(1)} %get-tuple-element.226.sent2), channel_id=1, source_target_pairs={{0,16},{8,24},{16,0},{24,8},{1,17},{9,25},{17,1},{25,9},{2,18},{10... | collective-permute-start | bytes 1179656 | tf_op jit(solution)/shard_map/ppermute | solution.py:65
  129.4 15.2 %collective-permute-start.30 = (bf16[128,768]{1,0:T(8,128)(2,1)S(1)}, bf16[128,768]{1,0:T(8,128)(2,1)S(1)}, u32[]{:S(2)}, u32[]{:S(2)}) collective-permute-start(bf16[128,768]{1,0:T(8,128)(2,1)S(1)} %shard_map.334.t0), channel_id=1, source_target_pairs={{0,1},{1,0},{2,3},{3,2},{4,5},{5,4},{6,7},{7,6},{8,9},{9,8},{10,11... | collective-permute-start | bytes 589832 | tf_op jit(solution)/shard_map/ppermute | solution.py:65
  134.2 14.8 %collective-permute-start.31 = (bf16[128,768]{1,0:T(8,128)(2,1)S(1)}, bf16[128,768]{1,0:T(8,128)(2,1)S(1)}, u32[]{:S(2)}, u32[]{:S(2)}) collective-permute-start(bf16[128,768]{1,0:T(8,128)(2,1)S(1)} %shard_map.334.t0), channel_id=1, source_target_pairs={{0,2},{1,3},{2,0},{3,1},{4,6},{5,7},{6,4},{7,5},{8,10},{9,11},{10,... | collective-permute-start | bytes 589832 | tf_op jit(solution)/shard_map/ppermute | solution.py:65
  134.2 14.8 %collective-permute-start.32 = (bf16[128,768]{1,0:T(8,128)(2,1)S(1)}, bf16[128,768]{1,0:T(8,128)(2,1)S(1)}, u32[]{:S(2)}, u32[]{:S(2)}) collective-permute-start(bf16[128,768]{1,0:T(8,128)(2,1)S(1)} %shard_map.334.t0), channel_id=1, source_target_pairs={{0,3},{1,2},{2,1},{3,0},{4,7},{5,6},{6,5},{7,4},{8,11},{9,10},{10,... | collective-permute-start | bytes 589832 | tf_op jit(solution)/shard_map/ppermute | solution.py:65
  136.7 4.7 %collective-permute-start.41 = (bf16[64,768]{1,0:T(8,128)(2,1)S(1)}, bf16[64,768]{1,0:T(8,128)(2,1)S(1)}, u32[]{:S(2)}, u32[]{:S(2)}) collective-permute-start(bf16[64,768]{1,0:T(8,128)(2,1)S(1)} %get-tuple-element.228.mid1), channel_id=1, source_target_pairs={{0,8},{8,0},{16,24},{24,16},{1,9},{9,1},{17,25},{25,17},{2,10},{10... | collective-permute-start | bytes 294920 | tf_op jit(solution)/shard_map/ppermute | solution.py:65
  137.3 4.6 %collective-permute-start.42 = (bf16[64,768]{1,0:T(8,128)(2,1)S(1)}, bf16[64,768]{1,0:T(8,128)(2,1)S(1)}, u32[]{:S(2)}, u32[]{:S(2)}) collective-permute-start(bf16[64,768]{1,0:T(8,128)(2,1)S(1)} %get-tuple-element.229.mid2), channel_id=1, source_target_pairs={{0,16},{8,24},{16,0},{24,8},{1,17},{9,25},{17,1},{25,9},{2,18},{10... | collective-permute-start | bytes 294920 | tf_op jit(solution)/shard_map/ppermute | solution.py:65
  141.9 7.7 %collective-permute-start.43 = (bf16[224,768]{1,0:T(8,128)(2,1)S(1)}, bf16[224,768]{1,0:T(8,128)(2,1)S(1)}, u32[]{:S(2)}, u32[]{:S(2)}) collective-permute-start(bf16[224,768]{1,0:T(8,128)(2,1)S(1)} %get-tuple-element.230.sent1), channel_id=1, source_target_pairs={{0,8},{8,0},{16,24},{24,16},{1,9},{9,1},{17,25},{25,17},{2,10},{10... | collective-permute-start | bytes 1032200 | tf_op jit(solution)/shard_map/ppermute | solution.py:65
  143.5 7.5 %collective-permute-start.44 = (bf16[224,768]{1,0:T(8,128)(2,1)S(1)}, bf16[224,768]{1,0:T(8,128)(2,1)S(1)}, u32[]{:S(2)}, u32[]{:S(2)}) collective-permute-start(bf16[224,768]{1,0:T(8,128)(2,1)S(1)} %get-tuple-element.231.sent2), channel_id=1, source_target_pairs={{0,16},{8,24},{16,0},{24,8},{1,17},{9,25},{17,1},{25,9},{2,18},{10... | collective-permute-start | bytes 1032200 | tf_op jit(solution)/shard_map/ppermute | solution.py:65
  152.3 6.6 %collective-permute-start.46 = (bf16[768,768]{1,0:T(8,128)(2,1)S(1)}, bf16[768,768]{1,0:T(8,128)(2,1)S(1)}, u32[]{:S(2)}, u32[]{:S(2)}) collective-permute-start(bf16[768,768]{1,0:T(8,128)(2,1)S(1)} %shard_map.346.rows), channel_id=1, source_target_pairs={{0,4},{4,0},{1,5},{5,1},{2,6},{6,2},{3,7},{7,3},{8,12},{12,8},{9,1... | collective-permute-start | bytes 3538952 | tf_op jit(solution)/shard_map/ppermute | solution.py:65
  152.3 4.3 %collective-permute-start.45 = (bf16[512,768]{1,0:T(8,128)(2,1)S(1)}, bf16[512,768]{1,0:T(8,128)(2,1)S(1)}, u32[]{:S(2)}, u32[]{:S(2)}) collective-permute-start(bf16[512,768]{1,0:T(8,128)(2,1)S(1)} %shard_map.345.mine), channel_id=1, source_target_pairs={{0,4},{4,0},{1,5},{5,1},{2,6},{6,2},{3,7},{7,3},{8,12},{12,8},{9,1... | collective-permute-start | bytes 2359304 | tf_op jit(solution)/shard_map/ppermute | solution.py:65
  (1 other events, 5.9 us)

commit v3 on v2

--- a/solution.py
+++ b/solution.py
@@ -388,7 +388,8 @@
         out[2 * few :, :] = near[few : few + done, :]
 
 
-def feed_join_body(ids, sent1, sent2, near1, near2, came1, came2, out):
+def joins_body(ids, along1, along2, came1, came2, sent1, sent2, near1, near2, seen, attend_out, out):
+    join_half(ids[0], along1, along2, came1, came2, attend_out)
     rows = out.shape[0] // 8
     few = sent1.shape[0] - 2 * rows
     skip = came1.shape[0] - rows
@@ -399,10 +400,6 @@
         for k, (ref, at) in enumerate(blocks):
             to = pl.multiple_of((4 * half + (ids[0] ^ k)) * rows, rows)
             out[pl.ds(to, rows), :] = ref[at, :]
-
-
-def attend_join_body(ids, sent1, sent2, came1, came2, seen, out):
-    join_half(ids[0], sent1, sent2, came1, came2, out)
 
 
 def norm_back_body(ids, *refs):
@@ -490,21 +487,43 @@
     out[...] = total_of(own, (r1, r2, r3)).astype(LOW)
 
 
-def widen_body(flip, ids, rows, *refs):
-    first, second, scr, sem = refs[-4:]
+def sender(sem):
+    copies = []
+
+    def send(source, target):
+        copy = pltpu.make_async_copy(source, target, sem.at[len(copies)])
+        copy.start()
+        copies.append(copy)
+
+    def wait():
+        for copy in copies:
+            copy.wait()
+
+    return send, wait
+
+
+def widen(which, rows, first, second, scr, sem):
     step = rows.shape[0] // 4
-    for c, out in ((0, first), (1, second)):
-
-        @pl.when((ids[2] ^ flip) == c)
-        def _(out=out):
-            copies = []
-            for n in range(4):
-                span = pl.ds(n * step, step)
-                scr[span, :] = rows[span, :].astype(F32)
-                copies.append(pltpu.make_async_copy(scr.at[span, :], out.at[span, :], sem.at[n]))
-                copies[-1].start()
-            for copy in copies:
-                copy.wait()
+    for n in range(4):
+        span = pl.ds(n * step, step)
+        scr[span, :] = rows[span, :].astype(F32)
+        for c, out in ((0, first), (1, second)):
+
+            @pl.when(which == c)
+            def _(out=out, n=n, span=span):
+                copy = pltpu.make_async_copy(scr.at[span, :], out.at[span, :], sem.at[n])
+                copy.start()
+
+
+def widen_wait(which, first, second, scr, sem):
+    step = scr.shape[0] // 4
+    for n in range(4):
+        span = pl.ds(n * step, step)
+        for c, out in ((0, first), (1, second)):
+
+            @pl.when(which == c)
+            def _(out=out, n=n, span=span):
+                pltpu.make_async_copy(scr.at[span, :], out.at[span, :], sem.at[n]).wait()
 
 
 def output_body(ids, n0, q1, q2, q3, output):
@@ -514,8 +533,16 @@
         output[ids[0] ^ b] = q[q.shape[0] - rows :, :]
 
 
-def unpack_attend_body(ids, mine, other, dq, dk, dv, do, *rest):
-    *rows_out, query_out, value_out, rel_out = rest
+def unpack_body(ids, mine, other, feed_other, _first, _second, first, second, *rest):
+    *rows_out, query_out, value_out, rel_out, dq, dk, dv, do, scr, wide, sem, wide_sem = rest
+    widen(1 - ids[2], feed_other, first, second, wide, wide_sem)
+    unpack_attend(ids, mine, other, rows_out, query_out, value_out, rel_out, (dq, dk, dv, do), scr, sem)
+    widen_wait(1 - ids[2], first, second, wide, wide_sem)
+
+
+def unpack_attend(ids, mine, other, rows_out, query_out, value_out, rel_out, larges, scr, sem):
+    dq, dk, dv, do = larges
+    send, wait = sender(sem)
     part = dq.shape[0]
     heads = rel_out.shape[0]
     head = part // heads
@@ -523,10 +550,10 @@
 
         @pl.when(ids[2] == c)
         def _(a=a, b=b):
-            dq[...] = a[:part, :].astype(F32)
-            dk[...] = a[part : 2 * part, :].astype(F32)
-            dv[...] = b[:part, :].astype(F32)
-            do[...] = b[part : 2 * part, :].astype(F32)
+            scr[0] = a[:part, :].astype(F32)
+            scr[1] = a[part : 2 * part, :].astype(F32)
+            scr[2] = b[:part, :].astype(F32)
+            scr[3] = b[part : 2 * part, :].astype(F32)
             small_a = a[2 * part :, :].astype(F32)
             small_b = b[2 * part :, :].astype(F32)
             for n, out in enumerate(rows_out):
@@ -543,6 +570,10 @@
                     at = h * BASES + index
                     rel_out[h : h + 1, index : index + 1] = table[at : at + 1, :1]
 
+    for n, out in enumerate(larges):
+        send(scr.at[n], out)
+    wait()
+
 
 def quarters_body(met, r1, r2, r3, own, n1, n2, n3, q0, q1, q2, q3):
     total = total_of(own, (r1, r2, r3)).astype(LOW)
@@ -564,12 +595,17 @@
     out[...] = t1[:rows, :] + t2[:rows, :] + t3[:rows, :]
 
 
-def place_body(ids, t0, t1, t2, t3, out):
-    rows = out.shape[1] // 4
-    for k, t in enumerate((t0, t1, t2, t3)):
-        at = pl.ds(pl.multiple_of((ids[1] ^ k) * rows, rows), rows)
-        for b in range(4):
-            out[ids[0] ^ b, at, :] = t[b * rows : (b + 1) * rows, :].astype(out.dtype)
+def place_body(ids, t0, t1, t2, t3, mine, out, first, second, scr, wide, sem, wide_sem):
+    send, wait = sender(sem)
+    rows = scr.shape[1] // 4
+    for b in range(4):
+        for k, t in enumerate((t0, t1, t2, t3)):
+            at = pl.ds(pl.multiple_of((ids[1] ^ k) * rows, rows), rows)
+            scr[b, at, :] = t[b * rows : (b + 1) * rows, :].astype(out.dtype)
+        send(scr.at[b], out.at[ids[0] ^ b])
+    widen(ids[2], mine, first, second, wide, wide_sem)
+    wait()
+    widen_wait(ids[2], first, second, wide, wide_sem)
 
 
 def dp_sum(values, dp_size):
@@ -777,45 +813,42 @@
     )
     came = both_ways(along1, along2, seq_size)
     seen = kernel(touch_body, low(SMALL_ROWS, width), tuple(spread), micros=8.0)
-    attend_mine = kernel(
-        attend_join_body,
-        low(half_rows, width),
-        (ids, along1, along2, *came, seen),
+    attend_mine, feed_mine = kernel(
+        joins_body,
+        [low(half_rows, width), low(width, width)],
+        (ids, along1, along2, *came, sent1, sent2, *near, seen),
         smem=1,
         micros=0.2,
-    )
-    feed_mine = kernel(
-        feed_join_body,
-        low(width, width),
-        (ids, sent1, sent2, *near, came[0], after(came[1], attend_mine)),
-        smem=1,
-        micros=0.1,
     )
     attend_mine, feed_mine = dp_sum((attend_mine, feed_mine), dp_size)
     attend_other = swap(attend_mine, "dp", dp_size, 1)
     feed_other = swap(feed_mine, "dp", dp_size, 1)
-    widen = lambda flip, *args: kernel(
-        functools.partial(widen_body, flip),
-        [f32(width, width)] * 2,
-        (ids, *args),
-        smem=1,
-        scratch=[pltpu.VMEM((width, width), F32), pltpu.SemaphoreType.DMA((4,))],
+    wide = pltpu.VMEM((width, width), F32)
+    sems = pltpu.SemaphoreType.DMA((4,))
+    input_all, *halves = kernel(
+        place_body,
+        [f32(4, block_len, width)] + [f32(width, width)] * 2,
+        (ids, joined, *spread, feed_mine),
+        smem=1,
+        scratch=[pltpu.VMEM((4, block_len, width), F32), wide, sems, sems],
         micros=0.1,
-        hbm=(0, 1),
-        reused=len(args) - 1,
-    )
-    halves = widen(0, feed_mine)
-    down_grad, up_grad = widen(1, feed_other, *halves)
-    input_all = kernel(
-        place_body, f32(4, block_len, width), (ids, joined, *spread), smem=1, micros=0.1
-    )
-    dq, dk, dv, do, *small, query_sum, value_sum, rel_sum = kernel(
-        unpack_attend_body,
-        [f32(part, width)] * 4 + [f32(width)] * 7 + [f32(part)] * 2 + [f32(heads, BASES)],
-        (ids, after(attend_mine, halves), attend_other),
-        smem=1,
-        micros=1.5,
-    )
+        hbm=range(3),
+    )
+    down_grad, up_grad, *rest = kernel(
+        unpack_body,
+        [f32(width, width)] * 2
+        + [f32(width)] * 7
+        + [f32(part)] * 2
+        + [f32(heads, BASES)]
+        + [f32(part, width)] * 4,
+        (ids, attend_mine, attend_other, feed_other, *halves),
+        smem=1,
+        scratch=[pltpu.VMEM((4, part, width), F32), wide, sems, sems],
+        micros=0.1,
+        hbm=(0, 1, 12, 13, 14, 15),
+        reused=2,
+    )
+    *small, query_sum, value_sum, rel_sum, dq, dk, dv, do = rest
     ffn_gain_sum, ffn_shift_sum, down_bias_sum, up_bias_sum, attn_gain_sum, attn_shift_sum, out_bias_sum = small
     return (
         output_all,

time: 163 us -> 157 us (0.963)
  starting transfers between devices: 65.6 us -> 61.7 us
  Pallas kernels: 35.5 us -> 32.9 us
    ppermute x47, starting transfers between devices: 65.6 us -> 61.7 us  [swap(): return lax.ppermute(block, axis, [(s, s ^ k) for s in range(size)])]
    pallas_call x28 -> x25, Pallas kernels: 35.5 us -> 32.9 us  [kernel(): pl.pallas_call(body, out_shape=outs, in_specs=in_specs, out_specs=out_spe...]
  transfers between devices with their start and end apart: 47 -> 47, of which waited for: 22 -> 26; matrix products, arithmetic and copies ran while one was open for 1% -> 1% of each run, Pallas kernels for 14% -> 12%
where the time goes in v3:
time: 157 us; the launch traced here: 154 us
  starting transfers between devices  61.7 us (39%)
  waiting for transfers between devices  55.3 us (35%)
  Pallas kernels  32.9 us (21%)
  local copies, waits for them, and re-layouts  2.24 us (1%)
    ppermute x47, starting transfers between devices, swap(): return lax.ppermute(block, axis, [(s, s ^ k) for s in range(size)])  61.7 us
    ppermute x47, waiting for transfers between devices, swap(): return lax.ppermute(block, axis, [(s, s ^ k) for s in range(size)])  55.3 us
    pallas_call x25, Pallas kernels, kernel(): pl.pallas_call(body, out_shape=outs, in_specs=in_specs, out_specs=out_spe...  32.9 us
  transfers between devices with their start and end apart: 47, of which 26 were waited for; matrix products, arithmetic and copies ran while one was open for 1% of the time, Pallas kernels for 12%

profile of v3, /device:TPU:0, one launch (start us, length us, event | category | flops | bytes accessed | tf_op | source)
XLA Modules:
  0.0 154.2 jit_solution(8280869849836486670)
XLA Ops:
  0.7 1.3 dynamic-slice_bitcast_fusion
  2.0 4.0 %collective-permute-start.2 = (bf16[128,768]{1,0:T(8,128)(2,1)S(1)}, bf16[128,768]{1,0:T(8,128)(2,1)S(1)}, u32[]{:S(2)}, u32[]{:S(2)}) collective-permute-start(bf16[128,768]{1,0:T(8,128)(2,1)S(1)} %get-tuple-element.254), channel_id=1, source_target_pairs={{0,24},{8,16},{16,8},{24,0},{1,25},{9,17},{17,9},{25,1},{2,26},{10... | collective-permute-start | bytes 589832 | tf_op jit(solution)/shard_map/ppermute | solution.py:65
  6.6 0.6 dynamic_slice.30
  7.5 0.7 pad_add_fusion.ids
  8.2 2.1 %shard_map.322.refs_11_ = f32[3,512,256]{2,1,0:T(8,128)S(1)} custom-call(s32[4]{0:T(128)S(1)} %pad_add_fusion.ids, f32[3,8]{1,0:T(4,128)S(1)} %copy-done.6), custom_call_target="tpu_custom_call" | custom-call | flops 1200000000 | bytes 9000000 | tf_op jit(solution)/shard_map/pallas_call | solution.py:37
  10.3 1.4 collective-permute-done.2.refs_3_
  11.7 3.7 %collective-permute-done.refs_1_ = bf16[128,768]{1,0:T(8,128)(2,1)S(1)} collective-permute-done((bf16[128,768]{1,0:T(8,128)(2,1)S(1)}, bf16[128,768]{1,0:T(8,128)(2,1)S(1)}, u32[]{:S(2)}, u32[]{:S(2)}) %collective-permute-start) | collective-permute-done | bytes 196640 | tf_op jit(solution)/shard_map/ppermute | solution.py:65
  15.5 6.4 %shard_map.323 = (f32[64,768]{1,0:T(8,128)S(1)}, bf16[64,768]{1,0:T(8,128)(2,1)S(1)}, bf16[64,768]{1,0:T(8,128)(2,1)S(1)}, bf16[64,768]{1,0:T(8,128)(2,1)S(1)}, ...) custom-call(s32[4]{0:T(128)S(1)} %pad_add_fusion.ids, ...), custom_call_target="tpu_custom_call" | custom-call | flops 2000000000 | bytes 15000000 | tf_op jit(solution)/shard_map/pallas_call | solution.py:37
  21.9 1.6 %collective-permute-start.3 = (bf16[64,768]{1,0:T(8,128)(2,1)S(1)}, bf16[64,768]{1,0:T(8,128)(2,1)S(1)}, u32[]{:S(2)}, u32[]{:S(2)}) collective-permute-start(bf16[64,768]{1,0:T(8,128)(2,1)S(1)} %get-tuple-element.136), channel_id=1, source_target_pairs={{0,1},{1,0},{2,3},{3,2},{4,5},{5,4},{6,7},{7,6},{8,9},{9,8},{10,11... | collective-permute-start | bytes 294920 | tf_op jit(solution)/shard_map/ppermute | solution.py:65
  23.5 2.6 %collective-permute-start.4 = (bf16[64,768]{1,0:T(8,128)(2,1)S(1)}, bf16[64,768]{1,0:T(8,128)(2,1)S(1)}, u32[]{:S(2)}, u32[]{:S(2)}) collective-permute-start(bf16[64,768]{1,0:T(8,128)(2,1)S(1)} %get-tuple-element.137), channel_id=1, source_target_pairs={{0,2},{1,3},{2,0},{3,1},{4,6},{5,7},{6,4},{7,5},{8,10},{9,11},{10,... | collective-permute-start | bytes 294920 | tf_op jit(solution)/shard_map/ppermute | solution.py:65
  26.5 7.5 %collective-permute-done.4.r2 = bf16[64,768]{1,0:T(8,128)(2,1)S(1)} collective-permute-done((bf16[64,768]{1,0:T(8,128)(2,1)S(1)}, bf16[64,768]{1,0:T(8,128)(2,1)S(1)}, u32[]{:S(2)}, u32[]{:S(2)}) %collective-permute-start.4) | collective-permute-done | bytes 98336 | tf_op jit(solution)/shard_map/ppermute | solution.py:65
  34.1 2.5 %collective-permute-start.8 = (bf16[64,768]{1,0:T(8,128)(2,1)S(1)}, bf16[64,768]{1,0:T(8,128)(2,1)S(1)}, u32[]{:S(2)}, u32[]{:S(2)}) collective-permute-start(bf16[64,768]{1,0:T(8,128)(2,1)S(1)} %shard_map.324.a0), channel_id=1, source_target_pairs={{0,3},{1,2},{2,1},{3,0},{4,7},{5,6},{6,5},{7,4},{8,11},{9,10},{10,... | collective-permute-start | bytes 294920 | tf_op jit(solution)/shard_map/ppermute | solution.py:65
  36.6 1.3 collective-permute-start.7
  37.9 0.6 collective-permute-start.6
  38.5 2.5 %collective-permute-start.11 = (bf16[64,768]{1,0:T(8,128)(2,1)S(1)}, bf16[64,768]{1,0:T(8,128)(2,1)S(1)}, u32[]{:S(2)}, u32[]{:S(2)}) collective-permute-start(bf16[64,768]{1,0:T(8,128)(2,1)S(1)} %get-tuple-element.258), channel_id=1, source_target_pairs={{0,24},{8,16},{16,8},{24,0},{1,25},{9,17},{17,9},{25,1},{2,26},{10... | collective-permute-start | bytes 294920 | tf_op jit(solution)/shard_map/ppermute | solution.py:65
  41.7 1.4 collective-permute-start.9
  43.1 1.8 %collective-permute-done.7.a2 = bf16[64,768]{1,0:T(8,128)(2,1)S(1)} collective-permute-done((bf16[64,768]{1,0:T(8,128)(2,1)S(1)}, bf16[64,768]{1,0:T(8,128)(2,1)S(1)}, u32[]{:S(2)}, u32[]{:S(2)}) %collective-permute-start.7) | collective-permute-done | bytes 98336 | tf_op jit(solution)/shard_map/ppermute | solution.py:65
  44.9 2.0 %shard_map.325 = (f32[64,768]{1,0:T(8,128)S(1)}, bf16[64,768]{1,0:T(8,128)(2,1)S(1)}, bf16[64,768]{1,0:T(8,128)(2,1)S(1)}, bf16[64,768]{1,0:T(8,128)(2,1)S(1)}, ...) custom-call(s32[4]{0:T(128)S(1)} %pad_add_fusion.ids, ...), custom_call_target="tpu_custom_call" | custom-call | flops 1200000000 | bytes 9000000 | tf_op jit(solution)/shard_map/pallas_call | solution.py:37
  46.9 2.1 %collective-permute-start.12 = (bf16[64,768]{1,0:T(8,128)(2,1)S(1)}, bf16[64,768]{1,0:T(8,128)(2,1)S(1)}, u32[]{:S(2)}, u32[]{:S(2)}) collective-permute-start(bf16[64,768]{1,0:T(8,128)(2,1)S(1)} %get-tuple-element.150), channel_id=1, source_target_pairs={{0,1},{1,0},{2,3},{3,2},{4,5},{5,4},{6,7},{7,6},{8,9},{9,8},{10,11... | collective-permute-start | bytes 294920 | tf_op jit(solution)/shard_map/ppermute | solution.py:65
  49.3 2.2 %collective-permute-start.14 = (bf16[64,768]{1,0:T(8,128)(2,1)S(1)}, bf16[64,768]{1,0:T(8,128)(2,1)S(1)}, u32[]{:S(2)}, u32[]{:S(2)}) collective-permute-start(bf16[64,768]{1,0:T(8,128)(2,1)S(1)} %get-tuple-element.152), channel_id=1, source_target_pairs={{0,3},{1,2},{2,1},{3,0},{4,7},{5,6},{6,5},{7,4},{8,11},{9,10},{10,... | collective-permute-start | bytes 294920 | tf_op jit(solution)/shard_map/ppermute | solution.py:65
  52.0 4.9 %collective-permute-done.13.r2 = bf16[64,768]{1,0:T(8,128)(2,1)S(1)} collective-permute-done((bf16[64,768]{1,0:T(8,128)(2,1)S(1)}, bf16[64,768]{1,0:T(8,128)(2,1)S(1)}, u32[]{:S(2)}, u32[]{:S(2)}) %collective-permute-start.13) | collective-permute-done | bytes 98336 | tf_op jit(solution)/shard_map/ppermute | solution.py:65
  56.9 1.8 %collective-permute-start.17 = (bf16[64,768]{1,0:T(8,128)(2,1)S(1)}, bf16[64,768]{1,0:T(8,128)(2,1)S(1)}, u32[]{:S(2)}, u32[]{:S(2)}) collective-permute-start(bf16[64,768]{1,0:T(8,128)(2,1)S(1)} %shard_map.326.refs_0_), channel_id=1, source_target_pairs={{0,3},{1,2},{2,1},{3,0},{4,7},{5,6},{6,5},{7,4},{8,11},{9,10},{10,... | collective-permute-start | bytes 294920 | tf_op jit(solution)/shard_map/ppermute | solution.py:65
  58.7 2.4 %collective-permute-start.16 = (bf16[64,768]{1,0:T(8,128)(2,1)S(1)}, bf16[64,768]{1,0:T(8,128)(2,1)S(1)}, u32[]{:S(2)}, u32[]{:S(2)}) collective-permute-start(bf16[64,768]{1,0:T(8,128)(2,1)S(1)} %shard_map.326.refs_0_), channel_id=1, source_target_pairs={{0,2},{1,3},{2,0},{3,1},{4,6},{5,7},{6,4},{7,5},{8,10},{9,11},{10,... | collective-permute-start | bytes 294920 | tf_op jit(solution)/shard_map/ppermute | solution.py:65
  61.4 2.1 %collective-permute-done.17.refs_3_ = bf16[64,768]{1,0:T(8,128)(2,1)S(1)} collective-permute-done((bf16[64,768]{1,0:T(8,128)(2,1)S(1)}, bf16[64,768]{1,0:T(8,128)(2,1)S(1)}, u32[]{:S(2)}, u32[]{:S(2)}) %collective-permute-start.17) | collective-permute-done | bytes 98336 | tf_op jit(solution)/shard_map/ppermute | solution.py:65
  63.5 3.2 %collective-permute-done.16.refs_2_ = bf16[64,768]{1,0:T(8,128)(2,1)S(1)} collective-permute-done((bf16[64,768]{1,0:T(8,128)(2,1)S(1)}, bf16[64,768]{1,0:T(8,128)(2,1)S(1)}, u32[]{:S(2)}, u32[]{:S(2)}) %collective-permute-start.16) | collective-permute-done | bytes 98336 | tf_op jit(solution)/shard_map/ppermute | solution.py:65
  66.8 2.3 %shard_map.327 = (f32[64,768]{1,0:T(8,128)S(1)}, bf16[64,768]{1,0:T(8,128)(2,1)S(1)}, bf16[64,768]{1,0:T(8,128)(2,1)S(1)}, bf16[64,768]{1,0:T(8,128)(2,1)S(1)}, ...) custom-call(s32[4]{0:T(128)S(1)} %pad_add_fusion.ids, ...), custom_call_target="tpu_custom_call" | custom-call | flops 1200000000 | bytes 9000000 | tf_op jit(solution)/shard_map/pallas_call | solution.py:37
  69.2 1.8 %collective-permute-start.19 = (bf16[64,768]{1,0:T(8,128)(2,1)S(1)}, bf16[64,768]{1,0:T(8,128)(2,1)S(1)}, u32[]{:S(2)}, u32[]{:S(2)}) collective-permute-start(bf16[64,768]{1,0:T(8,128)(2,1)S(1)} %get-tuple-element.163), channel_id=1, source_target_pairs={{0,2},{1,3},{2,0},{3,1},{4,6},{5,7},{6,4},{7,5},{8,10},{9,11},{10,... | collective-permute-start | bytes 294920 | tf_op jit(solution)/shard_map/ppermute | solution.py:65
  71.0 2.5 %collective-permute-start.20 = (bf16[64,768]{1,0:T(8,128)(2,1)S(1)}, bf16[64,768]{1,0:T(8,128)(2,1)S(1)}, u32[]{:S(2)}, u32[]{:S(2)}) collective-permute-start(bf16[64,768]{1,0:T(8,128)(2,1)S(1)} %get-tuple-element.164), channel_id=1, source_target_pairs={{0,3},{1,2},{2,1},{3,0},{4,7},{5,6},{6,5},{7,4},{8,11},{9,10},{10,... | collective-permute-start | bytes 294920 | tf_op jit(solution)/shard_map/ppermute | solution.py:65
  73.5 1.1 shard_map.335
  74.8 2.7 %collective-permute-done.20.r3 = bf16[64,768]{1,0:T(8,128)(2,1)S(1)} collective-permute-done((bf16[64,768]{1,0:T(8,128)(2,1)S(1)}, bf16[64,768]{1,0:T(8,128)(2,1)S(1)}, u32[]{:S(2)}, u32[]{:S(2)}) %collective-permute-start.20) | collective-permute-done | bytes 98336 | tf_op jit(solution)/shard_map/ppermute | solution.py:65
  77.5 2.6 %collective-permute-start.23 = (bf16[64,768]{1,0:T(8,128)(2,1)S(1)}, bf16[64,768]{1,0:T(8,128)(2,1)S(1)}, u32[]{:S(2)}, u32[]{:S(2)}) collective-permute-start(bf16[64,768]{1,0:T(8,128)(2,1)S(1)} %shard_map.328.refs_0_), channel_id=1, source_target_pairs={{0,3},{1,2},{2,1},{3,0},{4,7},{5,6},{6,5},{7,4},{8,11},{9,10},{10,... | collective-permute-start | bytes 294920 | tf_op jit(solution)/shard_map/ppermute | solution.py:65
  80.5 1.5 collective-permute-start.21
  82.0 1.4 shard_map.336
  83.4 5.4 %collective-permute-start.34 = (bf16[192,768]{1,0:T(8,128)(2,1)S(1)}, bf16[192,768]{1,0:T(8,128)(2,1)S(1)}, u32[]{:S(2)}, u32[]{:S(2)}) collective-permute-start(bf16[192,768]{1,0:T(8,128)(2,1)S(1)} %get-tuple-element.206), channel_id=1, source_target_pairs={{0,8},{8,0},{16,24},{24,16},{1,9},{9,1},{17,25},{25,17},{2,10},{10... | collective-permute-start | bytes 884744 | tf_op jit(solution)/shard_map/ppermute | solution.py:65
  88.9 1.1 shard_map.329
  90.0 3.6 %shard_map.330 = (f32[128,768]{1,0:T(8,128)S(1)}, bf16[128,768]{1,0:T(8,128)(2,1)S(1)}, bf16[128,768]{1,0:T(8,128)(2,1)S(1)}, bf16[128,768]{1,0:T(8,128)(2,1)S(1...) custom-call(s32[4]{0:T(128)S(1)} %pad_add_fusion.ids, ...), custom_call_target="tpu_custom_call" | custom-call | flops 40000000 | bytes 300000 | tf_op jit(solution)/shard_map/pallas_call | solution.py:37
  93.6 2.0 %collective-permute-done.35.came2 = bf16[192,768]{1,0:T(8,128)(2,1)S(1)} collective-permute-done((bf16[192,768]{1,0:T(8,128)(2,1)S(1)}, bf16[192,768]{1,0:T(8,128)(2,1)S(1)}, u32[]{:S(2)}, u32[]{:S(2)}) %collective-permute-start.35) | collective-permute-done | bytes 294944 | tf_op jit(solution)/shard_map/ppermute | solution.py:65
  95.6 1.4 shard_map.337
  97.0 1.0 collective-permute-start.24
  98.0 1.8 %collective-permute-start.25 = (bf16[128,768]{1,0:T(8,128)(2,1)S(1)}, bf16[128,768]{1,0:T(8,128)(2,1)S(1)}, u32[]{:S(2)}, u32[]{:S(2)}) collective-permute-start(bf16[128,768]{1,0:T(8,128)(2,1)S(1)} %get-tuple-element.181), channel_id=1, source_target_pairs={{0,2},{1,3},{2,0},{3,1},{4,6},{5,7},{6,4},{7,5},{8,10},{9,11},{10,... | collective-permute-start | bytes 589832 | tf_op jit(solution)/shard_map/ppermute | solution.py:65
  99.8 1.7 %collective-permute-start.26 = (bf16[128,768]{1,0:T(8,128)(2,1)S(1)}, bf16[128,768]{1,0:T(8,128)(2,1)S(1)}, u32[]{:S(2)}, u32[]{:S(2)}) collective-permute-start(bf16[128,768]{1,0:T(8,128)(2,1)S(1)} %get-tuple-element.182), channel_id=1, source_target_pairs={{0,3},{1,2},{2,1},{3,0},{4,7},{5,6},{6,5},{7,4},{8,11},{9,10},{10,... | collective-permute-start | bytes 589832 | tf_op jit(solution)/shard_map/ppermute | solution.py:65
  101.5 2.2 %shard_map.338.rel = f32[32,128]{1,0:T(8,128)S(1)} custom-call(s32[4]{0:T(128)S(1)} %pad_add_fusion.ids, f32[3,512,256]{2,1,0:T(8,128)S(1)} %get-tuple-element.217.scores_ref), custom_call_target="tpu_custom_call" | custom-call | flops 40000000 | bytes 300000 | tf_op jit(solution)/shard_map/pallas_call | solution.py:37
  103.6 1.0 shard_map.339
  104.6 1.3 collective-permute-start.37
  105.9 1.6 %collective-permute-done.24.t1.r1 = bf16[128,768]{1,0:T(8,128)(2,1)S(1)} collective-permute-done((bf16[128,768]{1,0:T(8,128)(2,1)S(1)}, bf16[128,768]{1,0:T(8,128)(2,1)S(1)}, u32[]{:S(2)}, u32[]{:S(2)}) %collective-permute-start.24) | collective-permute-done | bytes 196640 | tf_op jit(solution)/shard_map/ppermute | solution.py:65
  107.5 7.6 %collective-permute-done.25.t2.r2 = bf16[128,768]{1,0:T(8,128)(2,1)S(1)} collective-permute-done((bf16[128,768]{1,0:T(8,128)(2,1)S(1)}, bf16[128,768]{1,0:T(8,128)(2,1)S(1)}, u32[]{:S(2)}, u32[]{:S(2)}) %collective-permute-start.25) | collective-permute-done | bytes 196640 | tf_op jit(solution)/shard_map/ppermute | solution.py:65
  115.7 3.1 %collective-permute-start.29 = (bf16[96,768]{1,0:T(8,128)(2,1)S(1)}, bf16[96,768]{1,0:T(8,128)(2,1)S(1)}, u32[]{:S(2)}, u32[]{:S(2)}) collective-permute-start(bf16[96,768]{1,0:T(8,128)(2,1)S(1)} %get-tuple-element.192), channel_id=1, source_target_pairs={{0,24},{8,16},{16,8},{24,0},{1,25},{9,17},{17,9},{25,1},{2,26},{10... | collective-permute-start | bytes 442376 | tf_op jit(solution)/shard_map/ppermute | solution.py:65
  119.6 2.4 %collective-permute-done.27.q1 = bf16[96,768]{1,0:T(8,128)(2,1)S(1)} collective-permute-done((bf16[96,768]{1,0:T(8,128)(2,1)S(1)}, bf16[96,768]{1,0:T(8,128)(2,1)S(1)}, u32[]{:S(2)}, u32[]{:S(2)}) %collective-permute-start.27) | collective-permute-done | bytes 147488 | tf_op jit(solution)/shard_map/ppermute | solution.py:65
  122.0 2.8 %collective-permute-done.28.q2 = bf16[96,768]{1,0:T(8,128)(2,1)S(1)} collective-permute-done((bf16[96,768]{1,0:T(8,128)(2,1)S(1)}, bf16[96,768]{1,0:T(8,128)(2,1)S(1)}, u32[]{:S(2)}, u32[]{:S(2)}) %collective-permute-start.28) | collective-permute-done | bytes 147488 | tf_op jit(solution)/shard_map/ppermute | solution.py:65
  124.8 1.7 %collective-permute-start.32 = (bf16[128,768]{1,0:T(8,128)(2,1)S(1)}, bf16[128,768]{1,0:T(8,128)(2,1)S(1)}, u32[]{:S(2)}, u32[]{:S(2)}) collective-permute-start(bf16[128,768]{1,0:T(8,128)(2,1)S(1)} %shard_map.334.t0), channel_id=1, source_target_pairs={{0,3},{1,2},{2,1},{3,0},{4,7},{5,6},{6,5},{7,4},{8,11},{9,10},{10,... | collective-permute-start | bytes 589832 | tf_op jit(solution)/shard_map/ppermute | solution.py:65
  126.5 4.4 %collective-permute-start.31 = (bf16[128,768]{1,0:T(8,128)(2,1)S(1)}, bf16[128,768]{1,0:T(8,128)(2,1)S(1)}, u32[]{:S(2)}, u32[]{:S(2)}) collective-permute-start(bf16[128,768]{1,0:T(8,128)(2,1)S(1)} %shard_map.334.t0), channel_id=1, source_target_pairs={{0,2},{1,3},{2,0},{3,1},{4,6},{5,7},{6,4},{7,5},{8,10},{9,11},{10,... | collective-permute-start | bytes 589832 | tf_op jit(solution)/shard_map/ppermute | solution.py:65
  131.8 1.5 collective-permute-start.41
  133.3 0.9 collective-permute-start.42
  134.2 1.3 shard_map.333
  135.5 1.0 collective-permute-done.41.came1
  136.5 1.4 collective-permute-done.42.came2
  137.9 0.7 collective-permute-start.43
  138.6 0.7 collective-permute-start.44
  139.3 3.5 %collective-permute-done.31.t2 = bf16[128,768]{1,0:T(8,128)(2,1)S(1)} collective-permute-done((bf16[128,768]{1,0:T(8,128)(2,1)S(1)}, bf16[128,768]{1,0:T(8,128)(2,1)S(1)}, u32[]{:S(2)}, u32[]{:S(2)}) %collective-permute-start.31) | collective-permute-done | bytes 196640 | tf_op jit(solution)/shard_map/ppermute | solution.py:65
  142.8 2.6 %collective-permute-done.43.came1 = bf16[224,768]{1,0:T(8,128)(2,1)S(1)} collective-permute-done((bf16[224,768]{1,0:T(8,128)(2,1)S(1)}, bf16[224,768]{1,0:T(8,128)(2,1)S(1)}, u32[]{:S(2)}, u32[]{:S(2)}) %collective-permute-start.43) | collective-permute-done | bytes 344096 | tf_op jit(solution)/shard_map/ppermute | solution.py:65
  145.9 0.7 shard_map.344
  147.1 2.6 %shard_map.345 = (f32[4,128,768]{2,1,0:T(8,128)}, f32[768,768]{1,0:T(8,128)}, f32[768,768]{1,0:T(8,128)}) custom-call(s32[4]{0:T(128)S(1)} %pad_add_fusion.ids, bf16[128,768]{1,0:T(8,128)(2,1)S(1)} %shard_map.334.t0, bf16[128,768]{1,0:T(8,128)(2,1)S(1)} %collective-permute-done.30.t1, bf16[128,768]{1,0:T(8,128)(2,1)S(1)} %collective-permute-done.31.t2, ...), custom_call_target="tpu_custom_call" | custom-call | flops 40000000 | bytes 300000 | tf_op jit(solution)/shard_map/pallas_call | solution.py:37
  149.7 0.9 collective-permute-done.45.other
  150.6 3.4 %shard_map.346 = (f32[768,768]{1,0:T(8,128)}, f32[768,768]{1,0:T(8,128)}, f32[768]{0:T(1024)}, f32[768]{0:T(1024)}, f32[768]{0:T(1024)}, /*index=5*/f32[768]{0:T...) custom-call(s32[4]{0:T(128)S(1)} %pad_add_fusion.ids, ...), custom_call_target="tpu_custom_call", output_to_operand_aliasing={{0}: (4, {}), {1}: (5, {})} | custom-call | flops 40000000 | bytes 300000 | tf_op jit(solution)/shard_map/pallas_call | solution.py:37
  (104 shorter events, 7.3 us)
Async XLA Ops:
  0.7 6.5 %copy-start.8 = (f32[768]{0:T(1024)S(1)}, f32[768]{0:T(1024)}, u32[]{:S(2)}) copy-start(f32[768]{0:T(1024)} %param.28) | copy-start | bytes 9220
  0.7 6.5 %copy-start.15 = (f32[192]{0:T(256)S(1)}, f32[192]{0:T(256)}, u32[]{:S(2)}) copy-start(f32[192]{0:T(256)} %param.22) | copy-start | bytes 2308
  0.7 6.7 %copy-start.16 = (f32[192]{0:T(256)S(1)}, f32[192]{0:T(256)}, u32[]{:S(2)}) copy-start(f32[192]{0:T(256)} %param.25) | copy-start | bytes 2308
  0.7 7.5 %copy-start.6 = (f32[3,8]{1,0:T(4,128)S(1)}, f32[3,8]{1,0:T(4,128)}, u32[]{:S(2)}) copy-start(f32[3,8]{1,0:T(4,128)} %rel.1) | copy-start | bytes 292
  2.0 9.7 %collective-permute-start.2 = (bf16[128,768]{1,0:T(8,128)(2,1)S(1)}, bf16[128,768]{1,0:T(8,128)(2,1)S(1)}, u32[]{:S(2)}, u32[]{:S(2)}) collective-permute-start(bf16[128,768]{1,0:T(8,128)(2,1)S(1)} %get-tuple-element.254), channel_id=1, source_target_pairs={{0,24},{8,16},{16,8},{24,0},{1,25},{9,17},{17,9},{25,1},{2,26},{10... | collective-permute-start | bytes 589832 | tf_op jit(solution)/shard_map/ppermute | solution.py:65
  6.0 9.4 %collective-permute-start = (bf16[128,768]{1,0:T(8,128)(2,1)S(1)}, bf16[128,768]{1,0:T(8,128)(2,1)S(1)}, u32[]{:S(2)}, u32[]{:S(2)}) collective-permute-start(bf16[128,768]{1,0:T(8,128)(2,1)S(1)} %get-tuple-element.255), channel_id=1, source_target_pairs={{0,8},{8,0},{16,24},{24,16},{1,9},{9,1},{17,25},{25,17},{2,10},{10... | collective-permute-start | bytes 589832 | tf_op jit(solution)/shard_map/ppermute | solution.py:65
  6.5 8.9 %collective-permute-start.1 = (bf16[128,768]{1,0:T(8,128)(2,1)S(1)}, bf16[128,768]{1,0:T(8,128)(2,1)S(1)}, u32[]{:S(2)}, u32[]{:S(2)}) collective-permute-start(bf16[128,768]{1,0:T(8,128)(2,1)S(1)} %get-tuple-element.257), channel_id=1, source_target_pairs={{0,16},{8,24},{16,0},{24,8},{1,17},{9,25},{17,1},{25,9},{2,18},{10... | collective-permute-start | bytes 589832 | tf_op jit(solution)/shard_map/ppermute | solution.py:65
  8.2 7.2 %copy-start = (bf16[768,192]{0,1:T(8,128)(2,1)S(1)}, bf16[768,192]{0,1:T(8,128)(2,1)}, u32[]{:S(2)}) copy-start(bf16[768,192]{0,1:T(8,128)(2,1)} %param.21) | copy-start | bytes 884740
  8.2 7.2 %copy-start.1 = (bf16[768,192]{0,1:T(8,128)(2,1)S(1)}, bf16[768,192]{0,1:T(8,128)(2,1)}, u32[]{:S(2)}) copy-start(bf16[768,192]{0,1:T(8,128)(2,1)} %param.23) | copy-start | bytes 884740
  8.2 7.2 %copy-start.2 = (bf16[768,192]{0,1:T(8,128)(2,1)S(1)}, bf16[768,192]{0,1:T(8,128)(2,1)}, u32[]{:S(2)}) copy-start(bf16[768,192]{0,1:T(8,128)(2,1)} %param.24) | copy-start | bytes 884740
  8.2 7.2 %copy-start.3 = (bf16[192,768]{1,0:T(8,128)(2,1)S(1)}, bf16[192,768]{1,0:T(8,128)(2,1)}, u32[]{:S(2)}) copy-start(bf16[192,768]{1,0:T(8,128)(2,1)} %refs_5_.1) | copy-start | bytes 884740
  15.4 10.9 %copy-start.9 = (f32[768]{0:T(1024)S(1)}, f32[768]{0:T(1024)}, u32[]{:S(2)}) copy-start(f32[768]{0:T(1024)} %param.29) | copy-start | bytes 9220
  15.4 10.9 %copy-start.10 = (f32[768]{0:T(1024)S(1)}, f32[768]{0:T(1024)}, u32[]{:S(2)}) copy-start(f32[768]{0:T(1024)} %param.30) | copy-start | bytes 9220
  15.4 10.9 %copy-start.11 = (f32[768]{0:T(1024)S(1)}, f32[768]{0:T(1024)}, u32[]{:S(2)}) copy-start(f32[768]{0:T(1024)} %param.32) | copy-start | bytes 9220
  15.4 10.9 %copy-start.12 = (f32[768]{0:T(1024)S(1)}, f32[768]{0:T(1024)}, u32[]{:S(2)}) copy-start(f32[768]{0:T(1024)} %param.34) | copy-start | bytes 9220
  15.5 23.1 %copy-start.7 = (bf16[4,64,768]{2,1,0:T(8,128)(2,1)S(1)}, bf16[4,64,768]{2,1,0:T(8,128)(2,1)}, u32[]{:S(2)}) copy-start(bf16[4,64,768]{2,1,0:T(8,128)(2,1)} %param.37) | copy-start | bytes 1179652
  15.5 29.5 %copy-start.4 = (bf16[768,768]{1,0:T(8,128)(2,1)S(1)}, bf16[768,768]{1,0:T(8,128)(2,1)}, u32[]{:S(2)}) copy-start(bf16[768,768]{1,0:T(8,128)(2,1)} %refs_12_.1) | copy-start | bytes 3538948
  15.5 29.4 %copy-start.5 = (bf16[768,768]{1,0:T(8,128)(2,1)S(1)}, bf16[768,768]{1,0:T(8,128)(2,1)}, u32[]{:S(2)}) copy-start(bf16[768,768]{1,0:T(8,128)(2,1)} %refs_11_.1) | copy-start | bytes 3538948
  21.9 4.7 %collective-permute-start.3 = (bf16[64,768]{1,0:T(8,128)(2,1)S(1)}, bf16[64,768]{1,0:T(8,128)(2,1)S(1)}, u32[]{:S(2)}, u32[]{:S(2)}) collective-permute-start(bf16[64,768]{1,0:T(8,128)(2,1)S(1)} %get-tuple-element.136), channel_id=1, source_target_pairs={{0,1},{1,0},{2,3},{3,2},{4,5},{5,4},{6,7},{7,6},{8,9},{9,8},{10,11... | collective-permute-start | bytes 294920 | tf_op jit(solution)/shard_map/ppermute | solution.py:65
  23.5 10.5 %collective-permute-start.4 = (bf16[64,768]{1,0:T(8,128)(2,1)S(1)}, bf16[64,768]{1,0:T(8,128)(2,1)S(1)}, u32[]{:S(2)}, u32[]{:S(2)}) collective-permute-start(bf16[64,768]{1,0:T(8,128)(2,1)S(1)} %get-tuple-element.137), channel_id=1, source_target_pairs={{0,2},{1,3},{2,0},{3,1},{4,6},{5,7},{6,4},{7,5},{8,10},{9,11},{10,... | collective-permute-start | bytes 294920 | tf_op jit(solution)/shard_map/ppermute | solution.py:65
  26.1 7.9 %collective-permute-start.5 = (bf16[64,768]{1,0:T(8,128)(2,1)S(1)}, bf16[64,768]{1,0:T(8,128)(2,1)S(1)}, u32[]{:S(2)}, u32[]{:S(2)}) collective-permute-start(bf16[64,768]{1,0:T(8,128)(2,1)S(1)} %get-tuple-element.138), channel_id=1, source_target_pairs={{0,3},{1,2},{2,1},{3,0},{4,7},{5,6},{6,5},{7,4},{8,11},{9,10},{10,... | collective-permute-start | bytes 294920 | tf_op jit(solution)/shard_map/ppermute | solution.py:65
  34.1 7.6 %collective-permute-start.8 = (bf16[64,768]{1,0:T(8,128)(2,1)S(1)}, bf16[64,768]{1,0:T(8,128)(2,1)S(1)}, u32[]{:S(2)}, u32[]{:S(2)}) collective-permute-start(bf16[64,768]{1,0:T(8,128)(2,1)S(1)} %shard_map.324.a0), channel_id=1, source_target_pairs={{0,3},{1,2},{2,1},{3,0},{4,7},{5,6},{6,5},{7,4},{8,11},{9,10},{10,... | collective-permute-start | bytes 294920 | tf_op jit(solution)/shard_map/ppermute | solution.py:65
  36.6 8.3 %collective-permute-start.7 = (bf16[64,768]{1,0:T(8,128)(2,1)S(1)}, bf16[64,768]{1,0:T(8,128)(2,1)S(1)}, u32[]{:S(2)}, u32[]{:S(2)}) collective-permute-start(bf16[64,768]{1,0:T(8,128)(2,1)S(1)} %shard_map.324.a0), channel_id=1, source_target_pairs={{0,2},{1,3},{2,0},{3,1},{4,6},{5,7},{6,4},{7,5},{8,10},{9,11},{10,... | collective-permute-start | bytes 294920 | tf_op jit(solution)/shard_map/ppermute | solution.py:65
  37.9 7.1 %collective-permute-start.6 = (bf16[64,768]{1,0:T(8,128)(2,1)S(1)}, bf16[64,768]{1,0:T(8,128)(2,1)S(1)}, u32[]{:S(2)}, u32[]{:S(2)}) collective-permute-start(bf16[64,768]{1,0:T(8,128)(2,1)S(1)} %shard_map.324.a0), channel_id=1, source_target_pairs={{0,1},{1,0},{2,3},{3,2},{4,5},{5,4},{6,7},{7,6},{8,9},{9,8},{10,11... | collective-permute-start | bytes 294920 | tf_op jit(solution)/shard_map/ppermute | solution.py:65
  38.5 8.4 %collective-permute-start.11 = (bf16[64,768]{1,0:T(8,128)(2,1)S(1)}, bf16[64,768]{1,0:T(8,128)(2,1)S(1)}, u32[]{:S(2)}, u32[]{:S(2)}) collective-permute-start(bf16[64,768]{1,0:T(8,128)(2,1)S(1)} %get-tuple-element.258), channel_id=1, source_target_pairs={{0,24},{8,16},{16,8},{24,0},{1,25},{9,17},{17,9},{25,1},{2,26},{10... | collective-permute-start | bytes 294920 | tf_op jit(solution)/shard_map/ppermute | solution.py:65
  41.1 5.9 %collective-permute-start.10 = (bf16[64,768]{1,0:T(8,128)(2,1)S(1)}, bf16[64,768]{1,0:T(8,128)(2,1)S(1)}, u32[]{:S(2)}, u32[]{:S(2)}) collective-permute-start(bf16[64,768]{1,0:T(8,128)(2,1)S(1)} %get-tuple-element.259), channel_id=1, source_target_pairs={{0,16},{8,24},{16,0},{24,8},{1,17},{9,25},{17,1},{25,9},{2,18},{10... | collective-permute-start | bytes 294920 | tf_op jit(solution)/shard_map/ppermute | solution.py:65
  41.7 19.7 %copy-start.13 = (f32[768]{0:T(1024)S(1)}, f32[768]{0:T(1024)}, u32[]{:S(2)}) copy-start(f32[768]{0:T(1024)} %param.35) | copy-start | bytes 9220
  41.7 19.7 %copy-start.14 = (f32[768]{0:T(1024)S(1)}, f32[768]{0:T(1024)}, u32[]{:S(2)}) copy-start(f32[768]{0:T(1024)} %param.36) | copy-start | bytes 9220
  41.7 5.3 %collective-permute-start.9 = (bf16[64,768]{1,0:T(8,128)(2,1)S(1)}, bf16[64,768]{1,0:T(8,128)(2,1)S(1)}, u32[]{:S(2)}, u32[]{:S(2)}) collective-permute-start(bf16[64,768]{1,0:T(8,128)(2,1)S(1)} %get-tuple-element.260), channel_id=1, source_target_pairs={{0,8},{8,0},{16,24},{24,16},{1,9},{9,1},{17,25},{25,17},{2,10},{10... | collective-permute-start | bytes 294920 | tf_op jit(solution)/shard_map/ppermute | solution.py:65
  46.9 5.0 %collective-permute-start.12 = (bf16[64,768]{1,0:T(8,128)(2,1)S(1)}, bf16[64,768]{1,0:T(8,128)(2,1)S(1)}, u32[]{:S(2)}, u32[]{:S(2)}) collective-permute-start(bf16[64,768]{1,0:T(8,128)(2,1)S(1)} %get-tuple-element.150), channel_id=1, source_target_pairs={{0,1},{1,0},{2,3},{3,2},{4,5},{5,4},{6,7},{7,6},{8,9},{9,8},{10,11... | collective-permute-start | bytes 294920 | tf_op jit(solution)/shard_map/ppermute | solution.py:65
  49.1 7.8 %collective-permute-start.13 = (bf16[64,768]{1,0:T(8,128)(2,1)S(1)}, bf16[64,768]{1,0:T(8,128)(2,1)S(1)}, u32[]{:S(2)}, u32[]{:S(2)}) collective-permute-start(bf16[64,768]{1,0:T(8,128)(2,1)S(1)} %get-tuple-element.151), channel_id=1, source_target_pairs={{0,2},{1,3},{2,0},{3,1},{4,6},{5,7},{6,4},{7,5},{8,10},{9,11},{10,... | collective-permute-start | bytes 294920 | tf_op jit(solution)/shard_map/ppermute | solution.py:65
  49.3 7.6 %collective-permute-start.14 = (bf16[64,768]{1,0:T(8,128)(2,1)S(1)}, bf16[64,768]{1,0:T(8,128)(2,1)S(1)}, u32[]{:S(2)}, u32[]{:S(2)}) collective-permute-start(bf16[64,768]{1,0:T(8,128)(2,1)S(1)} %get-tuple-element.152), channel_id=1, source_target_pairs={{0,3},{1,2},{2,1},{3,0},{4,7},{5,6},{6,5},{7,4},{8,11},{9,10},{10,... | collective-permute-start | bytes 294920 | tf_op jit(solution)/shard_map/ppermute | solution.py:65
  56.9 6.6 %collective-permute-start.17 = (bf16[64,768]{1,0:T(8,128)(2,1)S(1)}, bf16[64,768]{1,0:T(8,128)(2,1)S(1)}, u32[]{:S(2)}, u32[]{:S(2)}) collective-permute-start(bf16[64,768]{1,0:T(8,128)(2,1)S(1)} %shard_map.326.refs_0_), channel_id=1, source_target_pairs={{0,3},{1,2},{2,1},{3,0},{4,7},{5,6},{6,5},{7,4},{8,11},{9,10},{10,... | collective-permute-start | bytes 294920 | tf_op jit(solution)/shard_map/ppermute | solution.py:65
  58.7 8.0 %collective-permute-start.16 = (bf16[64,768]{1,0:T(8,128)(2,1)S(1)}, bf16[64,768]{1,0:T(8,128)(2,1)S(1)}, u32[]{:S(2)}, u32[]{:S(2)}) collective-permute-start(bf16[64,768]{1,0:T(8,128)(2,1)S(1)} %shard_map.326.refs_0_), channel_id=1, source_target_pairs={{0,2},{1,3},{2,0},{3,1},{4,6},{5,7},{6,4},{7,5},{8,10},{9,11},{10,... | collective-permute-start | bytes 294920 | tf_op jit(solution)/shard_map/ppermute | solution.py:65
  61.1 5.7 %collective-permute-start.15 = (bf16[64,768]{1,0:T(8,128)(2,1)S(1)}, bf16[64,768]{1,0:T(8,128)(2,1)S(1)}, u32[]{:S(2)}, u32[]{:S(2)}) collective-permute-start(bf16[64,768]{1,0:T(8,128)(2,1)S(1)} %shard_map.326.refs_0_), channel_id=1, source_target_pairs={{0,1},{1,0},{2,3},{3,2},{4,5},{5,4},{6,7},{7,6},{8,9},{9,8},{10,11... | collective-permute-start | bytes 294920 | tf_op jit(solution)/shard_map/ppermute | solution.py:65
  69.1 5.7 %collective-permute-start.18 = (bf16[64,768]{1,0:T(8,128)(2,1)S(1)}, bf16[64,768]{1,0:T(8,128)(2,1)S(1)}, u32[]{:S(2)}, u32[]{:S(2)}) collective-permute-start(bf16[64,768]{1,0:T(8,128)(2,1)S(1)} %get-tuple-element.162), channel_id=1, source_target_pairs={{0,1},{1,0},{2,3},{3,2},{4,5},{5,4},{6,7},{7,6},{8,9},{9,8},{10,11... | collective-permute-start | bytes 294920 | tf_op jit(solution)/shard_map/ppermute | solution.py:65
  69.2 5.6 %collective-permute-start.19 = (bf16[64,768]{1,0:T(8,128)(2,1)S(1)}, bf16[64,768]{1,0:T(8,128)(2,1)S(1)}, u32[]{:S(2)}, u32[]{:S(2)}) collective-permute-start(bf16[64,768]{1,0:T(8,128)(2,1)S(1)} %get-tuple-element.163), channel_id=1, source_target_pairs={{0,2},{1,3},{2,0},{3,1},{4,6},{5,7},{6,4},{7,5},{8,10},{9,11},{10,... | collective-permute-start | bytes 294920 | tf_op jit(solution)/shard_map/ppermute | solution.py:65
  71.0 6.5 %collective-permute-start.20 = (bf16[64,768]{1,0:T(8,128)(2,1)S(1)}, bf16[64,768]{1,0:T(8,128)(2,1)S(1)}, u32[]{:S(2)}, u32[]{:S(2)}) collective-permute-start(bf16[64,768]{1,0:T(8,128)(2,1)S(1)} %get-tuple-element.164), channel_id=1, source_target_pairs={{0,3},{1,2},{2,1},{3,0},{4,7},{5,6},{6,5},{7,4},{8,11},{9,10},{10,... | collective-permute-start | bytes 294920 | tf_op jit(solution)/shard_map/ppermute | solution.py:65
  74.7 7.3 %collective-permute-start.33 = (bf16[768,768]{1,0:T(8,128)(2,1)S(1)}, bf16[768,768]{1,0:T(8,128)(2,1)S(1)}, u32[]{:S(2)}, u32[]{:S(2)}) collective-permute-start(bf16[768,768]{1,0:T(8,128)(2,1)S(1)} %shard_map.335), channel_id=1, source_target_pairs={{0,4},{4,0},{1,5},{5,1},{2,6},{6,2},{3,7},{7,3},{8,12},{12,8},{9,1... | collective-permute-start | bytes 3538952 | tf_op jit(solution)/shard_map/ppermute | solution.py:65
  77.5 11.3 %collective-permute-start.23 = (bf16[64,768]{1,0:T(8,128)(2,1)S(1)}, bf16[64,768]{1,0:T(8,128)(2,1)S(1)}, u32[]{:S(2)}, u32[]{:S(2)}) collective-permute-start(bf16[64,768]{1,0:T(8,128)(2,1)S(1)} %shard_map.328.refs_0_), channel_id=1, source_target_pairs={{0,3},{1,2},{2,1},{3,0},{4,7},{5,6},{6,5},{7,4},{8,11},{9,10},{10,... | collective-permute-start | bytes 294920 | tf_op jit(solution)/shard_map/ppermute | solution.py:65
  80.2 8.7 %collective-permute-start.22 = (bf16[64,768]{1,0:T(8,128)(2,1)S(1)}, bf16[64,768]{1,0:T(8,128)(2,1)S(1)}, u32[]{:S(2)}, u32[]{:S(2)}) collective-permute-start(bf16[64,768]{1,0:T(8,128)(2,1)S(1)} %shard_map.328.refs_0_), channel_id=1, source_target_pairs={{0,2},{1,3},{2,0},{3,1},{4,6},{5,7},{6,4},{7,5},{8,10},{9,11},{10,... | collective-permute-start | bytes 294920 | tf_op jit(solution)/shard_map/ppermute | solution.py:65
  80.5 8.4 %collective-permute-start.21 = (bf16[64,768]{1,0:T(8,128)(2,1)S(1)}, bf16[64,768]{1,0:T(8,128)(2,1)S(1)}, u32[]{:S(2)}, u32[]{:S(2)}) collective-permute-start(bf16[64,768]{1,0:T(8,128)(2,1)S(1)} %shard_map.328.refs_0_), channel_id=1, source_target_pairs={{0,1},{1,0},{2,3},{3,2},{4,5},{5,4},{6,7},{7,6},{8,9},{9,8},{10,11... | collective-permute-start | bytes 294920 | tf_op jit(solution)/shard_map/ppermute | solution.py:65
  83.4 10.2 %collective-permute-start.34 = (bf16[192,768]{1,0:T(8,128)(2,1)S(1)}, bf16[192,768]{1,0:T(8,128)(2,1)S(1)}, u32[]{:S(2)}, u32[]{:S(2)}) collective-permute-start(bf16[192,768]{1,0:T(8,128)(2,1)S(1)} %get-tuple-element.206), channel_id=1, source_target_pairs={{0,8},{8,0},{16,24},{24,16},{1,9},{9,1},{17,25},{25,17},{2,10},{10... | collective-permute-start | bytes 884744 | tf_op jit(solution)/shard_map/ppermute | solution.py:65
  88.9 6.7 %collective-permute-start.35 = (bf16[192,768]{1,0:T(8,128)(2,1)S(1)}, bf16[192,768]{1,0:T(8,128)(2,1)S(1)}, u32[]{:S(2)}, u32[]{:S(2)}) collective-permute-start(bf16[192,768]{1,0:T(8,128)(2,1)S(1)} %get-tuple-element.207), channel_id=1, source_target_pairs={{0,16},{8,24},{16,0},{24,8},{1,17},{9,25},{17,1},{25,9},{2,18},{10... | collective-permute-start | bytes 884744 | tf_op jit(solution)/shard_map/ppermute | solution.py:65
  96.9 6.7 %collective-permute-start.36 = (bf16[512,768]{1,0:T(8,128)(2,1)S(1)}, bf16[512,768]{1,0:T(8,128)(2,1)S(1)}, u32[]{:S(2)}, u32[]{:S(2)}) collective-permute-start(bf16[512,768]{1,0:T(8,128)(2,1)S(1)} %get-tuple-element.216), channel_id=1, source_target_pairs={{0,4},{4,0},{1,5},{5,1},{2,6},{6,2},{3,7},{7,3},{8,12},{12,8},{9,1... | collective-permute-start | bytes 2359304 | tf_op jit(solution)/shard_map/ppermute | solution.py:65
  97.0 10.5 %collective-permute-start.24 = (bf16[128,768]{1,0:T(8,128)(2,1)S(1)}, bf16[128,768]{1,0:T(8,128)(2,1)S(1)}, u32[]{:S(2)}, u32[]{:S(2)}) collective-permute-start(bf16[128,768]{1,0:T(8,128)(2,1)S(1)} %get-tuple-element.180), channel_id=1, source_target_pairs={{0,1},{1,0},{2,3},{3,2},{4,5},{5,4},{6,7},{7,6},{8,9},{9,8},{10,11... | collective-permute-start | bytes 589832 | tf_op jit(solution)/shard_map/ppermute | solution.py:65
  98.0 17.1 %collective-permute-start.25 = (bf16[128,768]{1,0:T(8,128)(2,1)S(1)}, bf16[128,768]{1,0:T(8,128)(2,1)S(1)}, u32[]{:S(2)}, u32[]{:S(2)}) collective-permute-start(bf16[128,768]{1,0:T(8,128)(2,1)S(1)} %get-tuple-element.181), channel_id=1, source_target_pairs={{0,2},{1,3},{2,0},{3,1},{4,6},{5,7},{6,4},{7,5},{8,10},{9,11},{10,... | collective-permute-start | bytes 589832 | tf_op jit(solution)/shard_map/ppermute | solution.py:65
  99.8 15.3 %collective-permute-start.26 = (bf16[128,768]{1,0:T(8,128)(2,1)S(1)}, bf16[128,768]{1,0:T(8,128)(2,1)S(1)}, u32[]{:S(2)}, u32[]{:S(2)}) collective-permute-start(bf16[128,768]{1,0:T(8,128)(2,1)S(1)} %get-tuple-element.182), channel_id=1, source_target_pairs={{0,3},{1,2},{2,1},{3,0},{4,7},{5,6},{6,5},{7,4},{8,11},{9,10},{10,... | collective-permute-start | bytes 589832 | tf_op jit(solution)/shard_map/ppermute | solution.py:65
  104.6 14.2 %collective-permute-start.37 = (bf16[224,768]{1,0:T(8,128)(2,1)S(1)}, bf16[224,768]{1,0:T(8,128)(2,1)S(1)}, u32[]{:S(2)}, u32[]{:S(2)}) collective-permute-start(bf16[224,768]{1,0:T(8,128)(2,1)S(1)} %get-tuple-element.222), channel_id=1, source_target_pairs={{0,8},{8,0},{16,24},{24,16},{1,9},{9,1},{17,25},{25,17},{2,10},{10... | collective-permute-start | bytes 1032200 | tf_op jit(solution)/shard_map/ppermute | solution.py:65
  105.9 12.9 %collective-permute-start.38 = (bf16[224,768]{1,0:T(8,128)(2,1)S(1)}, bf16[224,768]{1,0:T(8,128)(2,1)S(1)}, u32[]{:S(2)}, u32[]{:S(2)}) collective-permute-start(bf16[224,768]{1,0:T(8,128)(2,1)S(1)} %get-tuple-element.223), channel_id=1, source_target_pairs={{0,16},{8,24},{16,0},{24,8},{1,17},{9,25},{17,1},{25,9},{2,18},{10... | collective-permute-start | bytes 1032200 | tf_op jit(solution)/shard_map/ppermute | solution.py:65
  115.2 6.7 %collective-permute-start.27 = (bf16[96,768]{1,0:T(8,128)(2,1)S(1)}, bf16[96,768]{1,0:T(8,128)(2,1)S(1)}, u32[]{:S(2)}, u32[]{:S(2)}) collective-permute-start(bf16[96,768]{1,0:T(8,128)(2,1)S(1)} %get-tuple-element.190), channel_id=1, source_target_pairs={{0,8},{8,0},{16,24},{24,16},{1,9},{9,1},{17,25},{25,17},{2,10},{10... | collective-permute-start | bytes 442376 | tf_op jit(solution)/shard_map/ppermute | solution.py:65
  115.7 9.1 %collective-permute-start.28 = (bf16[96,768]{1,0:T(8,128)(2,1)S(1)}, bf16[96,768]{1,0:T(8,128)(2,1)S(1)}, u32[]{:S(2)}, u32[]{:S(2)}) collective-permute-start(bf16[96,768]{1,0:T(8,128)(2,1)S(1)} %get-tuple-element.191), channel_id=1, source_target_pairs={{0,16},{8,24},{16,0},{24,8},{1,17},{9,25},{17,1},{25,9},{2,18},{10... | collective-permute-start | bytes 442376 | tf_op jit(solution)/shard_map/ppermute | solution.py:65
  115.7 9.1 %collective-permute-start.29 = (bf16[96,768]{1,0:T(8,128)(2,1)S(1)}, bf16[96,768]{1,0:T(8,128)(2,1)S(1)}, u32[]{:S(2)}, u32[]{:S(2)}) collective-permute-start(bf16[96,768]{1,0:T(8,128)(2,1)S(1)} %get-tuple-element.192), channel_id=1, source_target_pairs={{0,24},{8,16},{16,8},{24,0},{1,25},{9,17},{17,9},{25,1},{2,26},{10... | collective-permute-start | bytes 442376 | tf_op jit(solution)/shard_map/ppermute | solution.py:65
  119.0 12.4 %collective-permute-start.39 = (bf16[256,768]{1,0:T(8,128)(2,1)S(1)}, bf16[256,768]{1,0:T(8,128)(2,1)S(1)}, u32[]{:S(2)}, u32[]{:S(2)}) collective-permute-start(bf16[256,768]{1,0:T(8,128)(2,1)S(1)} %get-tuple-element.226.sent1), channel_id=1, source_target_pairs={{0,8},{8,0},{16,24},{24,16},{1,9},{9,1},{17,25},{25,17},{2,10},{10... | collective-permute-start | bytes 1179656 | tf_op jit(solution)/shard_map/ppermute | solution.py:65
  119.4 12.3 %collective-permute-start.40 = (bf16[256,768]{1,0:T(8,128)(2,1)S(1)}, bf16[256,768]{1,0:T(8,128)(2,1)S(1)}, u32[]{:S(2)}, u32[]{:S(2)}) collective-permute-start(bf16[256,768]{1,0:T(8,128)(2,1)S(1)} %get-tuple-element.227.sent2), channel_id=1, source_target_pairs={{0,16},{8,24},{16,0},{24,8},{1,17},{9,25},{17,1},{25,9},{2,18},{10... | collective-permute-start | bytes 1179656 | tf_op jit(solution)/shard_map/ppermute | solution.py:65
  124.8 14.5 %collective-permute-start.32 = (bf16[128,768]{1,0:T(8,128)(2,1)S(1)}, bf16[128,768]{1,0:T(8,128)(2,1)S(1)}, u32[]{:S(2)}, u32[]{:S(2)}) collective-permute-start(bf16[128,768]{1,0:T(8,128)(2,1)S(1)} %shard_map.334.t0), channel_id=1, source_target_pairs={{0,3},{1,2},{2,1},{3,0},{4,7},{5,6},{6,5},{7,4},{8,11},{9,10},{10,... | collective-permute-start | bytes 589832 | tf_op jit(solution)/shard_map/ppermute | solution.py:65
  126.5 16.3 %collective-permute-start.31 = (bf16[128,768]{1,0:T(8,128)(2,1)S(1)}, bf16[128,768]{1,0:T(8,128)(2,1)S(1)}, u32[]{:S(2)}, u32[]{:S(2)}) collective-permute-start(bf16[128,768]{1,0:T(8,128)(2,1)S(1)} %shard_map.334.t0), channel_id=1, source_target_pairs={{0,2},{1,3},{2,0},{3,1},{4,6},{5,7},{6,4},{7,5},{8,10},{9,11},{10,... | collective-permute-start | bytes 589832 | tf_op jit(solution)/shard_map/ppermute | solution.py:65
  130.9 11.9 %collective-permute-start.30 = (bf16[128,768]{1,0:T(8,128)(2,1)S(1)}, bf16[128,768]{1,0:T(8,128)(2,1)S(1)}, u32[]{:S(2)}, u32[]{:S(2)}) collective-permute-start(bf16[128,768]{1,0:T(8,128)(2,1)S(1)} %shard_map.334.t0), channel_id=1, source_target_pairs={{0,1},{1,0},{2,3},{3,2},{4,5},{5,4},{6,7},{7,6},{8,9},{9,8},{10,11... | collective-permute-start | bytes 589832 | tf_op jit(solution)/shard_map/ppermute | solution.py:65
  131.8 4.7 %collective-permute-start.41 = (bf16[64,768]{1,0:T(8,128)(2,1)S(1)}, bf16[64,768]{1,0:T(8,128)(2,1)S(1)}, u32[]{:S(2)}, u32[]{:S(2)}) collective-permute-start(bf16[64,768]{1,0:T(8,128)(2,1)S(1)} %get-tuple-element.229.mid1), channel_id=1, source_target_pairs={{0,8},{8,0},{16,24},{24,16},{1,9},{9,1},{17,25},{25,17},{2,10},{10... | collective-permute-start | bytes 294920 | tf_op jit(solution)/shard_map/ppermute | solution.py:65
  133.3 4.6 %collective-permute-start.42 = (bf16[64,768]{1,0:T(8,128)(2,1)S(1)}, bf16[64,768]{1,0:T(8,128)(2,1)S(1)}, u32[]{:S(2)}, u32[]{:S(2)}) collective-permute-start(bf16[64,768]{1,0:T(8,128)(2,1)S(1)} %get-tuple-element.230.mid2), channel_id=1, source_target_pairs={{0,16},{8,24},{16,0},{24,8},{1,17},{9,25},{17,1},{25,9},{2,18},{10... | collective-permute-start | bytes 294920 | tf_op jit(solution)/shard_map/ppermute | solution.py:65
  137.9 7.5 %collective-permute-start.43 = (bf16[224,768]{1,0:T(8,128)(2,1)S(1)}, bf16[224,768]{1,0:T(8,128)(2,1)S(1)}, u32[]{:S(2)}, u32[]{:S(2)}) collective-permute-start(bf16[224,768]{1,0:T(8,128)(2,1)S(1)} %get-tuple-element.231.along1), channel_id=1, source_target_pairs={{0,8},{8,0},{16,24},{24,16},{1,9},{9,1},{17,25},{25,17},{2,10},{10... | collective-permute-start | bytes 1032200 | tf_op jit(solution)/shard_map/ppermute | solution.py:65
  138.6 7.2 %collective-permute-start.44 = (bf16[224,768]{1,0:T(8,128)(2,1)S(1)}, bf16[224,768]{1,0:T(8,128)(2,1)S(1)}, u32[]{:S(2)}, u32[]{:S(2)}) collective-permute-start(bf16[224,768]{1,0:T(8,128)(2,1)S(1)} %get-tuple-element.232.along2), channel_id=1, source_target_pairs={{0,16},{8,24},{16,0},{24,8},{1,17},{9,25},{17,1},{25,9},{2,18},{10... | collective-permute-start | bytes 1032200 | tf_op jit(solution)/shard_map/ppermute | solution.py:65
  146.5 4.0 %collective-permute-start.46 = (bf16[768,768]{1,0:T(8,128)(2,1)S(1)}, bf16[768,768]{1,0:T(8,128)(2,1)S(1)}, u32[]{:S(2)}, u32[]{:S(2)}) collective-permute-start(bf16[768,768]{1,0:T(8,128)(2,1)S(1)} %get-tuple-element.233.mine), channel_id=1, source_target_pairs={{0,4},{4,0},{1,5},{5,1},{2,6},{6,2},{3,7},{7,3},{8,12},{12,8},{9,1... | collective-permute-start | bytes 3538952 | tf_op jit(solution)/shard_map/ppermute | solution.py:65
  146.6 4.0 %collective-permute-start.45 = (bf16[512,768]{1,0:T(8,128)(2,1)S(1)}, bf16[512,768]{1,0:T(8,128)(2,1)S(1)}, u32[]{:S(2)}, u32[]{:S(2)}) collective-permute-start(bf16[512,768]{1,0:T(8,128)(2,1)S(1)} %get-tuple-element.235.mine), channel_id=1, source_target_pairs={{0,4},{4,0},{1,5},{5,1},{2,6},{6,2},{3,7},{7,3},{8,12},{12,8},{9,1... | collective-permute-start | bytes 2359304 | tf_op jit(solution)/shard_map/ppermute | solution.py:65
  (1 other events, 6.0 us)

commit v4 on v3

--- a/solution.py
+++ b/solution.py
@@ -71,14 +71,18 @@
     return values
 
 
+def ordered(blocks, axis, size, order):
+    landed = [swap(blocks[k - 1], axis, size, k) for k in order]
+    landed = deep(landed) if axis == "mp" else landed
+    return [landed[order.index(k)] for k in range(1, size)]
+
+
 def gather_low(block, axis, size):
-    landed = [swap(block, axis, size, k) for k in range(1, size)]
-    return deep(landed) if axis == "mp" else landed
+    return ordered([block] * (size - 1), axis, size, [1, 3, 2])
 
 
 def scatter_low(blocks, axis, size):
-    landed = [swap(blocks[k - 1], axis, size, k) for k in range(1, size)]
-    return deep(landed) if axis == "mp" else landed
+    return ordered(blocks, axis, size, [2, 1, 3])
 
 
 def pick(stacked, index):
@@ -170,12 +174,12 @@
 def attend_body(heads, query_scale, ids, *refs):
     x = refs[:4]
     wq, wk, wv, wo, qb, vb, ob, bias, own_out, p1, p2, p3 = refs[4:16]
-    hbm = refs[16:23]
-    scr, probs_ref, qt, kt, vt, ct, pooled_low, sem = refs[23:]
-    probs_hbm, qt_hbm, kt_hbm, vt_hbm, ct_hbm, pooled_hbm, x_hbm = hbm
+    probs_hbm, qt_hbm, kt_hbm, vt_hbm, ct_hbm, x_hbm = refs[16:22]
+    scr, probs_ref, qt, kt, vt, ct, tokens, weights, sem = refs[22:]
     block_len = x[0].shape[0]
     half = block_len // 2
-    head = wq.shape[0] // heads
+    part = wq.shape[0]
+    head = part // heads
     copies = []
 
     def send(source, target):
@@ -184,22 +188,21 @@
         copies.append(copy)
 
     for b in range(4):
-        send(x[b], x_hbm.at[pl.ds(b * block_len, block_len), :])
-    pairs = pair_matrix(half, block_len, False)
-    for b in range(4):
-        span = slice(b * block_len, (b + 1) * block_len)
-        kt[:, span] = mm_nt(wk[...], x[b][...]).astype(LOW)
-        vt[:, span] = (mm_nt(wv[...], x[b][...]) + vb[...]).astype(LOW)
-        pooled = mm(pairs, x[b][...])
-        scr[b] = pooled
-        pooled_low[b * half : (b + 1) * half, :] = pooled.astype(LOW)
-    turn = ids[0] ^ ids[1]
-    own_out[...] = scr[turn] + ob[...]
-    qt[...] = ((mm_nt(wq[...], pooled_low[...]) + qb[...]) * query_scale).astype(LOW)
+        tokens[b * block_len : (b + 1) * block_len, :] = x[b][...]
+    send(tokens, x_hbm)
+    for n, w in enumerate((wk, wv, wq)):
+        weights[n * part : (n + 1) * part, :] = w[...]
+    product = mm_nt(weights[...], tokens[...])
+    kt[...] = product[:part, :].astype(LOW)
+    vt[...] = (product[part : 2 * part, :] + vb[...]).astype(LOW)
+    pairs = pair_matrix(4 * block_len, 4 * half, True)
+    projected = product[2 * part :, :]
+    high = projected.astype(LOW)
+    pooled = mm(high, pairs) + mm((projected - high.astype(F32)).astype(LOW), pairs)
+    qt[...] = ((pooled + qb[...]) * query_scale).astype(LOW)
     send(kt, kt_hbm)
     send(vt, vt_hbm)
     send(qt, qt_hbm)
-    send(pooled_low, pooled_hbm)
     for h in range(heads):
         at = slice(h * head, (h + 1) * head)
         scores = mm_tn(kt[at, :], qt[at, :]) + bias[h]
@@ -209,10 +212,12 @@
         send(probs_ref.at[h], probs_hbm.at[h])
         ct[at, :] = mm(vt[at, :], probs.astype(LOW)).astype(LOW)
     send(ct, ct_hbm)
+    turn = ids[0] ^ ids[1]
+    mine = tokens[pl.ds(pl.multiple_of(turn * block_len, block_len), block_len), :]
+    own_pooled = mm(pair_matrix(half, block_len, False), mine)
     result = mm_tn(ct[...], wo[...])
-    for b in range(4):
-        scr[b] = result[b * half : (b + 1) * half, :]
-    own_out[...] += scr[turn]
+    scr[...] = result.reshape(scr.shape)
+    own_out[...] = own_pooled + ob[...] + scr[turn]
     for k, out in ((1, p1), (2, p2), (3, p3)):
         out[...] = scr[turn ^ k].astype(LOW)
     for copy in copies:
@@ -425,7 +430,7 @@
 def attend_back_body(heads, query_scale, ids, *refs):
     grad, grad_low, wq, wk, wv, wo, probs_ref, qt, kt, vt = refs[:10]
     o = refs[10:14]
-    scores_out, stack, sums_out, weights, dct, repeated, result = refs[14:]
+    scores_out, stack, sums_out, weights, dct, grad_q, result = refs[14:]
     part = wq.shape[0]
     head = part // heads
     slots, full = qt.shape[1], kt.shape[1]
@@ -446,15 +451,11 @@
         grad_queries = mm(kt[at, :], scores_low) * query_scale
         stack[at, :] = mm_nt(qt[at, :], scores_low).astype(LOW)
         stack[part + h * head : part + (h + 1) * head, :] = grad_values.astype(LOW)
-        stack[2 * part + h * head : 2 * part + (h + 1) * head, :slots] = grad_queries.astype(LOW)
+        grad_q[at, :] = grad_queries.astype(LOW)
         sums_out[h, :8, :] = row_sums(grad_queries)
         sums_out[h, 8:, :] = row_sums(grad_values)
-    pairs = pair_matrix(half, block_len, False)
-    for b in range(4):
-        repeated[:, b * block_len : (b + 1) * block_len] = mm(
-            stack[2 * part :, b * half : (b + 1) * half], pairs
-        ).astype(LOW)
-    result[...] = mm_tn(stack[: 2 * part, :], weights[: 2 * part, :]) + mm_tn(repeated[...], weights[2 * part :, :])
+    stack[2 * part :, :] = mm(grad_q[...], pair_matrix(slots, full, False)).astype(LOW)
+    result[...] = mm_tn(stack[...], weights[...])
     spread = pair_matrix(quarter, quarter // 2, True)
     for b in range(4):
         to = slice(b * quarter, (b + 1) * quarter)
@@ -467,12 +468,13 @@
             o[k][to, :] = result[rows(k), :].astype(LOW)
 
 
-def attend_weights_body(ids, x, grad, pooled_low, stack, ct, small_feed, small_attend, sums, keep, send, scr):
-    part, slots = ct.shape
+def attend_weights_body(ids, x, grad, stack, ct, small_feed, small_attend, sums, keep, send, scr):
+    part = ct.shape[0]
     heads = sums.shape[0]
-    scr[0, :part, :] = mm(stack[2 * part :, :slots], pooled_low[...])
-    scr[0, part : 2 * part, :] = mm(stack[:part, :], x[...])
-    scr[1, :part, :] = mm(stack[part : 2 * part, :], x[...])
+    product = mm(stack[...], x[...])
+    scr[0, part : 2 * part, :] = product[:part]
+    scr[1, :part, :] = product[part : 2 * part]
+    scr[0, :part, :] = product[2 * part :]
     scr[1, part : 2 * part, :] = mm(ct[...], grad[...])
     scr[:, 2 * part :, :] = jnp.zeros((2, scr.shape[1] - 2 * part, scr.shape[2]), F32)
     scr[0, 2 * part : 2 * part + SMALL_ROWS, :] = small_feed[...]
@@ -541,19 +543,23 @@
 
 
 def unpack_attend(ids, mine, other, rows_out, query_out, value_out, rel_out, larges, scr, sem):
-    dq, dk, dv, do = larges
-    send, wait = sender(sem)
-    part = dq.shape[0]
+    part = larges[0].shape[0]
     heads = rel_out.shape[0]
     head = part // heads
+    send, wait = sender(sem)
     for c, (a, b) in ((0, (mine, other)), (1, (other, mine))):
 
         @pl.when(ids[2] == c)
         def _(a=a, b=b):
-            scr[0] = a[:part, :].astype(F32)
-            scr[1] = a[part : 2 * part, :].astype(F32)
-            scr[2] = b[:part, :].astype(F32)
-            scr[3] = b[part : 2 * part, :].astype(F32)
+            for n, half in enumerate((a, a, b, b)):
+                scr[n] = half[n % 2 * part : (n % 2 + 1) * part, :].astype(F32)
+
+    for n, out in enumerate(larges):
+        send(scr.at[n], out)
+    for c, (a, b) in ((0, (mine, other)), (1, (other, mine))):
+
+        @pl.when(ids[2] == c)
+        def _(a=a, b=b):
             small_a = a[2 * part :, :].astype(F32)
             small_b = b[2 * part :, :].astype(F32)
             for n, out in enumerate(rows_out):
@@ -570,8 +576,6 @@
                     at = h * BASES + index
                     rel_out[h : h + 1, index : index + 1] = table[at : at + 1, :1]
 
-    for n, out in enumerate(larges):
-        send(scr.at[n], out)
     wait()
 
 
@@ -664,12 +668,12 @@
     bias = kernel(
         functools.partial(bias_body, heads, block_len, 32), f32(heads, full, slots), (ids, rel_weight), smem=2, micros=3.0
     )
-    own, p1, p2, p3, probs, qt, kt, vt, ct, pooled_low, tokens = kernel(
+    own, p1, p2, p3, probs, qt, kt, vt, ct, tokens = kernel(
         functools.partial(attend_body, heads, query_scale),
         [f32(half, width)]
         + [low(half, width)] * 3
         + [f32(heads, full, slots), low(part, slots), low(part, full), low(part, full), low(part, slots)]
-        + [low(slots, width), low(full, width)],
+        + [low(full, width)],
         (ids, *x, wq, wk, wv, out_weight, column(query_bias), column(value_bias), row(out_bias), bias),
         smem=1,
         scratch=[
@@ -679,11 +683,12 @@
             pltpu.VMEM((part, full), LOW),
             pltpu.VMEM((part, full), LOW),
             pltpu.VMEM((part, slots), LOW),
-            pltpu.VMEM((slots, width), LOW),
-            pltpu.SemaphoreType.DMA((9 + heads,)),
+            pltpu.VMEM((full, width), LOW),
+            pltpu.VMEM((3 * part, width), LOW),
+            pltpu.SemaphoreType.DMA((5 + heads,)),
         ],
         micros=5.0,
-        hbm=range(4, 11),
+        hbm=range(4, 10),
     )
     arrived = scatter_low((p1, p2, p3), "mp", mp_size)
     attended = kernel(total_body, low(half, width), (*arrived, own), micros=0.5)
@@ -750,7 +755,7 @@
         scratch=[
             pltpu.VMEM((3 * part, width), LOW),
             pltpu.VMEM((part, slots), LOW),
-            pltpu.VMEM((part, full), LOW),
+            pltpu.VMEM((part, slots), LOW),
             pltpu.VMEM((full, width), F32),
         ],
         micros=0.1,
@@ -767,7 +772,7 @@
     attend_keep, attend_send = kernel(
         attend_weights_body,
         [f32(half_rows, width), low(half_rows, width)],
-        (ids, after(tokens, came), grad_attended, pooled_low, stack, ct, small_feed, small_attend, sums),
+        (ids, after(tokens, came), grad_attended, stack, ct, small_feed, small_attend, sums),
         smem=1,
         scratch=[pltpu.VMEM((2, half_rows, width), F32)],
         micros=0.1,
@@ -798,7 +803,9 @@
         micros=0.1,
     )
     near = both_ways(sent1, sent2, seq_size)
-    q = deep(scatter_low(q, "seq", seq_size))
+    q = [swap(q[k - 1], "seq", seq_size, k) for k in [2, 1, 3]]
+    q = deep(q)
+    q = [q[[2, 1, 3].index(k)] for k in range(1, 4)]
     joined = kernel(join_body, low(block_len, width), (q0, *q), micros=8.0)
     spread = gather_low(joined, "mp", mp_size)
     mid = kernel(

time: 157 us -> 152 us (0.968)
  waiting for transfers between devices: 55.3 us -> 50 us
  starting transfers between devices: 61.7 us -> 64.1 us
  Pallas kernels: 32.9 us -> 31.2 us
    ppermute x47, waiting for transfers between devices: 55.3 us -> 50 us  [swap(): return lax.ppermute(block, axis, [(s, s ^ k) for s in range(size)])]
    ppermute x47, starting transfers between devices: 61.7 us -> 64.1 us  [swap(): return lax.ppermute(block, axis, [(s, s ^ k) for s in range(size)])]
    pallas_call x25, Pallas kernels: 32.9 us -> 31.2 us  [kernel(): pl.pallas_call(body, out_shape=outs, in_specs=in_specs, out_specs=out_spe...]
where the time goes in v4:
time: 152 us; the launch traced here: 150 us
  starting transfers between devices  64.1 us (42%)
  waiting for transfers between devices  50 us (33%)
  Pallas kernels  31.2 us (21%)
  local copies, waits for them, and re-layouts  2.24 us (1%)
    ppermute x47, starting transfers between devices, swap(): return lax.ppermute(block, axis, [(s, s ^ k) for s in range(size)])  64.1 us
    ppermute x47, waiting for transfers between devices, swap(): return lax.ppermute(block, axis, [(s, s ^ k) for s in range(size)])  50 us
    pallas_call x25, Pallas kernels, kernel(): pl.pallas_call(body, out_shape=outs, in_specs=in_specs, out_specs=out_spe...  31.2 us
  transfers between devices with their start and end apart: 47, of which 26 were waited for; matrix products, arithmetic and copies ran while one was open for 1% of the time, Pallas kernels for 12%

profile of v4, /device:TPU:0, one launch (start us, length us, event | category | flops | bytes accessed | tf_op | source)
XLA Modules:
  0.0 149.5 jit_solution(14564918235556444387)
XLA Ops:
  0.7 1.3 dynamic-slice_bitcast_fusion
  2.0 4.0 %collective-permute-start.2 = (bf16[128,768]{1,0:T(8,128)(2,1)S(1)}, bf16[128,768]{1,0:T(8,128)(2,1)S(1)}, u32[]{:S(2)}, u32[]{:S(2)}) collective-permute-start(bf16[128,768]{1,0:T(8,128)(2,1)S(1)} %get-tuple-element.252), channel_id=1, source_target_pairs={{0,24},{8,16},{16,8},{24,0},{1,25},{9,17},{17,9},{25,1},{2,26},{10... | collective-permute-start | bytes 589832 | tf_op jit(solution)/shard_map/ppermute | solution.py:65
  8.2 2.1 %shard_map.322.refs_11_ = f32[3,512,256]{2,1,0:T(8,128)S(1)} custom-call(s32[4]{0:T(128)S(1)} %pad_add_fusion.ids, f32[3,8]{1,0:T(4,128)S(1)} %copy-done.6), custom_call_target="tpu_custom_call" | custom-call | flops 1200000000 | bytes 9000000 | tf_op jit(solution)/shard_map/pallas_call | solution.py:37
  10.3 1.4 collective-permute-done.2.refs_3_
  11.7 3.7 %collective-permute-done.refs_1_ = bf16[128,768]{1,0:T(8,128)(2,1)S(1)} collective-permute-done((bf16[128,768]{1,0:T(8,128)(2,1)S(1)}, bf16[128,768]{1,0:T(8,128)(2,1)S(1)}, u32[]{:S(2)}, u32[]{:S(2)}) %collective-permute-start) | collective-permute-done | bytes 196640 | tf_op jit(solution)/shard_map/ppermute | solution.py:65
  15.5 4.7 %shard_map.323 = (f32[64,768]{1,0:T(8,128)S(1)}, bf16[64,768]{1,0:T(8,128)(2,1)S(1)}, bf16[64,768]{1,0:T(8,128)(2,1)S(1)}, bf16[64,768]{1,0:T(8,128)(2,1)S(1)}, ...) custom-call(s32[4]{0:T(128)S(1)} %pad_add_fusion.ids, ...), custom_call_target="tpu_custom_call" | custom-call | flops 2000000000 | bytes 15000000 | tf_op jit(solution)/shard_map/pallas_call | solution.py:37
  20.2 2.7 %collective-permute-start.3 = (bf16[64,768]{1,0:T(8,128)(2,1)S(1)}, bf16[64,768]{1,0:T(8,128)(2,1)S(1)}, u32[]{:S(2)}, u32[]{:S(2)}) collective-permute-start(bf16[64,768]{1,0:T(8,128)(2,1)S(1)} %get-tuple-element.135), channel_id=1, source_target_pairs={{0,2},{1,3},{2,0},{3,1},{4,6},{5,7},{6,4},{7,5},{8,10},{9,11},{10,... | collective-permute-start | bytes 294920 | tf_op jit(solution)/shard_map/ppermute | solution.py:65
  22.8 1.6 %collective-permute-start.4 = (bf16[64,768]{1,0:T(8,128)(2,1)S(1)}, bf16[64,768]{1,0:T(8,128)(2,1)S(1)}, u32[]{:S(2)}, u32[]{:S(2)}) collective-permute-start(bf16[64,768]{1,0:T(8,128)(2,1)S(1)} %get-tuple-element.136), channel_id=1, source_target_pairs={{0,1},{1,0},{2,3},{3,2},{4,5},{5,4},{6,7},{7,6},{8,9},{9,8},{10,11... | collective-permute-start | bytes 294920 | tf_op jit(solution)/shard_map/ppermute | solution.py:65
  24.7 4.3 %collective-permute-done.3.r2 = bf16[64,768]{1,0:T(8,128)(2,1)S(1)} collective-permute-done((bf16[64,768]{1,0:T(8,128)(2,1)S(1)}, bf16[64,768]{1,0:T(8,128)(2,1)S(1)}, u32[]{:S(2)}, u32[]{:S(2)}) %collective-permute-start.3) | collective-permute-done | bytes 98336 | tf_op jit(solution)/shard_map/ppermute | solution.py:65
  28.9 2.1 %collective-permute-done.5.r3 = bf16[64,768]{1,0:T(8,128)(2,1)S(1)} collective-permute-done((bf16[64,768]{1,0:T(8,128)(2,1)S(1)}, bf16[64,768]{1,0:T(8,128)(2,1)S(1)}, u32[]{:S(2)}, u32[]{:S(2)}) %collective-permute-start.5) | collective-permute-done | bytes 98336 | tf_op jit(solution)/shard_map/ppermute | solution.py:65
  31.1 3.7 %collective-permute-start.8 = (bf16[64,768]{1,0:T(8,128)(2,1)S(1)}, bf16[64,768]{1,0:T(8,128)(2,1)S(1)}, u32[]{:S(2)}, u32[]{:S(2)}) collective-permute-start(bf16[64,768]{1,0:T(8,128)(2,1)S(1)} %shard_map.324.a0), channel_id=1, source_target_pairs={{0,2},{1,3},{2,0},{3,1},{4,6},{5,7},{6,4},{7,5},{8,10},{9,11},{10,... | collective-permute-start | bytes 294920 | tf_op jit(solution)/shard_map/ppermute | solution.py:65
  35.4 2.5 %collective-permute-start.11 = (bf16[64,768]{1,0:T(8,128)(2,1)S(1)}, bf16[64,768]{1,0:T(8,128)(2,1)S(1)}, u32[]{:S(2)}, u32[]{:S(2)}) collective-permute-start(bf16[64,768]{1,0:T(8,128)(2,1)S(1)} %get-tuple-element.256), channel_id=1, source_target_pairs={{0,24},{8,16},{16,8},{24,0},{1,25},{9,17},{17,9},{25,1},{2,26},{10... | collective-permute-start | bytes 294920 | tf_op jit(solution)/shard_map/ppermute | solution.py:65
  38.4 3.8 %collective-permute-done.8.a2 = bf16[64,768]{1,0:T(8,128)(2,1)S(1)} collective-permute-done((bf16[64,768]{1,0:T(8,128)(2,1)S(1)}, bf16[64,768]{1,0:T(8,128)(2,1)S(1)}, u32[]{:S(2)}, u32[]{:S(2)}) %collective-permute-start.8) | collective-permute-done | bytes 98336 | tf_op jit(solution)/shard_map/ppermute | solution.py:65
  42.2 1.5 collective-permute-start.9
  43.7 2.0 %shard_map.325 = (f32[64,768]{1,0:T(8,128)S(1)}, bf16[64,768]{1,0:T(8,128)(2,1)S(1)}, bf16[64,768]{1,0:T(8,128)(2,1)S(1)}, bf16[64,768]{1,0:T(8,128)(2,1)S(1)}, ...) custom-call(s32[4]{0:T(128)S(1)} %pad_add_fusion.ids, ...), custom_call_target="tpu_custom_call" | custom-call | flops 1200000000 | bytes 9000000 | tf_op jit(solution)/shard_map/pallas_call | solution.py:37
  45.8 1.1 collective-permute-done.9.refs_5_
  46.9 2.4 %collective-permute-start.13 = (bf16[64,768]{1,0:T(8,128)(2,1)S(1)}, bf16[64,768]{1,0:T(8,128)(2,1)S(1)}, u32[]{:S(2)}, u32[]{:S(2)}) collective-permute-start(bf16[64,768]{1,0:T(8,128)(2,1)S(1)} %get-tuple-element.150), channel_id=1, source_target_pairs={{0,1},{1,0},{2,3},{3,2},{4,5},{5,4},{6,7},{7,6},{8,9},{9,8},{10,11... | collective-permute-start | bytes 294920 | tf_op jit(solution)/shard_map/ppermute | solution.py:65
  49.3 1.9 %collective-permute-start.14 = (bf16[64,768]{1,0:T(8,128)(2,1)S(1)}, bf16[64,768]{1,0:T(8,128)(2,1)S(1)}, u32[]{:S(2)}, u32[]{:S(2)}) collective-permute-start(bf16[64,768]{1,0:T(8,128)(2,1)S(1)} %get-tuple-element.151), channel_id=1, source_target_pairs={{0,3},{1,2},{2,1},{3,0},{4,7},{5,6},{6,5},{7,4},{8,11},{9,10},{10,... | collective-permute-start | bytes 294920 | tf_op jit(solution)/shard_map/ppermute | solution.py:65
  51.2 3.6 %collective-permute-done.12.r2 = bf16[64,768]{1,0:T(8,128)(2,1)S(1)} collective-permute-done((bf16[64,768]{1,0:T(8,128)(2,1)S(1)}, bf16[64,768]{1,0:T(8,128)(2,1)S(1)}, u32[]{:S(2)}, u32[]{:S(2)}) %collective-permute-start.12) | collective-permute-done | bytes 98336 | tf_op jit(solution)/shard_map/ppermute | solution.py:65
  54.8 1.1 collective-permute-done.14.r3
  56.0 2.4 %collective-permute-start.17 = (bf16[64,768]{1,0:T(8,128)(2,1)S(1)}, bf16[64,768]{1,0:T(8,128)(2,1)S(1)}, u32[]{:S(2)}, u32[]{:S(2)}) collective-permute-start(bf16[64,768]{1,0:T(8,128)(2,1)S(1)} %shard_map.326.refs_0_), channel_id=1, source_target_pairs={{0,2},{1,3},{2,0},{3,1},{4,6},{5,7},{6,4},{7,5},{8,10},{9,11},{10,... | collective-permute-start | bytes 294920 | tf_op jit(solution)/shard_map/ppermute | solution.py:65
  58.3 1.6 %collective-permute-start.16 = (bf16[64,768]{1,0:T(8,128)(2,1)S(1)}, bf16[64,768]{1,0:T(8,128)(2,1)S(1)}, u32[]{:S(2)}, u32[]{:S(2)}) collective-permute-start(bf16[64,768]{1,0:T(8,128)(2,1)S(1)} %shard_map.326.refs_0_), channel_id=1, source_target_pairs={{0,3},{1,2},{2,1},{3,0},{4,7},{5,6},{6,5},{7,4},{8,11},{9,10},{10,... | collective-permute-start | bytes 294920 | tf_op jit(solution)/shard_map/ppermute | solution.py:65
  60.0 3.8 %collective-permute-done.17.refs_2_ = bf16[64,768]{1,0:T(8,128)(2,1)S(1)} collective-permute-done((bf16[64,768]{1,0:T(8,128)(2,1)S(1)}, bf16[64,768]{1,0:T(8,128)(2,1)S(1)}, u32[]{:S(2)}, u32[]{:S(2)}) %collective-permute-start.17) | collective-permute-done | bytes 98336 | tf_op jit(solution)/shard_map/ppermute | solution.py:65
  63.8 1.1 collective-permute-done.16.refs_3_
  65.9 2.3 %shard_map.327 = (f32[64,768]{1,0:T(8,128)S(1)}, bf16[64,768]{1,0:T(8,128)(2,1)S(1)}, bf16[64,768]{1,0:T(8,128)(2,1)S(1)}, bf16[64,768]{1,0:T(8,128)(2,1)S(1)}, ...) custom-call(s32[4]{0:T(128)S(1)} %pad_add_fusion.ids, ...), custom_call_target="tpu_custom_call" | custom-call | flops 1200000000 | bytes 9000000 | tf_op jit(solution)/shard_map/pallas_call | solution.py:37
  68.8 1.6 %collective-permute-start.19 = (bf16[64,768]{1,0:T(8,128)(2,1)S(1)}, bf16[64,768]{1,0:T(8,128)(2,1)S(1)}, u32[]{:S(2)}, u32[]{:S(2)}) collective-permute-start(bf16[64,768]{1,0:T(8,128)(2,1)S(1)} %get-tuple-element.162), channel_id=1, source_target_pairs={{0,1},{1,0},{2,3},{3,2},{4,5},{5,4},{6,7},{7,6},{8,9},{9,8},{10,11... | collective-permute-start | bytes 294920 | tf_op jit(solution)/shard_map/ppermute | solution.py:65
  70.4 2.2 %collective-permute-start.20 = (bf16[64,768]{1,0:T(8,128)(2,1)S(1)}, bf16[64,768]{1,0:T(8,128)(2,1)S(1)}, u32[]{:S(2)}, u32[]{:S(2)}) collective-permute-start(bf16[64,768]{1,0:T(8,128)(2,1)S(1)} %get-tuple-element.163), channel_id=1, source_target_pairs={{0,3},{1,2},{2,1},{3,0},{4,7},{5,6},{6,5},{7,4},{8,11},{9,10},{10,... | collective-permute-start | bytes 294920 | tf_op jit(solution)/shard_map/ppermute | solution.py:65
  72.6 1.1 shard_map.335
  73.8 1.0 collective-permute-done.18.r2
  74.8 2.1 %collective-permute-done.20.r3 = bf16[64,768]{1,0:T(8,128)(2,1)S(1)} collective-permute-done((bf16[64,768]{1,0:T(8,128)(2,1)S(1)}, bf16[64,768]{1,0:T(8,128)(2,1)S(1)}, u32[]{:S(2)}, u32[]{:S(2)}) %collective-permute-start.20) | collective-permute-done | bytes 98336 | tf_op jit(solution)/shard_map/ppermute | solution.py:65
  77.0 2.2 %collective-permute-start.22 = (bf16[64,768]{1,0:T(8,128)(2,1)S(1)}, bf16[64,768]{1,0:T(8,128)(2,1)S(1)}, u32[]{:S(2)}, u32[]{:S(2)}) collective-permute-start(bf16[64,768]{1,0:T(8,128)(2,1)S(1)} %shard_map.328.refs_0_), channel_id=1, source_target_pairs={{0,3},{1,2},{2,1},{3,0},{4,7},{5,6},{6,5},{7,4},{8,11},{9,10},{10,... | collective-permute-start | bytes 294920 | tf_op jit(solution)/shard_map/ppermute | solution.py:65
  79.2 1.3 collective-permute-start.21
  80.5 1.4 shard_map.336
  81.9 1.6 %collective-permute-start.34 = (bf16[192,768]{1,0:T(8,128)(2,1)S(1)}, bf16[192,768]{1,0:T(8,128)(2,1)S(1)}, u32[]{:S(2)}, u32[]{:S(2)}) collective-permute-start(bf16[192,768]{1,0:T(8,128)(2,1)S(1)} %get-tuple-element.205), channel_id=1, source_target_pairs={{0,8},{8,0},{16,24},{24,16},{1,9},{9,1},{17,25},{25,17},{2,10},{10... | collective-permute-start | bytes 884744 | tf_op jit(solution)/shard_map/ppermute | solution.py:65
  83.5 1.5 %collective-permute-start.35 = (bf16[192,768]{1,0:T(8,128)(2,1)S(1)}, bf16[192,768]{1,0:T(8,128)(2,1)S(1)}, u32[]{:S(2)}, u32[]{:S(2)}) collective-permute-start(bf16[192,768]{1,0:T(8,128)(2,1)S(1)} %get-tuple-element.206), channel_id=1, source_target_pairs={{0,16},{8,24},{16,0},{24,8},{1,17},{9,25},{17,1},{25,9},{2,18},{10... | collective-permute-start | bytes 884744 | tf_op jit(solution)/shard_map/ppermute | solution.py:65
  85.5 1.1 shard_map.329
  86.6 3.6 %shard_map.330 = (f32[128,768]{1,0:T(8,128)S(1)}, bf16[128,768]{1,0:T(8,128)(2,1)S(1)}, bf16[128,768]{1,0:T(8,128)(2,1)S(1)}, bf16[128,768]{1,0:T(8,128)(2,1)S(1...) custom-call(s32[4]{0:T(128)S(1)} %pad_add_fusion.ids, ...), custom_call_target="tpu_custom_call" | custom-call | flops 40000000 | bytes 300000 | tf_op jit(solution)/shard_map/pallas_call | solution.py:37
  90.2 1.4 shard_map.337
  91.7 1.2 collective-permute-start.24
  92.9 1.6 %collective-permute-start.25 = (bf16[128,768]{1,0:T(8,128)(2,1)S(1)}, bf16[128,768]{1,0:T(8,128)(2,1)S(1)}, u32[]{:S(2)}, u32[]{:S(2)}) collective-permute-start(bf16[128,768]{1,0:T(8,128)(2,1)S(1)} %get-tuple-element.180), channel_id=1, source_target_pairs={{0,1},{1,0},{2,3},{3,2},{4,5},{5,4},{6,7},{7,6},{8,9},{9,8},{10,11... | collective-permute-start | bytes 589832 | tf_op jit(solution)/shard_map/ppermute | solution.py:65
  94.5 1.7 %collective-permute-start.26 = (bf16[128,768]{1,0:T(8,128)(2,1)S(1)}, bf16[128,768]{1,0:T(8,128)(2,1)S(1)}, u32[]{:S(2)}, u32[]{:S(2)}) collective-permute-start(bf16[128,768]{1,0:T(8,128)(2,1)S(1)} %get-tuple-element.181), channel_id=1, source_target_pairs={{0,3},{1,2},{2,1},{3,0},{4,7},{5,6},{6,5},{7,4},{8,11},{9,10},{10,... | collective-permute-start | bytes 589832 | tf_op jit(solution)/shard_map/ppermute | solution.py:65
  96.2 2.2 %shard_map.338.rel = f32[32,128]{1,0:T(8,128)S(1)} custom-call(s32[4]{0:T(128)S(1)} %pad_add_fusion.ids, f32[3,512,256]{2,1,0:T(8,128)S(1)} %get-tuple-element.215.scores_ref), custom_call_target="tpu_custom_call" | custom-call | flops 40000000 | bytes 300000 | tf_op jit(solution)/shard_map/pallas_call | solution.py:37
  98.3 1.0 shard_map.339
  99.3 1.5 %collective-permute-start.37 = (bf16[224,768]{1,0:T(8,128)(2,1)S(1)}, bf16[224,768]{1,0:T(8,128)(2,1)S(1)}, u32[]{:S(2)}, u32[]{:S(2)}) collective-permute-start(bf16[224,768]{1,0:T(8,128)(2,1)S(1)} %get-tuple-element.220), channel_id=1, source_target_pairs={{0,8},{8,0},{16,24},{24,16},{1,9},{9,1},{17,25},{25,17},{2,10},{10... | collective-permute-start | bytes 1032200 | tf_op jit(solution)/shard_map/ppermute | solution.py:65
  100.8 1.5 %collective-permute-start.38 = (bf16[224,768]{1,0:T(8,128)(2,1)S(1)}, bf16[224,768]{1,0:T(8,128)(2,1)S(1)}, u32[]{:S(2)}, u32[]{:S(2)}) collective-permute-start(bf16[224,768]{1,0:T(8,128)(2,1)S(1)} %get-tuple-element.221), channel_id=1, source_target_pairs={{0,16},{8,24},{16,0},{24,8},{1,17},{9,25},{17,1},{25,9},{2,18},{10... | collective-permute-start | bytes 1032200 | tf_op jit(solution)/shard_map/ppermute | solution.py:65
  102.3 2.6 %collective-permute-done.24.t2.r2 = bf16[128,768]{1,0:T(8,128)(2,1)S(1)} collective-permute-done((bf16[128,768]{1,0:T(8,128)(2,1)S(1)}, bf16[128,768]{1,0:T(8,128)(2,1)S(1)}, u32[]{:S(2)}, u32[]{:S(2)}) %collective-permute-start.24) | collective-permute-done | bytes 196640 | tf_op jit(solution)/shard_map/ppermute | solution.py:65
  104.9 3.8 %collective-permute-done.26.t3.r3 = bf16[128,768]{1,0:T(8,128)(2,1)S(1)} collective-permute-done((bf16[128,768]{1,0:T(8,128)(2,1)S(1)}, bf16[128,768]{1,0:T(8,128)(2,1)S(1)}, u32[]{:S(2)}, u32[]{:S(2)}) %collective-permute-start.26) | collective-permute-done | bytes 196640 | tf_op jit(solution)/shard_map/ppermute | solution.py:65
  108.8 1.6 %collective-permute-start.27 = (bf16[96,768]{1,0:T(8,128)(2,1)S(1)}, bf16[96,768]{1,0:T(8,128)(2,1)S(1)}, u32[]{:S(2)}, u32[]{:S(2)}) collective-permute-start(bf16[96,768]{1,0:T(8,128)(2,1)S(1)} %get-tuple-element.189), channel_id=1, source_target_pairs={{0,16},{8,24},{16,0},{24,8},{1,17},{9,25},{17,1},{25,9},{2,18},{10... | collective-permute-start | bytes 442376 | tf_op jit(solution)/shard_map/ppermute | solution.py:65
  110.4 1.3 collective-permute-start.28
  112.5 1.3 collective-permute-start.39
  113.9 1.5 %collective-permute-start.40 = (bf16[256,768]{1,0:T(8,128)(2,1)S(1)}, bf16[256,768]{1,0:T(8,128)(2,1)S(1)}, u32[]{:S(2)}, u32[]{:S(2)}) collective-permute-start(bf16[256,768]{1,0:T(8,128)(2,1)S(1)} %get-tuple-element.225.sent2), channel_id=1, source_target_pairs={{0,16},{8,24},{16,0},{24,8},{1,17},{9,25},{17,1},{25,9},{2,18},{10... | collective-permute-start | bytes 1179656 | tf_op jit(solution)/shard_map/ppermute | solution.py:65
  115.4 1.8 %collective-permute-done.28.q1 = bf16[96,768]{1,0:T(8,128)(2,1)S(1)} collective-permute-done((bf16[96,768]{1,0:T(8,128)(2,1)S(1)}, bf16[96,768]{1,0:T(8,128)(2,1)S(1)}, u32[]{:S(2)}, u32[]{:S(2)}) %collective-permute-start.28) | collective-permute-done | bytes 147488 | tf_op jit(solution)/shard_map/ppermute | solution.py:65
  117.2 2.7 %collective-permute-done.29.q3 = bf16[96,768]{1,0:T(8,128)(2,1)S(1)} collective-permute-done((bf16[96,768]{1,0:T(8,128)(2,1)S(1)}, bf16[96,768]{1,0:T(8,128)(2,1)S(1)}, u32[]{:S(2)}, u32[]{:S(2)}) %collective-permute-start.29) | collective-permute-done | bytes 147488 | tf_op jit(solution)/shard_map/ppermute | solution.py:65
  119.9 5.4 %collective-permute-start.32 = (bf16[128,768]{1,0:T(8,128)(2,1)S(1)}, bf16[128,768]{1,0:T(8,128)(2,1)S(1)}, u32[]{:S(2)}, u32[]{:S(2)}) collective-permute-start(bf16[128,768]{1,0:T(8,128)(2,1)S(1)} %shard_map.334.t0), channel_id=1, source_target_pairs={{0,2},{1,3},{2,0},{3,1},{4,6},{5,7},{6,4},{7,5},{8,10},{9,11},{10,... | collective-permute-start | bytes 589832 | tf_op jit(solution)/shard_map/ppermute | solution.py:65
  125.3 1.3 collective-permute-start.31
  127.1 1.6 %collective-permute-start.41 = (bf16[64,768]{1,0:T(8,128)(2,1)S(1)}, bf16[64,768]{1,0:T(8,128)(2,1)S(1)}, u32[]{:S(2)}, u32[]{:S(2)}) collective-permute-start(bf16[64,768]{1,0:T(8,128)(2,1)S(1)} %get-tuple-element.227.mid1), channel_id=1, source_target_pairs={{0,8},{8,0},{16,24},{24,16},{1,9},{9,1},{17,25},{25,17},{2,10},{10... | collective-permute-start | bytes 294920 | tf_op jit(solution)/shard_map/ppermute | solution.py:65
  128.7 1.5 %collective-permute-start.42 = (bf16[64,768]{1,0:T(8,128)(2,1)S(1)}, bf16[64,768]{1,0:T(8,128)(2,1)S(1)}, u32[]{:S(2)}, u32[]{:S(2)}) collective-permute-start(bf16[64,768]{1,0:T(8,128)(2,1)S(1)} %get-tuple-element.228.mid2), channel_id=1, source_target_pairs={{0,16},{8,24},{16,0},{24,8},{1,17},{9,25},{17,1},{25,9},{2,18},{10... | collective-permute-start | bytes 294920 | tf_op jit(solution)/shard_map/ppermute | solution.py:65
  130.2 1.3 shard_map.333
  131.8 1.6 %collective-permute-done.42.came2 = bf16[64,768]{1,0:T(8,128)(2,1)S(1)} collective-permute-done((bf16[64,768]{1,0:T(8,128)(2,1)S(1)}, bf16[64,768]{1,0:T(8,128)(2,1)S(1)}, u32[]{:S(2)}, u32[]{:S(2)}) %collective-permute-start.42) | collective-permute-done | bytes 98336 | tf_op jit(solution)/shard_map/ppermute | solution.py:65
  133.9 1.8 %collective-permute-start.44 = (bf16[224,768]{1,0:T(8,128)(2,1)S(1)}, bf16[224,768]{1,0:T(8,128)(2,1)S(1)}, u32[]{:S(2)}, u32[]{:S(2)}) collective-permute-start(bf16[224,768]{1,0:T(8,128)(2,1)S(1)} %get-tuple-element.230.along2), channel_id=1, source_target_pairs={{0,16},{8,24},{16,0},{24,8},{1,17},{9,25},{17,1},{25,9},{2,18},{10... | collective-permute-start | bytes 1032200 | tf_op jit(solution)/shard_map/ppermute | solution.py:65
  135.8 2.6 %collective-permute-done.32.t2 = bf16[128,768]{1,0:T(8,128)(2,1)S(1)} collective-permute-done((bf16[128,768]{1,0:T(8,128)(2,1)S(1)}, bf16[128,768]{1,0:T(8,128)(2,1)S(1)}, u32[]{:S(2)}, u32[]{:S(2)}) %collective-permute-start.32) | collective-permute-done | bytes 196640 | tf_op jit(solution)/shard_map/ppermute | solution.py:65
  138.3 2.5 %collective-permute-done.43.came1 = bf16[224,768]{1,0:T(8,128)(2,1)S(1)} collective-permute-done((bf16[224,768]{1,0:T(8,128)(2,1)S(1)}, bf16[224,768]{1,0:T(8,128)(2,1)S(1)}, u32[]{:S(2)}, u32[]{:S(2)}) %collective-permute-start.43) | collective-permute-done | bytes 344096 | tf_op jit(solution)/shard_map/ppermute | solution.py:65
  142.5 2.6 %shard_map.345 = (f32[4,128,768]{2,1,0:T(8,128)}, f32[768,768]{1,0:T(8,128)}, f32[768,768]{1,0:T(8,128)}) custom-call(s32[4]{0:T(128)S(1)} %pad_add_fusion.ids, bf16[128,768]{1,0:T(8,128)(2,1)S(1)} %shard_map.334.t0, bf16[128,768]{1,0:T(8,128)(2,1)S(1)} %collective-permute-done.30.t1, bf16[128,768]{1,0:T(8,128)(2,1)S(1)} %collective-permute-done.32.t2, ...), custom_call_target="tpu_custom_call" | custom-call | flops 40000000 | bytes 300000 | tf_op jit(solution)/shard_map/pallas_call | solution.py:37
  145.9 3.4 %shard_map.346 = (f32[768,768]{1,0:T(8,128)}, f32[768,768]{1,0:T(8,128)}, f32[768]{0:T(1024)}, f32[768]{0:T(1024)}, f32[768]{0:T(1024)}, /*index=5*/f32[768]{0:T...) custom-call(s32[4]{0:T(128)S(1)} %pad_add_fusion.ids, ...), custom_call_target="tpu_custom_call", output_to_operand_aliasing={{0}: (4, {}), {1}: (5, {})} | custom-call | flops 40000000 | bytes 300000 | tf_op jit(solution)/shard_map/pallas_call | solution.py:37
  (104 shorter events, 11.0 us)
Async XLA Ops:
  0.7 6.5 %copy-start.8 = (f32[768]{0:T(1024)S(1)}, f32[768]{0:T(1024)}, u32[]{:S(2)}) copy-start(f32[768]{0:T(1024)} %param.28) | copy-start | bytes 9220
  0.7 6.5 %copy-start.15 = (f32[192]{0:T(256)S(1)}, f32[192]{0:T(256)}, u32[]{:S(2)}) copy-start(f32[192]{0:T(256)} %param.22) | copy-start | bytes 2308
  0.7 6.7 %copy-start.16 = (f32[192]{0:T(256)S(1)}, f32[192]{0:T(256)}, u32[]{:S(2)}) copy-start(f32[192]{0:T(256)} %param.25) | copy-start | bytes 2308
  0.7 7.5 %copy-start.6 = (f32[3,8]{1,0:T(4,128)S(1)}, f32[3,8]{1,0:T(4,128)}, u32[]{:S(2)}) copy-start(f32[3,8]{1,0:T(4,128)} %rel.1) | copy-start | bytes 292
  2.0 9.7 %collective-permute-start.2 = (bf16[128,768]{1,0:T(8,128)(2,1)S(1)}, bf16[128,768]{1,0:T(8,128)(2,1)S(1)}, u32[]{:S(2)}, u32[]{:S(2)}) collective-permute-start(bf16[128,768]{1,0:T(8,128)(2,1)S(1)} %get-tuple-element.252), channel_id=1, source_target_pairs={{0,24},{8,16},{16,8},{24,0},{1,25},{9,17},{17,9},{25,1},{2,26},{10... | collective-permute-start | bytes 589832 | tf_op jit(solution)/shard_map/ppermute | solution.py:65
  6.0 9.4 %collective-permute-start = (bf16[128,768]{1,0:T(8,128)(2,1)S(1)}, bf16[128,768]{1,0:T(8,128)(2,1)S(1)}, u32[]{:S(2)}, u32[]{:S(2)}) collective-permute-start(bf16[128,768]{1,0:T(8,128)(2,1)S(1)} %get-tuple-element.253), channel_id=1, source_target_pairs={{0,8},{8,0},{16,24},{24,16},{1,9},{9,1},{17,25},{25,17},{2,10},{10... | collective-permute-start | bytes 589832 | tf_op jit(solution)/shard_map/ppermute | solution.py:65
  6.5 8.9 %collective-permute-start.1 = (bf16[128,768]{1,0:T(8,128)(2,1)S(1)}, bf16[128,768]{1,0:T(8,128)(2,1)S(1)}, u32[]{:S(2)}, u32[]{:S(2)}) collective-permute-start(bf16[128,768]{1,0:T(8,128)(2,1)S(1)} %get-tuple-element.255), channel_id=1, source_target_pairs={{0,16},{8,24},{16,0},{24,8},{1,17},{9,25},{17,1},{25,9},{2,18},{10... | collective-permute-start | bytes 589832 | tf_op jit(solution)/shard_map/ppermute | solution.py:65
  8.2 7.2 %copy-start = (bf16[768,192]{0,1:T(8,128)(2,1)S(1)}, bf16[768,192]{0,1:T(8,128)(2,1)}, u32[]{:S(2)}) copy-start(bf16[768,192]{0,1:T(8,128)(2,1)} %param.21) | copy-start | bytes 884740
  8.2 7.2 %copy-start.1 = (bf16[768,192]{0,1:T(8,128)(2,1)S(1)}, bf16[768,192]{0,1:T(8,128)(2,1)}, u32[]{:S(2)}) copy-start(bf16[768,192]{0,1:T(8,128)(2,1)} %param.23) | copy-start | bytes 884740
  8.2 7.2 %copy-start.2 = (bf16[768,192]{0,1:T(8,128)(2,1)S(1)}, bf16[768,192]{0,1:T(8,128)(2,1)}, u32[]{:S(2)}) copy-start(bf16[768,192]{0,1:T(8,128)(2,1)} %param.24) | copy-start | bytes 884740
  8.2 7.2 %copy-start.3 = (bf16[192,768]{1,0:T(8,128)(2,1)S(1)}, bf16[192,768]{1,0:T(8,128)(2,1)}, u32[]{:S(2)}) copy-start(bf16[192,768]{1,0:T(8,128)(2,1)} %refs_5_.1) | copy-start | bytes 884740
  15.4 9.2 %copy-start.9 = (f32[768]{0:T(1024)S(1)}, f32[768]{0:T(1024)}, u32[]{:S(2)}) copy-start(f32[768]{0:T(1024)} %param.29) | copy-start | bytes 9220
  15.4 9.2 %copy-start.10 = (f32[768]{0:T(1024)S(1)}, f32[768]{0:T(1024)}, u32[]{:S(2)}) copy-start(f32[768]{0:T(1024)} %param.30) | copy-start | bytes 9220
  15.4 9.2 %copy-start.11 = (f32[768]{0:T(1024)S(1)}, f32[768]{0:T(1024)}, u32[]{:S(2)}) copy-start(f32[768]{0:T(1024)} %param.32) | copy-start | bytes 9220
  15.4 9.2 %copy-start.12 = (f32[768]{0:T(1024)S(1)}, f32[768]{0:T(1024)}, u32[]{:S(2)}) copy-start(f32[768]{0:T(1024)} %param.34) | copy-start | bytes 9220
  15.5 19.9 %copy-start.7 = (bf16[4,64,768]{2,1,0:T(8,128)(2,1)S(1)}, bf16[4,64,768]{2,1,0:T(8,128)(2,1)}, u32[]{:S(2)}) copy-start(bf16[4,64,768]{2,1,0:T(8,128)(2,1)} %param.37) | copy-start | bytes 1179652
  15.5 28.3 %copy-start.4 = (bf16[768,768]{1,0:T(8,128)(2,1)S(1)}, bf16[768,768]{1,0:T(8,128)(2,1)}, u32[]{:S(2)}) copy-start(bf16[768,768]{1,0:T(8,128)(2,1)} %refs_12_.1) | copy-start | bytes 3538948
  15.5 28.3 %copy-start.5 = (bf16[768,768]{1,0:T(8,128)(2,1)S(1)}, bf16[768,768]{1,0:T(8,128)(2,1)}, u32[]{:S(2)}) copy-start(bf16[768,768]{1,0:T(8,128)(2,1)} %refs_11_.1) | copy-start | bytes 3538948
  20.2 8.8 %collective-permute-start.3 = (bf16[64,768]{1,0:T(8,128)(2,1)S(1)}, bf16[64,768]{1,0:T(8,128)(2,1)S(1)}, u32[]{:S(2)}, u32[]{:S(2)}) collective-permute-start(bf16[64,768]{1,0:T(8,128)(2,1)S(1)} %get-tuple-element.135), channel_id=1, source_target_pairs={{0,2},{1,3},{2,0},{3,1},{4,6},{5,7},{6,4},{7,5},{8,10},{9,11},{10,... | collective-permute-start | bytes 294920 | tf_op jit(solution)/shard_map/ppermute | solution.py:65
  22.8 6.1 %collective-permute-start.4 = (bf16[64,768]{1,0:T(8,128)(2,1)S(1)}, bf16[64,768]{1,0:T(8,128)(2,1)S(1)}, u32[]{:S(2)}, u32[]{:S(2)}) collective-permute-start(bf16[64,768]{1,0:T(8,128)(2,1)S(1)} %get-tuple-element.136), channel_id=1, source_target_pairs={{0,1},{1,0},{2,3},{3,2},{4,5},{5,4},{6,7},{7,6},{8,9},{9,8},{10,11... | collective-permute-start | bytes 294920 | tf_op jit(solution)/shard_map/ppermute | solution.py:65
  24.4 6.6 %collective-permute-start.5 = (bf16[64,768]{1,0:T(8,128)(2,1)S(1)}, bf16[64,768]{1,0:T(8,128)(2,1)S(1)}, u32[]{:S(2)}, u32[]{:S(2)}) collective-permute-start(bf16[64,768]{1,0:T(8,128)(2,1)S(1)} %get-tuple-element.137), channel_id=1, source_target_pairs={{0,3},{1,2},{2,1},{3,0},{4,7},{5,6},{6,5},{7,4},{8,11},{9,10},{10,... | collective-permute-start | bytes 294920 | tf_op jit(solution)/shard_map/ppermute | solution.py:65
  31.1 11.2 %collective-permute-start.8 = (bf16[64,768]{1,0:T(8,128)(2,1)S(1)}, bf16[64,768]{1,0:T(8,128)(2,1)S(1)}, u32[]{:S(2)}, u32[]{:S(2)}) collective-permute-start(bf16[64,768]{1,0:T(8,128)(2,1)S(1)} %shard_map.324.a0), channel_id=1, source_target_pairs={{0,2},{1,3},{2,0},{3,1},{4,6},{5,7},{6,4},{7,5},{8,10},{9,11},{10,... | collective-permute-start | bytes 294920 | tf_op jit(solution)/shard_map/ppermute | solution.py:65
  34.7 9.0 %collective-permute-start.7 = (bf16[64,768]{1,0:T(8,128)(2,1)S(1)}, bf16[64,768]{1,0:T(8,128)(2,1)S(1)}, u32[]{:S(2)}, u32[]{:S(2)}) collective-permute-start(bf16[64,768]{1,0:T(8,128)(2,1)S(1)} %shard_map.324.a0), channel_id=1, source_target_pairs={{0,3},{1,2},{2,1},{3,0},{4,7},{5,6},{6,5},{7,4},{8,11},{9,10},{10,... | collective-permute-start | bytes 294920 | tf_op jit(solution)/shard_map/ppermute | solution.py:65
  35.2 8.5 %collective-permute-start.6 = (bf16[64,768]{1,0:T(8,128)(2,1)S(1)}, bf16[64,768]{1,0:T(8,128)(2,1)S(1)}, u32[]{:S(2)}, u32[]{:S(2)}) collective-permute-start(bf16[64,768]{1,0:T(8,128)(2,1)S(1)} %shard_map.324.a0), channel_id=1, source_target_pairs={{0,1},{1,0},{2,3},{3,2},{4,5},{5,4},{6,7},{7,6},{8,9},{9,8},{10,11... | collective-permute-start | bytes 294920 | tf_op jit(solution)/shard_map/ppermute | solution.py:65
  35.4 10.3 %collective-permute-start.11 = (bf16[64,768]{1,0:T(8,128)(2,1)S(1)}, bf16[64,768]{1,0:T(8,128)(2,1)S(1)}, u32[]{:S(2)}, u32[]{:S(2)}) collective-permute-start(bf16[64,768]{1,0:T(8,128)(2,1)S(1)} %get-tuple-element.256), channel_id=1, source_target_pairs={{0,24},{8,16},{16,8},{24,0},{1,25},{9,17},{17,9},{25,1},{2,26},{10... | collective-permute-start | bytes 294920 | tf_op jit(solution)/shard_map/ppermute | solution.py:65
  37.9 7.8 %collective-permute-start.10 = (bf16[64,768]{1,0:T(8,128)(2,1)S(1)}, bf16[64,768]{1,0:T(8,128)(2,1)S(1)}, u32[]{:S(2)}, u32[]{:S(2)}) collective-permute-start(bf16[64,768]{1,0:T(8,128)(2,1)S(1)} %get-tuple-element.257), channel_id=1, source_target_pairs={{0,16},{8,24},{16,0},{24,8},{1,17},{9,25},{17,1},{25,9},{2,18},{10... | collective-permute-start | bytes 294920 | tf_op jit(solution)/shard_map/ppermute | solution.py:65
  42.2 17.7 %copy-start.13 = (f32[768]{0:T(1024)S(1)}, f32[768]{0:T(1024)}, u32[]{:S(2)}) copy-start(f32[768]{0:T(1024)} %param.35) | copy-start | bytes 9220
  42.2 17.7 %copy-start.14 = (f32[768]{0:T(1024)S(1)}, f32[768]{0:T(1024)}, u32[]{:S(2)}) copy-start(f32[768]{0:T(1024)} %param.36) | copy-start | bytes 9220
  42.2 4.6 %collective-permute-start.9 = (bf16[64,768]{1,0:T(8,128)(2,1)S(1)}, bf16[64,768]{1,0:T(8,128)(2,1)S(1)}, u32[]{:S(2)}, u32[]{:S(2)}) collective-permute-start(bf16[64,768]{1,0:T(8,128)(2,1)S(1)} %get-tuple-element.258), channel_id=1, source_target_pairs={{0,8},{8,0},{16,24},{24,16},{1,9},{9,1},{17,25},{25,17},{2,10},{10... | collective-permute-start | bytes 294920 | tf_op jit(solution)/shard_map/ppermute | solution.py:65
  46.9 7.9 %collective-permute-start.12 = (bf16[64,768]{1,0:T(8,128)(2,1)S(1)}, bf16[64,768]{1,0:T(8,128)(2,1)S(1)}, u32[]{:S(2)}, u32[]{:S(2)}) collective-permute-start(bf16[64,768]{1,0:T(8,128)(2,1)S(1)} %get-tuple-element.149), channel_id=1, source_target_pairs={{0,2},{1,3},{2,0},{3,1},{4,6},{5,7},{6,4},{7,5},{8,10},{9,11},{10,... | collective-permute-start | bytes 294920 | tf_op jit(solution)/shard_map/ppermute | solution.py:65
  46.9 7.9 %collective-permute-start.13 = (bf16[64,768]{1,0:T(8,128)(2,1)S(1)}, bf16[64,768]{1,0:T(8,128)(2,1)S(1)}, u32[]{:S(2)}, u32[]{:S(2)}) collective-permute-start(bf16[64,768]{1,0:T(8,128)(2,1)S(1)} %get-tuple-element.150), channel_id=1, source_target_pairs={{0,1},{1,0},{2,3},{3,2},{4,5},{5,4},{6,7},{7,6},{8,9},{9,8},{10,11... | collective-permute-start | bytes 294920 | tf_op jit(solution)/shard_map/ppermute | solution.py:65
  49.3 6.6 %collective-permute-start.14 = (bf16[64,768]{1,0:T(8,128)(2,1)S(1)}, bf16[64,768]{1,0:T(8,128)(2,1)S(1)}, u32[]{:S(2)}, u32[]{:S(2)}) collective-permute-start(bf16[64,768]{1,0:T(8,128)(2,1)S(1)} %get-tuple-element.151), channel_id=1, source_target_pairs={{0,3},{1,2},{2,1},{3,0},{4,7},{5,6},{6,5},{7,4},{8,11},{9,10},{10,... | collective-permute-start | bytes 294920 | tf_op jit(solution)/shard_map/ppermute | solution.py:65
  56.0 7.8 %collective-permute-start.17 = (bf16[64,768]{1,0:T(8,128)(2,1)S(1)}, bf16[64,768]{1,0:T(8,128)(2,1)S(1)}, u32[]{:S(2)}, u32[]{:S(2)}) collective-permute-start(bf16[64,768]{1,0:T(8,128)(2,1)S(1)} %shard_map.326.refs_0_), channel_id=1, source_target_pairs={{0,2},{1,3},{2,0},{3,1},{4,6},{5,7},{6,4},{7,5},{8,10},{9,11},{10,... | collective-permute-start | bytes 294920 | tf_op jit(solution)/shard_map/ppermute | solution.py:65
  58.3 6.6 %collective-permute-start.16 = (bf16[64,768]{1,0:T(8,128)(2,1)S(1)}, bf16[64,768]{1,0:T(8,128)(2,1)S(1)}, u32[]{:S(2)}, u32[]{:S(2)}) collective-permute-start(bf16[64,768]{1,0:T(8,128)(2,1)S(1)} %shard_map.326.refs_0_), channel_id=1, source_target_pairs={{0,3},{1,2},{2,1},{3,0},{4,7},{5,6},{6,5},{7,4},{8,11},{9,10},{10,... | collective-permute-start | bytes 294920 | tf_op jit(solution)/shard_map/ppermute | solution.py:65
  60.0 5.9 %collective-permute-start.15 = (bf16[64,768]{1,0:T(8,128)(2,1)S(1)}, bf16[64,768]{1,0:T(8,128)(2,1)S(1)}, u32[]{:S(2)}, u32[]{:S(2)}) collective-permute-start(bf16[64,768]{1,0:T(8,128)(2,1)S(1)} %shard_map.326.refs_0_), channel_id=1, source_target_pairs={{0,1},{1,0},{2,3},{3,2},{4,5},{5,4},{6,7},{7,6},{8,9},{9,8},{10,11... | collective-permute-start | bytes 294920 | tf_op jit(solution)/shard_map/ppermute | solution.py:65
  68.1 6.6 %collective-permute-start.18 = (bf16[64,768]{1,0:T(8,128)(2,1)S(1)}, bf16[64,768]{1,0:T(8,128)(2,1)S(1)}, u32[]{:S(2)}, u32[]{:S(2)}) collective-permute-start(bf16[64,768]{1,0:T(8,128)(2,1)S(1)} %get-tuple-element.161), channel_id=1, source_target_pairs={{0,2},{1,3},{2,0},{3,1},{4,6},{5,7},{6,4},{7,5},{8,10},{9,11},{10,... | collective-permute-start | bytes 294920 | tf_op jit(solution)/shard_map/ppermute | solution.py:65
  68.8 6.0 %collective-permute-start.19 = (bf16[64,768]{1,0:T(8,128)(2,1)S(1)}, bf16[64,768]{1,0:T(8,128)(2,1)S(1)}, u32[]{:S(2)}, u32[]{:S(2)}) collective-permute-start(bf16[64,768]{1,0:T(8,128)(2,1)S(1)} %get-tuple-element.162), channel_id=1, source_target_pairs={{0,1},{1,0},{2,3},{3,2},{4,5},{5,4},{6,7},{7,6},{8,9},{9,8},{10,11... | collective-permute-start | bytes 294920 | tf_op jit(solution)/shard_map/ppermute | solution.py:65
  70.4 6.5 %collective-permute-start.20 = (bf16[64,768]{1,0:T(8,128)(2,1)S(1)}, bf16[64,768]{1,0:T(8,128)(2,1)S(1)}, u32[]{:S(2)}, u32[]{:S(2)}) collective-permute-start(bf16[64,768]{1,0:T(8,128)(2,1)S(1)} %get-tuple-element.163), channel_id=1, source_target_pairs={{0,3},{1,2},{2,1},{3,0},{4,7},{5,6},{6,5},{7,4},{8,11},{9,10},{10,... | collective-permute-start | bytes 294920 | tf_op jit(solution)/shard_map/ppermute | solution.py:65
  73.7 6.8 %collective-permute-start.33 = (bf16[768,768]{1,0:T(8,128)(2,1)S(1)}, bf16[768,768]{1,0:T(8,128)(2,1)S(1)}, u32[]{:S(2)}, u32[]{:S(2)}) collective-permute-start(bf16[768,768]{1,0:T(8,128)(2,1)S(1)} %shard_map.335), channel_id=1, source_target_pairs={{0,4},{4,0},{1,5},{5,1},{2,6},{6,2},{3,7},{7,3},{8,12},{12,8},{9,1... | collective-permute-start | bytes 3538952 | tf_op jit(solution)/shard_map/ppermute | solution.py:65
  76.9 8.1 %collective-permute-start.23 = (bf16[64,768]{1,0:T(8,128)(2,1)S(1)}, bf16[64,768]{1,0:T(8,128)(2,1)S(1)}, u32[]{:S(2)}, u32[]{:S(2)}) collective-permute-start(bf16[64,768]{1,0:T(8,128)(2,1)S(1)} %shard_map.328.refs_0_), channel_id=1, source_target_pairs={{0,2},{1,3},{2,0},{3,1},{4,6},{5,7},{6,4},{7,5},{8,10},{9,11},{10,... | collective-permute-start | bytes 294920 | tf_op jit(solution)/shard_map/ppermute | solution.py:65
  77.0 8.0 %collective-permute-start.22 = (bf16[64,768]{1,0:T(8,128)(2,1)S(1)}, bf16[64,768]{1,0:T(8,128)(2,1)S(1)}, u32[]{:S(2)}, u32[]{:S(2)}) collective-permute-start(bf16[64,768]{1,0:T(8,128)(2,1)S(1)} %shard_map.328.refs_0_), channel_id=1, source_target_pairs={{0,3},{1,2},{2,1},{3,0},{4,7},{5,6},{6,5},{7,4},{8,11},{9,10},{10,... | collective-permute-start | bytes 294920 | tf_op jit(solution)/shard_map/ppermute | solution.py:65
  79.2 6.3 %collective-permute-start.21 = (bf16[64,768]{1,0:T(8,128)(2,1)S(1)}, bf16[64,768]{1,0:T(8,128)(2,1)S(1)}, u32[]{:S(2)}, u32[]{:S(2)}) collective-permute-start(bf16[64,768]{1,0:T(8,128)(2,1)S(1)} %shard_map.328.refs_0_), channel_id=1, source_target_pairs={{0,1},{1,0},{2,3},{3,2},{4,5},{5,4},{6,7},{7,6},{8,9},{9,8},{10,11... | collective-permute-start | bytes 294920 | tf_op jit(solution)/shard_map/ppermute | solution.py:65
  81.9 8.2 %collective-permute-start.34 = (bf16[192,768]{1,0:T(8,128)(2,1)S(1)}, bf16[192,768]{1,0:T(8,128)(2,1)S(1)}, u32[]{:S(2)}, u32[]{:S(2)}) collective-permute-start(bf16[192,768]{1,0:T(8,128)(2,1)S(1)} %get-tuple-element.205), channel_id=1, source_target_pairs={{0,8},{8,0},{16,24},{24,16},{1,9},{9,1},{17,25},{25,17},{2,10},{10... | collective-permute-start | bytes 884744 | tf_op jit(solution)/shard_map/ppermute | solution.py:65
  83.5 6.7 %collective-permute-start.35 = (bf16[192,768]{1,0:T(8,128)(2,1)S(1)}, bf16[192,768]{1,0:T(8,128)(2,1)S(1)}, u32[]{:S(2)}, u32[]{:S(2)}) collective-permute-start(bf16[192,768]{1,0:T(8,128)(2,1)S(1)} %get-tuple-element.206), channel_id=1, source_target_pairs={{0,16},{8,24},{16,0},{24,8},{1,17},{9,25},{17,1},{25,9},{2,18},{10... | collective-permute-start | bytes 884744 | tf_op jit(solution)/shard_map/ppermute | solution.py:65
  91.6 6.7 %collective-permute-start.36 = (bf16[512,768]{1,0:T(8,128)(2,1)S(1)}, bf16[512,768]{1,0:T(8,128)(2,1)S(1)}, u32[]{:S(2)}, u32[]{:S(2)}) collective-permute-start(bf16[512,768]{1,0:T(8,128)(2,1)S(1)} %get-tuple-element.214), channel_id=1, source_target_pairs={{0,4},{4,0},{1,5},{5,1},{2,6},{6,2},{3,7},{7,3},{8,12},{12,8},{9,1... | collective-permute-start | bytes 2359304 | tf_op jit(solution)/shard_map/ppermute | solution.py:65
  91.7 13.2 %collective-permute-start.24 = (bf16[128,768]{1,0:T(8,128)(2,1)S(1)}, bf16[128,768]{1,0:T(8,128)(2,1)S(1)}, u32[]{:S(2)}, u32[]{:S(2)}) collective-permute-start(bf16[128,768]{1,0:T(8,128)(2,1)S(1)} %get-tuple-element.179), channel_id=1, source_target_pairs={{0,2},{1,3},{2,0},{3,1},{4,6},{5,7},{6,4},{7,5},{8,10},{9,11},{10,... | collective-permute-start | bytes 589832 | tf_op jit(solution)/shard_map/ppermute | solution.py:65
  92.9 12.0 %collective-permute-start.25 = (bf16[128,768]{1,0:T(8,128)(2,1)S(1)}, bf16[128,768]{1,0:T(8,128)(2,1)S(1)}, u32[]{:S(2)}, u32[]{:S(2)}) collective-permute-start(bf16[128,768]{1,0:T(8,128)(2,1)S(1)} %get-tuple-element.180), channel_id=1, source_target_pairs={{0,1},{1,0},{2,3},{3,2},{4,5},{5,4},{6,7},{7,6},{8,9},{9,8},{10,11... | collective-permute-start | bytes 589832 | tf_op jit(solution)/shard_map/ppermute | solution.py:65
  94.5 14.2 %collective-permute-start.26 = (bf16[128,768]{1,0:T(8,128)(2,1)S(1)}, bf16[128,768]{1,0:T(8,128)(2,1)S(1)}, u32[]{:S(2)}, u32[]{:S(2)}) collective-permute-start(bf16[128,768]{1,0:T(8,128)(2,1)S(1)} %get-tuple-element.181), channel_id=1, source_target_pairs={{0,3},{1,2},{2,1},{3,0},{4,7},{5,6},{6,5},{7,4},{8,11},{9,10},{10,... | collective-permute-start | bytes 589832 | tf_op jit(solution)/shard_map/ppermute | solution.py:65
  99.3 13.1 %collective-permute-start.37 = (bf16[224,768]{1,0:T(8,128)(2,1)S(1)}, bf16[224,768]{1,0:T(8,128)(2,1)S(1)}, u32[]{:S(2)}, u32[]{:S(2)}) collective-permute-start(bf16[224,768]{1,0:T(8,128)(2,1)S(1)} %get-tuple-element.220), channel_id=1, source_target_pairs={{0,8},{8,0},{16,24},{24,16},{1,9},{9,1},{17,25},{25,17},{2,10},{10... | collective-permute-start | bytes 1032200 | tf_op jit(solution)/shard_map/ppermute | solution.py:65
  100.8 11.6 %collective-permute-start.38 = (bf16[224,768]{1,0:T(8,128)(2,1)S(1)}, bf16[224,768]{1,0:T(8,128)(2,1)S(1)}, u32[]{:S(2)}, u32[]{:S(2)}) collective-permute-start(bf16[224,768]{1,0:T(8,128)(2,1)S(1)} %get-tuple-element.221), channel_id=1, source_target_pairs={{0,16},{8,24},{16,0},{24,8},{1,17},{9,25},{17,1},{25,9},{2,18},{10... | collective-permute-start | bytes 1032200 | tf_op jit(solution)/shard_map/ppermute | solution.py:65
  108.8 6.6 %collective-permute-start.27 = (bf16[96,768]{1,0:T(8,128)(2,1)S(1)}, bf16[96,768]{1,0:T(8,128)(2,1)S(1)}, u32[]{:S(2)}, u32[]{:S(2)}) collective-permute-start(bf16[96,768]{1,0:T(8,128)(2,1)S(1)} %get-tuple-element.189), channel_id=1, source_target_pairs={{0,16},{8,24},{16,0},{24,8},{1,17},{9,25},{17,1},{25,9},{2,18},{10... | collective-permute-start | bytes 442376 | tf_op jit(solution)/shard_map/ppermute | solution.py:65
  110.4 6.8 %collective-permute-start.28 = (bf16[96,768]{1,0:T(8,128)(2,1)S(1)}, bf16[96,768]{1,0:T(8,128)(2,1)S(1)}, u32[]{:S(2)}, u32[]{:S(2)}) collective-permute-start(bf16[96,768]{1,0:T(8,128)(2,1)S(1)} %get-tuple-element.190), channel_id=1, source_target_pairs={{0,8},{8,0},{16,24},{24,16},{1,9},{9,1},{17,25},{25,17},{2,10},{10... | collective-permute-start | bytes 442376 | tf_op jit(solution)/shard_map/ppermute | solution.py:65
  111.7 8.2 %collective-permute-start.29 = (bf16[96,768]{1,0:T(8,128)(2,1)S(1)}, bf16[96,768]{1,0:T(8,128)(2,1)S(1)}, u32[]{:S(2)}, u32[]{:S(2)}) collective-permute-start(bf16[96,768]{1,0:T(8,128)(2,1)S(1)} %get-tuple-element.191), channel_id=1, source_target_pairs={{0,24},{8,16},{16,8},{24,0},{1,25},{9,17},{17,9},{25,1},{2,26},{10... | collective-permute-start | bytes 442376 | tf_op jit(solution)/shard_map/ppermute | solution.py:65
  112.5 14.5 %collective-permute-start.39 = (bf16[256,768]{1,0:T(8,128)(2,1)S(1)}, bf16[256,768]{1,0:T(8,128)(2,1)S(1)}, u32[]{:S(2)}, u32[]{:S(2)}) collective-permute-start(bf16[256,768]{1,0:T(8,128)(2,1)S(1)} %get-tuple-element.224.sent1), channel_id=1, source_target_pairs={{0,8},{8,0},{16,24},{24,16},{1,9},{9,1},{17,25},{25,17},{2,10},{10... | collective-permute-start | bytes 1179656 | tf_op jit(solution)/shard_map/ppermute | solution.py:65
  113.9 13.2 %collective-permute-start.40 = (bf16[256,768]{1,0:T(8,128)(2,1)S(1)}, bf16[256,768]{1,0:T(8,128)(2,1)S(1)}, u32[]{:S(2)}, u32[]{:S(2)}) collective-permute-start(bf16[256,768]{1,0:T(8,128)(2,1)S(1)} %get-tuple-element.225.sent2), channel_id=1, source_target_pairs={{0,16},{8,24},{16,0},{24,8},{1,17},{9,25},{17,1},{25,9},{2,18},{10... | collective-permute-start | bytes 1179656 | tf_op jit(solution)/shard_map/ppermute | solution.py:65
  119.9 18.4 %collective-permute-start.32 = (bf16[128,768]{1,0:T(8,128)(2,1)S(1)}, bf16[128,768]{1,0:T(8,128)(2,1)S(1)}, u32[]{:S(2)}, u32[]{:S(2)}) collective-permute-start(bf16[128,768]{1,0:T(8,128)(2,1)S(1)} %shard_map.334.t0), channel_id=1, source_target_pairs={{0,2},{1,3},{2,0},{3,1},{4,6},{5,7},{6,4},{7,5},{8,10},{9,11},{10,... | collective-permute-start | bytes 589832 | tf_op jit(solution)/shard_map/ppermute | solution.py:65
  125.3 13.0 %collective-permute-start.31 = (bf16[128,768]{1,0:T(8,128)(2,1)S(1)}, bf16[128,768]{1,0:T(8,128)(2,1)S(1)}, u32[]{:S(2)}, u32[]{:S(2)}) collective-permute-start(bf16[128,768]{1,0:T(8,128)(2,1)S(1)} %shard_map.334.t0), channel_id=1, source_target_pairs={{0,3},{1,2},{2,1},{3,0},{4,7},{5,6},{6,5},{7,4},{8,11},{9,10},{10,... | collective-permute-start | bytes 589832 | tf_op jit(solution)/shard_map/ppermute | solution.py:65
  126.7 11.7 %collective-permute-start.30 = (bf16[128,768]{1,0:T(8,128)(2,1)S(1)}, bf16[128,768]{1,0:T(8,128)(2,1)S(1)}, u32[]{:S(2)}, u32[]{:S(2)}) collective-permute-start(bf16[128,768]{1,0:T(8,128)(2,1)S(1)} %shard_map.334.t0), channel_id=1, source_target_pairs={{0,1},{1,0},{2,3},{3,2},{4,5},{5,4},{6,7},{7,6},{8,9},{9,8},{10,11... | collective-permute-start | bytes 589832 | tf_op jit(solution)/shard_map/ppermute | solution.py:65
  127.1 4.7 %collective-permute-start.41 = (bf16[64,768]{1,0:T(8,128)(2,1)S(1)}, bf16[64,768]{1,0:T(8,128)(2,1)S(1)}, u32[]{:S(2)}, u32[]{:S(2)}) collective-permute-start(bf16[64,768]{1,0:T(8,128)(2,1)S(1)} %get-tuple-element.227.mid1), channel_id=1, source_target_pairs={{0,8},{8,0},{16,24},{24,16},{1,9},{9,1},{17,25},{25,17},{2,10},{10... | collective-permute-start | bytes 294920 | tf_op jit(solution)/shard_map/ppermute | solution.py:65
  128.7 4.7 %collective-permute-start.42 = (bf16[64,768]{1,0:T(8,128)(2,1)S(1)}, bf16[64,768]{1,0:T(8,128)(2,1)S(1)}, u32[]{:S(2)}, u32[]{:S(2)}) collective-permute-start(bf16[64,768]{1,0:T(8,128)(2,1)S(1)} %get-tuple-element.228.mid2), channel_id=1, source_target_pairs={{0,16},{8,24},{16,0},{24,8},{1,17},{9,25},{17,1},{25,9},{2,18},{10... | collective-permute-start | bytes 294920 | tf_op jit(solution)/shard_map/ppermute | solution.py:65
  133.5 7.3 %collective-permute-start.43 = (bf16[224,768]{1,0:T(8,128)(2,1)S(1)}, bf16[224,768]{1,0:T(8,128)(2,1)S(1)}, u32[]{:S(2)}, u32[]{:S(2)}) collective-permute-start(bf16[224,768]{1,0:T(8,128)(2,1)S(1)} %get-tuple-element.229.along1), channel_id=1, source_target_pairs={{0,8},{8,0},{16,24},{24,16},{1,9},{9,1},{17,25},{25,17},{2,10},{10... | collective-permute-start | bytes 1032200 | tf_op jit(solution)/shard_map/ppermute | solution.py:65
  133.9 7.2 %collective-permute-start.44 = (bf16[224,768]{1,0:T(8,128)(2,1)S(1)}, bf16[224,768]{1,0:T(8,128)(2,1)S(1)}, u32[]{:S(2)}, u32[]{:S(2)}) collective-permute-start(bf16[224,768]{1,0:T(8,128)(2,1)S(1)} %get-tuple-element.230.along2), channel_id=1, source_target_pairs={{0,16},{8,24},{16,0},{24,8},{1,17},{9,25},{17,1},{25,9},{2,18},{10... | collective-permute-start | bytes 1032200 | tf_op jit(solution)/shard_map/ppermute | solution.py:65
  141.9 4.0 %collective-permute-start.46 = (bf16[768,768]{1,0:T(8,128)(2,1)S(1)}, bf16[768,768]{1,0:T(8,128)(2,1)S(1)}, u32[]{:S(2)}, u32[]{:S(2)}) collective-permute-start(bf16[768,768]{1,0:T(8,128)(2,1)S(1)} %get-tuple-element.231.mine), channel_id=1, source_target_pairs={{0,4},{4,0},{1,5},{5,1},{2,6},{6,2},{3,7},{7,3},{8,12},{12,8},{9,1... | collective-permute-start | bytes 3538952 | tf_op jit(solution)/shard_map/ppermute | solution.py:65
  142.0 4.0 %collective-permute-start.45 = (bf16[512,768]{1,0:T(8,128)(2,1)S(1)}, bf16[512,768]{1,0:T(8,128)(2,1)S(1)}, u32[]{:S(2)}, u32[]{:S(2)}) collective-permute-start(bf16[512,768]{1,0:T(8,128)(2,1)S(1)} %get-tuple-element.233.mine), channel_id=1, source_target_pairs={{0,4},{4,0},{1,5},{5,1},{2,6},{6,2},{3,7},{7,3},{8,12},{12,8},{9,1... | collective-permute-start | bytes 2359304 | tf_op jit(solution)/shard_map/ppermute | solution.py:65
  (1 other events, 6.0 us)

commit v5 on v4

--- a/solution.py
+++ b/solution.py
@@ -166,9 +166,12 @@
         return carry
 
     lax.fori_loop(0, full // rows, step, 0)
+    lane = lax.broadcasted_iota(jnp.int32, (1, out.shape[1]), 1)
+    line = jnp.zeros((1, out.shape[1]), F32)
     for row in range(heads * BASES):
         col = jnp.sum(jnp.sum(acc[row], axis=0, keepdims=True), axis=1, keepdims=True)
-        out[row : row + 1, :] = jnp.broadcast_to(col, (1, out.shape[1]))
+        line = jnp.where(lane == row, col, line)
+    out[...] = jnp.broadcast_to(line, out.shape)
 
 
 def attend_body(heads, query_scale, ids, *refs):
@@ -358,30 +361,43 @@
     first_step(ids[0], lambda at: scr[at, :], kept, (rows, along1), (rows, along2))
 
 
-def step_a_body(ids, keep, arrived, rel, feed_kept, came1, came2, kept, feed_own, along1, along2, scr):
-    rows = keep.shape[0] // 4
-    scr[...] = keep[...] + arrived[...].astype(F32)
-    scr[-rel.shape[0] :, : rel.shape[1]] = rel[...]
-    first_step(ids[0], lambda at: scr[at, :], kept, (rows, along1), (rows, along2))
-    second_step(feed_kept, came1, came2, feed_own, along1.at[rows:, :], along2.at[rows:, :])
-
-
-def step_b_body(kept, feed_own, came1, came2, own, along1, along2):
+def low_sum(a, b):
+    return a.astype(F32) + b.astype(F32)
+
+
+def step_a_body(
+    ids, keep, arrived, small, rel, feed_kept, came1, came2, kept, feed_own, along1, along2, scr, small_scr
+):
+    size = keep.shape[0]
+    few = size // 8
+    scr[...] = keep[...] + arrived[:size, :].astype(F32)
+    first_step(ids[0], lambda at: scr[at, :], kept, (2 * few, along1), (2 * few, along2))
+    at = slice(2 * few, 2 * few + feed_own.shape[0] // 2)
+    second_step(feed_kept, came1, came2, feed_own, along1.at[at, :], along2.at[at, :])
+    small_scr[...] = low_sum(small[...].astype(LOW), arrived[size:, :])
+    small_scr[8:9, : rel.shape[1]] = rel[:1, :]
+    along1[at.stop :, :] = small_scr[...].astype(LOW)
+
+
+def step_b_body(kept, feed_own, sent1, came1, came2, own, along1, along2):
     few = own.shape[0] // 2
-    skip = 2 * few
-    first = slice(0, skip)
-    second_step(
-        kept, came1.at[first, :], came2.at[first, :], own, along1.at[slice(0, few), :], along2.at[slice(0, few), :]
-    )
-    upper, lower = last_sums(feed_own, came1.at[skip:, :], came2.at[skip:, :])
+    rows = feed_own.shape[0] // 2
+    first, at, last = slice(0, 2 * few), slice(2 * few, 2 * few + rows), slice(2 * few + rows, None)
+    head = slice(0, few)
+    second_step(kept, came1.at[first, :], came2.at[first, :], own, along1.at[head, :], along2.at[head, :])
+    upper, lower = last_sums(feed_own, came1.at[at, :], came2.at[at, :])
     for out, parts in ((along1, (lower, upper)), (along2, (upper, lower))):
         for n, part in enumerate(parts):
-            out[few + n * part.shape[0] : few + (n + 1) * part.shape[0], :] = part
-
-
-def step_c_body(own, came1, came2, along1, along2):
-    first = slice(0, along1.shape[0])
-    along2[...], along1[...] = last_sums(own, came1.at[first, :], came2.at[first, :])
+            out[few + n * rows : few + (n + 1) * rows, :] = part
+    along2[few + 2 * rows :, :] = low_sum(sent1[last, :], came1[last, :]).astype(LOW)
+
+
+def step_c_body(own, sent2, came1, came2, along1, along2, small_out):
+    few = along1.shape[0]
+    head = slice(0, few)
+    last = slice(came1.shape[0], None)
+    along2[...], along1[...] = last_sums(own, came1.at[head, :], came2.at[head, :])
+    small_out[...] = low_sum(sent2[last, :], came2[last, :]).astype(LOW)
 
 
 def step_d_body(mid1, mid2, came1, came2, near1, near2, along1, along2):
@@ -393,8 +409,10 @@
         out[2 * few :, :] = near[few : few + done, :]
 
 
-def joins_body(ids, along1, along2, came1, came2, sent1, sent2, near1, near2, seen, attend_out, out):
-    join_half(ids[0], along1, along2, came1, came2, attend_out)
+def joins_body(ids, along1, along2, came1, came2, sent1, sent2, near1, near2, small, seen, attend_out, out):
+    size = attend_out.shape[0] - small.shape[0]
+    join_half(ids[0], along1, along2, came1, came2, attend_out.at[:size, :])
+    attend_out[size:, :] = small[...]
     rows = out.shape[0] // 8
     few = sent1.shape[0] - 2 * rows
     skip = came1.shape[0] - rows
@@ -468,21 +486,26 @@
             o[k][to, :] = result[rows(k), :].astype(LOW)
 
 
-def attend_weights_body(ids, x, grad, stack, ct, small_feed, small_attend, sums, keep, send, scr):
+def attend_weights_body(ids, x, grad, stack, ct, small_feed, small_attend, sums, keep, send, small_out):
     part = ct.shape[0]
     heads = sums.shape[0]
     product = mm(stack[...], x[...])
-    scr[0, part : 2 * part, :] = product[:part]
-    scr[1, :part, :] = product[part : 2 * part]
-    scr[0, :part, :] = product[2 * part :]
-    scr[1, part : 2 * part, :] = mm(ct[...], grad[...])
-    scr[:, 2 * part :, :] = jnp.zeros((2, scr.shape[1] - 2 * part, scr.shape[2]), F32)
-    scr[0, 2 * part : 2 * part + SMALL_ROWS, :] = small_feed[...]
-    scr[0, 2 * part + SMALL_ROWS : 2 * part + 2 * SMALL_ROWS, :] = small_attend[...]
-    for h in range(heads):
-        scr[1, 2 * part + h * SMALL_ROWS : 2 * part + (h + 1) * SMALL_ROWS, : sums.shape[2]] = sums[h]
-    keep[...] = scr[ids[2]]
-    send[...] = scr[1 - ids[2]].astype(LOW)
+    outer = mm(ct[...], grad[...])
+    rows = (product[2 * part :], product[:part], product[part : 2 * part], outer)
+    for half in (0, 1):
+        for c, out in ((half, keep), (1 - half, send)):
+
+            @pl.when(ids[2] == c)
+            def _(half=half, out=out):
+                for n in (0, 1):
+                    out[n * part : (n + 1) * part, :] = rows[2 * half + n].astype(out.dtype)
+
+    small_out[...] = jnp.zeros_like(small_out)
+    small_out[:4, :] = small_feed[:4, :]
+    small_out[4:7, :] = small_attend[:3, :]
+    line = [sums[h, at : at + 1, :] for at in (0, 8) for h in range(heads)]
+    small_out[7:8, : 2 * part] = jnp.concatenate(line, axis=1)
+    send[2 * part :, :] = small_out[...].astype(LOW)
 
 
 def total_body(r1, r2, r3, own, out):
@@ -545,7 +568,6 @@
 def unpack_attend(ids, mine, other, rows_out, query_out, value_out, rel_out, larges, scr, sem):
     part = larges[0].shape[0]
     heads = rel_out.shape[0]
-    head = part // heads
     send, wait = sender(sem)
     for c, (a, b) in ((0, (mine, other)), (1, (other, mine))):
 
@@ -556,26 +578,15 @@
 
     for n, out in enumerate(larges):
         send(scr.at[n], out)
-    for c, (a, b) in ((0, (mine, other)), (1, (other, mine))):
-
-        @pl.when(ids[2] == c)
-        def _(a=a, b=b):
-            small_a = a[2 * part :, :].astype(F32)
-            small_b = b[2 * part :, :].astype(F32)
-            for n, out in enumerate(rows_out):
-                row = n if n < 4 else SMALL_ROWS + n - 4
-                out[...] = small_a[row, :]
-            for out, row in ((query_out, 0), (value_out, 8)):
-                out[...] = jnp.concatenate(
-                    [small_b[h * SMALL_ROWS + row : h * SMALL_ROWS + row + 1, :head] for h in range(heads)], axis=1
-                )[0]
-            last = small_a.shape[0] - 32
-            table = small_a[last:, :128] + small_b[last:, :128]
-            for h in range(heads):
-                for index in range(BASES):
-                    at = h * BASES + index
-                    rel_out[h : h + 1, index : index + 1] = table[at : at + 1, :1]
-
+    last = slice(2 * part, None)
+    small = mine[last, :].astype(F32)
+    for row, out in enumerate(rows_out):
+        out[...] = small[row, :]
+    query_out[...] = small[7, :part]
+    value_out[...] = small[7, part : 2 * part]
+    line = small[8:9, :128] + other[last, :128].astype(F32)[8:9, :]
+    for h in range(heads):
+        rel_out[h : h + 1, :] = line[:, h * BASES : (h + 1) * BASES]
     wait()
 
 
@@ -762,33 +773,33 @@
     )
     rel = kernel(
         functools.partial(rel_body, heads, block_len, 32),
-        f32(32, 128),
+        f32(8, 128),
         (ids, scores),
         smem=1,
         scratch=[pltpu.VMEM((heads * BASES, 8, slots), F32)],
         micros=0.1,
     )
-    half_rows = 2 * part + 128
-    attend_keep, attend_send = kernel(
+    half_rows = 2 * part
+    attend_keep, attend_send, small = kernel(
         attend_weights_body,
-        [f32(half_rows, width), low(half_rows, width)],
+        [f32(half_rows, width), low(half_rows + SMALL_ROWS, width), f32(SMALL_ROWS, width)],
         (ids, after(tokens, came), grad_attended, stack, ct, small_feed, small_attend, sums),
         smem=1,
-        scratch=[pltpu.VMEM((2, half_rows, width), F32)],
         micros=0.1,
     )
-    landed = scatter_low((o1, o2, o3), "mp", mp_size)
+    landed = ordered((o1, o2, o3), "mp", mp_size, [1, 2, 3])
     attend_arrived = swap(attend_send, "dp", dp_size, 1)
     few = half_rows // 8
     attend_kept, feed_own, along1, along2 = kernel(
         step_a_body,
-        [f32(4 * few, width), f32(2 * rows, width)] + [low(2 * few + rows, width)] * 2,
-        (ids, attend_keep, attend_arrived, rel, feed_kept, *came),
-        smem=1,
-        scratch=[pltpu.VMEM((half_rows, width), F32)],
+        [f32(4 * few, width), f32(2 * rows, width)]
+        + [low(2 * few + rows + SMALL_ROWS, width), low(2 * few + rows, width)],
+        (ids, attend_keep, attend_arrived, small, rel, feed_kept, *came),
+        smem=1,
+        scratch=[pltpu.VMEM((half_rows, width), F32), pltpu.VMEM((SMALL_ROWS, width), F32)],
         micros=0.1,
     )
-    met = kernel(touch_body, low(SMALL_ROWS, width), tuple(landed), micros=6.0)
+    met = kernel(touch_body, low(SMALL_ROWS, width), tuple(landed), micros=4.2)
     quarter = block_len // 4
     q0, *q = kernel(
         quarters_body,
@@ -798,18 +809,21 @@
     )
     attend_own, sent1, sent2 = kernel(
         step_b_body,
-        [f32(2 * few, width)] + [low(few + 2 * rows, width)] * 2,
-        (attend_kept, after(feed_own, q0), *both_ways(along1, along2, seq_size)),
+        [f32(2 * few, width), low(few + 2 * rows, width), low(few + 2 * rows + SMALL_ROWS, width)],
+        (attend_kept, after(feed_own, q0), along1, *both_ways(along1, along2, seq_size)),
         micros=0.1,
     )
     near = both_ways(sent1, sent2, seq_size)
     q = [swap(q[k - 1], "seq", seq_size, k) for k in [2, 1, 3]]
     q = deep(q)
     q = [q[[2, 1, 3].index(k)] for k in range(1, 4)]
-    joined = kernel(join_body, low(block_len, width), (q0, *q), micros=8.0)
+    joined = kernel(join_body, low(block_len, width), (q0, *q), micros=6.8)
     spread = gather_low(joined, "mp", mp_size)
-    mid = kernel(
-        step_c_body, [low(few, width)] * 2, (after(attend_own, joined), *near), micros=0.1
+    *mid, small = kernel(
+        step_c_body,
+        [low(few, width)] * 2 + [low(SMALL_ROWS, width)],
+        (after(attend_own, joined), sent2, *near),
+        micros=0.1,
     )
     output_all = kernel(output_body, low(4, half, width), (ids, outputs[0], *q), smem=1, micros=0.1)
     along1, along2 = kernel(
@@ -819,11 +833,11 @@
         micros=0.1,
     )
     came = both_ways(along1, along2, seq_size)
-    seen = kernel(touch_body, low(SMALL_ROWS, width), tuple(spread), micros=8.0)
+    seen = kernel(touch_body, low(SMALL_ROWS, width), tuple(spread), micros=7.0)
     attend_mine, feed_mine = kernel(
         joins_body,
-        [low(half_rows, width), low(width, width)],
-        (ids, along1, along2, *came, sent1, sent2, *near, seen),
+        [low(half_rows + SMALL_ROWS, width), low(width, width)],
+        (ids, along1, along2, *came, sent1, sent2, *near, small, seen),
         smem=1,
         micros=0.2,
     )

time: 152 us -> 151 us (level)
  transfers between devices with their start and end apart: 47 -> 47, of which waited for: 26 -> 25; matrix products, arithmetic and copies ran while one was open for 1% -> 1% of each run, Pallas kernels for 12% -> 12%
where the time goes in v5:
time: 151 us; the launch traced here: 150 us
  starting transfers between devices  65.2 us (43%)
  waiting for transfers between devices  49.2 us (33%)
  Pallas kernels  31.2 us (21%)
  local copies, waits for them, and re-layouts  2.24 us (1%)
    ppermute x47, starting transfers between devices, swap(): return lax.ppermute(block, axis, [(s, s ^ k) for s in range(size)])  65.2 us
    ppermute x47, waiting for transfers between devices, swap(): return lax.ppermute(block, axis, [(s, s ^ k) for s in range(size)])  49.2 us
    pallas_call x25, Pallas kernels, kernel(): pl.pallas_call(body, out_shape=outs, in_specs=in_specs, out_specs=out_spe...  31.2 us
  transfers between devices with their start and end apart: 47, of which 25 were waited for; matrix products, arithmetic and copies ran while one was open for 1% of the time, Pallas kernels for 12%

profile of v5, /device:TPU:0, one launch (start us, length us, event | category | flops | bytes accessed | tf_op | source)
XLA Modules:
  0.0 149.8 jit_solution(2818690791505466508)
XLA Ops:
  0.7 1.3 dynamic-slice_bitcast_fusion
  2.0 4.0 %collective-permute-start.2 = (bf16[128,768]{1,0:T(8,128)(2,1)S(1)}, bf16[128,768]{1,0:T(8,128)(2,1)S(1)}, u32[]{:S(2)}, u32[]{:S(2)}) collective-permute-start(bf16[128,768]{1,0:T(8,128)(2,1)S(1)} %get-tuple-element.256), channel_id=1, source_target_pairs={{0,24},{8,16},{16,8},{24,0},{1,25},{9,17},{17,9},{25,1},{2,26},{10... | collective-permute-start | bytes 589832 | tf_op jit(solution)/shard_map/ppermute | solution.py:65
  8.2 2.1 %shard_map.322.refs_11_ = f32[3,512,256]{2,1,0:T(8,128)S(1)} custom-call(s32[4]{0:T(128)S(1)} %pad_add_fusion.ids, f32[3,8]{1,0:T(4,128)S(1)} %copy-done.6), custom_call_target="tpu_custom_call" | custom-call | flops 1200000000 | bytes 9000000 | tf_op jit(solution)/shard_map/pallas_call | solution.py:37
  10.3 1.4 collective-permute-done.2.refs_3_
  11.7 3.7 %collective-permute-done.refs_1_ = bf16[128,768]{1,0:T(8,128)(2,1)S(1)} collective-permute-done((bf16[128,768]{1,0:T(8,128)(2,1)S(1)}, bf16[128,768]{1,0:T(8,128)(2,1)S(1)}, u32[]{:S(2)}, u32[]{:S(2)}) %collective-permute-start) | collective-permute-done | bytes 196640 | tf_op jit(solution)/shard_map/ppermute | solution.py:65
  15.5 4.7 %shard_map.323 = (f32[64,768]{1,0:T(8,128)S(1)}, bf16[64,768]{1,0:T(8,128)(2,1)S(1)}, bf16[64,768]{1,0:T(8,128)(2,1)S(1)}, bf16[64,768]{1,0:T(8,128)(2,1)S(1)}, ...) custom-call(s32[4]{0:T(128)S(1)} %pad_add_fusion.ids, ...), custom_call_target="tpu_custom_call" | custom-call | flops 2000000000 | bytes 15000000 | tf_op jit(solution)/shard_map/pallas_call | solution.py:37
  20.2 2.7 %collective-permute-start.3 = (bf16[64,768]{1,0:T(8,128)(2,1)S(1)}, bf16[64,768]{1,0:T(8,128)(2,1)S(1)}, u32[]{:S(2)}, u32[]{:S(2)}) collective-permute-start(bf16[64,768]{1,0:T(8,128)(2,1)S(1)} %get-tuple-element.137), channel_id=1, source_target_pairs={{0,2},{1,3},{2,0},{3,1},{4,6},{5,7},{6,4},{7,5},{8,10},{9,11},{10,... | collective-permute-start | bytes 294920 | tf_op jit(solution)/shard_map/ppermute | solution.py:65
  22.8 1.6 %collective-permute-start.4 = (bf16[64,768]{1,0:T(8,128)(2,1)S(1)}, bf16[64,768]{1,0:T(8,128)(2,1)S(1)}, u32[]{:S(2)}, u32[]{:S(2)}) collective-permute-start(bf16[64,768]{1,0:T(8,128)(2,1)S(1)} %get-tuple-element.138), channel_id=1, source_target_pairs={{0,1},{1,0},{2,3},{3,2},{4,5},{5,4},{6,7},{7,6},{8,9},{9,8},{10,11... | collective-permute-start | bytes 294920 | tf_op jit(solution)/shard_map/ppermute | solution.py:65
  24.7 4.3 %collective-permute-done.3.r2 = bf16[64,768]{1,0:T(8,128)(2,1)S(1)} collective-permute-done((bf16[64,768]{1,0:T(8,128)(2,1)S(1)}, bf16[64,768]{1,0:T(8,128)(2,1)S(1)}, u32[]{:S(2)}, u32[]{:S(2)}) %collective-permute-start.3) | collective-permute-done | bytes 98336 | tf_op jit(solution)/shard_map/ppermute | solution.py:65
  28.9 2.1 %collective-permute-done.5.r3 = bf16[64,768]{1,0:T(8,128)(2,1)S(1)} collective-permute-done((bf16[64,768]{1,0:T(8,128)(2,1)S(1)}, bf16[64,768]{1,0:T(8,128)(2,1)S(1)}, u32[]{:S(2)}, u32[]{:S(2)}) %collective-permute-start.5) | collective-permute-done | bytes 98336 | tf_op jit(solution)/shard_map/ppermute | solution.py:65
  31.1 3.7 %collective-permute-start.8 = (bf16[64,768]{1,0:T(8,128)(2,1)S(1)}, bf16[64,768]{1,0:T(8,128)(2,1)S(1)}, u32[]{:S(2)}, u32[]{:S(2)}) collective-permute-start(bf16[64,768]{1,0:T(8,128)(2,1)S(1)} %shard_map.324.a0), channel_id=1, source_target_pairs={{0,2},{1,3},{2,0},{3,1},{4,6},{5,7},{6,4},{7,5},{8,10},{9,11},{10,... | collective-permute-start | bytes 294920 | tf_op jit(solution)/shard_map/ppermute | solution.py:65
  35.4 2.5 %collective-permute-start.11 = (bf16[64,768]{1,0:T(8,128)(2,1)S(1)}, bf16[64,768]{1,0:T(8,128)(2,1)S(1)}, u32[]{:S(2)}, u32[]{:S(2)}) collective-permute-start(bf16[64,768]{1,0:T(8,128)(2,1)S(1)} %get-tuple-element.260), channel_id=1, source_target_pairs={{0,24},{8,16},{16,8},{24,0},{1,25},{9,17},{17,9},{25,1},{2,26},{10... | collective-permute-start | bytes 294920 | tf_op jit(solution)/shard_map/ppermute | solution.py:65
  38.4 3.8 %collective-permute-done.8.a2 = bf16[64,768]{1,0:T(8,128)(2,1)S(1)} collective-permute-done((bf16[64,768]{1,0:T(8,128)(2,1)S(1)}, bf16[64,768]{1,0:T(8,128)(2,1)S(1)}, u32[]{:S(2)}, u32[]{:S(2)}) %collective-permute-start.8) | collective-permute-done | bytes 98336 | tf_op jit(solution)/shard_map/ppermute | solution.py:65
  42.2 1.5 collective-permute-start.9
  43.7 2.0 %shard_map.325 = (f32[64,768]{1,0:T(8,128)S(1)}, bf16[64,768]{1,0:T(8,128)(2,1)S(1)}, bf16[64,768]{1,0:T(8,128)(2,1)S(1)}, bf16[64,768]{1,0:T(8,128)(2,1)S(1)}, ...) custom-call(s32[4]{0:T(128)S(1)} %pad_add_fusion.ids, ...), custom_call_target="tpu_custom_call" | custom-call | flops 1200000000 | bytes 9000000 | tf_op jit(solution)/shard_map/pallas_call | solution.py:37
  45.7 1.1 collective-permute-done.9.refs_5_
  46.9 2.4 %collective-permute-start.13 = (bf16[64,768]{1,0:T(8,128)(2,1)S(1)}, bf16[64,768]{1,0:T(8,128)(2,1)S(1)}, u32[]{:S(2)}, u32[]{:S(2)}) collective-permute-start(bf16[64,768]{1,0:T(8,128)(2,1)S(1)} %get-tuple-element.152), channel_id=1, source_target_pairs={{0,1},{1,0},{2,3},{3,2},{4,5},{5,4},{6,7},{7,6},{8,9},{9,8},{10,11... | collective-permute-start | bytes 294920 | tf_op jit(solution)/shard_map/ppermute | solution.py:65
  49.3 1.9 %collective-permute-start.14 = (bf16[64,768]{1,0:T(8,128)(2,1)S(1)}, bf16[64,768]{1,0:T(8,128)(2,1)S(1)}, u32[]{:S(2)}, u32[]{:S(2)}) collective-permute-start(bf16[64,768]{1,0:T(8,128)(2,1)S(1)} %get-tuple-element.153), channel_id=1, source_target_pairs={{0,3},{1,2},{2,1},{3,0},{4,7},{5,6},{6,5},{7,4},{8,11},{9,10},{10,... | collective-permute-start | bytes 294920 | tf_op jit(solution)/shard_map/ppermute | solution.py:65
  51.2 3.5 %collective-permute-done.12.r2 = bf16[64,768]{1,0:T(8,128)(2,1)S(1)} collective-permute-done((bf16[64,768]{1,0:T(8,128)(2,1)S(1)}, bf16[64,768]{1,0:T(8,128)(2,1)S(1)}, u32[]{:S(2)}, u32[]{:S(2)}) %collective-permute-start.12) | collective-permute-done | bytes 98336 | tf_op jit(solution)/shard_map/ppermute | solution.py:65
  54.8 1.1 collective-permute-done.14.r3
  55.9 2.4 %collective-permute-start.17 = (bf16[64,768]{1,0:T(8,128)(2,1)S(1)}, bf16[64,768]{1,0:T(8,128)(2,1)S(1)}, u32[]{:S(2)}, u32[]{:S(2)}) collective-permute-start(bf16[64,768]{1,0:T(8,128)(2,1)S(1)} %shard_map.326.refs_0_), channel_id=1, source_target_pairs={{0,2},{1,3},{2,0},{3,1},{4,6},{5,7},{6,4},{7,5},{8,10},{9,11},{10,... | collective-permute-start | bytes 294920 | tf_op jit(solution)/shard_map/ppermute | solution.py:65
  58.3 1.6 %collective-permute-start.16 = (bf16[64,768]{1,0:T(8,128)(2,1)S(1)}, bf16[64,768]{1,0:T(8,128)(2,1)S(1)}, u32[]{:S(2)}, u32[]{:S(2)}) collective-permute-start(bf16[64,768]{1,0:T(8,128)(2,1)S(1)} %shard_map.326.refs_0_), channel_id=1, source_target_pairs={{0,3},{1,2},{2,1},{3,0},{4,7},{5,6},{6,5},{7,4},{8,11},{9,10},{10,... | collective-permute-start | bytes 294920 | tf_op jit(solution)/shard_map/ppermute | solution.py:65
  60.0 3.8 %collective-permute-done.17.refs_2_ = bf16[64,768]{1,0:T(8,128)(2,1)S(1)} collective-permute-done((bf16[64,768]{1,0:T(8,128)(2,1)S(1)}, bf16[64,768]{1,0:T(8,128)(2,1)S(1)}, u32[]{:S(2)}, u32[]{:S(2)}) %collective-permute-start.17) | collective-permute-done | bytes 98336 | tf_op jit(solution)/shard_map/ppermute | solution.py:65
  63.8 1.1 collective-permute-done.16.refs_3_
  64.9 0.9 collective-permute-done.15.refs_1_
  65.8 2.2 %shard_map.327 = (f32[64,768]{1,0:T(8,128)S(1)}, bf16[64,768]{1,0:T(8,128)(2,1)S(1)}, bf16[64,768]{1,0:T(8,128)(2,1)S(1)}, bf16[64,768]{1,0:T(8,128)(2,1)S(1)}, ...) custom-call(s32[4]{0:T(128)S(1)} %pad_add_fusion.ids, ...), custom_call_target="tpu_custom_call" | custom-call | flops 1200000000 | bytes 9000000 | tf_op jit(solution)/shard_map/pallas_call | solution.py:37
  68.8 1.6 %collective-permute-start.19 = (bf16[64,768]{1,0:T(8,128)(2,1)S(1)}, bf16[64,768]{1,0:T(8,128)(2,1)S(1)}, u32[]{:S(2)}, u32[]{:S(2)}) collective-permute-start(bf16[64,768]{1,0:T(8,128)(2,1)S(1)} %get-tuple-element.164), channel_id=1, source_target_pairs={{0,1},{1,0},{2,3},{3,2},{4,5},{5,4},{6,7},{7,6},{8,9},{9,8},{10,11... | collective-permute-start | bytes 294920 | tf_op jit(solution)/shard_map/ppermute | solution.py:65
  70.3 2.2 %collective-permute-start.20 = (bf16[64,768]{1,0:T(8,128)(2,1)S(1)}, bf16[64,768]{1,0:T(8,128)(2,1)S(1)}, u32[]{:S(2)}, u32[]{:S(2)}) collective-permute-start(bf16[64,768]{1,0:T(8,128)(2,1)S(1)} %get-tuple-element.165), channel_id=1, source_target_pairs={{0,3},{1,2},{2,1},{3,0},{4,7},{5,6},{6,5},{7,4},{8,11},{9,10},{10,... | collective-permute-start | bytes 294920 | tf_op jit(solution)/shard_map/ppermute | solution.py:65
  72.6 1.1 shard_map.335
  73.7 1.0 collective-permute-done.18.r2
  74.7 2.1 %collective-permute-done.20.r3 = bf16[64,768]{1,0:T(8,128)(2,1)S(1)} collective-permute-done((bf16[64,768]{1,0:T(8,128)(2,1)S(1)}, bf16[64,768]{1,0:T(8,128)(2,1)S(1)}, u32[]{:S(2)}, u32[]{:S(2)}) %collective-permute-start.20) | collective-permute-done | bytes 98336 | tf_op jit(solution)/shard_map/ppermute | solution.py:65
  77.0 2.2 %collective-permute-start.22 = (bf16[64,768]{1,0:T(8,128)(2,1)S(1)}, bf16[64,768]{1,0:T(8,128)(2,1)S(1)}, u32[]{:S(2)}, u32[]{:S(2)}) collective-permute-start(bf16[64,768]{1,0:T(8,128)(2,1)S(1)} %shard_map.328.refs_0_), channel_id=1, source_target_pairs={{0,3},{1,2},{2,1},{3,0},{4,7},{5,6},{6,5},{7,4},{8,11},{9,10},{10,... | collective-permute-start | bytes 294920 | tf_op jit(solution)/shard_map/ppermute | solution.py:65
  79.2 1.3 collective-permute-start.21
  80.5 1.4 shard_map.336
  81.9 1.6 %collective-permute-start.34 = (bf16[192,768]{1,0:T(8,128)(2,1)S(1)}, bf16[192,768]{1,0:T(8,128)(2,1)S(1)}, u32[]{:S(2)}, u32[]{:S(2)}) collective-permute-start(bf16[192,768]{1,0:T(8,128)(2,1)S(1)} %get-tuple-element.207), channel_id=1, source_target_pairs={{0,8},{8,0},{16,24},{24,16},{1,9},{9,1},{17,25},{25,17},{2,10},{10... | collective-permute-start | bytes 884744 | tf_op jit(solution)/shard_map/ppermute | solution.py:65
  83.4 1.5 %collective-permute-start.35 = (bf16[192,768]{1,0:T(8,128)(2,1)S(1)}, bf16[192,768]{1,0:T(8,128)(2,1)S(1)}, u32[]{:S(2)}, u32[]{:S(2)}) collective-permute-start(bf16[192,768]{1,0:T(8,128)(2,1)S(1)} %get-tuple-element.208), channel_id=1, source_target_pairs={{0,16},{8,24},{16,0},{24,8},{1,17},{9,25},{17,1},{25,9},{2,18},{10... | collective-permute-start | bytes 884744 | tf_op jit(solution)/shard_map/ppermute | solution.py:65
  85.4 1.1 shard_map.329
  86.5 3.6 %shard_map.330 = (f32[128,768]{1,0:T(8,128)S(1)}, bf16[128,768]{1,0:T(8,128)(2,1)S(1)}, bf16[128,768]{1,0:T(8,128)(2,1)S(1)}, bf16[128,768]{1,0:T(8,128)(2,1)S(1...) custom-call(s32[4]{0:T(128)S(1)} %pad_add_fusion.ids, ...), custom_call_target="tpu_custom_call" | custom-call | flops 40000000 | bytes 300000 | tf_op jit(solution)/shard_map/pallas_call | solution.py:37
  90.2 1.5 shard_map.337
  91.7 1.0 collective-permute-start.24
  92.7 1.7 %collective-permute-start.25 = (bf16[128,768]{1,0:T(8,128)(2,1)S(1)}, bf16[128,768]{1,0:T(8,128)(2,1)S(1)}, u32[]{:S(2)}, u32[]{:S(2)}) collective-permute-start(bf16[128,768]{1,0:T(8,128)(2,1)S(1)} %get-tuple-element.182), channel_id=1, source_target_pairs={{0,2},{1,3},{2,0},{3,1},{4,6},{5,7},{6,4},{7,5},{8,10},{9,11},{10,... | collective-permute-start | bytes 589832 | tf_op jit(solution)/shard_map/ppermute | solution.py:65
  94.4 1.7 %collective-permute-start.26 = (bf16[128,768]{1,0:T(8,128)(2,1)S(1)}, bf16[128,768]{1,0:T(8,128)(2,1)S(1)}, u32[]{:S(2)}, u32[]{:S(2)}) collective-permute-start(bf16[128,768]{1,0:T(8,128)(2,1)S(1)} %get-tuple-element.183), channel_id=1, source_target_pairs={{0,3},{1,2},{2,1},{3,0},{4,7},{5,6},{6,5},{7,4},{8,11},{9,10},{10,... | collective-permute-start | bytes 589832 | tf_op jit(solution)/shard_map/ppermute | solution.py:65
  96.1 2.2 %shard_map.338.rel = f32[8,128]{1,0:T(8,128)S(1)} custom-call(s32[4]{0:T(128)S(1)} %pad_add_fusion.ids, f32[3,512,256]{2,1,0:T(8,128)S(1)} %get-tuple-element.218.scores_ref), custom_call_target="tpu_custom_call" | custom-call | flops 40000000 | bytes 300000 | tf_op jit(solution)/shard_map/pallas_call | solution.py:37
  98.3 0.9 shard_map.339
  99.2 1.5 collective-permute-start.37
  100.7 1.7 %collective-permute-start.38 = (bf16[192,768]{1,0:T(8,128)(2,1)S(1)}, bf16[192,768]{1,0:T(8,128)(2,1)S(1)}, u32[]{:S(2)}, u32[]{:S(2)}) collective-permute-start(bf16[192,768]{1,0:T(8,128)(2,1)S(1)} %get-tuple-element.224), channel_id=1, source_target_pairs={{0,16},{8,24},{16,0},{24,8},{1,17},{9,25},{17,1},{25,9},{2,18},{10... | collective-permute-start | bytes 884744 | tf_op jit(solution)/shard_map/ppermute | solution.py:65
  102.4 7.4 %collective-permute-done.25.t2.r2 = bf16[128,768]{1,0:T(8,128)(2,1)S(1)} collective-permute-done((bf16[128,768]{1,0:T(8,128)(2,1)S(1)}, bf16[128,768]{1,0:T(8,128)(2,1)S(1)}, u32[]{:S(2)}, u32[]{:S(2)}) %collective-permute-start.25) | collective-permute-done | bytes 196640 | tf_op jit(solution)/shard_map/ppermute | solution.py:65
  109.9 2.1 %collective-permute-start.27 = (bf16[96,768]{1,0:T(8,128)(2,1)S(1)}, bf16[96,768]{1,0:T(8,128)(2,1)S(1)}, u32[]{:S(2)}, u32[]{:S(2)}) collective-permute-start(bf16[96,768]{1,0:T(8,128)(2,1)S(1)} %get-tuple-element.191), channel_id=1, source_target_pairs={{0,16},{8,24},{16,0},{24,8},{1,17},{9,25},{17,1},{25,9},{2,18},{10... | collective-permute-start | bytes 442376 | tf_op jit(solution)/shard_map/ppermute | solution.py:65
  112.8 0.8 collective-permute-start.29
  113.7 2.0 %collective-permute-start.40 = (bf16[256,768]{1,0:T(8,128)(2,1)S(1)}, bf16[256,768]{1,0:T(8,128)(2,1)S(1)}, u32[]{:S(2)}, u32[]{:S(2)}) collective-permute-start(bf16[256,768]{1,0:T(8,128)(2,1)S(1)} %get-tuple-element.227.sent2), channel_id=1, source_target_pairs={{0,16},{8,24},{16,0},{24,8},{1,17},{9,25},{17,1},{25,9},{2,18},{10... | collective-permute-start | bytes 1179656 | tf_op jit(solution)/shard_map/ppermute | solution.py:65
  115.7 0.8 collective-permute-start.39
  116.5 1.1 collective-permute-done.27.q2
  117.5 1.3 collective-permute-done.28.q1
  118.8 2.7 %collective-permute-done.29.q3 = bf16[96,768]{1,0:T(8,128)(2,1)S(1)} collective-permute-done((bf16[96,768]{1,0:T(8,128)(2,1)S(1)}, bf16[96,768]{1,0:T(8,128)(2,1)S(1)}, u32[]{:S(2)}, u32[]{:S(2)}) %collective-permute-start.29) | collective-permute-done | bytes 147488 | tf_op jit(solution)/shard_map/ppermute | solution.py:65
  121.5 3.8 %collective-permute-start.32 = (bf16[128,768]{1,0:T(8,128)(2,1)S(1)}, bf16[128,768]{1,0:T(8,128)(2,1)S(1)}, u32[]{:S(2)}, u32[]{:S(2)}) collective-permute-start(bf16[128,768]{1,0:T(8,128)(2,1)S(1)} %shard_map.334.t0), channel_id=1, source_target_pairs={{0,2},{1,3},{2,0},{3,1},{4,6},{5,7},{6,4},{7,5},{8,10},{9,11},{10,... | collective-permute-start | bytes 589832 | tf_op jit(solution)/shard_map/ppermute | solution.py:65
  125.3 2.7 %collective-permute-start.31 = (bf16[128,768]{1,0:T(8,128)(2,1)S(1)}, bf16[128,768]{1,0:T(8,128)(2,1)S(1)}, u32[]{:S(2)}, u32[]{:S(2)}) collective-permute-start(bf16[128,768]{1,0:T(8,128)(2,1)S(1)} %shard_map.334.t0), channel_id=1, source_target_pairs={{0,3},{1,2},{2,1},{3,0},{4,7},{5,6},{6,5},{7,4},{8,11},{9,10},{10,... | collective-permute-start | bytes 589832 | tf_op jit(solution)/shard_map/ppermute | solution.py:65
  128.7 2.0 %collective-permute-start.42 = (bf16[48,768]{1,0:T(8,128)(2,1)S(1)}, bf16[48,768]{1,0:T(8,128)(2,1)S(1)}, u32[]{:S(2)}, u32[]{:S(2)}) collective-permute-start(bf16[48,768]{1,0:T(8,128)(2,1)S(1)} %get-tuple-element.231.mid2), channel_id=1, source_target_pairs={{0,16},{8,24},{16,0},{24,8},{1,17},{9,25},{17,1},{25,9},{2,18},{10... | collective-permute-start | bytes 221192 | tf_op jit(solution)/shard_map/ppermute | solution.py:65
  130.7 1.3 shard_map.333
  133.1 1.5 %collective-permute-start.43 = (bf16[192,768]{1,0:T(8,128)(2,1)S(1)}, bf16[192,768]{1,0:T(8,128)(2,1)S(1)}, u32[]{:S(2)}, u32[]{:S(2)}) collective-permute-start(bf16[192,768]{1,0:T(8,128)(2,1)S(1)} %get-tuple-element.232.along1), channel_id=1, source_target_pairs={{0,8},{8,0},{16,24},{24,16},{1,9},{9,1},{17,25},{25,17},{2,10},{10... | collective-permute-start | bytes 884744 | tf_op jit(solution)/shard_map/ppermute | solution.py:65
  134.7 2.4 %collective-permute-start.44 = (bf16[192,768]{1,0:T(8,128)(2,1)S(1)}, bf16[192,768]{1,0:T(8,128)(2,1)S(1)}, u32[]{:S(2)}, u32[]{:S(2)}) collective-permute-start(bf16[192,768]{1,0:T(8,128)(2,1)S(1)} %get-tuple-element.233.along2), channel_id=1, source_target_pairs={{0,16},{8,24},{16,0},{24,8},{1,17},{9,25},{17,1},{25,9},{2,18},{10... | collective-permute-start | bytes 884744 | tf_op jit(solution)/shard_map/ppermute | solution.py:65
  137.8 2.1 %collective-permute-done.43.came1 = bf16[192,768]{1,0:T(8,128)(2,1)S(1)} collective-permute-done((bf16[192,768]{1,0:T(8,128)(2,1)S(1)}, bf16[192,768]{1,0:T(8,128)(2,1)S(1)}, u32[]{:S(2)}, u32[]{:S(2)}) %collective-permute-start.43) | collective-permute-done | bytes 294944 | tf_op jit(solution)/shard_map/ppermute | solution.py:65
  139.9 1.9 %collective-permute-done.44.came2 = bf16[192,768]{1,0:T(8,128)(2,1)S(1)} collective-permute-done((bf16[192,768]{1,0:T(8,128)(2,1)S(1)}, bf16[192,768]{1,0:T(8,128)(2,1)S(1)}, u32[]{:S(2)}, u32[]{:S(2)}) %collective-permute-start.44) | collective-permute-done | bytes 294944 | tf_op jit(solution)/shard_map/ppermute | solution.py:65
  143.0 2.6 %shard_map.345 = (f32[4,128,768]{2,1,0:T(8,128)}, f32[768,768]{1,0:T(8,128)}, f32[768,768]{1,0:T(8,128)}) custom-call(s32[4]{0:T(128)S(1)} %pad_add_fusion.ids, bf16[128,768]{1,0:T(8,128)(2,1)S(1)} %shard_map.334.t0, bf16[128,768]{1,0:T(8,128)(2,1)S(1)} %collective-permute-done.30.t1, bf16[128,768]{1,0:T(8,128)(2,1)S(1)} %collective-permute-done.32.t2, ...), custom_call_target="tpu_custom_call" | custom-call | flops 40000000 | bytes 300000 | tf_op jit(solution)/shard_map/pallas_call | solution.py:37
  146.2 3.4 %shard_map.346 = (f32[768,768]{1,0:T(8,128)}, f32[768,768]{1,0:T(8,128)}, f32[768]{0:T(1024)}, f32[768]{0:T(1024)}, f32[768]{0:T(1024)}, /*index=5*/f32[768]{0:T...) custom-call(s32[4]{0:T(128)S(1)} %pad_add_fusion.ids, ...), custom_call_target="tpu_custom_call", output_to_operand_aliasing={{0}: (4, {}), {1}: (5, {})} | custom-call | flops 40000000 | bytes 300000 | tf_op jit(solution)/shard_map/pallas_call | solution.py:37
  (104 shorter events, 10.7 us)
Async XLA Ops:
  0.7 6.5 %copy-start.8 = (f32[768]{0:T(1024)S(1)}, f32[768]{0:T(1024)}, u32[]{:S(2)}) copy-start(f32[768]{0:T(1024)} %param.28) | copy-start | bytes 9220
  0.7 6.5 %copy-start.15 = (f32[192]{0:T(256)S(1)}, f32[192]{0:T(256)}, u32[]{:S(2)}) copy-start(f32[192]{0:T(256)} %param.22) | copy-start | bytes 2308
  0.7 6.7 %copy-start.16 = (f32[192]{0:T(256)S(1)}, f32[192]{0:T(256)}, u32[]{:S(2)}) copy-start(f32[192]{0:T(256)} %param.25) | copy-start | bytes 2308
  0.7 7.5 %copy-start.6 = (f32[3,8]{1,0:T(4,128)S(1)}, f32[3,8]{1,0:T(4,128)}, u32[]{:S(2)}) copy-start(f32[3,8]{1,0:T(4,128)} %rel.1) | copy-start | bytes 292
  2.0 9.7 %collective-permute-start.2 = (bf16[128,768]{1,0:T(8,128)(2,1)S(1)}, bf16[128,768]{1,0:T(8,128)(2,1)S(1)}, u32[]{:S(2)}, u32[]{:S(2)}) collective-permute-start(bf16[128,768]{1,0:T(8,128)(2,1)S(1)} %get-tuple-element.256), channel_id=1, source_target_pairs={{0,24},{8,16},{16,8},{24,0},{1,25},{9,17},{17,9},{25,1},{2,26},{10... | collective-permute-start | bytes 589832 | tf_op jit(solution)/shard_map/ppermute | solution.py:65
  6.0 9.4 %collective-permute-start = (bf16[128,768]{1,0:T(8,128)(2,1)S(1)}, bf16[128,768]{1,0:T(8,128)(2,1)S(1)}, u32[]{:S(2)}, u32[]{:S(2)}) collective-permute-start(bf16[128,768]{1,0:T(8,128)(2,1)S(1)} %get-tuple-element.257), channel_id=1, source_target_pairs={{0,8},{8,0},{16,24},{24,16},{1,9},{9,1},{17,25},{25,17},{2,10},{10... | collective-permute-start | bytes 589832 | tf_op jit(solution)/shard_map/ppermute | solution.py:65
  6.5 8.9 %collective-permute-start.1 = (bf16[128,768]{1,0:T(8,128)(2,1)S(1)}, bf16[128,768]{1,0:T(8,128)(2,1)S(1)}, u32[]{:S(2)}, u32[]{:S(2)}) collective-permute-start(bf16[128,768]{1,0:T(8,128)(2,1)S(1)} %get-tuple-element.259), channel_id=1, source_target_pairs={{0,16},{8,24},{16,0},{24,8},{1,17},{9,25},{17,1},{25,9},{2,18},{10... | collective-permute-start | bytes 589832 | tf_op jit(solution)/shard_map/ppermute | solution.py:65
  8.2 7.2 %copy-start = (bf16[768,192]{0,1:T(8,128)(2,1)S(1)}, bf16[768,192]{0,1:T(8,128)(2,1)}, u32[]{:S(2)}) copy-start(bf16[768,192]{0,1:T(8,128)(2,1)} %param.21) | copy-start | bytes 884740
  8.2 7.2 %copy-start.1 = (bf16[768,192]{0,1:T(8,128)(2,1)S(1)}, bf16[768,192]{0,1:T(8,128)(2,1)}, u32[]{:S(2)}) copy-start(bf16[768,192]{0,1:T(8,128)(2,1)} %param.23) | copy-start | bytes 884740
  8.2 7.2 %copy-start.2 = (bf16[768,192]{0,1:T(8,128)(2,1)S(1)}, bf16[768,192]{0,1:T(8,128)(2,1)}, u32[]{:S(2)}) copy-start(bf16[768,192]{0,1:T(8,128)(2,1)} %param.24) | copy-start | bytes 884740
  8.2 7.2 %copy-start.3 = (bf16[192,768]{1,0:T(8,128)(2,1)S(1)}, bf16[192,768]{1,0:T(8,128)(2,1)}, u32[]{:S(2)}) copy-start(bf16[192,768]{1,0:T(8,128)(2,1)} %refs_5_.1) | copy-start | bytes 884740
  15.4 9.2 %copy-start.9 = (f32[768]{0:T(1024)S(1)}, f32[768]{0:T(1024)}, u32[]{:S(2)}) copy-start(f32[768]{0:T(1024)} %param.29) | copy-start | bytes 9220
  15.4 9.2 %copy-start.10 = (f32[768]{0:T(1024)S(1)}, f32[768]{0:T(1024)}, u32[]{:S(2)}) copy-start(f32[768]{0:T(1024)} %param.30) | copy-start | bytes 9220
  15.4 9.2 %copy-start.11 = (f32[768]{0:T(1024)S(1)}, f32[768]{0:T(1024)}, u32[]{:S(2)}) copy-start(f32[768]{0:T(1024)} %param.32) | copy-start | bytes 9220
  15.4 9.2 %copy-start.12 = (f32[768]{0:T(1024)S(1)}, f32[768]{0:T(1024)}, u32[]{:S(2)}) copy-start(f32[768]{0:T(1024)} %param.34) | copy-start | bytes 9220
  15.5 19.9 %copy-start.7 = (bf16[4,64,768]{2,1,0:T(8,128)(2,1)S(1)}, bf16[4,64,768]{2,1,0:T(8,128)(2,1)}, u32[]{:S(2)}) copy-start(bf16[4,64,768]{2,1,0:T(8,128)(2,1)} %param.37) | copy-start | bytes 1179652
  15.5 28.3 %copy-start.4 = (bf16[768,768]{1,0:T(8,128)(2,1)S(1)}, bf16[768,768]{1,0:T(8,128)(2,1)}, u32[]{:S(2)}) copy-start(bf16[768,768]{1,0:T(8,128)(2,1)} %refs_12_.1) | copy-start | bytes 3538948
  15.5 28.3 %copy-start.5 = (bf16[768,768]{1,0:T(8,128)(2,1)S(1)}, bf16[768,768]{1,0:T(8,128)(2,1)}, u32[]{:S(2)}) copy-start(bf16[768,768]{1,0:T(8,128)(2,1)} %refs_11_.1) | copy-start | bytes 3538948
  20.2 8.8 %collective-permute-start.3 = (bf16[64,768]{1,0:T(8,128)(2,1)S(1)}, bf16[64,768]{1,0:T(8,128)(2,1)S(1)}, u32[]{:S(2)}, u32[]{:S(2)}) collective-permute-start(bf16[64,768]{1,0:T(8,128)(2,1)S(1)} %get-tuple-element.137), channel_id=1, source_target_pairs={{0,2},{1,3},{2,0},{3,1},{4,6},{5,7},{6,4},{7,5},{8,10},{9,11},{10,... | collective-permute-start | bytes 294920 | tf_op jit(solution)/shard_map/ppermute | solution.py:65
  22.8 6.1 %collective-permute-start.4 = (bf16[64,768]{1,0:T(8,128)(2,1)S(1)}, bf16[64,768]{1,0:T(8,128)(2,1)S(1)}, u32[]{:S(2)}, u32[]{:S(2)}) collective-permute-start(bf16[64,768]{1,0:T(8,128)(2,1)S(1)} %get-tuple-element.138), channel_id=1, source_target_pairs={{0,1},{1,0},{2,3},{3,2},{4,5},{5,4},{6,7},{7,6},{8,9},{9,8},{10,11... | collective-permute-start | bytes 294920 | tf_op jit(solution)/shard_map/ppermute | solution.py:65
  24.4 6.6 %collective-permute-start.5 = (bf16[64,768]{1,0:T(8,128)(2,1)S(1)}, bf16[64,768]{1,0:T(8,128)(2,1)S(1)}, u32[]{:S(2)}, u32[]{:S(2)}) collective-permute-start(bf16[64,768]{1,0:T(8,128)(2,1)S(1)} %get-tuple-element.139), channel_id=1, source_target_pairs={{0,3},{1,2},{2,1},{3,0},{4,7},{5,6},{6,5},{7,4},{8,11},{9,10},{10,... | collective-permute-start | bytes 294920 | tf_op jit(solution)/shard_map/ppermute | solution.py:65
  31.1 11.2 %collective-permute-start.8 = (bf16[64,768]{1,0:T(8,128)(2,1)S(1)}, bf16[64,768]{1,0:T(8,128)(2,1)S(1)}, u32[]{:S(2)}, u32[]{:S(2)}) collective-permute-start(bf16[64,768]{1,0:T(8,128)(2,1)S(1)} %shard_map.324.a0), channel_id=1, source_target_pairs={{0,2},{1,3},{2,0},{3,1},{4,6},{5,7},{6,4},{7,5},{8,10},{9,11},{10,... | collective-permute-start | bytes 294920 | tf_op jit(solution)/shard_map/ppermute | solution.py:65
  34.7 9.0 %collective-permute-start.7 = (bf16[64,768]{1,0:T(8,128)(2,1)S(1)}, bf16[64,768]{1,0:T(8,128)(2,1)S(1)}, u32[]{:S(2)}, u32[]{:S(2)}) collective-permute-start(bf16[64,768]{1,0:T(8,128)(2,1)S(1)} %shard_map.324.a0), channel_id=1, source_target_pairs={{0,3},{1,2},{2,1},{3,0},{4,7},{5,6},{6,5},{7,4},{8,11},{9,10},{10,... | collective-permute-start | bytes 294920 | tf_op jit(solution)/shard_map/ppermute | solution.py:65
  35.2 8.5 %collective-permute-start.6 = (bf16[64,768]{1,0:T(8,128)(2,1)S(1)}, bf16[64,768]{1,0:T(8,128)(2,1)S(1)}, u32[]{:S(2)}, u32[]{:S(2)}) collective-permute-start(bf16[64,768]{1,0:T(8,128)(2,1)S(1)} %shard_map.324.a0), channel_id=1, source_target_pairs={{0,1},{1,0},{2,3},{3,2},{4,5},{5,4},{6,7},{7,6},{8,9},{9,8},{10,11... | collective-permute-start | bytes 294920 | tf_op jit(solution)/shard_map/ppermute | solution.py:65
  35.4 10.3 %collective-permute-start.11 = (bf16[64,768]{1,0:T(8,128)(2,1)S(1)}, bf16[64,768]{1,0:T(8,128)(2,1)S(1)}, u32[]{:S(2)}, u32[]{:S(2)}) collective-permute-start(bf16[64,768]{1,0:T(8,128)(2,1)S(1)} %get-tuple-element.260), channel_id=1, source_target_pairs={{0,24},{8,16},{16,8},{24,0},{1,25},{9,17},{17,9},{25,1},{2,26},{10... | collective-permute-start | bytes 294920 | tf_op jit(solution)/shard_map/ppermute | solution.py:65
  37.9 7.8 %collective-permute-start.10 = (bf16[64,768]{1,0:T(8,128)(2,1)S(1)}, bf16[64,768]{1,0:T(8,128)(2,1)S(1)}, u32[]{:S(2)}, u32[]{:S(2)}) collective-permute-start(bf16[64,768]{1,0:T(8,128)(2,1)S(1)} %get-tuple-element.261), channel_id=1, source_target_pairs={{0,16},{8,24},{16,0},{24,8},{1,17},{9,25},{17,1},{25,9},{2,18},{10... | collective-permute-start | bytes 294920 | tf_op jit(solution)/shard_map/ppermute | solution.py:65
  42.2 17.7 %copy-start.13 = (f32[768]{0:T(1024)S(1)}, f32[768]{0:T(1024)}, u32[]{:S(2)}) copy-start(f32[768]{0:T(1024)} %param.35) | copy-start | bytes 9220
  42.2 17.7 %copy-start.14 = (f32[768]{0:T(1024)S(1)}, f32[768]{0:T(1024)}, u32[]{:S(2)}) copy-start(f32[768]{0:T(1024)} %param.36) | copy-start | bytes 9220
  42.2 4.6 %collective-permute-start.9 = (bf16[64,768]{1,0:T(8,128)(2,1)S(1)}, bf16[64,768]{1,0:T(8,128)(2,1)S(1)}, u32[]{:S(2)}, u32[]{:S(2)}) collective-permute-start(bf16[64,768]{1,0:T(8,128)(2,1)S(1)} %get-tuple-element.262), channel_id=1, source_target_pairs={{0,8},{8,0},{16,24},{24,16},{1,9},{9,1},{17,25},{25,17},{2,10},{10... | collective-permute-start | bytes 294920 | tf_op jit(solution)/shard_map/ppermute | solution.py:65
  46.9 7.9 %collective-permute-start.12 = (bf16[64,768]{1,0:T(8,128)(2,1)S(1)}, bf16[64,768]{1,0:T(8,128)(2,1)S(1)}, u32[]{:S(2)}, u32[]{:S(2)}) collective-permute-start(bf16[64,768]{1,0:T(8,128)(2,1)S(1)} %get-tuple-element.151), channel_id=1, source_target_pairs={{0,2},{1,3},{2,0},{3,1},{4,6},{5,7},{6,4},{7,5},{8,10},{9,11},{10,... | collective-permute-start | bytes 294920 | tf_op jit(solution)/shard_map/ppermute | solution.py:65
  46.9 7.9 %collective-permute-start.13 = (bf16[64,768]{1,0:T(8,128)(2,1)S(1)}, bf16[64,768]{1,0:T(8,128)(2,1)S(1)}, u32[]{:S(2)}, u32[]{:S(2)}) collective-permute-start(bf16[64,768]{1,0:T(8,128)(2,1)S(1)} %get-tuple-element.152), channel_id=1, source_target_pairs={{0,1},{1,0},{2,3},{3,2},{4,5},{5,4},{6,7},{7,6},{8,9},{9,8},{10,11... | collective-permute-start | bytes 294920 | tf_op jit(solution)/shard_map/ppermute | solution.py:65
  49.3 6.6 %collective-permute-start.14 = (bf16[64,768]{1,0:T(8,128)(2,1)S(1)}, bf16[64,768]{1,0:T(8,128)(2,1)S(1)}, u32[]{:S(2)}, u32[]{:S(2)}) collective-permute-start(bf16[64,768]{1,0:T(8,128)(2,1)S(1)} %get-tuple-element.153), channel_id=1, source_target_pairs={{0,3},{1,2},{2,1},{3,0},{4,7},{5,6},{6,5},{7,4},{8,11},{9,10},{10,... | collective-permute-start | bytes 294920 | tf_op jit(solution)/shard_map/ppermute | solution.py:65
  55.9 7.8 %collective-permute-start.17 = (bf16[64,768]{1,0:T(8,128)(2,1)S(1)}, bf16[64,768]{1,0:T(8,128)(2,1)S(1)}, u32[]{:S(2)}, u32[]{:S(2)}) collective-permute-start(bf16[64,768]{1,0:T(8,128)(2,1)S(1)} %shard_map.326.refs_0_), channel_id=1, source_target_pairs={{0,2},{1,3},{2,0},{3,1},{4,6},{5,7},{6,4},{7,5},{8,10},{9,11},{10,... | collective-permute-start | bytes 294920 | tf_op jit(solution)/shard_map/ppermute | solution.py:65
  58.3 6.6 %collective-permute-start.16 = (bf16[64,768]{1,0:T(8,128)(2,1)S(1)}, bf16[64,768]{1,0:T(8,128)(2,1)S(1)}, u32[]{:S(2)}, u32[]{:S(2)}) collective-permute-start(bf16[64,768]{1,0:T(8,128)(2,1)S(1)} %shard_map.326.refs_0_), channel_id=1, source_target_pairs={{0,3},{1,2},{2,1},{3,0},{4,7},{5,6},{6,5},{7,4},{8,11},{9,10},{10,... | collective-permute-start | bytes 294920 | tf_op jit(solution)/shard_map/ppermute | solution.py:65
  59.9 5.9 %collective-permute-start.15 = (bf16[64,768]{1,0:T(8,128)(2,1)S(1)}, bf16[64,768]{1,0:T(8,128)(2,1)S(1)}, u32[]{:S(2)}, u32[]{:S(2)}) collective-permute-start(bf16[64,768]{1,0:T(8,128)(2,1)S(1)} %shard_map.326.refs_0_), channel_id=1, source_target_pairs={{0,1},{1,0},{2,3},{3,2},{4,5},{5,4},{6,7},{7,6},{8,9},{9,8},{10,11... | collective-permute-start | bytes 294920 | tf_op jit(solution)/shard_map/ppermute | solution.py:65
  68.1 6.6 %collective-permute-start.18 = (bf16[64,768]{1,0:T(8,128)(2,1)S(1)}, bf16[64,768]{1,0:T(8,128)(2,1)S(1)}, u32[]{:S(2)}, u32[]{:S(2)}) collective-permute-start(bf16[64,768]{1,0:T(8,128)(2,1)S(1)} %get-tuple-element.163), channel_id=1, source_target_pairs={{0,2},{1,3},{2,0},{3,1},{4,6},{5,7},{6,4},{7,5},{8,10},{9,11},{10,... | collective-permute-start | bytes 294920 | tf_op jit(solution)/shard_map/ppermute | solution.py:65
  68.8 6.0 %collective-permute-start.19 = (bf16[64,768]{1,0:T(8,128)(2,1)S(1)}, bf16[64,768]{1,0:T(8,128)(2,1)S(1)}, u32[]{:S(2)}, u32[]{:S(2)}) collective-permute-start(bf16[64,768]{1,0:T(8,128)(2,1)S(1)} %get-tuple-element.164), channel_id=1, source_target_pairs={{0,1},{1,0},{2,3},{3,2},{4,5},{5,4},{6,7},{7,6},{8,9},{9,8},{10,11... | collective-permute-start | bytes 294920 | tf_op jit(solution)/shard_map/ppermute | solution.py:65
  70.3 6.5 %collective-permute-start.20 = (bf16[64,768]{1,0:T(8,128)(2,1)S(1)}, bf16[64,768]{1,0:T(8,128)(2,1)S(1)}, u32[]{:S(2)}, u32[]{:S(2)}) collective-permute-start(bf16[64,768]{1,0:T(8,128)(2,1)S(1)} %get-tuple-element.165), channel_id=1, source_target_pairs={{0,3},{1,2},{2,1},{3,0},{4,7},{5,6},{6,5},{7,4},{8,11},{9,10},{10,... | collective-permute-start | bytes 294920 | tf_op jit(solution)/shard_map/ppermute | solution.py:65
  73.7 6.8 %collective-permute-start.33 = (bf16[768,768]{1,0:T(8,128)(2,1)S(1)}, bf16[768,768]{1,0:T(8,128)(2,1)S(1)}, u32[]{:S(2)}, u32[]{:S(2)}) collective-permute-start(bf16[768,768]{1,0:T(8,128)(2,1)S(1)} %shard_map.335), channel_id=1, source_target_pairs={{0,4},{4,0},{1,5},{5,1},{2,6},{6,2},{3,7},{7,3},{8,12},{12,8},{9,1... | collective-permute-start | bytes 3538952 | tf_op jit(solution)/shard_map/ppermute | solution.py:65
  76.9 8.1 %collective-permute-start.23 = (bf16[64,768]{1,0:T(8,128)(2,1)S(1)}, bf16[64,768]{1,0:T(8,128)(2,1)S(1)}, u32[]{:S(2)}, u32[]{:S(2)}) collective-permute-start(bf16[64,768]{1,0:T(8,128)(2,1)S(1)} %shard_map.328.refs_0_), channel_id=1, source_target_pairs={{0,2},{1,3},{2,0},{3,1},{4,6},{5,7},{6,4},{7,5},{8,10},{9,11},{10,... | collective-permute-start | bytes 294920 | tf_op jit(solution)/shard_map/ppermute | solution.py:65
  77.0 8.0 %collective-permute-start.22 = (bf16[64,768]{1,0:T(8,128)(2,1)S(1)}, bf16[64,768]{1,0:T(8,128)(2,1)S(1)}, u32[]{:S(2)}, u32[]{:S(2)}) collective-permute-start(bf16[64,768]{1,0:T(8,128)(2,1)S(1)} %shard_map.328.refs_0_), channel_id=1, source_target_pairs={{0,3},{1,2},{2,1},{3,0},{4,7},{5,6},{6,5},{7,4},{8,11},{9,10},{10,... | collective-permute-start | bytes 294920 | tf_op jit(solution)/shard_map/ppermute | solution.py:65
  79.2 6.3 %collective-permute-start.21 = (bf16[64,768]{1,0:T(8,128)(2,1)S(1)}, bf16[64,768]{1,0:T(8,128)(2,1)S(1)}, u32[]{:S(2)}, u32[]{:S(2)}) collective-permute-start(bf16[64,768]{1,0:T(8,128)(2,1)S(1)} %shard_map.328.refs_0_), channel_id=1, source_target_pairs={{0,1},{1,0},{2,3},{3,2},{4,5},{5,4},{6,7},{7,6},{8,9},{9,8},{10,11... | collective-permute-start | bytes 294920 | tf_op jit(solution)/shard_map/ppermute | solution.py:65
  81.9 8.2 %collective-permute-start.34 = (bf16[192,768]{1,0:T(8,128)(2,1)S(1)}, bf16[192,768]{1,0:T(8,128)(2,1)S(1)}, u32[]{:S(2)}, u32[]{:S(2)}) collective-permute-start(bf16[192,768]{1,0:T(8,128)(2,1)S(1)} %get-tuple-element.207), channel_id=1, source_target_pairs={{0,8},{8,0},{16,24},{24,16},{1,9},{9,1},{17,25},{25,17},{2,10},{10... | collective-permute-start | bytes 884744 | tf_op jit(solution)/shard_map/ppermute | solution.py:65
  83.4 6.7 %collective-permute-start.35 = (bf16[192,768]{1,0:T(8,128)(2,1)S(1)}, bf16[192,768]{1,0:T(8,128)(2,1)S(1)}, u32[]{:S(2)}, u32[]{:S(2)}) collective-permute-start(bf16[192,768]{1,0:T(8,128)(2,1)S(1)} %get-tuple-element.208), channel_id=1, source_target_pairs={{0,16},{8,24},{16,0},{24,8},{1,17},{9,25},{17,1},{25,9},{2,18},{10... | collective-permute-start | bytes 884744 | tf_op jit(solution)/shard_map/ppermute | solution.py:65
  91.6 6.6 %collective-permute-start.36 = (bf16[400,768]{1,0:T(8,128)(2,1)S(1)}, bf16[400,768]{1,0:T(8,128)(2,1)S(1)}, u32[]{:S(2)}, u32[]{:S(2)}) collective-permute-start(bf16[400,768]{1,0:T(8,128)(2,1)S(1)} %get-tuple-element.216), channel_id=1, source_target_pairs={{0,4},{4,0},{1,5},{5,1},{2,6},{6,2},{3,7},{7,3},{8,12},{12,8},{9,1... | collective-permute-start | bytes 1843208 | tf_op jit(solution)/shard_map/ppermute | solution.py:65
  91.7 10.8 %collective-permute-start.24 = (bf16[128,768]{1,0:T(8,128)(2,1)S(1)}, bf16[128,768]{1,0:T(8,128)(2,1)S(1)}, u32[]{:S(2)}, u32[]{:S(2)}) collective-permute-start(bf16[128,768]{1,0:T(8,128)(2,1)S(1)} %get-tuple-element.181), channel_id=1, source_target_pairs={{0,1},{1,0},{2,3},{3,2},{4,5},{5,4},{6,7},{7,6},{8,9},{9,8},{10,11... | collective-permute-start | bytes 589832 | tf_op jit(solution)/shard_map/ppermute | solution.py:65
  92.7 17.1 %collective-permute-start.25 = (bf16[128,768]{1,0:T(8,128)(2,1)S(1)}, bf16[128,768]{1,0:T(8,128)(2,1)S(1)}, u32[]{:S(2)}, u32[]{:S(2)}) collective-permute-start(bf16[128,768]{1,0:T(8,128)(2,1)S(1)} %get-tuple-element.182), channel_id=1, source_target_pairs={{0,2},{1,3},{2,0},{3,1},{4,6},{5,7},{6,4},{7,5},{8,10},{9,11},{10,... | collective-permute-start | bytes 589832 | tf_op jit(solution)/shard_map/ppermute | solution.py:65
  94.4 15.4 %collective-permute-start.26 = (bf16[128,768]{1,0:T(8,128)(2,1)S(1)}, bf16[128,768]{1,0:T(8,128)(2,1)S(1)}, u32[]{:S(2)}, u32[]{:S(2)}) collective-permute-start(bf16[128,768]{1,0:T(8,128)(2,1)S(1)} %get-tuple-element.183), channel_id=1, source_target_pairs={{0,3},{1,2},{2,1},{3,0},{4,7},{5,6},{6,5},{7,4},{8,11},{9,10},{10,... | collective-permute-start | bytes 589832 | tf_op jit(solution)/shard_map/ppermute | solution.py:65
  99.2 14.4 %collective-permute-start.37 = (bf16[208,768]{1,0:T(8,128)(2,1)S(1)}, bf16[208,768]{1,0:T(8,128)(2,1)S(1)}, u32[]{:S(2)}, u32[]{:S(2)}) collective-permute-start(bf16[208,768]{1,0:T(8,128)(2,1)S(1)} %get-tuple-element.223.sent1), channel_id=1, source_target_pairs={{0,8},{8,0},{16,24},{24,16},{1,9},{9,1},{17,25},{25,17},{2,10},{10... | collective-permute-start | bytes 958472 | tf_op jit(solution)/shard_map/ppermute | solution.py:65
  100.7 12.9 %collective-permute-start.38 = (bf16[192,768]{1,0:T(8,128)(2,1)S(1)}, bf16[192,768]{1,0:T(8,128)(2,1)S(1)}, u32[]{:S(2)}, u32[]{:S(2)}) collective-permute-start(bf16[192,768]{1,0:T(8,128)(2,1)S(1)} %get-tuple-element.224), channel_id=1, source_target_pairs={{0,16},{8,24},{16,0},{24,8},{1,17},{9,25},{17,1},{25,9},{2,18},{10... | collective-permute-start | bytes 884744 | tf_op jit(solution)/shard_map/ppermute | solution.py:65
  109.9 7.6 %collective-permute-start.27 = (bf16[96,768]{1,0:T(8,128)(2,1)S(1)}, bf16[96,768]{1,0:T(8,128)(2,1)S(1)}, u32[]{:S(2)}, u32[]{:S(2)}) collective-permute-start(bf16[96,768]{1,0:T(8,128)(2,1)S(1)} %get-tuple-element.191), channel_id=1, source_target_pairs={{0,16},{8,24},{16,0},{24,8},{1,17},{9,25},{17,1},{25,9},{2,18},{10... | collective-permute-start | bytes 442376 | tf_op jit(solution)/shard_map/ppermute | solution.py:65
  112.0 6.8 %collective-permute-start.28 = (bf16[96,768]{1,0:T(8,128)(2,1)S(1)}, bf16[96,768]{1,0:T(8,128)(2,1)S(1)}, u32[]{:S(2)}, u32[]{:S(2)}) collective-permute-start(bf16[96,768]{1,0:T(8,128)(2,1)S(1)} %get-tuple-element.192), channel_id=1, source_target_pairs={{0,8},{8,0},{16,24},{24,16},{1,9},{9,1},{17,25},{25,17},{2,10},{10... | collective-permute-start | bytes 442376 | tf_op jit(solution)/shard_map/ppermute | solution.py:65
  112.8 8.7 %collective-permute-start.29 = (bf16[96,768]{1,0:T(8,128)(2,1)S(1)}, bf16[96,768]{1,0:T(8,128)(2,1)S(1)}, u32[]{:S(2)}, u32[]{:S(2)}) collective-permute-start(bf16[96,768]{1,0:T(8,128)(2,1)S(1)} %get-tuple-element.193), channel_id=1, source_target_pairs={{0,24},{8,16},{16,8},{24,0},{1,25},{9,17},{17,9},{25,1},{2,26},{10... | collective-permute-start | bytes 442376 | tf_op jit(solution)/shard_map/ppermute | solution.py:65
  113.7 14.2 %collective-permute-start.40 = (bf16[256,768]{1,0:T(8,128)(2,1)S(1)}, bf16[256,768]{1,0:T(8,128)(2,1)S(1)}, u32[]{:S(2)}, u32[]{:S(2)}) collective-permute-start(bf16[256,768]{1,0:T(8,128)(2,1)S(1)} %get-tuple-element.227.sent2), channel_id=1, source_target_pairs={{0,16},{8,24},{16,0},{24,8},{1,17},{9,25},{17,1},{25,9},{2,18},{10... | collective-permute-start | bytes 1179656 | tf_op jit(solution)/shard_map/ppermute | solution.py:65
  115.7 12.2 %collective-permute-start.39 = (bf16[240,768]{1,0:T(8,128)(2,1)S(1)}, bf16[240,768]{1,0:T(8,128)(2,1)S(1)}, u32[]{:S(2)}, u32[]{:S(2)}) collective-permute-start(bf16[240,768]{1,0:T(8,128)(2,1)S(1)} %get-tuple-element.228.sent1), channel_id=1, source_target_pairs={{0,8},{8,0},{16,24},{24,16},{1,9},{9,1},{17,25},{25,17},{2,10},{10... | collective-permute-start | bytes 1105928 | tf_op jit(solution)/shard_map/ppermute | solution.py:65
  121.5 16.3 %collective-permute-start.32 = (bf16[128,768]{1,0:T(8,128)(2,1)S(1)}, bf16[128,768]{1,0:T(8,128)(2,1)S(1)}, u32[]{:S(2)}, u32[]{:S(2)}) collective-permute-start(bf16[128,768]{1,0:T(8,128)(2,1)S(1)} %shard_map.334.t0), channel_id=1, source_target_pairs={{0,2},{1,3},{2,0},{3,1},{4,6},{5,7},{6,4},{7,5},{8,10},{9,11},{10,... | collective-permute-start | bytes 589832 | tf_op jit(solution)/shard_map/ppermute | solution.py:65
  125.3 12.5 %collective-permute-start.31 = (bf16[128,768]{1,0:T(8,128)(2,1)S(1)}, bf16[128,768]{1,0:T(8,128)(2,1)S(1)}, u32[]{:S(2)}, u32[]{:S(2)}) collective-permute-start(bf16[128,768]{1,0:T(8,128)(2,1)S(1)} %shard_map.334.t0), channel_id=1, source_target_pairs={{0,3},{1,2},{2,1},{3,0},{4,7},{5,6},{6,5},{7,4},{8,11},{9,10},{10,... | collective-permute-start | bytes 589832 | tf_op jit(solution)/shard_map/ppermute | solution.py:65
  127.9 9.8 %collective-permute-start.30 = (bf16[128,768]{1,0:T(8,128)(2,1)S(1)}, bf16[128,768]{1,0:T(8,128)(2,1)S(1)}, u32[]{:S(2)}, u32[]{:S(2)}) collective-permute-start(bf16[128,768]{1,0:T(8,128)(2,1)S(1)} %shard_map.334.t0), channel_id=1, source_target_pairs={{0,1},{1,0},{2,3},{3,2},{4,5},{5,4},{6,7},{7,6},{8,9},{9,8},{10,11... | collective-permute-start | bytes 589832 | tf_op jit(solution)/shard_map/ppermute | solution.py:65
  128.0 4.4 %collective-permute-start.41 = (bf16[48,768]{1,0:T(8,128)(2,1)S(1)}, bf16[48,768]{1,0:T(8,128)(2,1)S(1)}, u32[]{:S(2)}, u32[]{:S(2)}) collective-permute-start(bf16[48,768]{1,0:T(8,128)(2,1)S(1)} %get-tuple-element.230.mid1), channel_id=1, source_target_pairs={{0,8},{8,0},{16,24},{24,16},{1,9},{9,1},{17,25},{25,17},{2,10},{10... | collective-permute-start | bytes 221192 | tf_op jit(solution)/shard_map/ppermute | solution.py:65
  128.7 4.4 %collective-permute-start.42 = (bf16[48,768]{1,0:T(8,128)(2,1)S(1)}, bf16[48,768]{1,0:T(8,128)(2,1)S(1)}, u32[]{:S(2)}, u32[]{:S(2)}) collective-permute-start(bf16[48,768]{1,0:T(8,128)(2,1)S(1)} %get-tuple-element.231.mid2), channel_id=1, source_target_pairs={{0,16},{8,24},{16,0},{24,8},{1,17},{9,25},{17,1},{25,9},{2,18},{10... | collective-permute-start | bytes 221192 | tf_op jit(solution)/shard_map/ppermute | solution.py:65
  133.1 6.8 %collective-permute-start.43 = (bf16[192,768]{1,0:T(8,128)(2,1)S(1)}, bf16[192,768]{1,0:T(8,128)(2,1)S(1)}, u32[]{:S(2)}, u32[]{:S(2)}) collective-permute-start(bf16[192,768]{1,0:T(8,128)(2,1)S(1)} %get-tuple-element.232.along1), channel_id=1, source_target_pairs={{0,8},{8,0},{16,24},{24,16},{1,9},{9,1},{17,25},{25,17},{2,10},{10... | collective-permute-start | bytes 884744 | tf_op jit(solution)/shard_map/ppermute | solution.py:65
  134.7 7.1 %collective-permute-start.44 = (bf16[192,768]{1,0:T(8,128)(2,1)S(1)}, bf16[192,768]{1,0:T(8,128)(2,1)S(1)}, u32[]{:S(2)}, u32[]{:S(2)}) collective-permute-start(bf16[192,768]{1,0:T(8,128)(2,1)S(1)} %get-tuple-element.233.along2), channel_id=1, source_target_pairs={{0,16},{8,24},{16,0},{24,8},{1,17},{9,25},{17,1},{25,9},{2,18},{10... | collective-permute-start | bytes 884744 | tf_op jit(solution)/shard_map/ppermute | solution.py:65
  142.4 3.8 %collective-permute-start.46 = (bf16[768,768]{1,0:T(8,128)(2,1)S(1)}, bf16[768,768]{1,0:T(8,128)(2,1)S(1)}, u32[]{:S(2)}, u32[]{:S(2)}) collective-permute-start(bf16[768,768]{1,0:T(8,128)(2,1)S(1)} %get-tuple-element.235.mine), channel_id=1, source_target_pairs={{0,4},{4,0},{1,5},{5,1},{2,6},{6,2},{3,7},{7,3},{8,12},{12,8},{9,1... | collective-permute-start | bytes 3538952 | tf_op jit(solution)/shard_map/ppermute | solution.py:65
  142.5 3.7 %collective-permute-start.45 = (bf16[400,768]{1,0:T(8,128)(2,1)S(1)}, bf16[400,768]{1,0:T(8,128)(2,1)S(1)}, u32[]{:S(2)}, u32[]{:S(2)}) collective-permute-start(bf16[400,768]{1,0:T(8,128)(2,1)S(1)} %get-tuple-element.237.mine), channel_id=1, source_target_pairs={{0,4},{4,0},{1,5},{5,1},{2,6},{6,2},{3,7},{7,3},{8,12},{12,8},{9,1... | collective-permute-start | bytes 1843208 | tf_op jit(solution)/shard_map/ppermute | solution.py:65
  (1 other events, 6.0 us)

commit v6 on v5

--- a/solution.py
+++ b/solution.py
@@ -77,8 +77,8 @@
     return [landed[order.index(k)] for k in range(1, size)]
 
 
-def gather_low(block, axis, size):
-    return ordered([block] * (size - 1), axis, size, [1, 3, 2])
+def gather_low(block, axis, size, order=(1, 3, 2)):
+    return ordered([block] * (size - 1), axis, size, order)
 
 
 def scatter_low(blocks, axis, size):
@@ -409,7 +409,7 @@
         out[2 * few :, :] = near[few : few + done, :]
 
 
-def joins_body(ids, along1, along2, came1, came2, sent1, sent2, near1, near2, small, seen, attend_out, out):
+def joins_body(ids, along1, along2, came1, came2, sent1, sent2, near1, near2, small, attend_out, out):
     size = attend_out.shape[0] - small.shape[0]
     join_half(ids[0], along1, along2, came1, came2, attend_out.at[:size, :])
     attend_out[size:, :] = small[...]
@@ -527,28 +527,27 @@
     return send, wait
 
 
-def widen(which, rows, first, second, scr, sem):
-    step = rows.shape[0] // 4
-    for n in range(4):
-        span = pl.ds(n * step, step)
-        scr[span, :] = rows[span, :].astype(F32)
-        for c, out in ((0, first), (1, second)):
-
-            @pl.when(which == c)
-            def _(out=out, n=n, span=span):
-                copy = pltpu.make_async_copy(scr.at[span, :], out.at[span, :], sem.at[n])
-                copy.start()
-
-
-def widen_wait(which, first, second, scr, sem):
-    step = scr.shape[0] // 4
-    for n in range(4):
-        span = pl.ds(n * step, step)
-        for c, out in ((0, first), (1, second)):
-
-            @pl.when(which == c)
-            def _(out=out, n=n, span=span):
-                pltpu.make_async_copy(scr.at[span, :], out.at[span, :], sem.at[n]).wait()
+def widen(flip, ids, attend, feed, results, scr, wide, sem):
+    first, second, dq, dk, dv, do = results
+    part = dq.shape[0]
+    step = feed.shape[0] // 4
+    for c, large, smalls in ((0, first, (dq, dk)), (1, second, (dv, do))):
+
+        @pl.when((ids[2] ^ flip) == c)
+        def _(large=large, smalls=smalls):
+            send, wait = sender(sem)
+            for n in range(4):
+                span = pl.ds(n * step, step)
+                wide[span, :] = feed[span, :].astype(F32)
+                send(wide.at[span, :], large.at[span, :])
+            for n, out in enumerate(smalls):
+                scr[n] = attend[n * part : (n + 1) * part, :].astype(F32)
+                send(scr.at[n], out)
+            wait()
+
+
+def widen_body(ids, attend, feed, *refs):
+    widen(0, ids, attend, feed, refs[:6], *refs[6:])
 
 
 def output_body(ids, n0, q1, q2, q3, output):
@@ -558,26 +557,10 @@
         output[ids[0] ^ b] = q[q.shape[0] - rows :, :]
 
 
-def unpack_body(ids, mine, other, feed_other, _first, _second, first, second, *rest):
-    *rows_out, query_out, value_out, rel_out, dq, dk, dv, do, scr, wide, sem, wide_sem = rest
-    widen(1 - ids[2], feed_other, first, second, wide, wide_sem)
-    unpack_attend(ids, mine, other, rows_out, query_out, value_out, rel_out, (dq, dk, dv, do), scr, sem)
-    widen_wait(1 - ids[2], first, second, wide, wide_sem)
-
-
-def unpack_attend(ids, mine, other, rows_out, query_out, value_out, rel_out, larges, scr, sem):
-    part = larges[0].shape[0]
+def unpack_body(ids, mine, other, feed_other, *refs):
+    results, (*rows_out, query_out, value_out, rel_out), scratch = refs[6:12], refs[12:22], refs[22:]
+    part = results[2].shape[0]
     heads = rel_out.shape[0]
-    send, wait = sender(sem)
-    for c, (a, b) in ((0, (mine, other)), (1, (other, mine))):
-
-        @pl.when(ids[2] == c)
-        def _(a=a, b=b):
-            for n, half in enumerate((a, a, b, b)):
-                scr[n] = half[n % 2 * part : (n % 2 + 1) * part, :].astype(F32)
-
-    for n, out in enumerate(larges):
-        send(scr.at[n], out)
     last = slice(2 * part, None)
     small = mine[last, :].astype(F32)
     for row, out in enumerate(rows_out):
@@ -587,7 +570,7 @@
     line = small[8:9, :128] + other[last, :128].astype(F32)[8:9, :]
     for h in range(heads):
         rel_out[h : h + 1, :] = line[:, h * BASES : (h + 1) * BASES]
-    wait()
+    widen(1, ids, other, feed_other, results, *scratch)
 
 
 def quarters_body(met, r1, r2, r3, own, n1, n2, n3, q0, q1, q2, q3):
@@ -610,7 +593,7 @@
     out[...] = t1[:rows, :] + t2[:rows, :] + t3[:rows, :]
 
 
-def place_body(ids, t0, t1, t2, t3, mine, out, first, second, scr, wide, sem, wide_sem):
+def place_body(ids, t0, t1, t2, t3, out, scr, sem):
     send, wait = sender(sem)
     rows = scr.shape[1] // 4
     for b in range(4):
@@ -618,9 +601,7 @@
             at = pl.ds(pl.multiple_of((ids[1] ^ k) * rows, rows), rows)
             scr[b, at, :] = t[b * rows : (b + 1) * rows, :].astype(out.dtype)
         send(scr.at[b], out.at[ids[0] ^ b])
-    widen(ids[2], mine, first, second, wide, wide_sem)
     wait()
-    widen_wait(ids[2], first, second, wide, wide_sem)
 
 
 def dp_sum(values, dp_size):
@@ -723,7 +704,7 @@
         [f32(half, width)]
         + [low(half, width)] * 7
         + [low(slots, width), low(slots, hidden_here), f32(SMALL_ROWS, width)],
-        (ids, mixed, *gather_low(mixed, "mp", mp_size), *cots, row(ffn_gain), row(ffn_shift), slope)
+        (ids, mixed, *gather_low(mixed, "mp", mp_size, (3, 1, 2)), *cots, row(ffn_gain), row(ffn_shift), slope)
         + (down_weight, up_weight),
         smem=1,
         scratch=[pltpu.VMEM((4, half, width), F32), pltpu.VMEM((slots, width), LOW)],
@@ -833,43 +814,40 @@
         micros=0.1,
     )
     came = both_ways(along1, along2, seq_size)
-    seen = kernel(touch_body, low(SMALL_ROWS, width), tuple(spread), micros=7.0)
+    input_all = kernel(
+        place_body,
+        [f32(4, block_len, width)],
+        (ids, joined, *spread),
+        smem=1,
+        scratch=[pltpu.VMEM((4, block_len, width), F32), pltpu.SemaphoreType.DMA((4,))],
+        micros=7.0,
+        hbm=(0,),
+    )[0]
     attend_mine, feed_mine = kernel(
         joins_body,
         [low(half_rows + SMALL_ROWS, width), low(width, width)],
-        (ids, along1, along2, *came, sent1, sent2, *near, small, seen),
+        (ids, along1, along2, after(came[0], input_all), came[1], sent1, sent2, *near, small),
         smem=1,
         micros=0.2,
     )
     attend_mine, feed_mine = dp_sum((attend_mine, feed_mine), dp_size)
     attend_other = swap(attend_mine, "dp", dp_size, 1)
     feed_other = swap(feed_mine, "dp", dp_size, 1)
-    wide = pltpu.VMEM((width, width), F32)
-    sems = pltpu.SemaphoreType.DMA((4,))
-    input_all, *halves = kernel(
-        place_body,
-        [f32(4, block_len, width)] + [f32(width, width)] * 2,
-        (ids, joined, *spread, feed_mine),
-        smem=1,
-        scratch=[pltpu.VMEM((4, block_len, width), F32), wide, sems, sems],
+    large = [f32(width, width)] * 2 + [f32(part, width)] * 4
+    work = [pltpu.VMEM((2, part, width), F32), pltpu.VMEM((width, width), F32), pltpu.SemaphoreType.DMA((6,))]
+    halves = kernel(
+        widen_body, large, (ids, attend_mine, feed_mine), smem=1, scratch=work, micros=0.1, hbm=range(6)
+    )
+    down_grad, up_grad, dq, dk, dv, do, *small, query_sum, value_sum, rel_sum = kernel(
+        unpack_body,
+        large + [f32(width)] * 7 + [f32(part)] * 2 + [f32(heads, BASES)],
+        (ids, attend_mine, attend_other, feed_other, *halves),
+        smem=1,
+        scratch=work,
         micros=0.1,
-        hbm=range(3),
-    )
-    down_grad, up_grad, *rest = kernel(
-        unpack_body,
-        [f32(width, width)] * 2
-        + [f32(width)] * 7
-        + [f32(part)] * 2
-        + [f32(heads, BASES)]
-        + [f32(part, width)] * 4,
-        (ids, attend_mine, attend_other, feed_other, *halves),
-        smem=1,
-        scratch=[pltpu.VMEM((4, part, width), F32), wide, sems, sems],
-        micros=0.1,
-        hbm=(0, 1, 12, 13, 14, 15),
-        reused=2,
-    )
-    *small, query_sum, value_sum, rel_sum, dq, dk, dv, do = rest
+        hbm=range(6),
+        reused=6,
+    )
     ffn_gain_sum, ffn_shift_sum, down_bias_sum, up_bias_sum, attn_gain_sum, attn_shift_sum, out_bias_sum = small
     return (
         output_all,

time: 151 us -> 149 us (0.987)
  transfers between devices with their start and end apart: 47 -> 47, of which waited for: 25 -> 24; matrix products, arithmetic and copies ran while one was open for 1% -> 1% of each run, Pallas kernels for 12% -> 14%
where the time goes in v6:
time: 149 us
  starting transfers between devices  63.9 us (43%)
  waiting for transfers between devices  48 us (32%)
  Pallas kernels  32.4 us (22%)
  local copies, waits for them, and re-layouts  2.24 us (2%)
    ppermute x47, starting transfers between devices, swap(): return lax.ppermute(block, axis, [(s, s ^ k) for s in range(size)])  63.9 us
    ppermute x47, waiting for transfers between devices, swap(): return lax.ppermute(block, axis, [(s, s ^ k) for s in range(size)])  48 us
    pallas_call x25, Pallas kernels, kernel(): pl.pallas_call(body, out_shape=outs, in_specs=in_specs, out_specs=out_spe...  32.4 us
  transfers between devices with their start and end apart: 47, of which 24 were waited for; matrix products, arithmetic and copies ran while one was open for 1% of the time, Pallas kernels for 14%

profile of v6, /device:TPU:0, one launch (start us, length us, event | category | flops | bytes accessed | tf_op | source)
XLA Modules:
  0.0 148.5 jit_solution(1820933401751301727)
XLA Ops:
  0.7 1.3 dynamic-slice_bitcast_fusion
  2.0 4.0 %collective-permute-start.2 = (bf16[128,768]{1,0:T(8,128)(2,1)S(1)}, bf16[128,768]{1,0:T(8,128)(2,1)S(1)}, u32[]{:S(2)}, u32[]{:S(2)}) collective-permute-start(bf16[128,768]{1,0:T(8,128)(2,1)S(1)} %get-tuple-element.264), channel_id=1, source_target_pairs={{0,24},{8,16},{16,8},{24,0},{1,25},{9,17},{17,9},{25,1},{2,26},{10... | collective-permute-start | bytes 589832 | tf_op jit(solution)/shard_map/ppermute | solution.py:65
  8.2 2.1 %shard_map.322.refs_11_ = f32[3,512,256]{2,1,0:T(8,128)S(1)} custom-call(s32[4]{0:T(128)S(1)} %pad_add_fusion.ids, f32[3,8]{1,0:T(4,128)S(1)} %copy-done.6), custom_call_target="tpu_custom_call" | custom-call | flops 1200000000 | bytes 9000000 | tf_op jit(solution)/shard_map/pallas_call | solution.py:37
  10.3 1.4 collective-permute-done.2.refs_3_
  11.7 3.7 %collective-permute-done.refs_1_ = bf16[128,768]{1,0:T(8,128)(2,1)S(1)} collective-permute-done((bf16[128,768]{1,0:T(8,128)(2,1)S(1)}, bf16[128,768]{1,0:T(8,128)(2,1)S(1)}, u32[]{:S(2)}, u32[]{:S(2)}) %collective-permute-start) | collective-permute-done | bytes 196640 | tf_op jit(solution)/shard_map/ppermute | solution.py:65
  15.5 4.7 %shard_map.323 = (f32[64,768]{1,0:T(8,128)S(1)}, bf16[64,768]{1,0:T(8,128)(2,1)S(1)}, bf16[64,768]{1,0:T(8,128)(2,1)S(1)}, bf16[64,768]{1,0:T(8,128)(2,1)S(1)}, ...) custom-call(s32[4]{0:T(128)S(1)} %pad_add_fusion.ids, ...), custom_call_target="tpu_custom_call" | custom-call | flops 2000000000 | bytes 15000000 | tf_op jit(solution)/shard_map/pallas_call | solution.py:37
  20.2 2.7 %collective-permute-start.3 = (bf16[64,768]{1,0:T(8,128)(2,1)S(1)}, bf16[64,768]{1,0:T(8,128)(2,1)S(1)}, u32[]{:S(2)}, u32[]{:S(2)}) collective-permute-start(bf16[64,768]{1,0:T(8,128)(2,1)S(1)} %get-tuple-element.141), channel_id=1, source_target_pairs={{0,2},{1,3},{2,0},{3,1},{4,6},{5,7},{6,4},{7,5},{8,10},{9,11},{10,... | collective-permute-start | bytes 294920 | tf_op jit(solution)/shard_map/ppermute | solution.py:65
  22.8 1.6 %collective-permute-start.4 = (bf16[64,768]{1,0:T(8,128)(2,1)S(1)}, bf16[64,768]{1,0:T(8,128)(2,1)S(1)}, u32[]{:S(2)}, u32[]{:S(2)}) collective-permute-start(bf16[64,768]{1,0:T(8,128)(2,1)S(1)} %get-tuple-element.142), channel_id=1, source_target_pairs={{0,1},{1,0},{2,3},{3,2},{4,5},{5,4},{6,7},{7,6},{8,9},{9,8},{10,11... | collective-permute-start | bytes 294920 | tf_op jit(solution)/shard_map/ppermute | solution.py:65
  24.7 4.3 %collective-permute-done.3.r2 = bf16[64,768]{1,0:T(8,128)(2,1)S(1)} collective-permute-done((bf16[64,768]{1,0:T(8,128)(2,1)S(1)}, bf16[64,768]{1,0:T(8,128)(2,1)S(1)}, u32[]{:S(2)}, u32[]{:S(2)}) %collective-permute-start.3) | collective-permute-done | bytes 98336 | tf_op jit(solution)/shard_map/ppermute | solution.py:65
  28.9 2.1 %collective-permute-done.5.r3 = bf16[64,768]{1,0:T(8,128)(2,1)S(1)} collective-permute-done((bf16[64,768]{1,0:T(8,128)(2,1)S(1)}, bf16[64,768]{1,0:T(8,128)(2,1)S(1)}, u32[]{:S(2)}, u32[]{:S(2)}) %collective-permute-start.5) | collective-permute-done | bytes 98336 | tf_op jit(solution)/shard_map/ppermute | solution.py:65
  31.1 3.7 %collective-permute-start.8 = (bf16[64,768]{1,0:T(8,128)(2,1)S(1)}, bf16[64,768]{1,0:T(8,128)(2,1)S(1)}, u32[]{:S(2)}, u32[]{:S(2)}) collective-permute-start(bf16[64,768]{1,0:T(8,128)(2,1)S(1)} %shard_map.324.a0), channel_id=1, source_target_pairs={{0,2},{1,3},{2,0},{3,1},{4,6},{5,7},{6,4},{7,5},{8,10},{9,11},{10,... | collective-permute-start | bytes 294920 | tf_op jit(solution)/shard_map/ppermute | solution.py:65
  35.4 2.5 %collective-permute-start.11 = (bf16[64,768]{1,0:T(8,128)(2,1)S(1)}, bf16[64,768]{1,0:T(8,128)(2,1)S(1)}, u32[]{:S(2)}, u32[]{:S(2)}) collective-permute-start(bf16[64,768]{1,0:T(8,128)(2,1)S(1)} %get-tuple-element.268), channel_id=1, source_target_pairs={{0,24},{8,16},{16,8},{24,0},{1,25},{9,17},{17,9},{25,1},{2,26},{10... | collective-permute-start | bytes 294920 | tf_op jit(solution)/shard_map/ppermute | solution.py:65
  38.4 3.8 %collective-permute-done.8.a2 = bf16[64,768]{1,0:T(8,128)(2,1)S(1)} collective-permute-done((bf16[64,768]{1,0:T(8,128)(2,1)S(1)}, bf16[64,768]{1,0:T(8,128)(2,1)S(1)}, u32[]{:S(2)}, u32[]{:S(2)}) %collective-permute-start.8) | collective-permute-done | bytes 98336 | tf_op jit(solution)/shard_map/ppermute | solution.py:65
  42.2 1.5 %collective-permute-start.9 = (bf16[64,768]{1,0:T(8,128)(2,1)S(1)}, bf16[64,768]{1,0:T(8,128)(2,1)S(1)}, u32[]{:S(2)}, u32[]{:S(2)}) collective-permute-start(bf16[64,768]{1,0:T(8,128)(2,1)S(1)} %get-tuple-element.270), channel_id=1, source_target_pairs={{0,8},{8,0},{16,24},{24,16},{1,9},{9,1},{17,25},{25,17},{2,10},{10... | collective-permute-start | bytes 294920 | tf_op jit(solution)/shard_map/ppermute | solution.py:65
  43.7 2.0 %shard_map.325 = (f32[64,768]{1,0:T(8,128)S(1)}, bf16[64,768]{1,0:T(8,128)(2,1)S(1)}, bf16[64,768]{1,0:T(8,128)(2,1)S(1)}, bf16[64,768]{1,0:T(8,128)(2,1)S(1)}, ...) custom-call(s32[4]{0:T(128)S(1)} %pad_add_fusion.ids, ...), custom_call_target="tpu_custom_call" | custom-call | flops 1200000000 | bytes 9000000 | tf_op jit(solution)/shard_map/pallas_call | solution.py:37
  45.7 1.1 collective-permute-done.9.refs_5_
  46.9 2.4 %collective-permute-start.13 = (bf16[64,768]{1,0:T(8,128)(2,1)S(1)}, bf16[64,768]{1,0:T(8,128)(2,1)S(1)}, u32[]{:S(2)}, u32[]{:S(2)}) collective-permute-start(bf16[64,768]{1,0:T(8,128)(2,1)S(1)} %get-tuple-element.156), channel_id=1, source_target_pairs={{0,1},{1,0},{2,3},{3,2},{4,5},{5,4},{6,7},{7,6},{8,9},{9,8},{10,11... | collective-permute-start | bytes 294920 | tf_op jit(solution)/shard_map/ppermute | solution.py:65
  49.3 1.9 %collective-permute-start.14 = (bf16[64,768]{1,0:T(8,128)(2,1)S(1)}, bf16[64,768]{1,0:T(8,128)(2,1)S(1)}, u32[]{:S(2)}, u32[]{:S(2)}) collective-permute-start(bf16[64,768]{1,0:T(8,128)(2,1)S(1)} %get-tuple-element.157), channel_id=1, source_target_pairs={{0,3},{1,2},{2,1},{3,0},{4,7},{5,6},{6,5},{7,4},{8,11},{9,10},{10,... | collective-permute-start | bytes 294920 | tf_op jit(solution)/shard_map/ppermute | solution.py:65
  51.2 3.5 %collective-permute-done.12.r2 = bf16[64,768]{1,0:T(8,128)(2,1)S(1)} collective-permute-done((bf16[64,768]{1,0:T(8,128)(2,1)S(1)}, bf16[64,768]{1,0:T(8,128)(2,1)S(1)}, u32[]{:S(2)}, u32[]{:S(2)}) %collective-permute-start.12) | collective-permute-done | bytes 98336 | tf_op jit(solution)/shard_map/ppermute | solution.py:65
  54.8 1.1 collective-permute-done.14.r3
  55.9 2.4 %collective-permute-start.17 = (bf16[64,768]{1,0:T(8,128)(2,1)S(1)}, bf16[64,768]{1,0:T(8,128)(2,1)S(1)}, u32[]{:S(2)}, u32[]{:S(2)}) collective-permute-start(bf16[64,768]{1,0:T(8,128)(2,1)S(1)} %shard_map.326.refs_0_), channel_id=1, source_target_pairs={{0,2},{1,3},{2,0},{3,1},{4,6},{5,7},{6,4},{7,5},{8,10},{9,11},{10,... | collective-permute-start | bytes 294920 | tf_op jit(solution)/shard_map/ppermute | solution.py:65
  58.5 1.9 %collective-permute-start.15 = (bf16[64,768]{1,0:T(8,128)(2,1)S(1)}, bf16[64,768]{1,0:T(8,128)(2,1)S(1)}, u32[]{:S(2)}, u32[]{:S(2)}) collective-permute-start(bf16[64,768]{1,0:T(8,128)(2,1)S(1)} %shard_map.326.refs_0_), channel_id=1, source_target_pairs={{0,3},{1,2},{2,1},{3,0},{4,7},{5,6},{6,5},{7,4},{8,11},{9,10},{10,... | collective-permute-start | bytes 294920 | tf_op jit(solution)/shard_map/ppermute | solution.py:65
  60.4 3.5 %collective-permute-done.17.refs_2_ = bf16[64,768]{1,0:T(8,128)(2,1)S(1)} collective-permute-done((bf16[64,768]{1,0:T(8,128)(2,1)S(1)}, bf16[64,768]{1,0:T(8,128)(2,1)S(1)}, u32[]{:S(2)}, u32[]{:S(2)}) %collective-permute-start.17) | collective-permute-done | bytes 98336 | tf_op jit(solution)/shard_map/ppermute | solution.py:65
  63.9 1.2 collective-permute-done.16.refs_1_
  65.1 2.2 %shard_map.327 = (f32[64,768]{1,0:T(8,128)S(1)}, bf16[64,768]{1,0:T(8,128)(2,1)S(1)}, bf16[64,768]{1,0:T(8,128)(2,1)S(1)}, bf16[64,768]{1,0:T(8,128)(2,1)S(1)}, ...) custom-call(s32[4]{0:T(128)S(1)} %pad_add_fusion.ids, ...), custom_call_target="tpu_custom_call" | custom-call | flops 1200000000 | bytes 9000000 | tf_op jit(solution)/shard_map/pallas_call | solution.py:37
  67.3 1.7 %collective-permute-start.18 = (bf16[64,768]{1,0:T(8,128)(2,1)S(1)}, bf16[64,768]{1,0:T(8,128)(2,1)S(1)}, u32[]{:S(2)}, u32[]{:S(2)}) collective-permute-start(bf16[64,768]{1,0:T(8,128)(2,1)S(1)} %get-tuple-element.167), channel_id=1, source_target_pairs={{0,2},{1,3},{2,0},{3,1},{4,6},{5,7},{6,4},{7,5},{8,10},{9,11},{10,... | collective-permute-start | bytes 294920 | tf_op jit(solution)/shard_map/ppermute | solution.py:65
  69.0 1.0 collective-permute-start.19
  70.0 1.8 %collective-permute-start.20 = (bf16[64,768]{1,0:T(8,128)(2,1)S(1)}, bf16[64,768]{1,0:T(8,128)(2,1)S(1)}, u32[]{:S(2)}, u32[]{:S(2)}) collective-permute-start(bf16[64,768]{1,0:T(8,128)(2,1)S(1)} %get-tuple-element.169), channel_id=1, source_target_pairs={{0,3},{1,2},{2,1},{3,0},{4,7},{5,6},{6,5},{7,4},{8,11},{9,10},{10,... | collective-permute-start | bytes 294920 | tf_op jit(solution)/shard_map/ppermute | solution.py:65
  71.8 1.1 shard_map.336
  73.0 1.1 collective-permute-done.18.r2
  74.1 2.3 %collective-permute-done.20.r3 = bf16[64,768]{1,0:T(8,128)(2,1)S(1)} collective-permute-done((bf16[64,768]{1,0:T(8,128)(2,1)S(1)}, bf16[64,768]{1,0:T(8,128)(2,1)S(1)}, u32[]{:S(2)}, u32[]{:S(2)}) %collective-permute-start.20) | collective-permute-done | bytes 98336 | tf_op jit(solution)/shard_map/ppermute | solution.py:65
  76.5 1.9 %collective-permute-start.22 = (bf16[64,768]{1,0:T(8,128)(2,1)S(1)}, bf16[64,768]{1,0:T(8,128)(2,1)S(1)}, u32[]{:S(2)}, u32[]{:S(2)}) collective-permute-start(bf16[64,768]{1,0:T(8,128)(2,1)S(1)} %shard_map.328.refs_0_), channel_id=1, source_target_pairs={{0,3},{1,2},{2,1},{3,0},{4,7},{5,6},{6,5},{7,4},{8,11},{9,10},{10,... | collective-permute-start | bytes 294920 | tf_op jit(solution)/shard_map/ppermute | solution.py:65
  78.5 1.6 %collective-permute-start.21 = (bf16[64,768]{1,0:T(8,128)(2,1)S(1)}, bf16[64,768]{1,0:T(8,128)(2,1)S(1)}, u32[]{:S(2)}, u32[]{:S(2)}) collective-permute-start(bf16[64,768]{1,0:T(8,128)(2,1)S(1)} %shard_map.328.refs_0_), channel_id=1, source_target_pairs={{0,1},{1,0},{2,3},{3,2},{4,5},{5,4},{6,7},{7,6},{8,9},{9,8},{10,11... | collective-permute-start | bytes 294920 | tf_op jit(solution)/shard_map/ppermute | solution.py:65
  80.0 1.4 shard_map.337
  81.5 1.6 %collective-permute-start.34 = (bf16[192,768]{1,0:T(8,128)(2,1)S(1)}, bf16[192,768]{1,0:T(8,128)(2,1)S(1)}, u32[]{:S(2)}, u32[]{:S(2)}) collective-permute-start(bf16[192,768]{1,0:T(8,128)(2,1)S(1)} %get-tuple-element.211), channel_id=1, source_target_pairs={{0,8},{8,0},{16,24},{24,16},{1,9},{9,1},{17,25},{25,17},{2,10},{10... | collective-permute-start | bytes 884744 | tf_op jit(solution)/shard_map/ppermute | solution.py:65
  83.0 1.5 %collective-permute-start.35 = (bf16[192,768]{1,0:T(8,128)(2,1)S(1)}, bf16[192,768]{1,0:T(8,128)(2,1)S(1)}, u32[]{:S(2)}, u32[]{:S(2)}) collective-permute-start(bf16[192,768]{1,0:T(8,128)(2,1)S(1)} %get-tuple-element.212), channel_id=1, source_target_pairs={{0,16},{8,24},{16,0},{24,8},{1,17},{9,25},{17,1},{25,9},{2,18},{10... | collective-permute-start | bytes 884744 | tf_op jit(solution)/shard_map/ppermute | solution.py:65
  85.0 1.1 shard_map.329
  86.0 3.6 %shard_map.330 = (f32[128,768]{1,0:T(8,128)S(1)}, bf16[128,768]{1,0:T(8,128)(2,1)S(1)}, bf16[128,768]{1,0:T(8,128)(2,1)S(1)}, bf16[128,768]{1,0:T(8,128)(2,1)S(1...) custom-call(s32[4]{0:T(128)S(1)} %pad_add_fusion.ids, ...), custom_call_target="tpu_custom_call" | custom-call | flops 40000000 | bytes 300000 | tf_op jit(solution)/shard_map/pallas_call | solution.py:37
  89.7 1.5 shard_map.338
  91.2 1.0 collective-permute-start.24
  92.3 1.5 collective-permute-start.25
  93.7 2.0 %collective-permute-start.26 = (bf16[128,768]{1,0:T(8,128)(2,1)S(1)}, bf16[128,768]{1,0:T(8,128)(2,1)S(1)}, u32[]{:S(2)}, u32[]{:S(2)}) collective-permute-start(bf16[128,768]{1,0:T(8,128)(2,1)S(1)} %get-tuple-element.187), channel_id=1, source_target_pairs={{0,3},{1,2},{2,1},{3,0},{4,7},{5,6},{6,5},{7,4},{8,11},{9,10},{10,... | collective-permute-start | bytes 589832 | tf_op jit(solution)/shard_map/ppermute | solution.py:65
  95.7 2.2 %shard_map.339.rel = f32[8,128]{1,0:T(8,128)S(1)} custom-call(s32[4]{0:T(128)S(1)} %pad_add_fusion.ids, f32[3,512,256]{2,1,0:T(8,128)S(1)} %get-tuple-element.222.scores_ref), custom_call_target="tpu_custom_call" | custom-call | flops 40000000 | bytes 300000 | tf_op jit(solution)/shard_map/pallas_call | solution.py:37
  98.8 1.5 collective-permute-start.37
  100.2 1.5 %collective-permute-start.38 = (bf16[192,768]{1,0:T(8,128)(2,1)S(1)}, bf16[192,768]{1,0:T(8,128)(2,1)S(1)}, u32[]{:S(2)}, u32[]{:S(2)}) collective-permute-start(bf16[192,768]{1,0:T(8,128)(2,1)S(1)} %get-tuple-element.228), channel_id=1, source_target_pairs={{0,16},{8,24},{16,0},{24,8},{1,17},{9,25},{17,1},{25,9},{2,18},{10... | collective-permute-start | bytes 884744 | tf_op jit(solution)/shard_map/ppermute | solution.py:65
  101.9 7.5 %collective-permute-done.25.t2.r2 = bf16[128,768]{1,0:T(8,128)(2,1)S(1)} collective-permute-done((bf16[128,768]{1,0:T(8,128)(2,1)S(1)}, bf16[128,768]{1,0:T(8,128)(2,1)S(1)}, u32[]{:S(2)}, u32[]{:S(2)}) %collective-permute-start.25) | collective-permute-done | bytes 196640 | tf_op jit(solution)/shard_map/ppermute | solution.py:65
  109.5 1.6 %collective-permute-start.27 = (bf16[96,768]{1,0:T(8,128)(2,1)S(1)}, bf16[96,768]{1,0:T(8,128)(2,1)S(1)}, u32[]{:S(2)}, u32[]{:S(2)}) collective-permute-start(bf16[96,768]{1,0:T(8,128)(2,1)S(1)} %get-tuple-element.195), channel_id=1, source_target_pairs={{0,16},{8,24},{16,0},{24,8},{1,17},{9,25},{17,1},{25,9},{2,18},{10... | collective-permute-start | bytes 442376 | tf_op jit(solution)/shard_map/ppermute | solution.py:65
  111.1 1.5 collective-permute-start.28
  113.2 1.6 %collective-permute-start.40 = (bf16[256,768]{1,0:T(8,128)(2,1)S(1)}, bf16[256,768]{1,0:T(8,128)(2,1)S(1)}, u32[]{:S(2)}, u32[]{:S(2)}) collective-permute-start(bf16[256,768]{1,0:T(8,128)(2,1)S(1)} %get-tuple-element.231.sent2), channel_id=1, source_target_pairs={{0,16},{8,24},{16,0},{24,8},{1,17},{9,25},{17,1},{25,9},{2,18},{10... | collective-permute-start | bytes 1179656 | tf_op jit(solution)/shard_map/ppermute | solution.py:65
  114.8 1.5 collective-permute-start.39
  116.3 1.2 collective-permute-done.27.q2
  117.9 3.0 %collective-permute-done.29.q3 = bf16[96,768]{1,0:T(8,128)(2,1)S(1)} collective-permute-done((bf16[96,768]{1,0:T(8,128)(2,1)S(1)}, bf16[96,768]{1,0:T(8,128)(2,1)S(1)}, u32[]{:S(2)}, u32[]{:S(2)}) %collective-permute-start.29) | collective-permute-done | bytes 147488 | tf_op jit(solution)/shard_map/ppermute | solution.py:65
  120.9 4.1 %collective-permute-start.32 = (bf16[128,768]{1,0:T(8,128)(2,1)S(1)}, bf16[128,768]{1,0:T(8,128)(2,1)S(1)}, u32[]{:S(2)}, u32[]{:S(2)}) collective-permute-start(bf16[128,768]{1,0:T(8,128)(2,1)S(1)} %shard_map.334.t0), channel_id=1, source_target_pairs={{0,2},{1,3},{2,0},{3,1},{4,6},{5,7},{6,4},{7,5},{8,10},{9,11},{10,... | collective-permute-start | bytes 589832 | tf_op jit(solution)/shard_map/ppermute | solution.py:65
  125.0 2.1 %collective-permute-start.31 = (bf16[128,768]{1,0:T(8,128)(2,1)S(1)}, bf16[128,768]{1,0:T(8,128)(2,1)S(1)}, u32[]{:S(2)}, u32[]{:S(2)}) collective-permute-start(bf16[128,768]{1,0:T(8,128)(2,1)S(1)} %shard_map.334.t0), channel_id=1, source_target_pairs={{0,3},{1,2},{2,1},{3,0},{4,7},{5,6},{6,5},{7,4},{8,11},{9,10},{10,... | collective-permute-start | bytes 589832 | tf_op jit(solution)/shard_map/ppermute | solution.py:65
  127.2 1.9 %collective-permute-start.41 = (bf16[48,768]{1,0:T(8,128)(2,1)S(1)}, bf16[48,768]{1,0:T(8,128)(2,1)S(1)}, u32[]{:S(2)}, u32[]{:S(2)}) collective-permute-start(bf16[48,768]{1,0:T(8,128)(2,1)S(1)} %get-tuple-element.234.mid1), channel_id=1, source_target_pairs={{0,8},{8,0},{16,24},{24,16},{1,9},{9,1},{17,25},{25,17},{2,10},{10... | collective-permute-start | bytes 221192 | tf_op jit(solution)/shard_map/ppermute | solution.py:65
  129.0 1.5 %collective-permute-start.42 = (bf16[48,768]{1,0:T(8,128)(2,1)S(1)}, bf16[48,768]{1,0:T(8,128)(2,1)S(1)}, u32[]{:S(2)}, u32[]{:S(2)}) collective-permute-start(bf16[48,768]{1,0:T(8,128)(2,1)S(1)} %get-tuple-element.235.mid2), channel_id=1, source_target_pairs={{0,16},{8,24},{16,0},{24,8},{1,17},{9,25},{17,1},{25,9},{2,18},{10... | collective-permute-start | bytes 221192 | tf_op jit(solution)/shard_map/ppermute | solution.py:65
  130.6 1.3 shard_map.333
  131.9 2.0 %collective-permute-done.42.came2 = bf16[48,768]{1,0:T(8,128)(2,1)S(1)} collective-permute-done((bf16[48,768]{1,0:T(8,128)(2,1)S(1)}, bf16[48,768]{1,0:T(8,128)(2,1)S(1)}, u32[]{:S(2)}, u32[]{:S(2)}) %collective-permute-start.42) | collective-permute-done | bytes 73760 | tf_op jit(solution)/shard_map/ppermute | solution.py:65
  134.0 1.6 %collective-permute-start.44 = (bf16[192,768]{1,0:T(8,128)(2,1)S(1)}, bf16[192,768]{1,0:T(8,128)(2,1)S(1)}, u32[]{:S(2)}, u32[]{:S(2)}) collective-permute-start(bf16[192,768]{1,0:T(8,128)(2,1)S(1)} %get-tuple-element.237.along2), channel_id=1, source_target_pairs={{0,16},{8,24},{16,0},{24,8},{1,17},{9,25},{17,1},{25,9},{2,18},{10... | collective-permute-start | bytes 884744 | tf_op jit(solution)/shard_map/ppermute | solution.py:65
  135.6 2.4 %collective-permute-done.32.t2 = bf16[128,768]{1,0:T(8,128)(2,1)S(1)} collective-permute-done((bf16[128,768]{1,0:T(8,128)(2,1)S(1)}, bf16[128,768]{1,0:T(8,128)(2,1)S(1)}, u32[]{:S(2)}, u32[]{:S(2)}) %collective-permute-start.32) | collective-permute-done | bytes 196640 | tf_op jit(solution)/shard_map/ppermute | solution.py:65
  138.0 1.7 %shard_map.335 = f32[4,128,768]{2,1,0:T(8,128)} custom-call(s32[4]{0:T(128)S(1)} %pad_add_fusion.ids, bf16[128,768]{1,0:T(8,128)(2,1)S(1)} %shard_map.334.t0, bf16[128,768]{1,0:T(8,128)(2,1)S(1)} %collective-permute-done.30.t1, bf16[128,768]{1,0:T(8,128)(2,1)S(1)} %collective-permute-done.32.t2, bf16[128,768]{1,0:T(8,128)(2,1)S(1)} %collective-permute-done.31.t3), custom_call_target="tpu_custom_call" | custom-call | flops 2800000000 | bytes 21000000 | tf_op jit(solution)/shard_map/pallas_call | solution.py:37
  139.7 1.0 collective-permute-done.43.came1
  142.0 2.4 %shard_map.345 = (f32[768,768]{1,0:T(8,128)}, f32[768,768]{1,0:T(8,128)}, f32[192,768]{1,0:T(8,128)}, f32[192,768]{1,0:T(8,128)}, f32[192,768]{1,0:T(8,128)}, /*index=5*/f32[192,768]{1,0:T(8,128)}) custom-call(s32[4]{0:T(128)S(1)} %pad_add_fusion.ids, bf16[400,768]{1,0:T(8,128)(2,1)S(1)} %get-tuple-element.240.attend.mine, ...), custom_call_target="tpu_custom_call" | custom-call | flops 40000000 | bytes 300000 | tf_op jit(solution)/shard_map/pallas_call | solution.py:37
  145.3 3.1 %shard_map.346 = (f32[768,768]{1,0:T(8,128)}, f32[768,768]{1,0:T(8,128)}, f32[192,768]{1,0:T(8,128)}, f32[192,768]{1,0:T(8,128)}, f32[192,768]{1,0:T(8,128)}, /*...) custom-call(s32[4]{0:T(128)S(1)} %pad_add_fusion.ids, ...), custom_call_target="tpu_custom_call", output_to_operand_aliasing={{0}: (4, {}), {1}: (5, {}), {2}: (6, {}), {3}: (7, {}), {4}... | custom-call | flops 40000000 | bytes 300000 | tf_op jit(solution)/shard_map/pallas_call | solution.py:37
  (104 shorter events, 9.1 us)
Async XLA Ops:
  0.7 6.5 %copy-start.8 = (f32[768]{0:T(1024)S(1)}, f32[768]{0:T(1024)}, u32[]{:S(2)}) copy-start(f32[768]{0:T(1024)} %param.28) | copy-start | bytes 9220
  0.7 6.5 %copy-start.15 = (f32[192]{0:T(256)S(1)}, f32[192]{0:T(256)}, u32[]{:S(2)}) copy-start(f32[192]{0:T(256)} %param.22) | copy-start | bytes 2308
  0.7 6.7 %copy-start.16 = (f32[192]{0:T(256)S(1)}, f32[192]{0:T(256)}, u32[]{:S(2)}) copy-start(f32[192]{0:T(256)} %param.25) | copy-start | bytes 2308
  0.7 7.5 %copy-start.6 = (f32[3,8]{1,0:T(4,128)S(1)}, f32[3,8]{1,0:T(4,128)}, u32[]{:S(2)}) copy-start(f32[3,8]{1,0:T(4,128)} %rel.1) | copy-start | bytes 292
  2.0 9.7 %collective-permute-start.2 = (bf16[128,768]{1,0:T(8,128)(2,1)S(1)}, bf16[128,768]{1,0:T(8,128)(2,1)S(1)}, u32[]{:S(2)}, u32[]{:S(2)}) collective-permute-start(bf16[128,768]{1,0:T(8,128)(2,1)S(1)} %get-tuple-element.264), channel_id=1, source_target_pairs={{0,24},{8,16},{16,8},{24,0},{1,25},{9,17},{17,9},{25,1},{2,26},{10... | collective-permute-start | bytes 589832 | tf_op jit(solution)/shard_map/ppermute | solution.py:65
  6.0 9.4 %collective-permute-start = (bf16[128,768]{1,0:T(8,128)(2,1)S(1)}, bf16[128,768]{1,0:T(8,128)(2,1)S(1)}, u32[]{:S(2)}, u32[]{:S(2)}) collective-permute-start(bf16[128,768]{1,0:T(8,128)(2,1)S(1)} %get-tuple-element.265), channel_id=1, source_target_pairs={{0,8},{8,0},{16,24},{24,16},{1,9},{9,1},{17,25},{25,17},{2,10},{10... | collective-permute-start | bytes 589832 | tf_op jit(solution)/shard_map/ppermute | solution.py:65
  6.5 8.9 %collective-permute-start.1 = (bf16[128,768]{1,0:T(8,128)(2,1)S(1)}, bf16[128,768]{1,0:T(8,128)(2,1)S(1)}, u32[]{:S(2)}, u32[]{:S(2)}) collective-permute-start(bf16[128,768]{1,0:T(8,128)(2,1)S(1)} %get-tuple-element.267), channel_id=1, source_target_pairs={{0,16},{8,24},{16,0},{24,8},{1,17},{9,25},{17,1},{25,9},{2,18},{10... | collective-permute-start | bytes 589832 | tf_op jit(solution)/shard_map/ppermute | solution.py:65
  8.2 7.2 %copy-start = (bf16[768,192]{0,1:T(8,128)(2,1)S(1)}, bf16[768,192]{0,1:T(8,128)(2,1)}, u32[]{:S(2)}) copy-start(bf16[768,192]{0,1:T(8,128)(2,1)} %param.21) | copy-start | bytes 884740
  8.2 7.2 %copy-start.1 = (bf16[768,192]{0,1:T(8,128)(2,1)S(1)}, bf16[768,192]{0,1:T(8,128)(2,1)}, u32[]{:S(2)}) copy-start(bf16[768,192]{0,1:T(8,128)(2,1)} %param.23) | copy-start | bytes 884740
  8.2 7.2 %copy-start.2 = (bf16[768,192]{0,1:T(8,128)(2,1)S(1)}, bf16[768,192]{0,1:T(8,128)(2,1)}, u32[]{:S(2)}) copy-start(bf16[768,192]{0,1:T(8,128)(2,1)} %param.24) | copy-start | bytes 884740
  8.2 7.2 %copy-start.3 = (bf16[192,768]{1,0:T(8,128)(2,1)S(1)}, bf16[192,768]{1,0:T(8,128)(2,1)}, u32[]{:S(2)}) copy-start(bf16[192,768]{1,0:T(8,128)(2,1)} %refs_5_.1) | copy-start | bytes 884740
  15.4 9.2 %copy-start.9 = (f32[768]{0:T(1024)S(1)}, f32[768]{0:T(1024)}, u32[]{:S(2)}) copy-start(f32[768]{0:T(1024)} %param.29) | copy-start | bytes 9220
  15.4 9.2 %copy-start.10 = (f32[768]{0:T(1024)S(1)}, f32[768]{0:T(1024)}, u32[]{:S(2)}) copy-start(f32[768]{0:T(1024)} %param.30) | copy-start | bytes 9220
  15.4 9.2 %copy-start.11 = (f32[768]{0:T(1024)S(1)}, f32[768]{0:T(1024)}, u32[]{:S(2)}) copy-start(f32[768]{0:T(1024)} %param.32) | copy-start | bytes 9220
  15.4 9.2 %copy-start.12 = (f32[768]{0:T(1024)S(1)}, f32[768]{0:T(1024)}, u32[]{:S(2)}) copy-start(f32[768]{0:T(1024)} %param.34) | copy-start | bytes 9220
  15.5 19.9 %copy-start.7 = (bf16[4,64,768]{2,1,0:T(8,128)(2,1)S(1)}, bf16[4,64,768]{2,1,0:T(8,128)(2,1)}, u32[]{:S(2)}) copy-start(bf16[4,64,768]{2,1,0:T(8,128)(2,1)} %param.37) | copy-start | bytes 1179652
  15.5 28.3 %copy-start.4 = (bf16[768,768]{1,0:T(8,128)(2,1)S(1)}, bf16[768,768]{1,0:T(8,128)(2,1)}, u32[]{:S(2)}) copy-start(bf16[768,768]{1,0:T(8,128)(2,1)} %refs_12_.1) | copy-start | bytes 3538948
  15.5 28.3 %copy-start.5 = (bf16[768,768]{1,0:T(8,128)(2,1)S(1)}, bf16[768,768]{1,0:T(8,128)(2,1)}, u32[]{:S(2)}) copy-start(bf16[768,768]{1,0:T(8,128)(2,1)} %refs_11_.1) | copy-start | bytes 3538948
  20.2 8.8 %collective-permute-start.3 = (bf16[64,768]{1,0:T(8,128)(2,1)S(1)}, bf16[64,768]{1,0:T(8,128)(2,1)S(1)}, u32[]{:S(2)}, u32[]{:S(2)}) collective-permute-start(bf16[64,768]{1,0:T(8,128)(2,1)S(1)} %get-tuple-element.141), channel_id=1, source_target_pairs={{0,2},{1,3},{2,0},{3,1},{4,6},{5,7},{6,4},{7,5},{8,10},{9,11},{10,... | collective-permute-start | bytes 294920 | tf_op jit(solution)/shard_map/ppermute | solution.py:65
  22.8 6.1 %collective-permute-start.4 = (bf16[64,768]{1,0:T(8,128)(2,1)S(1)}, bf16[64,768]{1,0:T(8,128)(2,1)S(1)}, u32[]{:S(2)}, u32[]{:S(2)}) collective-permute-start(bf16[64,768]{1,0:T(8,128)(2,1)S(1)} %get-tuple-element.142), channel_id=1, source_target_pairs={{0,1},{1,0},{2,3},{3,2},{4,5},{5,4},{6,7},{7,6},{8,9},{9,8},{10,11... | collective-permute-start | bytes 294920 | tf_op jit(solution)/shard_map/ppermute | solution.py:65
  24.4 6.6 %collective-permute-start.5 = (bf16[64,768]{1,0:T(8,128)(2,1)S(1)}, bf16[64,768]{1,0:T(8,128)(2,1)S(1)}, u32[]{:S(2)}, u32[]{:S(2)}) collective-permute-start(bf16[64,768]{1,0:T(8,128)(2,1)S(1)} %get-tuple-element.143), channel_id=1, source_target_pairs={{0,3},{1,2},{2,1},{3,0},{4,7},{5,6},{6,5},{7,4},{8,11},{9,10},{10,... | collective-permute-start | bytes 294920 | tf_op jit(solution)/shard_map/ppermute | solution.py:65
  31.1 11.2 %collective-permute-start.8 = (bf16[64,768]{1,0:T(8,128)(2,1)S(1)}, bf16[64,768]{1,0:T(8,128)(2,1)S(1)}, u32[]{:S(2)}, u32[]{:S(2)}) collective-permute-start(bf16[64,768]{1,0:T(8,128)(2,1)S(1)} %shard_map.324.a0), channel_id=1, source_target_pairs={{0,2},{1,3},{2,0},{3,1},{4,6},{5,7},{6,4},{7,5},{8,10},{9,11},{10,... | collective-permute-start | bytes 294920 | tf_op jit(solution)/shard_map/ppermute | solution.py:65
  34.7 9.0 %collective-permute-start.7 = (bf16[64,768]{1,0:T(8,128)(2,1)S(1)}, bf16[64,768]{1,0:T(8,128)(2,1)S(1)}, u32[]{:S(2)}, u32[]{:S(2)}) collective-permute-start(bf16[64,768]{1,0:T(8,128)(2,1)S(1)} %shard_map.324.a0), channel_id=1, source_target_pairs={{0,3},{1,2},{2,1},{3,0},{4,7},{5,6},{6,5},{7,4},{8,11},{9,10},{10,... | collective-permute-start | bytes 294920 | tf_op jit(solution)/shard_map/ppermute | solution.py:65
  35.2 8.5 %collective-permute-start.6 = (bf16[64,768]{1,0:T(8,128)(2,1)S(1)}, bf16[64,768]{1,0:T(8,128)(2,1)S(1)}, u32[]{:S(2)}, u32[]{:S(2)}) collective-permute-start(bf16[64,768]{1,0:T(8,128)(2,1)S(1)} %shard_map.324.a0), channel_id=1, source_target_pairs={{0,1},{1,0},{2,3},{3,2},{4,5},{5,4},{6,7},{7,6},{8,9},{9,8},{10,11... | collective-permute-start | bytes 294920 | tf_op jit(solution)/shard_map/ppermute | solution.py:65
  35.4 10.3 %collective-permute-start.11 = (bf16[64,768]{1,0:T(8,128)(2,1)S(1)}, bf16[64,768]{1,0:T(8,128)(2,1)S(1)}, u32[]{:S(2)}, u32[]{:S(2)}) collective-permute-start(bf16[64,768]{1,0:T(8,128)(2,1)S(1)} %get-tuple-element.268), channel_id=1, source_target_pairs={{0,24},{8,16},{16,8},{24,0},{1,25},{9,17},{17,9},{25,1},{2,26},{10... | collective-permute-start | bytes 294920 | tf_op jit(solution)/shard_map/ppermute | solution.py:65
  37.9 7.8 %collective-permute-start.10 = (bf16[64,768]{1,0:T(8,128)(2,1)S(1)}, bf16[64,768]{1,0:T(8,128)(2,1)S(1)}, u32[]{:S(2)}, u32[]{:S(2)}) collective-permute-start(bf16[64,768]{1,0:T(8,128)(2,1)S(1)} %get-tuple-element.269), channel_id=1, source_target_pairs={{0,16},{8,24},{16,0},{24,8},{1,17},{9,25},{17,1},{25,9},{2,18},{10... | collective-permute-start | bytes 294920 | tf_op jit(solution)/shard_map/ppermute | solution.py:65
  42.2 18.2 %copy-start.13 = (f32[768]{0:T(1024)S(1)}, f32[768]{0:T(1024)}, u32[]{:S(2)}) copy-start(f32[768]{0:T(1024)} %param.35) | copy-start | bytes 9220
  42.2 18.2 %copy-start.14 = (f32[768]{0:T(1024)S(1)}, f32[768]{0:T(1024)}, u32[]{:S(2)}) copy-start(f32[768]{0:T(1024)} %param.36) | copy-start | bytes 9220
  42.2 4.6 %collective-permute-start.9 = (bf16[64,768]{1,0:T(8,128)(2,1)S(1)}, bf16[64,768]{1,0:T(8,128)(2,1)S(1)}, u32[]{:S(2)}, u32[]{:S(2)}) collective-permute-start(bf16[64,768]{1,0:T(8,128)(2,1)S(1)} %get-tuple-element.270), channel_id=1, source_target_pairs={{0,8},{8,0},{16,24},{24,16},{1,9},{9,1},{17,25},{25,17},{2,10},{10... | collective-permute-start | bytes 294920 | tf_op jit(solution)/shard_map/ppermute | solution.py:65
  46.9 7.9 %collective-permute-start.12 = (bf16[64,768]{1,0:T(8,128)(2,1)S(1)}, bf16[64,768]{1,0:T(8,128)(2,1)S(1)}, u32[]{:S(2)}, u32[]{:S(2)}) collective-permute-start(bf16[64,768]{1,0:T(8,128)(2,1)S(1)} %get-tuple-element.155), channel_id=1, source_target_pairs={{0,2},{1,3},{2,0},{3,1},{4,6},{5,7},{6,4},{7,5},{8,10},{9,11},{10,... | collective-permute-start | bytes 294920 | tf_op jit(solution)/shard_map/ppermute | solution.py:65
  46.9 7.9 %collective-permute-start.13 = (bf16[64,768]{1,0:T(8,128)(2,1)S(1)}, bf16[64,768]{1,0:T(8,128)(2,1)S(1)}, u32[]{:S(2)}, u32[]{:S(2)}) collective-permute-start(bf16[64,768]{1,0:T(8,128)(2,1)S(1)} %get-tuple-element.156), channel_id=1, source_target_pairs={{0,1},{1,0},{2,3},{3,2},{4,5},{5,4},{6,7},{7,6},{8,9},{9,8},{10,11... | collective-permute-start | bytes 294920 | tf_op jit(solution)/shard_map/ppermute | solution.py:65
  49.3 6.6 %collective-permute-start.14 = (bf16[64,768]{1,0:T(8,128)(2,1)S(1)}, bf16[64,768]{1,0:T(8,128)(2,1)S(1)}, u32[]{:S(2)}, u32[]{:S(2)}) collective-permute-start(bf16[64,768]{1,0:T(8,128)(2,1)S(1)} %get-tuple-element.157), channel_id=1, source_target_pairs={{0,3},{1,2},{2,1},{3,0},{4,7},{5,6},{6,5},{7,4},{8,11},{9,10},{10,... | collective-permute-start | bytes 294920 | tf_op jit(solution)/shard_map/ppermute | solution.py:65
  55.9 7.9 %collective-permute-start.17 = (bf16[64,768]{1,0:T(8,128)(2,1)S(1)}, bf16[64,768]{1,0:T(8,128)(2,1)S(1)}, u32[]{:S(2)}, u32[]{:S(2)}) collective-permute-start(bf16[64,768]{1,0:T(8,128)(2,1)S(1)} %shard_map.326.refs_0_), channel_id=1, source_target_pairs={{0,2},{1,3},{2,0},{3,1},{4,6},{5,7},{6,4},{7,5},{8,10},{9,11},{10,... | collective-permute-start | bytes 294920 | tf_op jit(solution)/shard_map/ppermute | solution.py:65
  58.3 6.7 %collective-permute-start.16 = (bf16[64,768]{1,0:T(8,128)(2,1)S(1)}, bf16[64,768]{1,0:T(8,128)(2,1)S(1)}, u32[]{:S(2)}, u32[]{:S(2)}) collective-permute-start(bf16[64,768]{1,0:T(8,128)(2,1)S(1)} %shard_map.326.refs_0_), channel_id=1, source_target_pairs={{0,1},{1,0},{2,3},{3,2},{4,5},{5,4},{6,7},{7,6},{8,9},{9,8},{10,11... | collective-permute-start | bytes 294920 | tf_op jit(solution)/shard_map/ppermute | solution.py:65
  58.5 6.6 %collective-permute-start.15 = (bf16[64,768]{1,0:T(8,128)(2,1)S(1)}, bf16[64,768]{1,0:T(8,128)(2,1)S(1)}, u32[]{:S(2)}, u32[]{:S(2)}) collective-permute-start(bf16[64,768]{1,0:T(8,128)(2,1)S(1)} %shard_map.326.refs_0_), channel_id=1, source_target_pairs={{0,3},{1,2},{2,1},{3,0},{4,7},{5,6},{6,5},{7,4},{8,11},{9,10},{10,... | collective-permute-start | bytes 294920 | tf_op jit(solution)/shard_map/ppermute | solution.py:65
  67.3 6.8 %collective-permute-start.18 = (bf16[64,768]{1,0:T(8,128)(2,1)S(1)}, bf16[64,768]{1,0:T(8,128)(2,1)S(1)}, u32[]{:S(2)}, u32[]{:S(2)}) collective-permute-start(bf16[64,768]{1,0:T(8,128)(2,1)S(1)} %get-tuple-element.167), channel_id=1, source_target_pairs={{0,2},{1,3},{2,0},{3,1},{4,6},{5,7},{6,4},{7,5},{8,10},{9,11},{10,... | collective-permute-start | bytes 294920 | tf_op jit(solution)/shard_map/ppermute | solution.py:65
  69.0 5.1 %collective-permute-start.19 = (bf16[64,768]{1,0:T(8,128)(2,1)S(1)}, bf16[64,768]{1,0:T(8,128)(2,1)S(1)}, u32[]{:S(2)}, u32[]{:S(2)}) collective-permute-start(bf16[64,768]{1,0:T(8,128)(2,1)S(1)} %get-tuple-element.168), channel_id=1, source_target_pairs={{0,1},{1,0},{2,3},{3,2},{4,5},{5,4},{6,7},{7,6},{8,9},{9,8},{10,11... | collective-permute-start | bytes 294920 | tf_op jit(solution)/shard_map/ppermute | solution.py:65
  70.0 6.4 %collective-permute-start.20 = (bf16[64,768]{1,0:T(8,128)(2,1)S(1)}, bf16[64,768]{1,0:T(8,128)(2,1)S(1)}, u32[]{:S(2)}, u32[]{:S(2)}) collective-permute-start(bf16[64,768]{1,0:T(8,128)(2,1)S(1)} %get-tuple-element.169), channel_id=1, source_target_pairs={{0,3},{1,2},{2,1},{3,0},{4,7},{5,6},{6,5},{7,4},{8,11},{9,10},{10,... | collective-permute-start | bytes 294920 | tf_op jit(solution)/shard_map/ppermute | solution.py:65
  72.9 7.1 %collective-permute-start.33 = (bf16[768,768]{1,0:T(8,128)(2,1)S(1)}, bf16[768,768]{1,0:T(8,128)(2,1)S(1)}, u32[]{:S(2)}, u32[]{:S(2)}) collective-permute-start(bf16[768,768]{1,0:T(8,128)(2,1)S(1)} %shard_map.336), channel_id=1, source_target_pairs={{0,4},{4,0},{1,5},{5,1},{2,6},{6,2},{3,7},{7,3},{8,12},{12,8},{9,1... | collective-permute-start | bytes 3538952 | tf_op jit(solution)/shard_map/ppermute | solution.py:65
  76.5 8.1 %collective-permute-start.23 = (bf16[64,768]{1,0:T(8,128)(2,1)S(1)}, bf16[64,768]{1,0:T(8,128)(2,1)S(1)}, u32[]{:S(2)}, u32[]{:S(2)}) collective-permute-start(bf16[64,768]{1,0:T(8,128)(2,1)S(1)} %shard_map.328.refs_0_), channel_id=1, source_target_pairs={{0,2},{1,3},{2,0},{3,1},{4,6},{5,7},{6,4},{7,5},{8,10},{9,11},{10,... | collective-permute-start | bytes 294920 | tf_op jit(solution)/shard_map/ppermute | solution.py:65
  76.5 8.0 %collective-permute-start.22 = (bf16[64,768]{1,0:T(8,128)(2,1)S(1)}, bf16[64,768]{1,0:T(8,128)(2,1)S(1)}, u32[]{:S(2)}, u32[]{:S(2)}) collective-permute-start(bf16[64,768]{1,0:T(8,128)(2,1)S(1)} %shard_map.328.refs_0_), channel_id=1, source_target_pairs={{0,3},{1,2},{2,1},{3,0},{4,7},{5,6},{6,5},{7,4},{8,11},{9,10},{10,... | collective-permute-start | bytes 294920 | tf_op jit(solution)/shard_map/ppermute | solution.py:65
  78.5 6.5 %collective-permute-start.21 = (bf16[64,768]{1,0:T(8,128)(2,1)S(1)}, bf16[64,768]{1,0:T(8,128)(2,1)S(1)}, u32[]{:S(2)}, u32[]{:S(2)}) collective-permute-start(bf16[64,768]{1,0:T(8,128)(2,1)S(1)} %shard_map.328.refs_0_), channel_id=1, source_target_pairs={{0,1},{1,0},{2,3},{3,2},{4,5},{5,4},{6,7},{7,6},{8,9},{9,8},{10,11... | collective-permute-start | bytes 294920 | tf_op jit(solution)/shard_map/ppermute | solution.py:65
  81.5 8.2 %collective-permute-start.34 = (bf16[192,768]{1,0:T(8,128)(2,1)S(1)}, bf16[192,768]{1,0:T(8,128)(2,1)S(1)}, u32[]{:S(2)}, u32[]{:S(2)}) collective-permute-start(bf16[192,768]{1,0:T(8,128)(2,1)S(1)} %get-tuple-element.211), channel_id=1, source_target_pairs={{0,8},{8,0},{16,24},{24,16},{1,9},{9,1},{17,25},{25,17},{2,10},{10... | collective-permute-start | bytes 884744 | tf_op jit(solution)/shard_map/ppermute | solution.py:65
  83.0 6.7 %collective-permute-start.35 = (bf16[192,768]{1,0:T(8,128)(2,1)S(1)}, bf16[192,768]{1,0:T(8,128)(2,1)S(1)}, u32[]{:S(2)}, u32[]{:S(2)}) collective-permute-start(bf16[192,768]{1,0:T(8,128)(2,1)S(1)} %get-tuple-element.212), channel_id=1, source_target_pairs={{0,16},{8,24},{16,0},{24,8},{1,17},{9,25},{17,1},{25,9},{2,18},{10... | collective-permute-start | bytes 884744 | tf_op jit(solution)/shard_map/ppermute | solution.py:65
  91.2 6.6 %collective-permute-start.36 = (bf16[400,768]{1,0:T(8,128)(2,1)S(1)}, bf16[400,768]{1,0:T(8,128)(2,1)S(1)}, u32[]{:S(2)}, u32[]{:S(2)}) collective-permute-start(bf16[400,768]{1,0:T(8,128)(2,1)S(1)} %get-tuple-element.220), channel_id=1, source_target_pairs={{0,4},{4,0},{1,5},{5,1},{2,6},{6,2},{3,7},{7,3},{8,12},{12,8},{9,1... | collective-permute-start | bytes 1843208 | tf_op jit(solution)/shard_map/ppermute | solution.py:65
  91.2 10.7 %collective-permute-start.24 = (bf16[128,768]{1,0:T(8,128)(2,1)S(1)}, bf16[128,768]{1,0:T(8,128)(2,1)S(1)}, u32[]{:S(2)}, u32[]{:S(2)}) collective-permute-start(bf16[128,768]{1,0:T(8,128)(2,1)S(1)} %get-tuple-element.185), channel_id=1, source_target_pairs={{0,1},{1,0},{2,3},{3,2},{4,5},{5,4},{6,7},{7,6},{8,9},{9,8},{10,11... | collective-permute-start | bytes 589832 | tf_op jit(solution)/shard_map/ppermute | solution.py:65
  92.3 17.1 %collective-permute-start.25 = (bf16[128,768]{1,0:T(8,128)(2,1)S(1)}, bf16[128,768]{1,0:T(8,128)(2,1)S(1)}, u32[]{:S(2)}, u32[]{:S(2)}) collective-permute-start(bf16[128,768]{1,0:T(8,128)(2,1)S(1)} %get-tuple-element.186), channel_id=1, source_target_pairs={{0,2},{1,3},{2,0},{3,1},{4,6},{5,7},{6,4},{7,5},{8,10},{9,11},{10,... | collective-permute-start | bytes 589832 | tf_op jit(solution)/shard_map/ppermute | solution.py:65
  93.7 15.7 %collective-permute-start.26 = (bf16[128,768]{1,0:T(8,128)(2,1)S(1)}, bf16[128,768]{1,0:T(8,128)(2,1)S(1)}, u32[]{:S(2)}, u32[]{:S(2)}) collective-permute-start(bf16[128,768]{1,0:T(8,128)(2,1)S(1)} %get-tuple-element.187), channel_id=1, source_target_pairs={{0,3},{1,2},{2,1},{3,0},{4,7},{5,6},{6,5},{7,4},{8,11},{9,10},{10,... | collective-permute-start | bytes 589832 | tf_op jit(solution)/shard_map/ppermute | solution.py:65
  98.8 14.3 %collective-permute-start.37 = (bf16[208,768]{1,0:T(8,128)(2,1)S(1)}, bf16[208,768]{1,0:T(8,128)(2,1)S(1)}, u32[]{:S(2)}, u32[]{:S(2)}) collective-permute-start(bf16[208,768]{1,0:T(8,128)(2,1)S(1)} %get-tuple-element.227.sent1), channel_id=1, source_target_pairs={{0,8},{8,0},{16,24},{24,16},{1,9},{9,1},{17,25},{25,17},{2,10},{10... | collective-permute-start | bytes 958472 | tf_op jit(solution)/shard_map/ppermute | solution.py:65
  100.2 12.9 %collective-permute-start.38 = (bf16[192,768]{1,0:T(8,128)(2,1)S(1)}, bf16[192,768]{1,0:T(8,128)(2,1)S(1)}, u32[]{:S(2)}, u32[]{:S(2)}) collective-permute-start(bf16[192,768]{1,0:T(8,128)(2,1)S(1)} %get-tuple-element.228), channel_id=1, source_target_pairs={{0,16},{8,24},{16,0},{24,8},{1,17},{9,25},{17,1},{25,9},{2,18},{10... | collective-permute-start | bytes 884744 | tf_op jit(solution)/shard_map/ppermute | solution.py:65
  109.5 8.0 %collective-permute-start.27 = (bf16[96,768]{1,0:T(8,128)(2,1)S(1)}, bf16[96,768]{1,0:T(8,128)(2,1)S(1)}, u32[]{:S(2)}, u32[]{:S(2)}) collective-permute-start(bf16[96,768]{1,0:T(8,128)(2,1)S(1)} %get-tuple-element.195), channel_id=1, source_target_pairs={{0,16},{8,24},{16,0},{24,8},{1,17},{9,25},{17,1},{25,9},{2,18},{10... | collective-permute-start | bytes 442376 | tf_op jit(solution)/shard_map/ppermute | solution.py:65
  111.1 6.8 %collective-permute-start.28 = (bf16[96,768]{1,0:T(8,128)(2,1)S(1)}, bf16[96,768]{1,0:T(8,128)(2,1)S(1)}, u32[]{:S(2)}, u32[]{:S(2)}) collective-permute-start(bf16[96,768]{1,0:T(8,128)(2,1)S(1)} %get-tuple-element.196), channel_id=1, source_target_pairs={{0,8},{8,0},{16,24},{24,16},{1,9},{9,1},{17,25},{25,17},{2,10},{10... | collective-permute-start | bytes 442376 | tf_op jit(solution)/shard_map/ppermute | solution.py:65
  112.6 8.3 %collective-permute-start.29 = (bf16[96,768]{1,0:T(8,128)(2,1)S(1)}, bf16[96,768]{1,0:T(8,128)(2,1)S(1)}, u32[]{:S(2)}, u32[]{:S(2)}) collective-permute-start(bf16[96,768]{1,0:T(8,128)(2,1)S(1)} %get-tuple-element.197), channel_id=1, source_target_pairs={{0,24},{8,16},{16,8},{24,0},{1,25},{9,17},{17,9},{25,1},{2,26},{10... | collective-permute-start | bytes 442376 | tf_op jit(solution)/shard_map/ppermute | solution.py:65
  113.2 13.9 %collective-permute-start.40 = (bf16[256,768]{1,0:T(8,128)(2,1)S(1)}, bf16[256,768]{1,0:T(8,128)(2,1)S(1)}, u32[]{:S(2)}, u32[]{:S(2)}) collective-permute-start(bf16[256,768]{1,0:T(8,128)(2,1)S(1)} %get-tuple-element.231.sent2), channel_id=1, source_target_pairs={{0,16},{8,24},{16,0},{24,8},{1,17},{9,25},{17,1},{25,9},{2,18},{10... | collective-permute-start | bytes 1179656 | tf_op jit(solution)/shard_map/ppermute | solution.py:65
  114.8 12.3 %collective-permute-start.39 = (bf16[240,768]{1,0:T(8,128)(2,1)S(1)}, bf16[240,768]{1,0:T(8,128)(2,1)S(1)}, u32[]{:S(2)}, u32[]{:S(2)}) collective-permute-start(bf16[240,768]{1,0:T(8,128)(2,1)S(1)} %get-tuple-element.232.sent1), channel_id=1, source_target_pairs={{0,8},{8,0},{16,24},{24,16},{1,9},{9,1},{17,25},{25,17},{2,10},{10... | collective-permute-start | bytes 1105928 | tf_op jit(solution)/shard_map/ppermute | solution.py:65
  120.9 17.1 %collective-permute-start.32 = (bf16[128,768]{1,0:T(8,128)(2,1)S(1)}, bf16[128,768]{1,0:T(8,128)(2,1)S(1)}, u32[]{:S(2)}, u32[]{:S(2)}) collective-permute-start(bf16[128,768]{1,0:T(8,128)(2,1)S(1)} %shard_map.334.t0), channel_id=1, source_target_pairs={{0,2},{1,3},{2,0},{3,1},{4,6},{5,7},{6,4},{7,5},{8,10},{9,11},{10,... | collective-permute-start | bytes 589832 | tf_op jit(solution)/shard_map/ppermute | solution.py:65
  125.0 13.0 %collective-permute-start.31 = (bf16[128,768]{1,0:T(8,128)(2,1)S(1)}, bf16[128,768]{1,0:T(8,128)(2,1)S(1)}, u32[]{:S(2)}, u32[]{:S(2)}) collective-permute-start(bf16[128,768]{1,0:T(8,128)(2,1)S(1)} %shard_map.334.t0), channel_id=1, source_target_pairs={{0,3},{1,2},{2,1},{3,0},{4,7},{5,6},{6,5},{7,4},{8,11},{9,10},{10,... | collective-permute-start | bytes 589832 | tf_op jit(solution)/shard_map/ppermute | solution.py:65
  127.1 10.9 %collective-permute-start.30 = (bf16[128,768]{1,0:T(8,128)(2,1)S(1)}, bf16[128,768]{1,0:T(8,128)(2,1)S(1)}, u32[]{:S(2)}, u32[]{:S(2)}) collective-permute-start(bf16[128,768]{1,0:T(8,128)(2,1)S(1)} %shard_map.334.t0), channel_id=1, source_target_pairs={{0,1},{1,0},{2,3},{3,2},{4,5},{5,4},{6,7},{7,6},{8,9},{9,8},{10,11... | collective-permute-start | bytes 589832 | tf_op jit(solution)/shard_map/ppermute | solution.py:65
  127.2 4.7 %collective-permute-start.41 = (bf16[48,768]{1,0:T(8,128)(2,1)S(1)}, bf16[48,768]{1,0:T(8,128)(2,1)S(1)}, u32[]{:S(2)}, u32[]{:S(2)}) collective-permute-start(bf16[48,768]{1,0:T(8,128)(2,1)S(1)} %get-tuple-element.234.mid1), channel_id=1, source_target_pairs={{0,8},{8,0},{16,24},{24,16},{1,9},{9,1},{17,25},{25,17},{2,10},{10... | collective-permute-start | bytes 221192 | tf_op jit(solution)/shard_map/ppermute | solution.py:65
  129.0 4.9 %collective-permute-start.42 = (bf16[48,768]{1,0:T(8,128)(2,1)S(1)}, bf16[48,768]{1,0:T(8,128)(2,1)S(1)}, u32[]{:S(2)}, u32[]{:S(2)}) collective-permute-start(bf16[48,768]{1,0:T(8,128)(2,1)S(1)} %get-tuple-element.235.mid2), channel_id=1, source_target_pairs={{0,16},{8,24},{16,0},{24,8},{1,17},{9,25},{17,1},{25,9},{2,18},{10... | collective-permute-start | bytes 221192 | tf_op jit(solution)/shard_map/ppermute | solution.py:65
  133.9 6.8 %collective-permute-start.43 = (bf16[192,768]{1,0:T(8,128)(2,1)S(1)}, bf16[192,768]{1,0:T(8,128)(2,1)S(1)}, u32[]{:S(2)}, u32[]{:S(2)}) collective-permute-start(bf16[192,768]{1,0:T(8,128)(2,1)S(1)} %get-tuple-element.236.along1), channel_id=1, source_target_pairs={{0,8},{8,0},{16,24},{24,16},{1,9},{9,1},{17,25},{25,17},{2,10},{10... | collective-permute-start | bytes 884744 | tf_op jit(solution)/shard_map/ppermute | solution.py:65
  134.0 6.8 %collective-permute-start.44 = (bf16[192,768]{1,0:T(8,128)(2,1)S(1)}, bf16[192,768]{1,0:T(8,128)(2,1)S(1)}, u32[]{:S(2)}, u32[]{:S(2)}) collective-permute-start(bf16[192,768]{1,0:T(8,128)(2,1)S(1)} %get-tuple-element.237.along2), channel_id=1, source_target_pairs={{0,16},{8,24},{16,0},{24,8},{1,17},{9,25},{17,1},{25,9},{2,18},{10... | collective-permute-start | bytes 884744 | tf_op jit(solution)/shard_map/ppermute | solution.py:65
  141.5 3.8 %collective-permute-start.46 = (bf16[768,768]{1,0:T(8,128)(2,1)S(1)}, bf16[768,768]{1,0:T(8,128)(2,1)S(1)}, u32[]{:S(2)}, u32[]{:S(2)}) collective-permute-start(bf16[768,768]{1,0:T(8,128)(2,1)S(1)} %get-tuple-element.241.feed), channel_id=1, source_target_pairs={{0,4},{4,0},{1,5},{5,1},{2,6},{6,2},{3,7},{7,3},{8,12},{12,8},{9,1... | collective-permute-start | bytes 3538952 | tf_op jit(solution)/shard_map/ppermute | solution.py:65
  141.6 3.7 %collective-permute-start.45 = (bf16[400,768]{1,0:T(8,128)(2,1)S(1)}, bf16[400,768]{1,0:T(8,128)(2,1)S(1)}, u32[]{:S(2)}, u32[]{:S(2)}) collective-permute-start(bf16[400,768]{1,0:T(8,128)(2,1)S(1)} %get-tuple-element.240.attend.mine), channel_id=1, source_target_pairs={{0,4},{4,0},{1,5},{5,1},{2,6},{6,2},{3,7},{7,3},{8,12},{12,8},{9,1... | collective-permute-start | bytes 1843208 | tf_op jit(solution)/shard_map/ppermute | solution.py:65
  (1 other events, 6.0 us)
